TPU v7x, 256 devices: a whole 4x4x8 slice. The times are simulated.
256 devices in a mesh: dp: 16 (over x_lo, z), tensor: 16 (over y, x_hi, core).
Axes of the slice: x: 4 (x_hi: 2, x_lo: 2; x = x_hi * 2 + x_lo), y: 4, z: 8, core: 2. Of those that a mesh axis runs over, the one named last changes fastest.
Arguments:
- tokens: bfloat16 [2048, 65536], P('dp', 'tensor'), may hold values from -6 to 6
- cotangent: bfloat16 [2048, 65536], P('dp', 'tensor'), may hold values from -6 to 6
- diag_factor: bfloat16 [64, 65536], P(None, 'tensor'), may hold values from -0.3125 to 0.3125
- section_factors: bfloat16 [4, 64, 65536], P(None, None, 'tensor'), may hold values from -0.3125 to 0.3125
- low_down: bfloat16 [65536, 128], P('tensor'), may hold values from -0.0234375 to 0.0234375
- low_up: bfloat16 [128, 65536], P(None, 'tensor'), may hold values from -0.21875 to 0.21875
Outputs:
- token_grad: bfloat16 [2048, 65536], P('dp', 'tensor')
- diag_grad: float32 [64, 65536], P(None, ('tensor', 'dp'))
- section_grad: float32 [4, 64, 65536], P(None, None, ('tensor', 'dp'))
- low_down_grad: float32 [65536, 128], P(('tensor', 'dp'))
- low_up_grad: float32 [128, 65536], P(None, ('tensor', 'dp'))
All inputs are finite; a program needn't handle non-finite values.
Results may differ from a plain program's by a relative error of at most 0.0057.
Values may be sent and summed in bfloat16 or wider, within the bound.
No kernel may reach another device: no remote copies, remote signals or barrier semaphores. Data moves between devices by JAX's collectives and lax.ppermute only.
A program may use at most 128 MiB of HBM per device.

v0:
```python
import jax
import jax.numpy as jnp
from jax import lax
from jax.experimental import pallas as pl
from jax.experimental.pallas import tpu as pltpu
from jax.sharding import PartitionSpec as P

BLOCK = 64
CHUNK = 256
STEP = 512
RING = 8
VMEM = 56 << 20
F32 = jnp.float32
BF16 = jnp.bfloat16


def dot(a, b, ca, cb):
    return lax.dot_general(a, b, (((ca,), (cb,)), ((), ())), preferred_element_type=F32)


def gelu_slope(values):
    return (
        0.5 * (1.0 + lax.erf(values * 0.7071067811865476))
        + values * jnp.exp(-0.5 * values * values) * 0.3989422804014327
    )


def block_mask():
    row = lax.broadcasted_iota(jnp.int32, (CHUNK, CHUNK), 0) // BLOCK
    col = lax.broadcasted_iota(jnp.int32, (CHUNK, CHUNK), 1) // BLOCK
    return row == col


def spread(factor, mask):
    tall = jnp.concatenate([factor] * (CHUNK // BLOCK), axis=0)
    return jnp.where(mask, tall, jnp.zeros_like(tall))


def slope_kernel(tok, m1, m2, m4, m8, cot, diag, sec, latent, up, slope_out, lat_out):
    mask = block_mask()
    lat = latent[...]
    lat_sum = jnp.zeros((lat.shape[0], up.shape[0]), F32)
    for c in range(STEP // CHUNK):
        cs = slice(c * CHUNK, (c + 1) * CHUNK)
        up_c = up[:, cs]
        factors = [spread(diag[:, cs], mask)] + [spread(sec[b, :, cs], mask) for b in range(4)]
        left = jnp.concatenate([tok[:, cs], m1[:, cs], m2[:, cs], m4[:, cs], m8[:, cs], lat], axis=1)
        right = jnp.concatenate(factors + [up_c], axis=0)
        pre = dot(left, right, 1, 0)
        slope = (cot[:, cs].astype(F32) * gelu_slope(pre)).astype(BF16)
        slope_out[:, cs] = slope
        lat_sum = lat_sum + dot(slope, up_c, 1, 1)

    @pl.when(pl.program_id(0) == 0)
    def _():
        lat_out[...] = lat_sum

    @pl.when(pl.program_id(0) > 0)
    def _():
        lat_out[...] += lat_sum


def outer_kernel(slope_in, tok, m1, m2, m4, m8, latent, *refs):
    grads = refs[-1]
    rows = tok.shape[0]
    lat = latent[...]
    group = CHUNK // BLOCK
    owner = lax.broadcasted_iota(jnp.int32, (group * rows, CHUNK), 0) // rows
    tall_mask = owner == lax.broadcasted_iota(jnp.int32, (group * rows, CHUNK), 1) // BLOCK
    for c in range(STEP // CHUNK):
        cs = slice(c * CHUNK, (c + 1) * CHUNK)
        slope = slope_in[:, cs]
        tall = jnp.concatenate([slope] * group, axis=0)
        tall = jnp.where(tall_mask, tall, jnp.zeros_like(tall))
        for k, side in enumerate((tok, m1, m2, m4, m8)):
            turned = side[:, cs].T
            wide = jnp.concatenate([turned[i * BLOCK : (i + 1) * BLOCK] for i in range(group)], axis=1)
            grads[c, 0, k * BLOCK : (k + 1) * BLOCK, :] = dot(wide, tall, 1, 0).astype(BF16)
        grads[c, 0, 5 * BLOCK :, :] = dot(lat, slope, 0, 0).astype(BF16)


def pick_half(low, high):
    first = pl.program_id(0) < pl.num_programs(0) // 2
    return jnp.where(first, low[...], high[...])


def half_specs(rows, steps):
    half = steps // 2
    return [
        pl.BlockSpec((rows, STEP), lambda i: (0, jnp.minimum(i, half - 1))),
        pl.BlockSpec((rows, STEP), lambda i: (0, jnp.maximum(i - half, 0))),
    ]


def back_kernel(low, high, sec, b1, b2, b4, b8):
    mask = block_mask()
    slope = pick_half(low, high)
    for c in range(STEP // CHUNK):
        cs = slice(c * CHUNK, (c + 1) * CHUNK)
        for b, ref in enumerate((b1, b2, b4, b8)):
            ref[:, cs] = dot(slope[:, cs], spread(sec[b, :, cs], mask), 1, 1).astype(BF16)


def run_back(slopes, section):
    rows = slopes[0].shape[0]
    width = section.shape[2]
    steps = width // STEP
    return pl.pallas_call(
        back_kernel,
        grid=(steps,),
        in_specs=half_specs(rows, steps) + [pl.BlockSpec((4, BLOCK, STEP), lambda i: (0, 0, i))],
        out_specs=[pl.BlockSpec((rows, STEP), lambda i: (0, i))] * 4,
        out_shape=[jax.ShapeDtypeStruct((rows, width), BF16)] * 4,
        compiler_params=pltpu.CompilerParams(vmem_limit_bytes=VMEM),
        cost_estimate=pl.CostEstimate(flops=3_000_000_000, bytes_accessed=7 << 20, transcendentals=0),
        name="back_products",
    )(*slopes, section)


def specs_of(part, rows, width, rank):
    steps = width // STEP
    base = part * steps
    whole = lambda r: pl.BlockSpec((r, STEP), lambda i: (0, base + i))
    local = pl.BlockSpec((rows, STEP), lambda i: (0, i))
    square = pl.BlockSpec((rows, rank), lambda i: (0, 0))
    section = pl.BlockSpec((4, BLOCK, STEP), lambda i: (0, 0, base + i))
    return steps, whole, local, square, section


def run_slope(part, tokens, moved, cotangent, diag, section, latent, up):
    rows, width = moved[2].shape
    rank = up.shape[0]
    steps, whole, local, square, sec_spec = specs_of(part, rows, width, rank)
    return pl.pallas_call(
        slope_kernel,
        grid=(steps,),
        in_specs=[whole(rows), whole(rows), local, local, local, whole(rows), whole(BLOCK), sec_spec, square, whole(rank)],
        out_specs=[local, square],
        out_shape=[jax.ShapeDtypeStruct((rows, width), BF16), jax.ShapeDtypeStruct((rows, rank), F32)],
        compiler_params=pltpu.CompilerParams(vmem_limit_bytes=VMEM),
        cost_estimate=pl.CostEstimate(flops=2_000_000_000, bytes_accessed=6 << 20, transcendentals=0),
        name="slope_part",
    )(tokens, *moved, cotangent, diag, section, latent, up)


def run_outer(part, slope, tokens, moved, latent, held):
    rows, width = slope.shape
    rank = latent.shape[1]
    steps, whole, local, square, _ = specs_of(part, rows, width, rank)
    per = STEP // CHUNK
    grad_rows = 5 * BLOCK + rank
    in_specs = [local, whole(rows), whole(rows), local, local, local, square]
    args = [slope, tokens, *moved, latent]
    if held is not None:
        in_specs.append(pl.BlockSpec(memory_space=pl.ANY))
        args.append(held)
    return pl.pallas_call(
        outer_kernel,
        grid=(steps,),
        in_specs=in_specs,
        out_specs=pl.BlockSpec((per, 1, grad_rows, CHUNK), lambda i: (i, part, 0, 0)),
        out_shape=jax.ShapeDtypeStruct((RING, 2, grad_rows, CHUNK), BF16),
        input_output_aliases={} if held is None else {7: 0},
        compiler_params=pltpu.CompilerParams(vmem_limit_bytes=VMEM),
        cost_estimate=pl.CostEstimate(flops=2_000_000_000, bytes_accessed=5 << 20, transcendentals=0),
        name="outer_part",
    )(*args)


def down_kernel(tok, lat, out):
    for c in range(tok.shape[1] // CHUNK):
        full = dot(tok[:, c * CHUNK : (c + 1) * CHUNK], lat[...], 0, 0)
        half = CHUNK // 2
        out[c] = jnp.concatenate([full[:half], full[half:]], axis=1).astype(BF16)


def run_down(tokens, latent_grad):
    rows, width = tokens.shape
    rank = latent_grad.shape[1]
    wide = 1024
    return pl.pallas_call(
        down_kernel,
        grid=(width // wide,),
        in_specs=[pl.BlockSpec((rows, wide), lambda i: (0, i)), pl.BlockSpec((rows, rank), lambda i: (0, 0))],
        out_specs=pl.BlockSpec((wide // CHUNK, CHUNK // 2, 2 * rank), lambda i: (i, 0, 0)),
        out_shape=jax.ShapeDtypeStruct((width // CHUNK, CHUNK // 2, 2 * rank), BF16),
        cost_estimate=pl.CostEstimate(flops=300_000_000, bytes_accessed=2 << 20, transcendentals=0),
        name="down_part",
    )(tokens, latent_grad)


def final_kernel(low, high, r1, r2, r4, r8, diag, down, lat, out):
    mask = block_mask()
    slope = pick_half(low, high)
    for c in range(STEP // CHUNK):
        cs = slice(c * CHUNK, (c + 1) * CHUNK)
        total = dot(slope[:, cs], spread(diag[:, cs], mask), 1, 1)
        total = total + dot(lat[...], down[cs, :], 1, 1)
        for ref in (r1, r2, r4, r8):
            total = total + ref[:, cs].astype(F32)
        out[:, cs] = total.astype(BF16)


def run_final(slopes, received, diag, low_down, latent_grad):
    rows, width = received[0].shape
    rank = latent_grad.shape[1]
    steps = width // STEP
    col = lambda r: pl.BlockSpec((r, STEP), lambda i: (0, i))
    return pl.pallas_call(
        final_kernel,
        grid=(steps,),
        in_specs=half_specs(rows, steps)
        + [col(rows)] * 4
        + [
            col(BLOCK),
            pl.BlockSpec((STEP, rank), lambda i: (i, 0)),
            pl.BlockSpec((rows, rank), lambda i: (0, 0)),
        ],
        out_specs=col(rows),
        out_shape=jax.ShapeDtypeStruct((rows, width), BF16),
        compiler_params=pltpu.CompilerParams(vmem_limit_bytes=VMEM),
        cost_estimate=pl.CostEstimate(flops=2_000_000_000, bytes_accessed=9 << 20, transcendentals=0),
        name="token_grad",
    )(*slopes, *received, diag, low_down, latent_grad)


def flip(value, mask):
    return lax.ppermute(value, "tensor", [(i, i ^ mask) for i in range(16)])


def after(value, *events):
    return lax.optimization_barrier((value, *events))[0]


def ring_sum(grads):
    ring, sides, rows, width = grads.shape
    groups = [[x * RING + z for z in range(RING)] for x in range(2)]
    total = lax.psum_scatter(
        grads.reshape(ring * sides * rows, width), "dp", scatter_dimension=0, axis_index_groups=groups, tiled=True
    )
    return total.reshape(sides, rows, width)


def pair_sum(low, high, x):
    mine = jnp.where(x == 0, low, high).astype(F32)
    other = jnp.where(x == 0, high, low)
    return mine + lax.ppermute(other, "dp", [(i, i ^ RING) for i in range(2 * RING)]).astype(F32)


def per_device(tokens, cotangent, diag_factor, section_factors, low_down, low_up):
    rows, width = tokens.shape
    rank = low_up.shape[0]
    scale = (rows * lax.axis_size("dp")) ** -0.5
    x = lax.axis_index("dp") // RING
    half = width // 2

    m4_0 = flip(tokens[:, :half], 4)
    m1 = flip(tokens, 1)
    part = jnp.dot(tokens, low_down, preferred_element_type=F32)
    part = part + flip(part, 1)
    h1 = after(tokens, part)[:, half:]
    part = part + flip(part, 2)
    m2_0 = flip(after(tokens, part)[:, :half], 2)
    part = part + flip(part, 4)
    m8_0 = flip(after(m4_0, part), 12)
    m4_1 = flip(after(h1, m4_0, part), 4)
    arrived = flip(part, 12)
    m2_1 = flip(after(h1, m2_0), 2)
    m8_1 = flip(m4_1, 12)
    part = part + after(arrived, m2_0, m4_1)
    latent = part.astype(BF16)

    moved0 = (m1, m2_0, m4_0, m8_0)
    slope0, lat0 = run_slope(0, tokens, moved0, cotangent, diag_factor, section_factors, latent, low_up)
    grads = run_outer(0, slope0, tokens, moved0, latent, None)
    moved1 = (m1, m2_1, m4_1, after(m8_1, grads))
    slope1, lat1 = run_slope(1, tokens, moved1, cotangent, diag_factor, section_factors, latent, low_up)
    part = lat0 + lat1
    arrived = flip(part, 4)
    grads = run_outer(1, slope1, tokens, moved1, latent, grads)
    summed = ring_sum(grads)
    part = part + after(arrived, grads)
    arrived = flip(part, 12)
    slopes = (slope0, after(slope1, part))
    back = run_back(slopes, section_factors)
    part = part + after(arrived, back[0])
    sent = after(back[2], part)
    r4, r8, r1 = flip(sent, 4), flip(after(back[3], part), 8), flip(after(back[0], part), 1)
    part = part + flip(part, 2)
    r2 = flip(after(back[1], part), 2)
    part = part + flip(part, 1)
    latent_grad = part.astype(BF16)
    down = run_down(tokens, latent_grad)
    down_all = lax.all_to_all(down, "dp", 0, 0, tiled=True)
    down_sum = jnp.sum(down_all.astype(F32), axis=0) * scale
    down_grad = jnp.concatenate([down_sum[:, :rank], down_sum[:, rank:]], axis=0)
    token_grad = run_final((slope0, slope1), (r1, r2, r4, r8), diag_factor, low_down, latent_grad)
    grads = pair_sum(summed[0], summed[1], x) * scale
    return (
        token_grad,
        grads[:BLOCK],
        grads[BLOCK : 5 * BLOCK].reshape(4, BLOCK, CHUNK),
        down_grad,
        grads[5 * BLOCK :],
    )


def solution(mesh):
    placed = (
        P("dp", "tensor"),
        P("dp", "tensor"),
        P(None, "tensor"),
        P(None, None, "tensor"),
        P("tensor", None),
        P(None, "tensor"),
    )
    return jax.shard_map(
        per_device,
        mesh=mesh,
        in_specs=placed,
        out_specs=(
            P("dp", "tensor"),
            P(None, ("tensor", "dp")),
            P(None, None, ("tensor", "dp")),
            P(("tensor", "dp"), None),
            P(None, ("tensor", "dp")),
        ),
        check_vma=False,
    )
```

profile of v0, /device:TPU:8, one launch (start us, length us, event | category | flops | bytes accessed | tf_op | source)
XLA Modules:
  0.0 178.4 jit_solution(6475155603387930904)
XLA Ops:
  7.2 0.0 copy-start
  7.2 0.0 reduce-scatter.2.cloned.1.call-start
  7.2 1.2 slice.33
  8.4 2.3 %collective-permute-start.4 = (bf16[128,2048]{1,0:T(8,128)(2,1)S(1)}, bf16[128,2048]{1,0:T(8,128)(2,1)S(1)}, u32[]{:S(2)}, u32[]{:S(2)}) collective-permute-start(bf16[128,2048]{1,0:T(8,128)(2,1)S(1)} %slice.33), channel_id=1, source_target_pairs={{0,4},{1,5},{2,6},{3,7},{4,0},{5,1},{6,2},{7,3},{8,12},{9,13},{10,... | collective-permute-start | bytes 1572872 | tf_op jit(solution)/shard_map/ppermute | solution.py:228
  10.7 0.0 collective-permute-start
  10.7 2.0 %fusion.1 = f32[128,128]{1,0:T(8,128)S(1)} fusion(bf16[128,4096]{1,0:T(8,128)(2,1)} %tok.9, bf16[4096,128]{1,0:T(8,128)(2,1)} %down.1), kind=kOutput, calls=%fused_computation.8 | convolution fusion | flops 134217728 | bytes 2162688 | tf_op jit(solution)/shard_map/dot_general | solution.py:259
  12.6 0.6 collective-permute-start.1
  13.2 0.9 collective-permute-done.1
  14.1 1.4 collective-permute-start.2
  15.5 4.6 %collective-permute-done.2 = f32[128,128]{1,0:T(8,128)S(1)} collective-permute-done((f32[128,128]{1,0:T(8,128)S(1)}, f32[128,128]{1,0:T(8,128)S(1)}, u32[]{:S(2)}, u32[]{:S(2)}) %collective-permute-start.2) | collective-permute-done | bytes 65568 | tf_op jit(solution)/shard_map/ppermute | solution.py:228
  20.1 0.2 collective-permute-start.5
  20.4 2.8 %collective-permute-start.3 = (bf16[128,2048]{1,0:T(8,128)(2,1)S(1)}, bf16[128,2048]{1,0:T(8,128)(2,1)S(1)}, u32[]{:S(2)}, u32[]{:S(2)}) collective-permute-start(bf16[128,2048]{1,0:T(8,128)(2,1)S(1)} %slice.32), channel_id=1, source_target_pairs={{0,2},{1,3},{2,0},{3,1},{4,6},{5,7},{6,4},{7,5},{8,10},{9,11},{10,... | collective-permute-start | bytes 1572872 | tf_op jit(solution)/shard_map/ppermute | solution.py:228
  23.2 1.2 collective-permute-done.5
  24.5 0.0 collective-permute-done.4.m4
  24.5 0.2 collective-permute-start.8
  24.7 1.9 %collective-permute-start.6 = (bf16[128,2048]{1,0:T(8,128)(2,1)S(1)}, bf16[128,2048]{1,0:T(8,128)(2,1)S(1)}, u32[]{:S(2)}, u32[]{:S(2)}) collective-permute-start(bf16[128,2048]{1,0:T(8,128)(2,1)S(1)} %collective-permute-done.4.m4), channel_id=1, source_target_pairs={{0,12},{1,13},{2,14},{3,15},{4,8},{5,9},{6,10},{7,11},{8,4},{9,5},... | collective-permute-start | bytes 1572872 | tf_op jit(solution)/shard_map/ppermute | solution.py:228
  26.5 0.2 collective-permute-start.7
  26.7 8.6 %collective-permute-done.3.m2 = bf16[128,2048]{1,0:T(8,128)(2,1)S(1)} collective-permute-done((bf16[128,2048]{1,0:T(8,128)(2,1)S(1)}, bf16[128,2048]{1,0:T(8,128)(2,1)S(1)}, u32[]{:S(2)}, u32[]{:S(2)}) %collective-permute-start.3) | collective-permute-done | bytes 524320 | tf_op jit(solution)/shard_map/ppermute | solution.py:228
  35.3 2.6 %collective-permute-start.9 = (bf16[128,2048]{1,0:T(8,128)(2,1)S(1)}, bf16[128,2048]{1,0:T(8,128)(2,1)S(1)}, u32[]{:S(2)}, u32[]{:S(2)}) collective-permute-start(bf16[128,2048]{1,0:T(8,128)(2,1)S(1)} %slice.34), channel_id=1, source_target_pairs={{0,2},{1,3},{2,0},{3,1},{4,6},{5,7},{6,4},{7,5},{8,10},{9,11},{10,... | collective-permute-start | bytes 1572872 | tf_op jit(solution)/shard_map/ppermute | solution.py:228
  37.8 0.9 collective-permute-done.7
  38.7 1.7 collective-permute-start.10
  40.4 0.6 add_convert_fusion.1.latent
  41.1 0.0 collective-permute-done.m1
  41.1 0.0 collective-permute-done.6.m8
  41.1 0.9 copy-done.1
  42.0 0.8 copy-done.7
  42.8 5.4 %slope_part.2 = (bf16[128,2048]{1,0:T(8,128)(2,1)}, f32[128,128]{1,0:T(8,128)}) custom-call(bf16[128,4096]{1,0:T(8,128)(2,1)} %tok.9, bf16[128,4096]{1,0:T(8,128)(2,1)} %copy-done.1, bf16[128,2048]{1,0:T(8,128)(2,1)} %copy-done.6, bf16[128,2048]{1,0:T(8,128)(2,1)} %copy-done.5, bf16[128,2048]{1,0:T(8,128)(2,1)} %copy-done.7, bf16[128,4096]{1,0:T(8,128)(2,1)} %cot.3, ...), custom_call_target="tpu_custom_call" | custom-call | flops 2000000000 | bytes 6291456 | tf_op jit(solution)/shard_map/slope_part/pallas_call | solution.py:134
  48.2 5.2 %outer_part.2.refs_0_ = bf16[8,2,448,256]{3,2,1,0:T(8,128)(2,1)} custom-call(bf16[128,2048]{1,0:T(8,128)(2,1)} %get-tuple-element.32.slope_in.low, bf16[128,4096]{1,0:T(8,128)(2,1)} %tok.9, bf16[128,4096]{1,0:T(8,128)(2,1)} %copy-done.1, bf16[128,2048]{1,0:T(8,128)(2,1)} %copy-done.6, bf16[128,2048]{1,0:T(8,128)(2,1)} %copy-done.5, ...), custom_call_target="tpu_custom_call" | custom-call | flops 2000000000 | bytes 5242880 | tf_op jit(solution)/shard_map/outer_part/pallas_call | solution.py:157
  53.4 0.0 collective-permute-done.10.m8
  53.4 0.8 copy-done.4
  54.2 0.8 copy-done.3
  55.0 5.4 %slope_part.3 = (bf16[128,2048]{1,0:T(8,128)(2,1)}, f32[128,128]{1,0:T(8,128)}) custom-call(bf16[128,4096]{1,0:T(8,128)(2,1)} %tok.9, bf16[128,4096]{1,0:T(8,128)(2,1)} %copy-done.1, bf16[128,2048]{1,0:T(8,128)(2,1)} %copy-done.3, bf16[128,2048]{1,0:T(8,128)(2,1)} %copy-done.2, bf16[128,2048]{1,0:T(8,128)(2,1)} %copy-done.4, bf16[128,4096]{1,0:T(8,128)(2,1)} %cot.3, ...), custom_call_target="tpu_custom_call" | custom-call | flops 2000000000 | bytes 6291456 | tf_op jit(solution)/shard_map/slope_part/pallas_call | solution.py:134
  60.5 5.2 %outer_part.3 = bf16[8,2,448,256]{3,2,1,0:T(8,128)(2,1)} custom-call(bf16[128,2048]{1,0:T(8,128)(2,1)} %get-tuple-element.39.slope_in.high, bf16[128,4096]{1,0:T(8,128)(2,1)} %tok.9, bf16[128,4096]{1,0:T(8,128)(2,1)} %copy-done.1, bf16[128,2048]{1,0:T(8,128)(2,1)} %copy-done.3, bf16[128,2048]{1,0:T(8,128)(2,1)} %copy-done.2, ...), custom_call_target="tpu_custom_call", output_to_operand_aliasing={{}: (7, {})} | custom-call | flops 2000000000 | bytes 5242880 | tf_op jit(solution)/shard_map/outer_part/pallas_call | solution.py:157
  65.7 0.0 reduce-scatter.2.cloned.1.call-update
  65.7 0.8 copy-done.10
  66.5 0.0 copy-done.11
  66.5 3.0 %collective-permute-start.11 = (f32[128,128]{1,0:T(8,128)S(1)}, f32[128,128]{1,0:T(8,128)S(1)}, u32[]{:S(2)}, u32[]{:S(2)}) collective-permute-start(f32[128,128]{1,0:T(8,128)S(1)} %add.37), channel_id=1, source_target_pairs={{0,4},{1,5},{2,6},{3,7},{4,0},{5,1},{6,2},{7,3},{8,12},{9,13},{10,... | collective-permute-start | bytes 196616 | tf_op jit(solution)/shard_map/ppermute | solution.py:228
  69.6 2.2 %collective-permute-done.11 = f32[128,128]{1,0:T(8,128)S(1)} collective-permute-done((f32[128,128]{1,0:T(8,128)S(1)}, f32[128,128]{1,0:T(8,128)S(1)}, u32[]{:S(2)}, u32[]{:S(2)}) %collective-permute-start.11) | collective-permute-done | bytes 65568 | tf_op jit(solution)/shard_map/ppermute | solution.py:228
  71.8 0.5 collective-permute-start.12
  72.3 7.8 %back_products.1 = (bf16[128,4096]{1,0:T(8,128)(2,1)}, bf16[128,4096]{1,0:T(8,128)(2,1)}, bf16[128,4096]{1,0:T(8,128)(2,1)}, bf16[128,4096]{1,0:T(8,128)(2,1)}) custom-call(bf16[128,2048]{1,0:T(8,128)(2,1)} %get-tuple-element.32.slope_in.low, bf16[128,2048]{1,0:T(8,128)(2,1)} %get-tuple-element.39.slope_in.high, bf16[4,64,4096]{2,1,0:T(8,128)(2,1)} %sec.5), custom_call_target="tpu_custom_call" | custom-call | flops 3000000000 | bytes 7340032 | tf_op jit(solution)/shard_map/back_products/pallas_call | solution.py:108
  80.1 2.8 %collective-permute-start.14 = (f32[128,128]{1,0:T(8,128)S(1)}, f32[128,128]{1,0:T(8,128)S(1)}, u32[]{:S(2)}, u32[]{:S(2)}) collective-permute-start(f32[128,128]{1,0:T(8,128)S(1)} %add.39), channel_id=1, source_target_pairs={{0,2},{1,3},{2,0},{3,1},{4,6},{5,7},{6,4},{7,5},{8,10},{9,11},{10,... | collective-permute-start | bytes 196616 | tf_op jit(solution)/shard_map/ppermute | solution.py:228
  82.9 3.1 %collective-permute-done.14 = f32[128,128]{1,0:T(8,128)S(1)} collective-permute-done((f32[128,128]{1,0:T(8,128)S(1)}, f32[128,128]{1,0:T(8,128)S(1)}, u32[]{:S(2)}, u32[]{:S(2)}) %collective-permute-start.14) | collective-permute-done | bytes 65568 | tf_op jit(solution)/shard_map/ppermute | solution.py:228
  86.0 0.1 collective-permute-start.18
  86.1 1.2 collective-permute-done.18
  87.3 0.6 add_convert_fusion.lat
  88.0 3.9 %down_part.1 = bf16[16,128,256]{2,1,0:T(8,128)(2,1)} custom-call(bf16[128,4096]{1,0:T(8,128)(2,1)} %tok.9, bf16[128,128]{1,0:T(8,128)(2,1)} %add_convert_fusion.lat), custom_call_target="tpu_custom_call" | custom-call | flops 300000000 | bytes 2097152 | tf_op jit(solution)/shard_map/down_part/pallas_call | solution.py:181
  91.8 9.2 %all-to-all-start = ((bf16[16,128,256]{2,1,0:T(8,128)(2,1)}), bf16[16,128,256]{2,1,0:T(8,128)(2,1)S(1)}, u32[]{:S(2)}, u32[]{:S(2)}) async-start(bf16[16,128,256]{2,1,0:T(8,128)(2,1)} %down_part.1), calls=%async_computation.1 | async-start | bytes 2097152 | tf_op jit(solution)/shard_map/all_to_all | solution.py:294
  101.0 0.3 collective-permute-start.13
  101.3 2.8 %collective-permute-start.16 = (bf16[128,4096]{1,0:T(8,128)(2,1)}, bf16[128,4096]{1,0:T(8,128)(2,1)S(1)}, u32[]{:S(2)}, u32[]{:S(2)}) collective-permute-start(bf16[128,4096]{1,0:T(8,128)(2,1)} %get-tuple-element.46), channel_id=1, source_target_pairs={{0,4},{1,5},{2,6},{3,7},{4,0},{5,1},{6,2},{7,3},{8,12},{9,13},{10,... | collective-permute-start | bytes 3145736 | tf_op jit(solution)/shard_map/ppermute | solution.py:228
  104.1 1.5 collective-permute-start.17
  105.6 2.7 %collective-permute-start.15 = (bf16[128,4096]{1,0:T(8,128)(2,1)}, bf16[128,4096]{1,0:T(8,128)(2,1)}, u32[]{:S(2)}, u32[]{:S(2)}) collective-permute-start(bf16[128,4096]{1,0:T(8,128)(2,1)} %get-tuple-element.44), channel_id=1, source_target_pairs={{0,2},{1,3},{2,0},{3,1},{4,6},{5,7},{6,4},{7,5},{8,10},{9,11},{10,... | collective-permute-start | bytes 3145736 | tf_op jit(solution)/shard_map/ppermute | solution.py:228
  108.3 20.0 %collective-permute-done.16.r4 = bf16[128,4096]{1,0:T(8,128)(2,1)S(1)} collective-permute-done((bf16[128,4096]{1,0:T(8,128)(2,1)}, bf16[128,4096]{1,0:T(8,128)(2,1)S(1)}, u32[]{:S(2)}, u32[]{:S(2)}) %collective-permute-start.16) | collective-permute-done | bytes 1048608 | tf_op jit(solution)/shard_map/ppermute | solution.py:228
  128.3 23.7 %collective-permute-done.17.r8 = bf16[128,4096]{1,0:T(8,128)(2,1)} collective-permute-done((bf16[128,4096]{1,0:T(8,128)(2,1)}, bf16[128,4096]{1,0:T(8,128)(2,1)}, u32[]{:S(2)}, u32[]{:S(2)}) %collective-permute-start.17) | collective-permute-done | bytes 1048608 | tf_op jit(solution)/shard_map/ppermute | solution.py:228
  152.0 7.6 %token_grad.1 = bf16[128,4096]{1,0:T(8,128)(2,1)} custom-call(bf16[128,2048]{1,0:T(8,128)(2,1)} %get-tuple-element.32.slope_in.low, bf16[128,2048]{1,0:T(8,128)(2,1)} %get-tuple-element.39.slope_in.high, bf16[128,4096]{1,0:T(8,128)(2,1)} %copy-done.8, bf16[128,4096]{1,0:T(8,128)(2,1)} %collective-permute-done.15.r2, bf16[128,4096]{1,0:T(8,128)(2,1)} %copy-done.9, ...), custom_call_target="tpu_custom_call" | custom-call | flops 2000000000 | bytes 9437184 | tf_op jit(solution)/shard_map/token_grad/pallas_call | solution.py:209
  159.7 0.1 convert_reduce_fusion
  159.8 0.0 reduce-scatter.2.cloned.1.call-done
  159.9 1.1 broadcast_select_fusion
  160.9 1.8 collective-permute-start.19
  162.7 0.7 pad_maximum_fusion
  163.4 5.0 %collective-permute-done.19 = bf16[448,256]{1,0:T(8,128)(2,1)S(1)} collective-permute-done((bf16[448,256]{1,0:T(8,128)(2,1)S(1)}, bf16[448,256]{1,0:T(8,128)(2,1)S(1)}, u32[]{:S(2)}, u32[]{:S(2)}) %collective-permute-start.19) | collective-permute-done | bytes 229408 | tf_op jit(solution)/shard_map/ppermute | solution.py:247
  168.4 1.1 add_multiply_fusion
  169.5 0.6 slice.44
  170.1 0.7 slice.45
  170.9 0.7 slice.48
  (34 shorter events, 0.2 us)
Async XLA Ops:
  7.2 13.1 %copy-start = (bf16[128,4096]{1,0:T(8,128)(2,1)S(1)}, bf16[128,4096]{1,0:T(8,128)(2,1)}, u32[]{:S(2)}) copy-start(bf16[128,4096]{1,0:T(8,128)(2,1)} %tok.9) | copy-start | bytes 3145732
  7.2 152.7 %reduce-scatter.2.cloned.1.call-start = ((), (), s32[]{:S(2)}) async-start(), calls=%async_computation.2 | async-start | bytes 4128768 | tf_op jit(solution)/shard_map/reduce_scatter | solution.py:238
  8.4 16.1 %collective-permute-start.4 = (bf16[128,2048]{1,0:T(8,128)(2,1)S(1)}, bf16[128,2048]{1,0:T(8,128)(2,1)S(1)}, u32[]{:S(2)}, u32[]{:S(2)}) collective-permute-start(bf16[128,2048]{1,0:T(8,128)(2,1)S(1)} %slice.33), channel_id=1, source_target_pairs={{0,4},{1,5},{2,6},{3,7},{4,0},{5,1},{6,2},{7,3},{8,12},{9,13},{10,... | collective-permute-start | bytes 1572872 | tf_op jit(solution)/shard_map/ppermute | solution.py:228
  10.7 30.4 %collective-permute-start = (bf16[128,4096]{1,0:T(8,128)(2,1)}, bf16[128,4096]{1,0:T(8,128)(2,1)S(1)}, u32[]{:S(2)}, u32[]{:S(2)}) collective-permute-start(bf16[128,4096]{1,0:T(8,128)(2,1)} %tok.9), channel_id=1, source_target_pairs={{0,1},{1,0},{2,3},{3,2},{4,5},{5,4},{6,7},{7,6},{8,9},{9,8},{10,11... | collective-permute-start | bytes 3145736 | tf_op jit(solution)/shard_map/ppermute | solution.py:228
  12.6 1.5 collective-permute-start.1
  14.1 5.9 %collective-permute-start.2 = (f32[128,128]{1,0:T(8,128)S(1)}, f32[128,128]{1,0:T(8,128)S(1)}, u32[]{:S(2)}, u32[]{:S(2)}) collective-permute-start(f32[128,128]{1,0:T(8,128)S(1)} %add.33), channel_id=1, source_target_pairs={{0,2},{1,3},{2,0},{3,1},{4,6},{5,7},{6,4},{7,5},{8,10},{9,11},{10,... | collective-permute-start | bytes 196616 | tf_op jit(solution)/shard_map/ppermute | solution.py:228
  20.1 4.4 %collective-permute-start.5 = (f32[128,128]{1,0:T(8,128)S(1)}, f32[128,128]{1,0:T(8,128)S(1)}, u32[]{:S(2)}, u32[]{:S(2)}) collective-permute-start(f32[128,128]{1,0:T(8,128)S(1)} %add.34), channel_id=1, source_target_pairs={{0,4},{1,5},{2,6},{3,7},{4,0},{5,1},{6,2},{7,3},{8,12},{9,13},{10,... | collective-permute-start | bytes 196616 | tf_op jit(solution)/shard_map/ppermute | solution.py:228
  20.4 14.9 %collective-permute-start.3 = (bf16[128,2048]{1,0:T(8,128)(2,1)S(1)}, bf16[128,2048]{1,0:T(8,128)(2,1)S(1)}, u32[]{:S(2)}, u32[]{:S(2)}) collective-permute-start(bf16[128,2048]{1,0:T(8,128)(2,1)S(1)} %slice.32), channel_id=1, source_target_pairs={{0,2},{1,3},{2,0},{3,1},{4,6},{5,7},{6,4},{7,5},{8,10},{9,11},{10,... | collective-permute-start | bytes 1572872 | tf_op jit(solution)/shard_map/ppermute | solution.py:228
  24.5 16.6 %copy-start.5 = (bf16[128,2048]{1,0:T(8,128)(2,1)}, bf16[128,2048]{1,0:T(8,128)(2,1)S(1)}, u32[]{:S(2)}) copy-start(bf16[128,2048]{1,0:T(8,128)(2,1)S(1)} %collective-permute-done.4.m4) | copy-start | bytes 1572868
  24.5 14.2 %collective-permute-start.8 = (bf16[128,2048]{1,0:T(8,128)(2,1)S(1)}, bf16[128,2048]{1,0:T(8,128)(2,1)S(1)}, u32[]{:S(2)}, u32[]{:S(2)}) collective-permute-start(bf16[128,2048]{1,0:T(8,128)(2,1)S(1)} %slice.34), channel_id=1, source_target_pairs={{0,4},{1,5},{2,6},{3,7},{4,0},{5,1},{6,2},{7,3},{8,12},{9,13},{10,... | collective-permute-start | bytes 1572872 | tf_op jit(solution)/shard_map/ppermute | solution.py:228
  24.7 16.4 %collective-permute-start.6 = (bf16[128,2048]{1,0:T(8,128)(2,1)S(1)}, bf16[128,2048]{1,0:T(8,128)(2,1)S(1)}, u32[]{:S(2)}, u32[]{:S(2)}) collective-permute-start(bf16[128,2048]{1,0:T(8,128)(2,1)S(1)} %collective-permute-done.4.m4), channel_id=1, source_target_pairs={{0,12},{1,13},{2,14},{3,15},{4,8},{5,9},{6,10},{7,11},{8,4},{9,5},... | collective-permute-start | bytes 1572872 | tf_op jit(solution)/shard_map/ppermute | solution.py:228
  26.5 12.2 %collective-permute-start.7 = (f32[128,128]{1,0:T(8,128)S(1)}, f32[128,128]{1,0:T(8,128)S(1)}, u32[]{:S(2)}, u32[]{:S(2)}) collective-permute-start(f32[128,128]{1,0:T(8,128)S(1)} %add.35), channel_id=1, source_target_pairs={{0,12},{1,13},{2,14},{3,15},{4,8},{5,9},{6,10},{7,11},{8,4},{9,5},... | collective-permute-start | bytes 196616 | tf_op jit(solution)/shard_map/ppermute | solution.py:228
  35.3 5.8 %copy-start.6 = (bf16[128,2048]{1,0:T(8,128)(2,1)}, bf16[128,2048]{1,0:T(8,128)(2,1)S(1)}, u32[]{:S(2)}) copy-start(bf16[128,2048]{1,0:T(8,128)(2,1)S(1)} %collective-permute-done.3.m2) | copy-start | bytes 1572868
  35.3 18.1 %collective-permute-start.9 = (bf16[128,2048]{1,0:T(8,128)(2,1)S(1)}, bf16[128,2048]{1,0:T(8,128)(2,1)S(1)}, u32[]{:S(2)}, u32[]{:S(2)}) collective-permute-start(bf16[128,2048]{1,0:T(8,128)(2,1)S(1)} %slice.34), channel_id=1, source_target_pairs={{0,2},{1,3},{2,0},{3,1},{4,6},{5,7},{6,4},{7,5},{8,10},{9,11},{10,... | collective-permute-start | bytes 1572872 | tf_op jit(solution)/shard_map/ppermute | solution.py:228
  38.7 14.7 %copy-start.2 = (bf16[128,2048]{1,0:T(8,128)(2,1)}, bf16[128,2048]{1,0:T(8,128)(2,1)S(1)}, u32[]{:S(2)}) copy-start(bf16[128,2048]{1,0:T(8,128)(2,1)S(1)} %collective-permute-done.8.m4) | copy-start | bytes 1572868
  38.7 14.7 %collective-permute-start.10 = (bf16[128,2048]{1,0:T(8,128)(2,1)S(1)}, bf16[128,2048]{1,0:T(8,128)(2,1)S(1)}, u32[]{:S(2)}, u32[]{:S(2)}) collective-permute-start(bf16[128,2048]{1,0:T(8,128)(2,1)S(1)} %collective-permute-done.8.m4), channel_id=1, source_target_pairs={{0,12},{1,13},{2,14},{3,15},{4,8},{5,9},{6,10},{7,11},{8,4},{9,5},... | collective-permute-start | bytes 1572872 | tf_op jit(solution)/shard_map/ppermute | solution.py:228
  41.1 1.0 copy-start.1
  42.0 0.8 copy-start.7
  53.4 0.8 copy-start.4
  54.2 0.8 copy-start.3
  65.7 0.8 copy-start.10
  65.7 0.9 copy-start.11
  66.5 5.3 %collective-permute-start.11 = (f32[128,128]{1,0:T(8,128)S(1)}, f32[128,128]{1,0:T(8,128)S(1)}, u32[]{:S(2)}, u32[]{:S(2)}) collective-permute-start(f32[128,128]{1,0:T(8,128)S(1)} %add.37), channel_id=1, source_target_pairs={{0,4},{1,5},{2,6},{3,7},{4,0},{5,1},{6,2},{7,3},{8,12},{9,13},{10,... | collective-permute-start | bytes 196616 | tf_op jit(solution)/shard_map/ppermute | solution.py:228
  71.8 8.3 %collective-permute-start.12 = (f32[128,128]{1,0:T(8,128)S(1)}, f32[128,128]{1,0:T(8,128)S(1)}, u32[]{:S(2)}, u32[]{:S(2)}) collective-permute-start(f32[128,128]{1,0:T(8,128)S(1)} %add.38), channel_id=1, source_target_pairs={{0,12},{1,13},{2,14},{3,15},{4,8},{5,9},{6,10},{7,11},{8,4},{9,5},... | collective-permute-start | bytes 196616 | tf_op jit(solution)/shard_map/ppermute | solution.py:228
  80.1 5.9 %collective-permute-start.14 = (f32[128,128]{1,0:T(8,128)S(1)}, f32[128,128]{1,0:T(8,128)S(1)}, u32[]{:S(2)}, u32[]{:S(2)}) collective-permute-start(f32[128,128]{1,0:T(8,128)S(1)} %add.39), channel_id=1, source_target_pairs={{0,2},{1,3},{2,0},{3,1},{4,6},{5,7},{6,4},{7,5},{8,10},{9,11},{10,... | collective-permute-start | bytes 196616 | tf_op jit(solution)/shard_map/ppermute | solution.py:228
  86.0 1.3 collective-permute-start.18
  91.8 67.8 %all-to-all-start = ((bf16[16,128,256]{2,1,0:T(8,128)(2,1)}), bf16[16,128,256]{2,1,0:T(8,128)(2,1)S(1)}, u32[]{:S(2)}, u32[]{:S(2)}) async-start(bf16[16,128,256]{2,1,0:T(8,128)(2,1)} %down_part.1), calls=%async_computation.1 | async-start | bytes 2097152 | tf_op jit(solution)/shard_map/all_to_all | solution.py:294
  101.0 7.3 %collective-permute-start.13 = (bf16[128,4096]{1,0:T(8,128)(2,1)}, bf16[128,4096]{1,0:T(8,128)(2,1)S(1)}, u32[]{:S(2)}, u32[]{:S(2)}) collective-permute-start(bf16[128,4096]{1,0:T(8,128)(2,1)} %get-tuple-element.42), channel_id=1, source_target_pairs={{0,1},{1,0},{2,3},{3,2},{4,5},{5,4},{6,7},{7,6},{8,9},{9,8},{10,11... | collective-permute-start | bytes 3145736 | tf_op jit(solution)/shard_map/ppermute | solution.py:228
  101.3 27.1 %collective-permute-start.16 = (bf16[128,4096]{1,0:T(8,128)(2,1)}, bf16[128,4096]{1,0:T(8,128)(2,1)S(1)}, u32[]{:S(2)}, u32[]{:S(2)}) collective-permute-start(bf16[128,4096]{1,0:T(8,128)(2,1)} %get-tuple-element.46), channel_id=1, source_target_pairs={{0,4},{1,5},{2,6},{3,7},{4,0},{5,1},{6,2},{7,3},{8,12},{9,13},{10,... | collective-permute-start | bytes 3145736 | tf_op jit(solution)/shard_map/ppermute | solution.py:228
  104.1 47.9 %collective-permute-start.17 = (bf16[128,4096]{1,0:T(8,128)(2,1)}, bf16[128,4096]{1,0:T(8,128)(2,1)}, u32[]{:S(2)}, u32[]{:S(2)}) collective-permute-start(bf16[128,4096]{1,0:T(8,128)(2,1)} %get-tuple-element.48), channel_id=1, source_target_pairs={{0,8},{1,9},{2,10},{3,11},{4,12},{5,13},{6,14},{7,15},{8,0},{9,1},... | collective-permute-start | bytes 3145736 | tf_op jit(solution)/shard_map/ppermute | solution.py:228
  105.6 46.4 %collective-permute-start.15 = (bf16[128,4096]{1,0:T(8,128)(2,1)}, bf16[128,4096]{1,0:T(8,128)(2,1)}, u32[]{:S(2)}, u32[]{:S(2)}) collective-permute-start(bf16[128,4096]{1,0:T(8,128)(2,1)} %get-tuple-element.44), channel_id=1, source_target_pairs={{0,2},{1,3},{2,0},{3,1},{4,6},{5,7},{6,4},{7,5},{8,10},{9,11},{10,... | collective-permute-start | bytes 3145736 | tf_op jit(solution)/shard_map/ppermute | solution.py:228
  108.3 43.7 %copy-start.8 = (bf16[128,4096]{1,0:T(8,128)(2,1)}, bf16[128,4096]{1,0:T(8,128)(2,1)S(1)}, u32[]{:S(2)}) copy-start(bf16[128,4096]{1,0:T(8,128)(2,1)S(1)} %collective-permute-done.13.r1) | copy-start | bytes 3145732
  128.3 23.7 %copy-start.9 = (bf16[128,4096]{1,0:T(8,128)(2,1)}, bf16[128,4096]{1,0:T(8,128)(2,1)S(1)}, u32[]{:S(2)}) copy-start(bf16[128,4096]{1,0:T(8,128)(2,1)S(1)} %collective-permute-done.16.r4) | copy-start | bytes 3145732
  160.9 7.4 %collective-permute-start.19 = (bf16[448,256]{1,0:T(8,128)(2,1)S(1)}, bf16[448,256]{1,0:T(8,128)(2,1)S(1)}, u32[]{:S(2)}, u32[]{:S(2)}) collective-permute-start(bf16[448,256]{1,0:T(8,128)(2,1)S(1)} %broadcast_select_fusion), channel_id=1, source_target_pairs={{0,128},{16,144},{32,160},{48,176},{64,192},{80,208},{96,224},{112... | collective-permute-start | bytes 688136 | tf_op jit(solution)/shard_map/ppermute | solution.py:247
Sparse Core Ops, SparseCore 0:
  65.8 75.6 reduce-scatter.1
where the time goes:
time: 181 us; the launch traced here: 178 us
  waiting for transfers between devices  71.5 us (40%)
  Pallas kernels  40.4 us (22%)
  starting transfers between devices  38.5 us (21%)
  between operations  14.3 us (8%)
  local copies, waits for them, and re-layouts  7.46 us (4%)
  other arithmetic  4.36 us (2%)
  matrix products  1.96 us (1%)
    ppermute x19, waiting for transfers between devices, flip(): return lax.ppermute(value, 'tensor', [(i, i ^ mask) for i in range(16)])  66.4 us
    ppermute x19, starting transfers between devices, flip(): return lax.ppermute(value, 'tensor', [(i, i ^ mask) for i in range(16)])  27.5 us
    pallas_call x2, Pallas kernels, run_slope(): pl.pallas_call(slope_kernel, grid=(steps,), in_specs=[whole(rows), whole(...  10.8 us
    pallas_call x2, Pallas kernels, run_outer(): pl.pallas_call(outer_kernel, grid=(steps,), in_specs=in_specs, out_specs=...  10.4 us
    all_to_all x1, starting transfers between devices, per_device(): down_all = lax.all_to_all(down, 'dp', 0, 0, tiled=True)  9.17 us
    pallas_call x1, Pallas kernels, run_back(): pl.pallas_call(back_kernel, grid=(steps,), in_specs=half_specs(rows, step...  7.78 us
    pallas_call x1, Pallas kernels, run_final(): pl.pallas_call(final_kernel, grid=(steps,), in_specs=half_specs(rows, ste...  7.63 us
    ppermute x1, waiting for transfers between devices, pair_sum(): lax.ppermute(other, 'dp', [(i, i ^ RING) for i in range(2 * RING)])  4.99 us
  transfers between devices with their start and end apart: 22, of which 11 were waited for; matrix products, arithmetic and copies ran while one was open for 2% of the time, Pallas kernels for 17%

commit v1 on v0

v1 whole, which is shorter than its diff:
```python
import functools

import jax
import jax.numpy as jnp
from jax import lax
from jax.experimental import pallas as pl
from jax.experimental.pallas import tpu as pltpu
from jax.sharding import PartitionSpec as P

BLOCK = 64
CHUNK = 256
MAIN_STEP, BACK_STEP, FINAL_STEP = 512, 1024, 2048
RING = 8
VMEM = 60 << 20
F32 = jnp.float32
BF16 = jnp.bfloat16


def dot(a, b, ca, cb):
    return lax.dot_general(a, b, (((ca,), (cb,)), ((), ())), preferred_element_type=F32)


def gelu_slope(values):
    return (
        0.5 * (1.0 + lax.erf(values * 0.7071067811865476))
        + values * jnp.exp(-0.5 * values * values) * 0.3989422804014327
    )


def block_mask():
    row = lax.broadcasted_iota(jnp.int32, (CHUNK, CHUNK), 0) // BLOCK
    col = lax.broadcasted_iota(jnp.int32, (CHUNK, CHUNK), 1) // BLOCK
    return row == col


def spread(factor, mask):
    tall = jnp.concatenate([factor] * (CHUNK // BLOCK), axis=0)
    return jnp.where(mask, tall, jnp.zeros_like(tall))


def main_kernel(tok, m1, m2, m4, m8, cot, diag, sec, latent, up, *refs):
    slope_out, lat_out, grads = refs[-3:]
    mask = block_mask()
    lat = latent[...]
    group = CHUNK // BLOCK
    lat_sum = jnp.zeros((lat.shape[0], up.shape[0]), F32)
    for c in range(MAIN_STEP // CHUNK):
        cs = slice(c * CHUNK, (c + 1) * CHUNK)
        up_c = up[:, cs]
        sides = [tok[:, cs], m1[:, cs], m2[:, cs], m4[:, cs], m8[:, cs]]
        factors = [spread(diag[:, cs], mask)] + [spread(sec[b, :, cs], mask) for b in range(4)]
        left = jnp.concatenate(sides + [lat], axis=1)
        right = jnp.concatenate(factors + [up_c], axis=0)
        pre = dot(left, right, 1, 0)
        slope = (cot[:, cs].astype(F32) * gelu_slope(pre)).astype(BF16)
        slope_out[:, cs] = slope
        lat_sum = lat_sum + dot(slope, up_c, 1, 1)
        for k, side in enumerate(sides):
            full = dot(side, slope, 0, 0)
            kept = jnp.where(mask, full, jnp.zeros_like(full))
            part = sum(kept[i * BLOCK : (i + 1) * BLOCK] for i in range(group))
            grads[c, 0, k * BLOCK : (k + 1) * BLOCK, :] = part.astype(BF16)
        grads[c, 0, 5 * BLOCK :, :] = dot(lat, slope, 0, 0).astype(BF16)

    @pl.when(pl.program_id(0) == 0)
    def _():
        lat_out[...] = lat_sum

    @pl.when(pl.program_id(0) > 0)
    def _():
        lat_out[...] += lat_sum


def run_main(part, tokens, moved, cotangent, diag, section, latent, up, held):
    rows, width = moved[2].shape
    rank = up.shape[0]
    steps = width // MAIN_STEP
    base = part * steps
    whole = lambda r: pl.BlockSpec((r, MAIN_STEP), lambda i: (0, base + i))
    local = pl.BlockSpec((rows, MAIN_STEP), lambda i: (0, i))
    square = pl.BlockSpec((rows, rank), lambda i: (0, 0))
    section_spec = pl.BlockSpec((4, BLOCK, MAIN_STEP), lambda i: (0, 0, base + i))
    grad_rows = 5 * BLOCK + rank
    in_specs = [whole(rows), whole(rows), local, local, local, whole(rows), whole(BLOCK), section_spec, square, whole(rank)]
    args = [tokens, *moved, cotangent, diag, section, latent, up]
    if held is not None:
        in_specs.append(pl.BlockSpec(memory_space=pl.ANY))
        args.append(held)
    return pl.pallas_call(
        main_kernel,
        grid=(steps,),
        in_specs=in_specs,
        out_specs=[local, square, pl.BlockSpec((MAIN_STEP // CHUNK, 1, grad_rows, CHUNK), lambda i: (i, part, 0, 0))],
        out_shape=[
            jax.ShapeDtypeStruct((rows, width), BF16),
            jax.ShapeDtypeStruct((rows, rank), F32),
            jax.ShapeDtypeStruct((RING, 2, grad_rows, CHUNK), BF16),
        ],
        input_output_aliases={} if held is None else {10: 2},
        compiler_params=pltpu.CompilerParams(vmem_limit_bytes=VMEM),
        cost_estimate=pl.CostEstimate(flops=2_000_000_000, bytes_accessed=28 << 20, transcendentals=0),
        name="main_part",
    )(*args)


def pick_half(low, high):
    first = pl.program_id(0) < pl.num_programs(0) // 2
    return jnp.where(first, low[...], high[...])


def half_specs(rows, steps):
    half = steps // 2
    return [
        pl.BlockSpec((rows, FINAL_STEP), lambda i: (0, jnp.minimum(i, half - 1))),
        pl.BlockSpec((rows, FINAL_STEP), lambda i: (0, jnp.maximum(i - half, 0))),
    ]


def back_kernel(slope, sec, b1, b2, b4, b8):
    mask = block_mask()
    for c in range(slope.shape[1] // CHUNK):
        cs = slice(c * CHUNK, (c + 1) * CHUNK)
        for b, ref in enumerate((b1, b2, b4, b8)):
            ref[:, cs] = dot(slope[:, cs], spread(sec[b, :, cs], mask), 1, 1).astype(BF16)


def run_back(part, slope, section):
    rows, width = slope.shape
    steps = width // BACK_STEP
    base = part * steps
    local = pl.BlockSpec((rows, BACK_STEP), lambda i: (0, i))
    return pl.pallas_call(
        back_kernel,
        grid=(steps,),
        in_specs=[local, pl.BlockSpec((4, BLOCK, BACK_STEP), lambda i: (0, 0, base + i))],
        out_specs=[local] * 4,
        out_shape=[jax.ShapeDtypeStruct((rows, width), BF16)] * 4,
        compiler_params=pltpu.CompilerParams(vmem_limit_bytes=VMEM),
        cost_estimate=pl.CostEstimate(flops=1_000_000_000, bytes_accessed=13 << 20, transcendentals=0),
        name="back_products",
    )(slope, section)


def down_kernel(tok, lat, out):
    for c in range(tok.shape[1] // CHUNK):
        out[0, c] = dot(lat[...], tok[:, c * CHUNK : (c + 1) * CHUNK], 0, 0).astype(BF16)


def run_down(tokens, latent_grad):
    rows, width = tokens.shape
    rank = latent_grad.shape[1]
    half = width // 2
    return pl.pallas_call(
        down_kernel,
        grid=(2,),
        in_specs=[pl.BlockSpec((rows, half), lambda i: (0, i)), pl.BlockSpec((rows, rank), lambda i: (0, 0))],
        out_specs=pl.BlockSpec((1, RING, rank, CHUNK), lambda i: (i, 0, 0, 0)),
        out_shape=jax.ShapeDtypeStruct((2, RING, rank, CHUNK), BF16),
        cost_estimate=pl.CostEstimate(flops=300_000_000, bytes_accessed=10 << 20, transcendentals=0),
        name="down_part",
    )(tokens, latent_grad)


def final_kernel(*refs):
    pairs, (diag, down, lat, out) = refs[:8], refs[8:]
    mask = block_mask()
    slope, r1, r2, r48 = (pick_half(pairs[2 * k], pairs[2 * k + 1]) for k in range(4))
    for c in range(FINAL_STEP // CHUNK):
        cs = slice(c * CHUNK, (c + 1) * CHUNK)
        total = dot(slope[:, cs], spread(diag[:, cs], mask), 1, 1)
        total = total + dot(lat[...], down[cs, :], 1, 1)
        for value in (r1, r2, r48):
            total = total + value[:, cs].astype(F32)
        out[:, cs] = total.astype(BF16)


def run_final(pairs, diag, low_down, latent_grad):
    rows, half_width = pairs[0][0].shape
    width = 2 * half_width
    rank = latent_grad.shape[1]
    steps = width // FINAL_STEP
    col = lambda r: pl.BlockSpec((r, FINAL_STEP), lambda i: (0, i))
    return pl.pallas_call(
        final_kernel,
        grid=(steps,),
        in_specs=half_specs(rows, steps) * 4
        + [
            col(BLOCK),
            pl.BlockSpec((FINAL_STEP, rank), lambda i: (i, 0)),
            pl.BlockSpec((rows, rank), lambda i: (0, 0)),
        ],
        out_specs=col(rows),
        out_shape=jax.ShapeDtypeStruct((rows, width), BF16),
        compiler_params=pltpu.CompilerParams(vmem_limit_bytes=VMEM),
        cost_estimate=pl.CostEstimate(flops=2_000_000_000, bytes_accessed=17 << 20, transcendentals=0),
        name="token_grad",
    )(*[value for pair in pairs for value in pair], diag, low_down, latent_grad)


def finish_kernel(scale, side, summed, arrived, diag, section, up):
    total = (summed[0].astype(F32) + arrived[...].astype(F32)) * scale
    diag[...] = total[:BLOCK]
    for b in range(4):
        section[b] = total[(b + 1) * BLOCK : (b + 2) * BLOCK]
    up[...] = total[5 * BLOCK :]


def run_finish(x, summed, arrived, scale):
    _, rows, width = summed.shape
    rank = rows - 5 * BLOCK
    return pl.pallas_call(
        functools.partial(finish_kernel, scale),
        grid_spec=pltpu.PrefetchScalarGridSpec(
            num_scalar_prefetch=1,
            grid=(1,),
            in_specs=[
                pl.BlockSpec((1, rows, width), lambda i, side: (side[0], 0, 0)),
                pl.BlockSpec((rows, width), lambda i, side: (0, 0)),
            ],
            out_specs=[
                pl.BlockSpec((BLOCK, width), lambda i, side: (0, 0)),
                pl.BlockSpec((4, BLOCK, width), lambda i, side: (0, 0, 0)),
                pl.BlockSpec((rank, width), lambda i, side: (0, 0)),
            ],
        ),
        out_shape=[
            jax.ShapeDtypeStruct((BLOCK, width), F32),
            jax.ShapeDtypeStruct((4, BLOCK, width), F32),
            jax.ShapeDtypeStruct((rank, width), F32),
        ],
        cost_estimate=pl.CostEstimate(flops=300_000, bytes_accessed=4 << 20, transcendentals=0),
        name="finish",
    )(jnp.full((1,), x, jnp.int32), summed, arrived)


def flip(value, mask):
    return lax.ppermute(value, "tensor", [(i, i ^ mask) for i in range(16)])


def after(value, *events):
    return lax.optimization_barrier((value, *events))[0]


def ring_sum(grads):
    ring, sides, rows, width = grads.shape
    groups = [[x * RING + z for z in range(RING)] for x in range(2)]
    total = lax.psum_scatter(
        grads.reshape(ring * sides * rows, width), "dp", scatter_dimension=0, axis_index_groups=groups, tiled=True
    )
    return total.reshape(sides, rows, width)


def cross(value):
    return lax.ppermute(value, "dp", [(i, i ^ RING) for i in range(2 * RING)])


def per_device(tokens, cotangent, diag_factor, section_factors, low_down, low_up):
    rows, width = tokens.shape
    scale = (rows * lax.axis_size("dp")) ** -0.5
    x = lax.axis_index("dp") // RING
    half = width // 2

    h0 = tokens[:, :half]
    m4_0 = flip(h0, 4)
    m2_0 = flip(h0, 2)
    m1 = flip(tokens, 1)
    part = jnp.dot(tokens, low_down, preferred_element_type=F32)
    part = part + flip(part, 12)
    h1 = after(tokens, part)[:, half:]
    part = part + flip(part, 1)
    part = part + flip(part, 2)
    m4_1 = flip(after(h1, m4_0), 4)
    m8_0 = flip(m4_0, 12)
    m2_1 = flip(after(h1, m2_0), 2)
    part = part + flip(part, 4)
    m8_1 = flip(m4_1, 12)
    latent = part.astype(BF16)

    factors = (cotangent, diag_factor, section_factors, latent, low_up)
    slope0, lat0, grads = run_main(0, tokens, (m1, m2_0, m4_0, m8_0), *factors, None)
    b1_0, b2_0, b4_0, b8_0 = run_back(0, slope0, section_factors)
    moved1 = (m1, m2_1, m4_1, after(m8_1, b8_0))
    slope1, lat1, grads = run_main(1, tokens, moved1, *factors, grads)
    summed = ring_sum(grads)

    part = lat0 + lat1
    arrived = flip(part, 4)
    b1_1, b2_1, b4_1, b8_1 = run_back(1, slope1, section_factors)
    part = part + after(arrived, b8_1)
    part = part + flip(part, 12)
    q0, q1 = flip(after(b8_0, part), 12), flip(after(b8_1, part), 12)
    part = part + flip(part, 2)
    r2_0, r1_0 = flip(after(b2_0, part), 2), flip(after(b1_0, part), 1)
    part = part + flip(part, 1)
    latent_grad = part.astype(BF16)

    down = run_down(after(tokens, q0), latent_grad)
    keep = lax.dynamic_index_in_dim(down, x, 0, keepdims=False)
    send = lax.dynamic_index_in_dim(down, 1 - x, 0, keepdims=False)
    s0 = flip(b4_0 + q0, 4)
    pair = (keep.astype(F32) + after(cross(after(send, r2_0, r1_0)), q1).astype(F32)).astype(BF16)
    r2_1, r1_1 = flip(after(b2_1, pair), 2), flip(after(b1_1, pair), 1)
    groups = [[side * RING + z for z in range(RING)] for side in range(2)]
    pair = lax.all_to_all(pair, "dp", 0, 0, axis_index_groups=groups, tiled=True)
    down_grad = (jnp.sum(pair.astype(F32), axis=0) * scale).T
    s1 = flip(b4_1 + q1, 4)
    pairs = ((slope0, slope1), (r1_0, r1_1), (r2_0, r2_1), (s0, s1))
    token_grad = run_final(pairs, diag_factor, low_down, latent_grad)
    arrived = cross(lax.dynamic_index_in_dim(summed, 1 - x, 0, keepdims=False))
    diag_grad, section_grad, up_grad = run_finish(x, summed, arrived, scale)
    return token_grad, diag_grad, section_grad, down_grad, up_grad


def solution(mesh):
    placed = (
        P("dp", "tensor"),
        P("dp", "tensor"),
        P(None, "tensor"),
        P(None, None, "tensor"),
        P("tensor", None),
        P(None, "tensor"),
    )
    return jax.shard_map(
        per_device,
        mesh=mesh,
        in_specs=placed,
        out_specs=(
            P("dp", "tensor"),
            P(None, ("tensor", "dp")),
            P(None, None, ("tensor", "dp")),
            P(("tensor", "dp"), None),
            P(None, ("tensor", "dp")),
        ),
        check_vma=False,
    )
```

time: 181 us -> 174 us (0.961)
  Pallas kernels: 40.4 us -> 32.1 us
  local copies, waits for them, and re-layouts: 7.46 us -> 11.6 us
  waiting for transfers between devices: 71.5 us -> 68.8 us
    ppermute x19 -> x23, waiting for transfers between devices: 66.4 us -> 52.2 us  [flip(): return lax.ppermute(value, 'tensor', [(i, i ^ mask) for i in range(16)])]
    ppermute x1 -> x2, waiting for transfers between devices: 4.99 us -> 16.6 us  [cross(): return lax.ppermute(value, 'dp', [(i, i ^ RING) for i in range(2 * RING)])]
    pallas_call x6, Pallas kernels: 32.8 us -> 27.4 us  [the longest x2 15.5 us: run_main(): pl.pallas_call(main_kernel, grid=(steps,), in_specs=in_specs, out_specs=[...]
    unnamed x24 -> x39, local copies, waits for them, and re-layouts: 4.2 us -> 7.54 us
    pallas_call x1, Pallas kernels: 7.63 us -> 4.73 us  [run_final(): pl.pallas_call(final_kernel, grid=(steps,), in_specs=half_specs(rows, ste...]
    slice x6 -> x1, local copies, waits for them, and re-layouts: 3.22 us -> 1.16 us  [per_device(): h0 = tokens[:, :half]]
    convert_element_type x0 -> x1, other arithmetic: none -> 2.05 us  [per_device(): (keep.astype(F32) + after(cross(after(send, r2_0, r1_0)), q1).astype(F32)...]
    squeeze x0 -> x2, local copies, waits for them, and re-layouts: none -> 2.04 us  [the longest x1 1.08 us: per_device(): send = lax.dynamic_index_in_dim(down, 1 - x, 0, keepdims=False)]
  transfers between devices with their start and end apart: 22 -> 27, of which waited for: 11 -> 12; matrix products, arithmetic and copies ran while one was open for 2% -> 5% of each run, Pallas kernels for 17% -> 13%
where the time goes in v1:
time: 174 us; the launch traced here: 172 us
  waiting for transfers between devices  68.8 us (40%)
  starting transfers between devices  39.7 us (23%)
  Pallas kernels  32.1 us (18%)
  between operations  14.3 us (8%)
  local copies, waits for them, and re-layouts  11.6 us (7%)
  other arithmetic  3.69 us (2%)
  matrix products  1.96 us (1%)
    ppermute x23, waiting for transfers between devices, flip(): return lax.ppermute(value, 'tensor', [(i, i ^ mask) for i in range(16)])  52.2 us
    ppermute x23, starting transfers between devices, flip(): return lax.ppermute(value, 'tensor', [(i, i ^ mask) for i in range(16)])  28.9 us
    ppermute x2, waiting for transfers between devices, cross(): return lax.ppermute(value, 'dp', [(i, i ^ RING) for i in range(2 * RING)])  16.6 us
    pallas_call x2, Pallas kernels, run_main(): pl.pallas_call(main_kernel, grid=(steps,), in_specs=in_specs, out_specs=[...  15.5 us
    all_to_all x1, starting transfers between devices, per_device(): lax.all_to_all(pair, 'dp', 0, 0, axis_index_groups=groups, tiled=True)  8.46 us
    unnamed x39, local copies, waits for them, and re-layouts  7.54 us
    pallas_call x2, Pallas kernels, run_back(): pl.pallas_call(back_kernel, grid=(steps,), in_specs=[local, pl.BlockSpec(...  7.45 us
    pallas_call x1, Pallas kernels, run_final(): pl.pallas_call(final_kernel, grid=(steps,), in_specs=half_specs(rows, ste...  4.73 us
  transfers between devices with their start and end apart: 27, of which 12 were waited for; matrix products, arithmetic and copies ran while one was open for 5% of the time, Pallas kernels for 13%

profile of v1, /device:TPU:8, one launch (start us, length us, event | category | flops | bytes accessed | tf_op | source)
XLA Modules:
  0.0 172.1 jit_solution(11923109929015951224)
XLA Ops:
  7.2 1.2 slice.6
  8.4 2.3 %collective-permute-start.2 = (bf16[128,2048]{1,0:T(8,128)(2,1)S(1)}, bf16[128,2048]{1,0:T(8,128)(2,1)S(1)}, u32[]{:S(2)}, u32[]{:S(2)}) collective-permute-start(bf16[128,2048]{1,0:T(8,128)(2,1)S(1)} %slice.6), channel_id=1, source_target_pairs={{0,4},{1,5},{2,6},{3,7},{4,0},{5,1},{6,2},{7,3},{8,12},{9,13},{10,... | collective-permute-start | bytes 1572872 | tf_op jit(solution)/shard_map/ppermute | solution.py:237
  10.7 2.0 %fusion.1 = f32[128,128]{1,0:T(8,128)S(1)} fusion(bf16[128,4096]{1,0:T(8,128)(2,1)} %tok.4, bf16[4096,128]{1,0:T(8,128)(2,1)} %refs_9_.1), kind=kOutput, calls=%fused_computation.8 | convolution fusion | flops 134217728 | bytes 2162688 | tf_op jit(solution)/shard_map/dot_general | solution.py:267
  12.6 0.8 collective-permute-start.4
  13.4 3.8 %collective-permute-done.4 = f32[128,128]{1,0:T(8,128)S(1)} collective-permute-done((f32[128,128]{1,0:T(8,128)S(1)}, f32[128,128]{1,0:T(8,128)S(1)}, u32[]{:S(2)}, u32[]{:S(2)}) %collective-permute-start.4) | collective-permute-done | bytes 65568 | tf_op jit(solution)/shard_map/ppermute | solution.py:237
  17.2 0.8 slice.7
  18.1 4.1 %collective-permute-done.2.m4 = bf16[128,2048]{1,0:T(8,128)(2,1)S(1)} collective-permute-done((bf16[128,2048]{1,0:T(8,128)(2,1)S(1)}, bf16[128,2048]{1,0:T(8,128)(2,1)S(1)}, u32[]{:S(2)}, u32[]{:S(2)}) %collective-permute-start.2) | collective-permute-done | bytes 524320 | tf_op jit(solution)/shard_map/ppermute | solution.py:237
  22.1 0.3 collective-permute-start.9
  22.4 3.2 %collective-permute-start.1 = (bf16[128,2048]{1,0:T(8,128)(2,1)S(1)}, bf16[128,2048]{1,0:T(8,128)(2,1)S(1)}, u32[]{:S(2)}, u32[]{:S(2)}) collective-permute-start(bf16[128,2048]{1,0:T(8,128)(2,1)S(1)} %slice.6), channel_id=1, source_target_pairs={{0,2},{1,3},{2,0},{3,1},{4,6},{5,7},{6,4},{7,5},{8,10},{9,11},{10,... | collective-permute-start | bytes 1572872 | tf_op jit(solution)/shard_map/ppermute | solution.py:237
  25.6 2.4 %collective-permute-start.3 = (bf16[128,2048]{1,0:T(8,128)(2,1)S(1)}, bf16[128,2048]{1,0:T(8,128)(2,1)S(1)}, u32[]{:S(2)}, u32[]{:S(2)}) collective-permute-start(bf16[128,2048]{1,0:T(8,128)(2,1)S(1)} %collective-permute-done.2.m4), channel_id=1, source_target_pairs={{0,12},{1,13},{2,14},{3,15},{4,8},{5,9},{6,10},{7,11},{8,4},{9,5},... | collective-permute-start | bytes 1572872 | tf_op jit(solution)/shard_map/ppermute | solution.py:237
  28.0 1.3 collective-permute-done.5
  29.3 0.6 collective-permute-start.6
  29.9 7.9 %collective-permute-done.6 = f32[128,128]{1,0:T(8,128)S(1)} collective-permute-done((f32[128,128]{1,0:T(8,128)S(1)}, f32[128,128]{1,0:T(8,128)S(1)}, u32[]{:S(2)}, u32[]{:S(2)}) %collective-permute-start.6) | collective-permute-done | bytes 65568 | tf_op jit(solution)/shard_map/ppermute | solution.py:237
  37.8 1.7 collective-permute-start.7
  39.5 1.8 %collective-permute-start.10 = (bf16[128,2048]{1,0:T(8,128)(2,1)S(1)}, bf16[128,2048]{1,0:T(8,128)(2,1)S(1)}, u32[]{:S(2)}, u32[]{:S(2)}) collective-permute-start(bf16[128,2048]{1,0:T(8,128)(2,1)S(1)} %collective-permute-done.9.m4), channel_id=1, source_target_pairs={{0,12},{1,13},{2,14},{3,15},{4,8},{5,9},{6,10},{7,11},{8,4},{9,5},... | collective-permute-start | bytes 1572872 | tf_op jit(solution)/shard_map/ppermute | solution.py:237
  41.3 3.0 %collective-permute-start.8 = (bf16[128,2048]{1,0:T(8,128)(2,1)}, bf16[128,2048]{1,0:T(8,128)(2,1)}, u32[]{:S(2)}, u32[]{:S(2)}) collective-permute-start(bf16[128,2048]{1,0:T(8,128)(2,1)} %slice.7), channel_id=1, source_target_pairs={{0,2},{1,3},{2,0},{3,1},{4,6},{5,7},{6,4},{7,5},{8,10},{9,11},{10,... | collective-permute-start | bytes 1572872 | tf_op jit(solution)/shard_map/ppermute | solution.py:237
  44.3 0.6 add_convert_fusion.1.latent
  45.0 0.9 copy-done.1
  45.9 0.8 copy-done.7
  46.7 7.7 %main_part.2 = (bf16[128,2048]{1,0:T(8,128)(2,1)}, f32[128,128]{1,0:T(8,128)}, bf16[8,2,448,256]{3,2,1,0:T(8,128)(2,1)}) custom-call(bf16[128,4096]{1,0:T(8,128)(2,1)} %tok.4, bf16[128,4096]{1,0:T(8,128)(2,1)} %copy-done.1, bf16[128,2048]{1,0:T(8,128)(2,1)} %copy-done.6, bf16[128,2048]{1,0:T(8,128)(2,1)} %copy-done.4, bf16[128,2048]{1,0:T(8,128)(2,1)} %copy-done.7, ...), custom_call_target="tpu_custom_call" | custom-call | flops 2000000000 | bytes 29360128 | tf_op jit(solution)/shard_map/main_part/pallas_call | solution.py:89
  54.4 3.7 %back_products.2 = (bf16[128,2048]{1,0:T(8,128)(2,1)}, bf16[128,2048]{1,0:T(8,128)(2,1)}, bf16[128,2048]{1,0:T(8,128)(2,1)}, bf16[128,2048]{1,0:T(8,128)(2,1)}) custom-call(bf16[128,2048]{1,0:T(8,128)(2,1)} %get-tuple-element.36.slope.refs_0_, bf16[4,64,4096]{2,1,0:T(8,128)(2,1)} %sec.7), custom_call_target="tpu_custom_call" | custom-call | flops 1000000000 | bytes 13631488 | tf_op jit(solution)/shard_map/back_products/pallas_call | solution.py:132
  58.2 0.8 copy-done.8
  59.0 7.8 %main_part.3 = (bf16[128,2048]{1,0:T(8,128)(2,1)}, f32[128,128]{1,0:T(8,128)}, bf16[8,2,448,256]{3,2,1,0:T(8,128)(2,1)}) custom-call(bf16[128,4096]{1,0:T(8,128)(2,1)} %tok.4, bf16[128,4096]{1,0:T(8,128)(2,1)} %copy-done.1, bf16[128,2048]{1,0:T(8,128)(2,1)} %collective-permute-done.8.m2, ...), custom_call_target="tpu_custom_call", output_to_operand_aliasing={{2}: (10, {})} | custom-call | flops 2000000000 | bytes 29360128 | tf_op jit(solution)/shard_map/main_part/pallas_call | solution.py:89
  66.8 0.8 copy-done.10
  67.6 2.0 %collective-permute-start.11 = (f32[128,128]{1,0:T(8,128)S(1)}, f32[128,128]{1,0:T(8,128)S(1)}, u32[]{:S(2)}, u32[]{:S(2)}) collective-permute-start(f32[128,128]{1,0:T(8,128)S(1)} %add.53), channel_id=1, source_target_pairs={{0,4},{1,5},{2,6},{3,7},{4,0},{5,1},{6,2},{7,3},{8,12},{9,13},{10,... | collective-permute-start | bytes 196616 | tf_op jit(solution)/shard_map/ppermute | solution.py:237
  69.6 3.7 %back_products.3 = (bf16[128,2048]{1,0:T(8,128)(2,1)}, bf16[128,2048]{1,0:T(8,128)(2,1)}, bf16[128,2048]{1,0:T(8,128)(2,1)}, bf16[128,2048]{1,0:T(8,128)(2,1)}) custom-call(bf16[128,2048]{1,0:T(8,128)(2,1)} %get-tuple-element.43.slope.refs_1_, bf16[4,64,4096]{2,1,0:T(8,128)(2,1)} %sec.7), custom_call_target="tpu_custom_call" | custom-call | flops 1000000000 | bytes 13631488 | tf_op jit(solution)/shard_map/back_products/pallas_call | solution.py:132
  73.4 0.1 collective-permute-start.12
  73.5 5.0 %collective-permute-done.12 = f32[128,128]{1,0:T(8,128)S(1)} collective-permute-done((f32[128,128]{1,0:T(8,128)S(1)}, f32[128,128]{1,0:T(8,128)S(1)}, u32[]{:S(2)}, u32[]{:S(2)}) %collective-permute-start.12) | collective-permute-done | bytes 65568 | tf_op jit(solution)/shard_map/ppermute | solution.py:237
  78.5 0.1 collective-permute-start.15
  78.6 2.3 %collective-permute-start.13 = (f32[128,128]{1,0:T(8,128)S(1)}, f32[128,128]{1,0:T(8,128)S(1)}, u32[]{:S(2)}, u32[]{:S(2)}) collective-permute-start(f32[128,128]{1,0:T(8,128)S(1)} %add.55), channel_id=1, source_target_pairs={{0,2},{1,3},{2,0},{3,1},{4,6},{5,7},{6,4},{7,5},{8,10},{9,11},{10,... | collective-permute-start | bytes 196616 | tf_op jit(solution)/shard_map/ppermute | solution.py:237
  80.9 3.7 %collective-permute-done.13 = f32[128,128]{1,0:T(8,128)S(1)} collective-permute-done((f32[128,128]{1,0:T(8,128)S(1)}, f32[128,128]{1,0:T(8,128)S(1)}, u32[]{:S(2)}, u32[]{:S(2)}) %collective-permute-start.13) | collective-permute-done | bytes 65568 | tf_op jit(solution)/shard_map/ppermute | solution.py:237
  84.6 0.1 collective-permute-start.14
  84.7 2.2 %collective-permute-start.17 = (bf16[128,2048]{1,0:T(8,128)(2,1)}, bf16[128,2048]{1,0:T(8,128)(2,1)}, u32[]{:S(2)}, u32[]{:S(2)}) collective-permute-start(bf16[128,2048]{1,0:T(8,128)(2,1)} %get-tuple-element.54), channel_id=1, source_target_pairs={{0,2},{1,3},{2,0},{3,1},{4,6},{5,7},{6,4},{7,5},{8,10},{9,11},{10,... | collective-permute-start | bytes 1572872 | tf_op jit(solution)/shard_map/ppermute | solution.py:237
  86.9 0.1 collective-permute-start.16
  87.0 0.5 collective-permute-start.19
  87.5 0.6 collective-permute-done.16
  88.1 0.6 add_convert_fusion.lat.refs_10_
  88.7 2.6 %down_part.1 = bf16[2,8,128,256]{3,2,1,0:T(8,128)(2,1)} custom-call(bf16[128,4096]{1,0:T(8,128)(2,1)} %tok.4, bf16[128,128]{1,0:T(8,128)(2,1)} %add_convert_fusion.lat.refs_10_), custom_call_target="tpu_custom_call" | custom-call | flops 300000000 | bytes 10485760 | tf_op jit(solution)/shard_map/down_part/pallas_call | solution.py:153
  91.3 1.1 dynamic-slice_bitcast_fusion
  92.4 0.8 copy-done.13
  93.2 7.6 %collective-permute-done.17.refs_4_ = bf16[128,2048]{1,0:T(8,128)(2,1)} collective-permute-done((bf16[128,2048]{1,0:T(8,128)(2,1)}, bf16[128,2048]{1,0:T(8,128)(2,1)}, u32[]{:S(2)}, u32[]{:S(2)}) %collective-permute-start.17) | collective-permute-done | bytes 524320 | tf_op jit(solution)/shard_map/ppermute | solution.py:237
  100.9 0.6 collective-permute-start.18
  101.5 12.9 %collective-permute-done.18 = bf16[8,128,256]{2,1,0:T(8,128)(2,1)S(1)} collective-permute-done((bf16[8,128,256]{2,1,0:T(8,128)(2,1)S(1)}, bf16[8,128,256]{2,1,0:T(8,128)(2,1)S(1)}, u32[]{:S(2)}, u32[]{:S(2)}) %collective-permute-start.18) | collective-permute-done | bytes 524320 | tf_op jit(solution)/shard_map/ppermute | solution.py:254
  114.3 2.0 %fusion = bf16[8,128,256]{2,1,0:T(8,128)(2,1)} fusion(bf16[8,128,256]{2,1,0:T(8,128)(2,1)S(1)} %collective-permute-done.18, bf16[2,8,128,256]{3,2,1,0:T(8,128)(2,1)} %down_part.1, s32[]{:T(128)S(6)} %select_n.15), kind=kLoop, calls=%fused_computation.1 | loop fusion | flops 1048576 | bytes 1572868 | tf_op jit(solution)/shard_map/convert_element_type | solution.py:301
  116.4 8.5 %all-to-all-start = ((bf16[8,128,256]{2,1,0:T(8,128)(2,1)}), bf16[8,128,256]{2,1,0:T(8,128)(2,1)S(1)}, u32[]{:S(2)}, u32[]{:S(2)}) async-start(bf16[8,128,256]{2,1,0:T(8,128)(2,1)} %fusion), calls=%async_computation.1 | async-start | bytes 1048576 | tf_op jit(solution)/shard_map/all_to_all | solution.py:304
  124.8 0.1 add.61
  125.0 2.1 %collective-permute-start.22 = (bf16[128,2048]{1,0:T(8,128)(2,1)S(1)}, bf16[128,2048]{1,0:T(8,128)(2,1)S(1)}, u32[]{:S(2)}, u32[]{:S(2)}) collective-permute-start(bf16[128,2048]{1,0:T(8,128)(2,1)S(1)} %add.61), channel_id=1, source_target_pairs={{0,4},{1,5},{2,6},{3,7},{4,0},{5,1},{6,2},{7,3},{8,12},{9,13},{10,... | collective-permute-start | bytes 1572872 | tf_op jit(solution)/shard_map/ppermute | solution.py:237
  127.1 0.1 add.62
  127.3 0.1 collective-permute-start.23
  127.4 0.1 collective-permute-start.20
  127.5 3.2 %collective-permute-start.21 = (bf16[128,2048]{1,0:T(8,128)(2,1)S(1)}, bf16[128,2048]{1,0:T(8,128)(2,1)S(1)}, u32[]{:S(2)}, u32[]{:S(2)}) collective-permute-start(bf16[128,2048]{1,0:T(8,128)(2,1)S(1)} %copy-done.12), channel_id=1, source_target_pairs={{0,2},{1,3},{2,0},{3,1},{4,6},{5,7},{6,4},{7,5},{8,10},{9,11},{10,... | collective-permute-start | bytes 1572872 | tf_op jit(solution)/shard_map/ppermute | solution.py:237
  130.7 9.3 %collective-permute-done.22.refs_6_ = bf16[128,2048]{1,0:T(8,128)(2,1)S(1)} collective-permute-done((bf16[128,2048]{1,0:T(8,128)(2,1)S(1)}, bf16[128,2048]{1,0:T(8,128)(2,1)S(1)}, u32[]{:S(2)}, u32[]{:S(2)}) %collective-permute-start.22) | collective-permute-done | bytes 524320 | tf_op jit(solution)/shard_map/ppermute | solution.py:237
  140.0 8.9 %collective-permute-done.23.refs_7_ = bf16[128,2048]{1,0:T(8,128)(2,1)S(1)} collective-permute-done((bf16[128,2048]{1,0:T(8,128)(2,1)S(1)}, bf16[128,2048]{1,0:T(8,128)(2,1)S(1)}, u32[]{:S(2)}, u32[]{:S(2)}) %collective-permute-start.23) | collective-permute-done | bytes 524320 | tf_op jit(solution)/shard_map/ppermute | solution.py:237
  148.9 0.8 copy-done.16
  149.7 0.2 copy-done.17
  150.0 0.8 copy-done.18
  150.8 4.7 %token_grad.1 = bf16[128,4096]{1,0:T(8,128)(2,1)} custom-call(bf16[128,2048]{1,0:T(8,128)(2,1)} %get-tuple-element.36.slope.refs_0_, bf16[128,2048]{1,0:T(8,128)(2,1)} %get-tuple-element.43.slope.refs_1_, bf16[128,2048]{1,0:T(8,128)(2,1)} %copy-done.13, bf16[128,2048]{1,0:T(8,128)(2,1)} %copy-done.17, bf16[128,2048]{1,0:T(8,128)(2,1)} %collective-permute-done.17.refs_4_, ...), custom_call_target="tpu_custom_call" | custom-call | flops 2000000000 | bytes 17825792 | tf_op jit(solution)/shard_map/token_grad/pallas_call | solution.py:183
  155.5 0.1 convert_reduce_fusion
  155.6 1.0 dynamic-slice_bitcast_fusion.1
  156.6 1.7 collective-permute-start.24
  158.3 0.8 copy.12
  159.0 3.7 %collective-permute-done.24.arrived = bf16[448,256]{1,0:T(8,128)(2,1)S(1)} collective-permute-done((bf16[448,256]{1,0:T(8,128)(2,1)S(1)}, bf16[448,256]{1,0:T(8,128)(2,1)S(1)}, u32[]{:S(2)}, u32[]{:S(2)}) %collective-permute-start.24) | collective-permute-done | bytes 229408 | tf_op jit(solution)/shard_map/ppermute | solution.py:254
  162.7 0.7 copy-done.9
  163.4 1.8 %finish.1 = (f32[64,256]{1,0:T(8,128)}, f32[4,64,256]{2,1,0:T(8,128)}, f32[128,256]{1,0:T(8,128)}) custom-call(s32[1]{0:T(128)} %bitcast.2.side, bf16[2,448,256]{2,1,0:T(8,128)(2,1)} %bitcast.16, bf16[448,256]{1,0:T(8,128)(2,1)} %copy-done.9), custom_call_target="tpu_custom_call" | custom-call | flops 300000 | bytes 4194304 | tf_op jit(solution)/shard_map/finish/pallas_call | solution.py:211
  (56 shorter events, 0.3 us)
Async XLA Ops:
  7.2 10.1 %copy-start = (bf16[128,4096]{1,0:T(8,128)(2,1)S(1)}, bf16[128,4096]{1,0:T(8,128)(2,1)}, u32[]{:S(2)}) copy-start(bf16[128,4096]{1,0:T(8,128)(2,1)} %tok.4) | copy-start | bytes 3145732
  7.2 148.5 %reduce-scatter.2.cloned.1.call-start = ((), (), s32[]{:S(2)}) async-start(), calls=%async_computation.2 | async-start | bytes 4128768 | tf_op jit(solution)/shard_map/reduce_scatter | solution.py:247
  8.4 13.8 %collective-permute-start.2 = (bf16[128,2048]{1,0:T(8,128)(2,1)S(1)}, bf16[128,2048]{1,0:T(8,128)(2,1)S(1)}, u32[]{:S(2)}, u32[]{:S(2)}) collective-permute-start(bf16[128,2048]{1,0:T(8,128)(2,1)S(1)} %slice.6), channel_id=1, source_target_pairs={{0,4},{1,5},{2,6},{3,7},{4,0},{5,1},{6,2},{7,3},{8,12},{9,13},{10,... | collective-permute-start | bytes 1572872 | tf_op jit(solution)/shard_map/ppermute | solution.py:237
  10.7 34.3 %collective-permute-start = (bf16[128,4096]{1,0:T(8,128)(2,1)}, bf16[128,4096]{1,0:T(8,128)(2,1)S(1)}, u32[]{:S(2)}, u32[]{:S(2)}) collective-permute-start(bf16[128,4096]{1,0:T(8,128)(2,1)} %tok.4), channel_id=1, source_target_pairs={{0,1},{1,0},{2,3},{3,2},{4,5},{5,4},{6,7},{7,6},{8,9},{9,8},{10,11... | collective-permute-start | bytes 3145736 | tf_op jit(solution)/shard_map/ppermute | solution.py:237
  12.6 4.6 %collective-permute-start.4 = (f32[128,128]{1,0:T(8,128)S(1)}, f32[128,128]{1,0:T(8,128)S(1)}, u32[]{:S(2)}, u32[]{:S(2)}) collective-permute-start(f32[128,128]{1,0:T(8,128)S(1)} %fusion.1), channel_id=1, source_target_pairs={{0,12},{1,13},{2,14},{3,15},{4,8},{5,9},{6,10},{7,11},{8,4},{9,5},... | collective-permute-start | bytes 196616 | tf_op jit(solution)/shard_map/ppermute | solution.py:237
  22.1 22.8 %copy-start.4 = (bf16[128,2048]{1,0:T(8,128)(2,1)}, bf16[128,2048]{1,0:T(8,128)(2,1)S(1)}, u32[]{:S(2)}) copy-start(bf16[128,2048]{1,0:T(8,128)(2,1)S(1)} %collective-permute-done.2.m4) | copy-start | bytes 1572868
  22.1 17.4 %collective-permute-start.9 = (bf16[128,2048]{1,0:T(8,128)(2,1)}, bf16[128,2048]{1,0:T(8,128)(2,1)S(1)}, u32[]{:S(2)}, u32[]{:S(2)}) collective-permute-start(bf16[128,2048]{1,0:T(8,128)(2,1)} %slice.7), channel_id=1, source_target_pairs={{0,4},{1,5},{2,6},{3,7},{4,0},{5,1},{6,2},{7,3},{8,12},{9,13},{10,... | collective-permute-start | bytes 1572872 | tf_op jit(solution)/shard_map/ppermute | solution.py:237
  22.4 18.8 %collective-permute-start.1 = (bf16[128,2048]{1,0:T(8,128)(2,1)S(1)}, bf16[128,2048]{1,0:T(8,128)(2,1)S(1)}, u32[]{:S(2)}, u32[]{:S(2)}) collective-permute-start(bf16[128,2048]{1,0:T(8,128)(2,1)S(1)} %slice.6), channel_id=1, source_target_pairs={{0,2},{1,3},{2,0},{3,1},{4,6},{5,7},{6,4},{7,5},{8,10},{9,11},{10,... | collective-permute-start | bytes 1572872 | tf_op jit(solution)/shard_map/ppermute | solution.py:237
  25.6 19.3 %collective-permute-start.3 = (bf16[128,2048]{1,0:T(8,128)(2,1)S(1)}, bf16[128,2048]{1,0:T(8,128)(2,1)S(1)}, u32[]{:S(2)}, u32[]{:S(2)}) collective-permute-start(bf16[128,2048]{1,0:T(8,128)(2,1)S(1)} %collective-permute-done.2.m4), channel_id=1, source_target_pairs={{0,12},{1,13},{2,14},{3,15},{4,8},{5,9},{6,10},{7,11},{8,4},{9,5},... | collective-permute-start | bytes 1572872 | tf_op jit(solution)/shard_map/ppermute | solution.py:237
  28.0 1.3 collective-permute-start.5
  29.3 8.5 %collective-permute-start.6 = (f32[128,128]{1,0:T(8,128)S(1)}, f32[128,128]{1,0:T(8,128)S(1)}, u32[]{:S(2)}, u32[]{:S(2)}) collective-permute-start(f32[128,128]{1,0:T(8,128)S(1)} %add.50), channel_id=1, source_target_pairs={{0,2},{1,3},{2,0},{3,1},{4,6},{5,7},{6,4},{7,5},{8,10},{9,11},{10,... | collective-permute-start | bytes 196616 | tf_op jit(solution)/shard_map/ppermute | solution.py:237
  37.8 6.5 %collective-permute-start.7 = (f32[128,128]{1,0:T(8,128)S(1)}, f32[128,128]{1,0:T(8,128)S(1)}, u32[]{:S(2)}, u32[]{:S(2)}) collective-permute-start(f32[128,128]{1,0:T(8,128)S(1)} %add.51), channel_id=1, source_target_pairs={{0,4},{1,5},{2,6},{3,7},{4,0},{5,1},{6,2},{7,3},{8,12},{9,13},{10,... | collective-permute-start | bytes 196616 | tf_op jit(solution)/shard_map/ppermute | solution.py:237
  39.5 18.7 %copy-start.5 = (bf16[128,2048]{1,0:T(8,128)(2,1)}, bf16[128,2048]{1,0:T(8,128)(2,1)S(1)}, u32[]{:S(2)}) copy-start(bf16[128,2048]{1,0:T(8,128)(2,1)S(1)} %collective-permute-done.9.m4) | copy-start | bytes 1572868
  39.5 18.7 %collective-permute-start.10 = (bf16[128,2048]{1,0:T(8,128)(2,1)S(1)}, bf16[128,2048]{1,0:T(8,128)(2,1)S(1)}, u32[]{:S(2)}, u32[]{:S(2)}) collective-permute-start(bf16[128,2048]{1,0:T(8,128)(2,1)S(1)} %collective-permute-done.9.m4), channel_id=1, source_target_pairs={{0,12},{1,13},{2,14},{3,15},{4,8},{5,9},{6,10},{7,11},{8,4},{9,5},... | collective-permute-start | bytes 1572872 | tf_op jit(solution)/shard_map/ppermute | solution.py:237
  41.3 3.7 %copy-start.6 = (bf16[128,2048]{1,0:T(8,128)(2,1)}, bf16[128,2048]{1,0:T(8,128)(2,1)S(1)}, u32[]{:S(2)}) copy-start(bf16[128,2048]{1,0:T(8,128)(2,1)S(1)} %collective-permute-done.1.m2) | copy-start | bytes 1572868
  41.3 16.9 %collective-permute-start.8 = (bf16[128,2048]{1,0:T(8,128)(2,1)}, bf16[128,2048]{1,0:T(8,128)(2,1)}, u32[]{:S(2)}, u32[]{:S(2)}) collective-permute-start(bf16[128,2048]{1,0:T(8,128)(2,1)} %slice.7), channel_id=1, source_target_pairs={{0,2},{1,3},{2,0},{3,1},{4,6},{5,7},{6,4},{7,5},{8,10},{9,11},{10,... | collective-permute-start | bytes 1572872 | tf_op jit(solution)/shard_map/ppermute | solution.py:237
  44.9 1.0 copy-start.1
  45.9 0.8 copy-start.7
  58.2 0.8 copy-start.8
  66.8 0.8 copy-start.10
  66.8 0.9 copy-start.11
  66.8 11.7 %copy-start.14 = (bf16[128,2048]{1,0:T(8,128)(2,1)S(1)}, bf16[128,2048]{1,0:T(8,128)(2,1)}, u32[]{:S(2)}) copy-start(bf16[128,2048]{1,0:T(8,128)(2,1)} %get-tuple-element.51) | copy-start | bytes 1572868
  67.6 5.7 %collective-permute-start.11 = (f32[128,128]{1,0:T(8,128)S(1)}, f32[128,128]{1,0:T(8,128)S(1)}, u32[]{:S(2)}, u32[]{:S(2)}) collective-permute-start(f32[128,128]{1,0:T(8,128)S(1)} %add.53), channel_id=1, source_target_pairs={{0,4},{1,5},{2,6},{3,7},{4,0},{5,1},{6,2},{7,3},{8,12},{9,13},{10,... | collective-permute-start | bytes 196616 | tf_op jit(solution)/shard_map/ppermute | solution.py:237
  73.3 51.5 %copy-start.2 = (bf16[128,2048]{1,0:T(8,128)(2,1)S(1)}, bf16[128,2048]{1,0:T(8,128)(2,1)}, u32[]{:S(2)}) copy-start(bf16[128,2048]{1,0:T(8,128)(2,1)} %get-tuple-element.61) | copy-start | bytes 1572868
  73.4 5.1 %collective-permute-start.12 = (f32[128,128]{1,0:T(8,128)S(1)}, f32[128,128]{1,0:T(8,128)S(1)}, u32[]{:S(2)}, u32[]{:S(2)}) collective-permute-start(f32[128,128]{1,0:T(8,128)S(1)} %add.54), channel_id=1, source_target_pairs={{0,12},{1,13},{2,14},{3,15},{4,8},{5,9},{6,10},{7,11},{8,4},{9,5},... | collective-permute-start | bytes 196616 | tf_op jit(solution)/shard_map/ppermute | solution.py:237
  78.5 10.3 %collective-permute-start.15 = (bf16[128,2048]{1,0:T(8,128)(2,1)S(1)}, bf16[128,2048]{1,0:T(8,128)(2,1)S(1)}, u32[]{:S(2)}, u32[]{:S(2)}) collective-permute-start(bf16[128,2048]{1,0:T(8,128)(2,1)S(1)} %copy-done.14), channel_id=1, source_target_pairs={{0,12},{1,13},{2,14},{3,15},{4,8},{5,9},{6,10},{7,11},{8,4},{9,5},... | collective-permute-start | bytes 1572872 | tf_op jit(solution)/shard_map/ppermute | solution.py:237
  78.6 6.0 %collective-permute-start.13 = (f32[128,128]{1,0:T(8,128)S(1)}, f32[128,128]{1,0:T(8,128)S(1)}, u32[]{:S(2)}, u32[]{:S(2)}) collective-permute-start(f32[128,128]{1,0:T(8,128)S(1)} %add.55), channel_id=1, source_target_pairs={{0,2},{1,3},{2,0},{3,1},{4,6},{5,7},{6,4},{7,5},{8,10},{9,11},{10,... | collective-permute-start | bytes 196616 | tf_op jit(solution)/shard_map/ppermute | solution.py:237
  84.6 7.8 %collective-permute-start.14 = (bf16[128,2048]{1,0:T(8,128)(2,1)}, bf16[128,2048]{1,0:T(8,128)(2,1)S(1)}, u32[]{:S(2)}, u32[]{:S(2)}) collective-permute-start(bf16[128,2048]{1,0:T(8,128)(2,1)} %get-tuple-element.49), channel_id=1, source_target_pairs={{0,1},{1,0},{2,3},{3,2},{4,5},{5,4},{6,7},{7,6},{8,9},{9,8},{10,11... | collective-permute-start | bytes 1572872 | tf_op jit(solution)/shard_map/ppermute | solution.py:237
  84.7 16.2 %collective-permute-start.17 = (bf16[128,2048]{1,0:T(8,128)(2,1)}, bf16[128,2048]{1,0:T(8,128)(2,1)}, u32[]{:S(2)}, u32[]{:S(2)}) collective-permute-start(bf16[128,2048]{1,0:T(8,128)(2,1)} %get-tuple-element.54), channel_id=1, source_target_pairs={{0,2},{1,3},{2,0},{3,1},{4,6},{5,7},{6,4},{7,5},{8,10},{9,11},{10,... | collective-permute-start | bytes 1572872 | tf_op jit(solution)/shard_map/ppermute | solution.py:237
  86.9 1.3 collective-permute-start.16
  87.0 14.4 %collective-permute-start.19 = (bf16[128,2048]{1,0:T(8,128)(2,1)}, bf16[128,2048]{1,0:T(8,128)(2,1)S(1)}, u32[]{:S(2)}, u32[]{:S(2)}) collective-permute-start(bf16[128,2048]{1,0:T(8,128)(2,1)} %get-tuple-element.56), channel_id=1, source_target_pairs={{0,12},{1,13},{2,14},{3,15},{4,8},{5,9},{6,10},{7,11},{8,4},{9,5},... | collective-permute-start | bytes 1572872 | tf_op jit(solution)/shard_map/ppermute | solution.py:237
  88.7 38.4 %copy-start.3 = (bf16[128,2048]{1,0:T(8,128)(2,1)S(1)}, bf16[128,2048]{1,0:T(8,128)(2,1)}, u32[]{:S(2)}) copy-start(bf16[128,2048]{1,0:T(8,128)(2,1)} %get-tuple-element.62) | copy-start | bytes 1572868
  92.4 0.8 copy-start.13
  100.9 13.5 %collective-permute-start.18 = (bf16[8,128,256]{2,1,0:T(8,128)(2,1)S(1)}, bf16[8,128,256]{2,1,0:T(8,128)(2,1)S(1)}, u32[]{:S(2)}, u32[]{:S(2)}) collective-permute-start(bf16[8,128,256]{2,1,0:T(8,128)(2,1)S(1)} %dynamic-slice_bitcast_fusion), channel_id=1, source_target_pairs={{0,128},{16,144},{32,160},{48,176},{64,192},{80,208},{96,224},{112... | collective-permute-start | bytes 1572872 | tf_op jit(solution)/shard_map/ppermute | solution.py:254
  114.3 13.1 %copy-start.12 = (bf16[128,2048]{1,0:T(8,128)(2,1)S(1)}, bf16[128,2048]{1,0:T(8,128)(2,1)}, u32[]{:S(2)}) copy-start(bf16[128,2048]{1,0:T(8,128)(2,1)} %get-tuple-element.60) | copy-start | bytes 1572868
  116.4 39.1 %all-to-all-start = ((bf16[8,128,256]{2,1,0:T(8,128)(2,1)}), bf16[8,128,256]{2,1,0:T(8,128)(2,1)S(1)}, u32[]{:S(2)}, u32[]{:S(2)}) async-start(bf16[8,128,256]{2,1,0:T(8,128)(2,1)} %fusion), calls=%async_computation.1 | async-start | bytes 1048576 | tf_op jit(solution)/shard_map/all_to_all | solution.py:304
  125.0 15.0 %collective-permute-start.22 = (bf16[128,2048]{1,0:T(8,128)(2,1)S(1)}, bf16[128,2048]{1,0:T(8,128)(2,1)S(1)}, u32[]{:S(2)}, u32[]{:S(2)}) collective-permute-start(bf16[128,2048]{1,0:T(8,128)(2,1)S(1)} %add.61), channel_id=1, source_target_pairs={{0,4},{1,5},{2,6},{3,7},{4,0},{5,1},{6,2},{7,3},{8,12},{9,13},{10,... | collective-permute-start | bytes 1572872 | tf_op jit(solution)/shard_map/ppermute | solution.py:237
  127.3 21.7 %collective-permute-start.23 = (bf16[128,2048]{1,0:T(8,128)(2,1)S(1)}, bf16[128,2048]{1,0:T(8,128)(2,1)S(1)}, u32[]{:S(2)}, u32[]{:S(2)}) collective-permute-start(bf16[128,2048]{1,0:T(8,128)(2,1)S(1)} %add.62), channel_id=1, source_target_pairs={{0,4},{1,5},{2,6},{3,7},{4,0},{5,1},{6,2},{7,3},{8,12},{9,13},{10,... | collective-permute-start | bytes 1572872 | tf_op jit(solution)/shard_map/ppermute | solution.py:237
  127.4 21.6 %collective-permute-start.20 = (bf16[128,2048]{1,0:T(8,128)(2,1)}, bf16[128,2048]{1,0:T(8,128)(2,1)S(1)}, u32[]{:S(2)}, u32[]{:S(2)}) collective-permute-start(bf16[128,2048]{1,0:T(8,128)(2,1)} %get-tuple-element.58), channel_id=1, source_target_pairs={{0,1},{1,0},{2,3},{3,2},{4,5},{5,4},{6,7},{7,6},{8,9},{9,8},{10,11... | collective-permute-start | bytes 1572872 | tf_op jit(solution)/shard_map/ppermute | solution.py:237
  127.5 21.5 %collective-permute-start.21 = (bf16[128,2048]{1,0:T(8,128)(2,1)S(1)}, bf16[128,2048]{1,0:T(8,128)(2,1)S(1)}, u32[]{:S(2)}, u32[]{:S(2)}) collective-permute-start(bf16[128,2048]{1,0:T(8,128)(2,1)S(1)} %copy-done.12), channel_id=1, source_target_pairs={{0,2},{1,3},{2,0},{3,1},{4,6},{5,7},{6,4},{7,5},{8,10},{9,11},{10,... | collective-permute-start | bytes 1572872 | tf_op jit(solution)/shard_map/ppermute | solution.py:237
  140.0 9.0 %copy-start.15 = (bf16[128,2048]{1,0:T(8,128)(2,1)}, bf16[128,2048]{1,0:T(8,128)(2,1)S(1)}, u32[]{:S(2)}) copy-start(bf16[128,2048]{1,0:T(8,128)(2,1)S(1)} %collective-permute-done.22.refs_6_) | copy-start | bytes 1572868
  148.9 0.8 copy-start.16
  148.9 1.0 copy-start.17
  150.0 0.8 copy-start.18
  156.6 6.1 %collective-permute-start.24 = (bf16[448,256]{1,0:T(8,128)(2,1)S(1)}, bf16[448,256]{1,0:T(8,128)(2,1)S(1)}, u32[]{:S(2)}, u32[]{:S(2)}) collective-permute-start(bf16[448,256]{1,0:T(8,128)(2,1)S(1)} %dynamic-slice_bitcast_fusion.1), channel_id=1, source_target_pairs={{0,128},{16,144},{32,160},{48,176},{64,192},{80,208},{96,224},{112... | collective-permute-start | bytes 688136 | tf_op jit(solution)/shard_map/ppermute | solution.py:254
  162.7 0.7 copy-start.9
Sparse Core Ops, SparseCore 0:
  66.9 52.1 reduce-scatter.1

commit v2 on v1

--- a/solution.py
+++ b/solution.py
@@ -141,24 +141,35 @@
     )(slope, section)
 
 
-def down_kernel(tok, lat, out):
-    for c in range(tok.shape[1] // CHUNK):
-        out[0, c] = dot(lat[...], tok[:, c * CHUNK : (c + 1) * CHUNK], 0, 0).astype(BF16)
-
-
-def run_down(tokens, latent_grad):
+def down_kernel(side, tok, lat, keep, send):
+    def fill(out):
+        for c in range(tok.shape[1] // CHUNK):
+            out[c] = dot(lat[...], tok[:, c * CHUNK : (c + 1) * CHUNK], 0, 0).astype(BF16)
+
+    pl.when(pl.program_id(0) == 0)(lambda: fill(send))
+    pl.when(pl.program_id(0) == 1)(lambda: fill(keep))
+
+
+def run_down(x, tokens, latent_grad):
     rows, width = tokens.shape
     rank = latent_grad.shape[1]
     half = width // 2
+    block = pl.BlockSpec((RING, rank, CHUNK), lambda i, side: (0, 0, 0))
     return pl.pallas_call(
         down_kernel,
-        grid=(2,),
-        in_specs=[pl.BlockSpec((rows, half), lambda i: (0, i)), pl.BlockSpec((rows, rank), lambda i: (0, 0))],
-        out_specs=pl.BlockSpec((1, RING, rank, CHUNK), lambda i: (i, 0, 0, 0)),
-        out_shape=jax.ShapeDtypeStruct((2, RING, rank, CHUNK), BF16),
+        grid_spec=pltpu.PrefetchScalarGridSpec(
+            num_scalar_prefetch=1,
+            grid=(2,),
+            in_specs=[
+                pl.BlockSpec((rows, half), lambda i, side: (0, (1 + i + side[0]) % 2)),
+                pl.BlockSpec((rows, rank), lambda i, side: (0, 0)),
+            ],
+            out_specs=[block, block],
+        ),
+        out_shape=[jax.ShapeDtypeStruct((RING, rank, CHUNK), BF16)] * 2,
         cost_estimate=pl.CostEstimate(flops=300_000_000, bytes_accessed=10 << 20, transcendentals=0),
         name="down_part",
-    )(tokens, latent_grad)
+    )(jnp.full((1,), x, jnp.int32), tokens, latent_grad)
 
 
 def final_kernel(*refs):
@@ -262,18 +273,18 @@
 
     h0 = tokens[:, :half]
     m4_0 = flip(h0, 4)
-    m2_0 = flip(h0, 2)
     m1 = flip(tokens, 1)
     part = jnp.dot(tokens, low_down, preferred_element_type=F32)
     part = part + flip(part, 12)
+    part = part + flip(part, 1)
     h1 = after(tokens, part)[:, half:]
-    part = part + flip(part, 1)
+    m4_1 = flip(after(h1, m4_0, part), 4)
+    m8_0 = flip(after(m4_0, part), 12)
     part = part + flip(part, 2)
-    m4_1 = flip(after(h1, m4_0), 4)
-    m8_0 = flip(m4_0, 12)
-    m2_1 = flip(after(h1, m2_0), 2)
+    m2_0 = flip(after(h0, part), 2)
     part = part + flip(part, 4)
     m8_1 = flip(m4_1, 12)
+    m2_1 = flip(after(h1, m2_0), 2)
     latent = part.astype(BF16)
 
     factors = (cotangent, diag_factor, section_factors, latent, low_up)
@@ -284,21 +295,19 @@
     summed = ring_sum(grads)
 
     part = lat0 + lat1
-    arrived = flip(part, 4)
+    arrived = flip(part, 2)
     b1_1, b2_1, b4_1, b8_1 = run_back(1, slope1, section_factors)
     part = part + after(arrived, b8_1)
+    r2_0, r1_0 = flip(after(b2_0, part), 2), flip(after(b1_0, part), 1)
+    part = part + flip(part, 4)
     part = part + flip(part, 12)
     q0, q1 = flip(after(b8_0, part), 12), flip(after(b8_1, part), 12)
-    part = part + flip(part, 2)
-    r2_0, r1_0 = flip(after(b2_0, part), 2), flip(after(b1_0, part), 1)
-    part = part + flip(part, 1)
+    part = part + after(flip(part, 1), r2_0, r1_0)
     latent_grad = part.astype(BF16)
 
-    down = run_down(after(tokens, q0), latent_grad)
-    keep = lax.dynamic_index_in_dim(down, x, 0, keepdims=False)
-    send = lax.dynamic_index_in_dim(down, 1 - x, 0, keepdims=False)
+    keep, send = run_down(x, tokens, latent_grad)
+    pair = (keep.astype(F32) + after(cross(send), q0, q1).astype(F32)).astype(BF16)
     s0 = flip(b4_0 + q0, 4)
-    pair = (keep.astype(F32) + after(cross(after(send, r2_0, r1_0)), q1).astype(F32)).astype(BF16)
     r2_1, r1_1 = flip(after(b2_1, pair), 2), flip(after(b1_1, pair), 1)
     groups = [[side * RING + z for z in range(RING)] for side in range(2)]
     pair = lax.all_to_all(pair, "dp", 0, 0, axis_index_groups=groups, tiled=True)

time: 174 us -> 170 us (0.977)
  local copies, waits for them, and re-layouts: 11.6 us -> 9.04 us
    ppermute x2, waiting for transfers between devices: 16.6 us -> 4.89 us  [cross(): return lax.ppermute(value, 'dp', [(i, i ^ RING) for i in range(2 * RING)])]
    ppermute x23, waiting for transfers between devices: 52.2 us -> 63.2 us  [flip(): return lax.ppermute(value, 'tensor', [(i, i ^ mask) for i in range(16)])]
    unnamed x39 -> x35, local copies, waits for them, and re-layouts: 7.54 us -> 6.07 us
  transfers between devices with their start and end apart: 27 -> 27, of which waited for: 12 -> 14; matrix products, arithmetic and copies ran while one was open for 5% -> 4% of each run, Pallas kernels for 13% -> 13%
where the time goes in v2:
time: 170 us; the launch traced here: 169 us
  waiting for transfers between devices  68.2 us (40%)
  starting transfers between devices  39.4 us (23%)
  Pallas kernels  32.1 us (19%)
  between operations  14.3 us (8%)
  local copies, waits for them, and re-layouts  9.04 us (5%)
  other arithmetic  3.68 us (2%)
  matrix products  1.96 us (1%)
    ppermute x23, waiting for transfers between devices, flip(): return lax.ppermute(value, 'tensor', [(i, i ^ mask) for i in range(16)])  63.2 us
    ppermute x23, starting transfers between devices, flip(): return lax.ppermute(value, 'tensor', [(i, i ^ mask) for i in range(16)])  29.6 us
    pallas_call x2, Pallas kernels, run_main(): pl.pallas_call(main_kernel, grid=(steps,), in_specs=in_specs, out_specs=[...  15.5 us
    all_to_all x1, starting transfers between devices, per_device(): lax.all_to_all(pair, 'dp', 0, 0, axis_index_groups=groups, tiled=True)  8.47 us
    pallas_call x2, Pallas kernels, run_back(): pl.pallas_call(back_kernel, grid=(steps,), in_specs=[local, pl.BlockSpec(...  7.35 us
    unnamed x35, local copies, waits for them, and re-layouts  6.07 us
    ppermute x2, waiting for transfers between devices, cross(): return lax.ppermute(value, 'dp', [(i, i ^ RING) for i in range(2 * RING)])  4.89 us
    pallas_call x1, Pallas kernels, run_final(): pl.pallas_call(final_kernel, grid=(steps,), in_specs=half_specs(rows, ste...  4.74 us
  transfers between devices with their start and end apart: 27, of which 14 were waited for; matrix products, arithmetic and copies ran while one was open for 4% of the time, Pallas kernels for 13%

profile of v2, /device:TPU:8, one launch (start us, length us, event | category | flops | bytes accessed | tf_op | source)
XLA Modules:
  0.0 168.6 jit_solution(2953810793241500066)
XLA Ops:
  7.2 0.0 reduce-scatter.2.cloned.1.call-start
  7.2 1.2 slice.6
  8.4 2.3 %collective-permute-start.5 = (bf16[128,2048]{1,0:T(8,128)(2,1)S(1)}, bf16[128,2048]{1,0:T(8,128)(2,1)S(1)}, u32[]{:S(2)}, u32[]{:S(2)}) collective-permute-start(bf16[128,2048]{1,0:T(8,128)(2,1)S(1)} %slice.6), channel_id=1, source_target_pairs={{0,4},{1,5},{2,6},{3,7},{4,0},{5,1},{6,2},{7,3},{8,12},{9,13},{10,... | collective-permute-start | bytes 1572872 | tf_op jit(solution)/shard_map/ppermute | solution.py:248
  10.7 2.0 %fusion = f32[128,128]{1,0:T(8,128)S(1)} fusion(bf16[128,4096]{1,0:T(8,128)(2,1)} %tok.5, bf16[4096,128]{1,0:T(8,128)(2,1)} %refs_9_.1), kind=kOutput, calls=%fused_computation.6 | convolution fusion | flops 134217728 | bytes 2162688 | tf_op jit(solution)/shard_map/dot_general | solution.py:277
  12.6 0.8 collective-permute-start.1
  13.4 3.8 %collective-permute-done.1 = f32[128,128]{1,0:T(8,128)S(1)} collective-permute-done((f32[128,128]{1,0:T(8,128)S(1)}, f32[128,128]{1,0:T(8,128)S(1)}, u32[]{:S(2)}, u32[]{:S(2)}) %collective-permute-start.1) | collective-permute-done | bytes 65568 | tf_op jit(solution)/shard_map/ppermute | solution.py:248
  17.2 0.1 collective-permute-start.2
  17.3 1.2 collective-permute-done.2
  18.6 2.0 %collective-permute-start.3 = (f32[128,128]{1,0:T(8,128)S(1)}, f32[128,128]{1,0:T(8,128)S(1)}, u32[]{:S(2)}, u32[]{:S(2)}) collective-permute-start(f32[128,128]{1,0:T(8,128)S(1)} %add.45), channel_id=1, source_target_pairs={{0,2},{1,3},{2,0},{3,1},{4,6},{5,7},{6,4},{7,5},{8,10},{9,11},{10,... | collective-permute-start | bytes 196616 | tf_op jit(solution)/shard_map/ppermute | solution.py:248
  20.6 0.9 slice.7
  21.5 3.0 %collective-permute-done.3 = f32[128,128]{1,0:T(8,128)S(1)} collective-permute-done((f32[128,128]{1,0:T(8,128)S(1)}, f32[128,128]{1,0:T(8,128)S(1)}, u32[]{:S(2)}, u32[]{:S(2)}) %collective-permute-start.3) | collective-permute-done | bytes 65568 | tf_op jit(solution)/shard_map/ppermute | solution.py:248
  24.5 1.4 collective-permute-start.9
  25.9 2.8 %collective-permute-start.4 = (bf16[128,2048]{1,0:T(8,128)(2,1)S(1)}, bf16[128,2048]{1,0:T(8,128)(2,1)S(1)}, u32[]{:S(2)}, u32[]{:S(2)}) collective-permute-start(bf16[128,2048]{1,0:T(8,128)(2,1)S(1)} %slice.6), channel_id=1, source_target_pairs={{0,2},{1,3},{2,0},{3,1},{4,6},{5,7},{6,4},{7,5},{8,10},{9,11},{10,... | collective-permute-start | bytes 1572872 | tf_op jit(solution)/shard_map/ppermute | solution.py:248
  28.6 1.6 collective-permute-start.6
  30.2 0.7 collective-permute-start.7
  30.9 7.4 %collective-permute-done.9.m4 = bf16[128,2048]{1,0:T(8,128)(2,1)S(1)} collective-permute-done((bf16[128,2048]{1,0:T(8,128)(2,1)}, bf16[128,2048]{1,0:T(8,128)(2,1)S(1)}, u32[]{:S(2)}, u32[]{:S(2)}) %collective-permute-start.9) | collective-permute-done | bytes 524320 | tf_op jit(solution)/shard_map/ppermute | solution.py:248
  38.3 0.9 collective-permute-start.10
  39.2 0.7 collective-permute-done.4.m2
  39.9 2.8 %collective-permute-start.8 = (bf16[128,2048]{1,0:T(8,128)(2,1)}, bf16[128,2048]{1,0:T(8,128)(2,1)S(1)}, u32[]{:S(2)}, u32[]{:S(2)}) collective-permute-start(bf16[128,2048]{1,0:T(8,128)(2,1)} %slice.7), channel_id=1, source_target_pairs={{0,2},{1,3},{2,0},{3,1},{4,6},{5,7},{6,4},{7,5},{8,10},{9,11},{10,... | collective-permute-start | bytes 1572872 | tf_op jit(solution)/shard_map/ppermute | solution.py:248
  42.7 0.6 add_convert_fusion.2.latent
  43.3 0.2 collective-permute-done.6.m8
  43.5 0.8 copy-done.9
  44.3 1.0 copy-done.1
  45.3 7.8 %main_part.2 = (bf16[128,2048]{1,0:T(8,128)(2,1)}, f32[128,128]{1,0:T(8,128)}, bf16[8,2,448,256]{3,2,1,0:T(8,128)(2,1)}) custom-call(bf16[128,4096]{1,0:T(8,128)(2,1)} %tok.5, bf16[128,4096]{1,0:T(8,128)(2,1)} %copy-done.1, bf16[128,2048]{1,0:T(8,128)(2,1)} %copy-done.7, bf16[128,2048]{1,0:T(8,128)(2,1)} %copy-done.4, bf16[128,2048]{1,0:T(8,128)(2,1)} %copy-done.9, ...), custom_call_target="tpu_custom_call" | custom-call | flops 2000000000 | bytes 29360128 | tf_op jit(solution)/shard_map/main_part/pallas_call | solution.py:89
  53.0 3.7 %back_products.2 = (bf16[128,2048]{1,0:T(8,128)(2,1)}, bf16[128,2048]{1,0:T(8,128)(2,1)}, bf16[128,2048]{1,0:T(8,128)(2,1)}, bf16[128,2048]{1,0:T(8,128)(2,1)}) custom-call(bf16[128,2048]{1,0:T(8,128)(2,1)} %get-tuple-element.41.slope.refs_0_, bf16[4,64,4096]{2,1,0:T(8,128)(2,1)} %sec.7), custom_call_target="tpu_custom_call" | custom-call | flops 1000000000 | bytes 13631488 | tf_op jit(solution)/shard_map/back_products/pallas_call | solution.py:132
  56.8 0.8 copy-done.6
  57.6 0.2 copy-done.8
  57.8 7.7 %main_part.3 = (bf16[128,2048]{1,0:T(8,128)(2,1)}, f32[128,128]{1,0:T(8,128)}, bf16[8,2,448,256]{3,2,1,0:T(8,128)(2,1)}) custom-call(bf16[128,4096]{1,0:T(8,128)(2,1)} %tok.5, bf16[128,4096]{1,0:T(8,128)(2,1)} %copy-done.1, bf16[128,2048]{1,0:T(8,128)(2,1)} %copy-done.8, bf16[128,2048]{1,0:T(8,128)(2,1)} %copy-done.5, ...), custom_call_target="tpu_custom_call", output_to_operand_aliasing={{2}: (10, {})} | custom-call | flops 2000000000 | bytes 29360128 | tf_op jit(solution)/shard_map/main_part/pallas_call | solution.py:89
  65.6 0.8 copy-done.11
  66.4 0.7 collective-permute-start.11
  67.1 3.6 %back_products.3 = (bf16[128,2048]{1,0:T(8,128)(2,1)}, bf16[128,2048]{1,0:T(8,128)(2,1)}, bf16[128,2048]{1,0:T(8,128)(2,1)}, bf16[128,2048]{1,0:T(8,128)(2,1)}) custom-call(bf16[128,2048]{1,0:T(8,128)(2,1)} %get-tuple-element.48.slope.refs_1_, bf16[4,64,4096]{2,1,0:T(8,128)(2,1)} %sec.7), custom_call_target="tpu_custom_call" | custom-call | flops 1000000000 | bytes 13631488 | tf_op jit(solution)/shard_map/back_products/pallas_call | solution.py:132
  70.8 1.5 collective-permute-done.11
  72.3 1.5 collective-permute-start.16
  73.8 1.7 %collective-permute-start.13 = (f32[128,128]{1,0:T(8,128)S(1)}, f32[128,128]{1,0:T(8,128)S(1)}, u32[]{:S(2)}, u32[]{:S(2)}) collective-permute-start(f32[128,128]{1,0:T(8,128)S(1)} %add.49), channel_id=1, source_target_pairs={{0,4},{1,5},{2,6},{3,7},{4,0},{5,1},{6,2},{7,3},{8,12},{9,13},{10,... | collective-permute-start | bytes 196616 | tf_op jit(solution)/shard_map/ppermute | solution.py:248
  75.5 2.8 %collective-permute-done.13 = f32[128,128]{1,0:T(8,128)S(1)} collective-permute-done((f32[128,128]{1,0:T(8,128)S(1)}, f32[128,128]{1,0:T(8,128)S(1)}, u32[]{:S(2)}, u32[]{:S(2)}) %collective-permute-start.13) | collective-permute-done | bytes 65568 | tf_op jit(solution)/shard_map/ppermute | solution.py:248
  78.3 1.7 collective-permute-start.14
  80.0 2.7 %collective-permute-done.14 = f32[128,128]{1,0:T(8,128)S(1)} collective-permute-done((f32[128,128]{1,0:T(8,128)S(1)}, f32[128,128]{1,0:T(8,128)S(1)}, u32[]{:S(2)}, u32[]{:S(2)}) %collective-permute-start.14) | collective-permute-done | bytes 65568 | tf_op jit(solution)/shard_map/ppermute | solution.py:248
  82.7 0.1 collective-permute-start.15
  82.8 1.7 %collective-permute-start.19 = (bf16[128,2048]{1,0:T(8,128)(2,1)}, bf16[128,2048]{1,0:T(8,128)(2,1)S(1)}, u32[]{:S(2)}, u32[]{:S(2)}) collective-permute-start(bf16[128,2048]{1,0:T(8,128)(2,1)} %get-tuple-element.62), channel_id=1, source_target_pairs={{0,12},{1,13},{2,14},{3,15},{4,8},{5,9},{6,10},{7,11},{8,4},{9,5},... | collective-permute-start | bytes 1572872 | tf_op jit(solution)/shard_map/ppermute | solution.py:248
  84.5 0.4 collective-permute-start.18
  85.0 0.7 add_convert_fusion.1.lat.refs_10_
  85.6 2.7 %down_part.1 = (bf16[8,128,256]{2,1,0:T(8,128)(2,1)}, bf16[8,128,256]{2,1,0:T(8,128)(2,1)}) custom-call(s32[1]{0:T(128)} %bitcast.side, bf16[128,4096]{1,0:T(8,128)(2,1)} %tok.5, bf16[128,128]{1,0:T(8,128)(2,1)} %add_convert_fusion.1.lat.refs_10_), custom_call_target="tpu_custom_call" | custom-call | flops 300000000 | bytes 10485760 | tf_op jit(solution)/shard_map/down_part/pallas_call | solution.py:158
  88.4 0.6 collective-permute-start.17
  88.9 8.9 %collective-permute-done.19 = bf16[128,2048]{1,0:T(8,128)(2,1)S(1)} collective-permute-done((bf16[128,2048]{1,0:T(8,128)(2,1)}, bf16[128,2048]{1,0:T(8,128)(2,1)S(1)}, u32[]{:S(2)}, u32[]{:S(2)}) %collective-permute-start.19) | collective-permute-done | bytes 524320 | tf_op jit(solution)/shard_map/ppermute | solution.py:248
  97.9 10.7 %collective-permute-done.18 = bf16[128,2048]{1,0:T(8,128)(2,1)S(1)} collective-permute-done((bf16[128,2048]{1,0:T(8,128)(2,1)}, bf16[128,2048]{1,0:T(8,128)(2,1)S(1)}, u32[]{:S(2)}, u32[]{:S(2)}) %collective-permute-start.18) | collective-permute-done | bytes 524320 | tf_op jit(solution)/shard_map/ppermute | solution.py:248
  108.6 2.0 %add_convert_fusion = bf16[8,128,256]{2,1,0:T(8,128)(2,1)} fusion(bf16[8,128,256]{2,1,0:T(8,128)(2,1)S(1)} %collective-permute-done.17, bf16[8,128,256]{2,1,0:T(8,128)(2,1)} %get-tuple-element.59), kind=kLoop, calls=%fused_computation.1 | loop fusion | flops 1048576 | bytes 1572864 | tf_op jit(solution)/shard_map/convert_element_type | solution.py:309
  110.5 8.5 %all-to-all-start = ((bf16[8,128,256]{2,1,0:T(8,128)(2,1)}), bf16[8,128,256]{2,1,0:T(8,128)(2,1)S(1)}, u32[]{:S(2)}, u32[]{:S(2)}) async-start(bf16[8,128,256]{2,1,0:T(8,128)(2,1)} %add_convert_fusion), calls=%async_computation.1 | async-start | bytes 1048576 | tf_op jit(solution)/shard_map/all_to_all | solution.py:313
  119.0 0.1 add.55
  119.2 4.2 %collective-permute-start.23 = (bf16[128,2048]{1,0:T(8,128)(2,1)S(1)}, bf16[128,2048]{1,0:T(8,128)(2,1)S(1)}, u32[]{:S(2)}, u32[]{:S(2)}) collective-permute-start(bf16[128,2048]{1,0:T(8,128)(2,1)S(1)} %add.55), channel_id=1, source_target_pairs={{0,4},{1,5},{2,6},{3,7},{4,0},{5,1},{6,2},{7,3},{8,12},{9,13},{10,... | collective-permute-start | bytes 1572872 | tf_op jit(solution)/shard_map/ppermute | solution.py:248
  123.4 0.1 add.54
  123.5 0.1 collective-permute-start.22
  123.6 2.2 %collective-permute-start.21 = (bf16[128,2048]{1,0:T(8,128)(2,1)}, bf16[128,2048]{1,0:T(8,128)(2,1)S(1)}, u32[]{:S(2)}, u32[]{:S(2)}) collective-permute-start(bf16[128,2048]{1,0:T(8,128)(2,1)} %get-tuple-element.66), channel_id=1, source_target_pairs={{0,2},{1,3},{2,0},{3,1},{4,6},{5,7},{6,4},{7,5},{8,10},{9,11},{10,... | collective-permute-start | bytes 1572872 | tf_op jit(solution)/shard_map/ppermute | solution.py:248
  125.8 10.4 %collective-permute-done.23.refs_7_ = bf16[128,2048]{1,0:T(8,128)(2,1)S(1)} collective-permute-done((bf16[128,2048]{1,0:T(8,128)(2,1)S(1)}, bf16[128,2048]{1,0:T(8,128)(2,1)S(1)}, u32[]{:S(2)}, u32[]{:S(2)}) %collective-permute-start.23) | collective-permute-done | bytes 524320 | tf_op jit(solution)/shard_map/ppermute | solution.py:248
  136.2 9.9 %collective-permute-done.22.refs_6_ = bf16[128,2048]{1,0:T(8,128)(2,1)S(1)} collective-permute-done((bf16[128,2048]{1,0:T(8,128)(2,1)S(1)}, bf16[128,2048]{1,0:T(8,128)(2,1)S(1)}, u32[]{:S(2)}, u32[]{:S(2)}) %collective-permute-start.22) | collective-permute-done | bytes 524320 | tf_op jit(solution)/shard_map/ppermute | solution.py:248
  146.1 0.8 copy-done.15
  146.9 0.2 copy-done.16
  147.1 4.7 %token_grad.1 = bf16[128,4096]{1,0:T(8,128)(2,1)} custom-call(bf16[128,2048]{1,0:T(8,128)(2,1)} %get-tuple-element.41.slope.refs_0_, bf16[128,2048]{1,0:T(8,128)(2,1)} %get-tuple-element.48.slope.refs_1_, bf16[128,2048]{1,0:T(8,128)(2,1)} %collective-permute-done.12.refs_2_, bf16[128,2048]{1,0:T(8,128)(2,1)} %collective-permute-done.20.refs_3_, ...), custom_call_target="tpu_custom_call" | custom-call | flops 2000000000 | bytes 17825792 | tf_op jit(solution)/shard_map/token_grad/pallas_call | solution.py:194
  151.8 0.1 convert_reduce_fusion
  152.0 1.0 dynamic-slice_bitcast_fusion
  152.9 0.7 collective-permute-start.24
  153.6 0.8 copy.12
  154.4 4.9 %collective-permute-done.24.arrived = bf16[448,256]{1,0:T(8,128)(2,1)S(1)} collective-permute-done((bf16[448,256]{1,0:T(8,128)(2,1)S(1)}, bf16[448,256]{1,0:T(8,128)(2,1)S(1)}, u32[]{:S(2)}, u32[]{:S(2)}) %collective-permute-start.24) | collective-permute-done | bytes 229408 | tf_op jit(solution)/shard_map/ppermute | solution.py:265
  159.3 0.7 copy-done.10
  160.0 1.8 %finish.1 = (f32[64,256]{1,0:T(8,128)}, f32[4,64,256]{2,1,0:T(8,128)}, f32[128,256]{1,0:T(8,128)}) custom-call(s32[1]{0:T(128)} %bitcast.side, bf16[2,448,256]{2,1,0:T(8,128)(2,1)} %bitcast.11, bf16[448,256]{1,0:T(8,128)(2,1)} %copy-done.10), custom_call_target="tpu_custom_call" | custom-call | flops 300000 | bytes 4194304 | tf_op jit(solution)/shard_map/finish/pallas_call | solution.py:222
  (51 shorter events, 0.2 us)
Async XLA Ops:
  7.2 13.5 %copy-start = (bf16[128,4096]{1,0:T(8,128)(2,1)S(1)}, bf16[128,4096]{1,0:T(8,128)(2,1)}, u32[]{:S(2)}) copy-start(bf16[128,4096]{1,0:T(8,128)(2,1)} %tok.5) | copy-start | bytes 3145732
  7.2 144.8 %reduce-scatter.2.cloned.1.call-start = ((), (), s32[]{:S(2)}) async-start(), calls=%async_computation.2 | async-start | bytes 4128768 | tf_op jit(solution)/shard_map/reduce_scatter | solution.py:258
  8.4 16.1 %collective-permute-start.5 = (bf16[128,2048]{1,0:T(8,128)(2,1)S(1)}, bf16[128,2048]{1,0:T(8,128)(2,1)S(1)}, u32[]{:S(2)}, u32[]{:S(2)}) collective-permute-start(bf16[128,2048]{1,0:T(8,128)(2,1)S(1)} %slice.6), channel_id=1, source_target_pairs={{0,4},{1,5},{2,6},{3,7},{4,0},{5,1},{6,2},{7,3},{8,12},{9,13},{10,... | collective-permute-start | bytes 1572872 | tf_op jit(solution)/shard_map/ppermute | solution.py:248
  10.7 33.6 %collective-permute-start = (bf16[128,4096]{1,0:T(8,128)(2,1)}, bf16[128,4096]{1,0:T(8,128)(2,1)S(1)}, u32[]{:S(2)}, u32[]{:S(2)}) collective-permute-start(bf16[128,4096]{1,0:T(8,128)(2,1)} %tok.5), channel_id=1, source_target_pairs={{0,1},{1,0},{2,3},{3,2},{4,5},{5,4},{6,7},{7,6},{8,9},{9,8},{10,11... | collective-permute-start | bytes 3145736 | tf_op jit(solution)/shard_map/ppermute | solution.py:248
  12.6 4.6 %collective-permute-start.1 = (f32[128,128]{1,0:T(8,128)S(1)}, f32[128,128]{1,0:T(8,128)S(1)}, u32[]{:S(2)}, u32[]{:S(2)}) collective-permute-start(f32[128,128]{1,0:T(8,128)S(1)} %fusion), channel_id=1, source_target_pairs={{0,12},{1,13},{2,14},{3,15},{4,8},{5,9},{6,10},{7,11},{8,4},{9,5},... | collective-permute-start | bytes 196616 | tf_op jit(solution)/shard_map/ppermute | solution.py:248
  17.2 1.3 collective-permute-start.2
  18.6 5.9 %collective-permute-start.3 = (f32[128,128]{1,0:T(8,128)S(1)}, f32[128,128]{1,0:T(8,128)S(1)}, u32[]{:S(2)}, u32[]{:S(2)}) collective-permute-start(f32[128,128]{1,0:T(8,128)S(1)} %add.45), channel_id=1, source_target_pairs={{0,2},{1,3},{2,0},{3,1},{4,6},{5,7},{6,4},{7,5},{8,10},{9,11},{10,... | collective-permute-start | bytes 196616 | tf_op jit(solution)/shard_map/ppermute | solution.py:248
  24.5 19.8 %copy-start.4 = (bf16[128,2048]{1,0:T(8,128)(2,1)}, bf16[128,2048]{1,0:T(8,128)(2,1)S(1)}, u32[]{:S(2)}) copy-start(bf16[128,2048]{1,0:T(8,128)(2,1)S(1)} %collective-permute-done.5.m4) | copy-start | bytes 1572868
  24.5 13.8 %collective-permute-start.9 = (bf16[128,2048]{1,0:T(8,128)(2,1)}, bf16[128,2048]{1,0:T(8,128)(2,1)S(1)}, u32[]{:S(2)}, u32[]{:S(2)}) collective-permute-start(bf16[128,2048]{1,0:T(8,128)(2,1)} %slice.7), channel_id=1, source_target_pairs={{0,4},{1,5},{2,6},{3,7},{4,0},{5,1},{6,2},{7,3},{8,12},{9,13},{10,... | collective-permute-start | bytes 1572872 | tf_op jit(solution)/shard_map/ppermute | solution.py:248
  25.9 14.1 %collective-permute-start.4 = (bf16[128,2048]{1,0:T(8,128)(2,1)S(1)}, bf16[128,2048]{1,0:T(8,128)(2,1)S(1)}, u32[]{:S(2)}, u32[]{:S(2)}) collective-permute-start(bf16[128,2048]{1,0:T(8,128)(2,1)S(1)} %slice.6), channel_id=1, source_target_pairs={{0,2},{1,3},{2,0},{3,1},{4,6},{5,7},{6,4},{7,5},{8,10},{9,11},{10,... | collective-permute-start | bytes 1572872 | tf_op jit(solution)/shard_map/ppermute | solution.py:248
  28.6 14.9 %collective-permute-start.6 = (bf16[128,2048]{1,0:T(8,128)(2,1)S(1)}, bf16[128,2048]{1,0:T(8,128)(2,1)S(1)}, u32[]{:S(2)}, u32[]{:S(2)}) collective-permute-start(bf16[128,2048]{1,0:T(8,128)(2,1)S(1)} %collective-permute-done.5.m4), channel_id=1, source_target_pairs={{0,12},{1,13},{2,14},{3,15},{4,8},{5,9},{6,10},{7,11},{8,4},{9,5},... | collective-permute-start | bytes 1572872 | tf_op jit(solution)/shard_map/ppermute | solution.py:248
  30.2 12.5 %collective-permute-start.7 = (f32[128,128]{1,0:T(8,128)S(1)}, f32[128,128]{1,0:T(8,128)S(1)}, u32[]{:S(2)}, u32[]{:S(2)}) collective-permute-start(f32[128,128]{1,0:T(8,128)S(1)} %add.46), channel_id=1, source_target_pairs={{0,4},{1,5},{2,6},{3,7},{4,0},{5,1},{6,2},{7,3},{8,12},{9,13},{10,... | collective-permute-start | bytes 196616 | tf_op jit(solution)/shard_map/ppermute | solution.py:248
  38.3 18.4 %copy-start.5 = (bf16[128,2048]{1,0:T(8,128)(2,1)}, bf16[128,2048]{1,0:T(8,128)(2,1)S(1)}, u32[]{:S(2)}) copy-start(bf16[128,2048]{1,0:T(8,128)(2,1)S(1)} %collective-permute-done.9.m4) | copy-start | bytes 1572868
  38.3 18.4 %collective-permute-start.10 = (bf16[128,2048]{1,0:T(8,128)(2,1)S(1)}, bf16[128,2048]{1,0:T(8,128)(2,1)S(1)}, u32[]{:S(2)}, u32[]{:S(2)}) collective-permute-start(bf16[128,2048]{1,0:T(8,128)(2,1)S(1)} %collective-permute-done.9.m4), channel_id=1, source_target_pairs={{0,12},{1,13},{2,14},{3,15},{4,8},{5,9},{6,10},{7,11},{8,4},{9,5},... | collective-permute-start | bytes 1572872 | tf_op jit(solution)/shard_map/ppermute | solution.py:248
  39.9 4.4 %copy-start.7 = (bf16[128,2048]{1,0:T(8,128)(2,1)}, bf16[128,2048]{1,0:T(8,128)(2,1)S(1)}, u32[]{:S(2)}) copy-start(bf16[128,2048]{1,0:T(8,128)(2,1)S(1)} %collective-permute-done.4.m2) | copy-start | bytes 1572868
  39.9 16.8 %collective-permute-start.8 = (bf16[128,2048]{1,0:T(8,128)(2,1)}, bf16[128,2048]{1,0:T(8,128)(2,1)S(1)}, u32[]{:S(2)}, u32[]{:S(2)}) collective-permute-start(bf16[128,2048]{1,0:T(8,128)(2,1)} %slice.7), channel_id=1, source_target_pairs={{0,2},{1,3},{2,0},{3,1},{4,6},{5,7},{6,4},{7,5},{8,10},{9,11},{10,... | collective-permute-start | bytes 1572872 | tf_op jit(solution)/shard_map/ppermute | solution.py:248
  43.5 0.8 copy-start.9
  44.3 1.0 copy-start.1
  56.7 0.8 copy-start.6
  56.7 1.0 copy-start.8
  65.5 0.8 copy-start.11
  65.5 0.9 copy-start.12
  66.4 5.9 %collective-permute-start.11 = (f32[128,128]{1,0:T(8,128)S(1)}, f32[128,128]{1,0:T(8,128)S(1)}, u32[]{:S(2)}, u32[]{:S(2)}) collective-permute-start(f32[128,128]{1,0:T(8,128)S(1)} %add.48), channel_id=1, source_target_pairs={{0,2},{1,3},{2,0},{3,1},{4,6},{5,7},{6,4},{7,5},{8,10},{9,11},{10,... | collective-permute-start | bytes 196616 | tf_op jit(solution)/shard_map/ppermute | solution.py:248
  70.8 48.3 %copy-start.3 = (bf16[128,2048]{1,0:T(8,128)(2,1)S(1)}, bf16[128,2048]{1,0:T(8,128)(2,1)}, u32[]{:S(2)}) copy-start(bf16[128,2048]{1,0:T(8,128)(2,1)} %get-tuple-element.68) | copy-start | bytes 1572868
  70.8 52.6 %copy-start.2 = (bf16[128,2048]{1,0:T(8,128)(2,1)S(1)}, bf16[128,2048]{1,0:T(8,128)(2,1)}, u32[]{:S(2)}) copy-start(bf16[128,2048]{1,0:T(8,128)(2,1)} %get-tuple-element.67) | copy-start | bytes 1572868
  72.3 12.7 %collective-permute-start.16 = (bf16[128,2048]{1,0:T(8,128)(2,1)}, bf16[128,2048]{1,0:T(8,128)(2,1)S(1)}, u32[]{:S(2)}, u32[]{:S(2)}) collective-permute-start(bf16[128,2048]{1,0:T(8,128)(2,1)} %get-tuple-element.57), channel_id=1, source_target_pairs={{0,2},{1,3},{2,0},{3,1},{4,6},{5,7},{6,4},{7,5},{8,10},{9,11},{10,... | collective-permute-start | bytes 1572872 | tf_op jit(solution)/shard_map/ppermute | solution.py:248
  73.8 11.2 %collective-permute-start.12 = (bf16[128,2048]{1,0:T(8,128)(2,1)}, bf16[128,2048]{1,0:T(8,128)(2,1)}, u32[]{:S(2)}, u32[]{:S(2)}) collective-permute-start(bf16[128,2048]{1,0:T(8,128)(2,1)} %get-tuple-element.54), channel_id=1, source_target_pairs={{0,1},{1,0},{2,3},{3,2},{4,5},{5,4},{6,7},{7,6},{8,9},{9,8},{10,11... | collective-permute-start | bytes 1572872 | tf_op jit(solution)/shard_map/ppermute | solution.py:248
  73.8 4.5 %collective-permute-start.13 = (f32[128,128]{1,0:T(8,128)S(1)}, f32[128,128]{1,0:T(8,128)S(1)}, u32[]{:S(2)}, u32[]{:S(2)}) collective-permute-start(f32[128,128]{1,0:T(8,128)S(1)} %add.49), channel_id=1, source_target_pairs={{0,4},{1,5},{2,6},{3,7},{4,0},{5,1},{6,2},{7,3},{8,12},{9,13},{10,... | collective-permute-start | bytes 196616 | tf_op jit(solution)/shard_map/ppermute | solution.py:248
  78.3 4.4 %collective-permute-start.14 = (f32[128,128]{1,0:T(8,128)S(1)}, f32[128,128]{1,0:T(8,128)S(1)}, u32[]{:S(2)}, u32[]{:S(2)}) collective-permute-start(f32[128,128]{1,0:T(8,128)S(1)} %add.50), channel_id=1, source_target_pairs={{0,12},{1,13},{2,14},{3,15},{4,8},{5,9},{6,10},{7,11},{8,4},{9,5},... | collective-permute-start | bytes 196616 | tf_op jit(solution)/shard_map/ppermute | solution.py:248
  82.7 2.3 %collective-permute-start.15 = (f32[128,128]{1,0:T(8,128)S(1)}, f32[128,128]{1,0:T(8,128)S(1)}, u32[]{:S(2)}, u32[]{:S(2)}) collective-permute-start(f32[128,128]{1,0:T(8,128)S(1)} %add.51), channel_id=1, source_target_pairs={{0,1},{1,0},{2,3},{3,2},{4,5},{5,4},{6,7},{7,6},{8,9},{9,8},{10,11... | collective-permute-start | bytes 196616 | tf_op jit(solution)/shard_map/ppermute | solution.py:248
  82.8 15.1 %collective-permute-start.19 = (bf16[128,2048]{1,0:T(8,128)(2,1)}, bf16[128,2048]{1,0:T(8,128)(2,1)S(1)}, u32[]{:S(2)}, u32[]{:S(2)}) collective-permute-start(bf16[128,2048]{1,0:T(8,128)(2,1)} %get-tuple-element.62), channel_id=1, source_target_pairs={{0,12},{1,13},{2,14},{3,15},{4,8},{5,9},{6,10},{7,11},{8,4},{9,5},... | collective-permute-start | bytes 1572872 | tf_op jit(solution)/shard_map/ppermute | solution.py:248
  84.5 24.1 %collective-permute-start.18 = (bf16[128,2048]{1,0:T(8,128)(2,1)}, bf16[128,2048]{1,0:T(8,128)(2,1)S(1)}, u32[]{:S(2)}, u32[]{:S(2)}) collective-permute-start(bf16[128,2048]{1,0:T(8,128)(2,1)} %get-tuple-element.61), channel_id=1, source_target_pairs={{0,12},{1,13},{2,14},{3,15},{4,8},{5,9},{6,10},{7,11},{8,4},{9,5},... | collective-permute-start | bytes 1572872 | tf_op jit(solution)/shard_map/ppermute | solution.py:248
  84.9 34.1 %copy-start.13 = (bf16[128,2048]{1,0:T(8,128)(2,1)}, bf16[128,2048]{1,0:T(8,128)(2,1)S(1)}, u32[]{:S(2)}) copy-start(bf16[128,2048]{1,0:T(8,128)(2,1)S(1)} %collective-permute-done.16.refs_4_) | copy-start | bytes 1572868
  88.4 20.2 %collective-permute-start.17 = (bf16[8,128,256]{2,1,0:T(8,128)(2,1)}, bf16[8,128,256]{2,1,0:T(8,128)(2,1)S(1)}, u32[]{:S(2)}, u32[]{:S(2)}) collective-permute-start(bf16[8,128,256]{2,1,0:T(8,128)(2,1)} %get-tuple-element.60), channel_id=1, source_target_pairs={{0,128},{16,144},{32,160},{48,176},{64,192},{80,208},{96,224},{112... | collective-permute-start | bytes 1572872 | tf_op jit(solution)/shard_map/ppermute | solution.py:265
  110.5 41.3 %all-to-all-start = ((bf16[8,128,256]{2,1,0:T(8,128)(2,1)}), bf16[8,128,256]{2,1,0:T(8,128)(2,1)S(1)}, u32[]{:S(2)}, u32[]{:S(2)}) async-start(bf16[8,128,256]{2,1,0:T(8,128)(2,1)} %add_convert_fusion), calls=%async_computation.1 | async-start | bytes 1048576 | tf_op jit(solution)/shard_map/all_to_all | solution.py:313
  119.2 17.0 %collective-permute-start.23 = (bf16[128,2048]{1,0:T(8,128)(2,1)S(1)}, bf16[128,2048]{1,0:T(8,128)(2,1)S(1)}, u32[]{:S(2)}, u32[]{:S(2)}) collective-permute-start(bf16[128,2048]{1,0:T(8,128)(2,1)S(1)} %add.55), channel_id=1, source_target_pairs={{0,4},{1,5},{2,6},{3,7},{4,0},{5,1},{6,2},{7,3},{8,12},{9,13},{10,... | collective-permute-start | bytes 1572872 | tf_op jit(solution)/shard_map/ppermute | solution.py:248
  123.5 22.6 %collective-permute-start.22 = (bf16[128,2048]{1,0:T(8,128)(2,1)S(1)}, bf16[128,2048]{1,0:T(8,128)(2,1)S(1)}, u32[]{:S(2)}, u32[]{:S(2)}) collective-permute-start(bf16[128,2048]{1,0:T(8,128)(2,1)S(1)} %add.54), channel_id=1, source_target_pairs={{0,4},{1,5},{2,6},{3,7},{4,0},{5,1},{6,2},{7,3},{8,12},{9,13},{10,... | collective-permute-start | bytes 1572872 | tf_op jit(solution)/shard_map/ppermute | solution.py:248
  123.6 22.5 %collective-permute-start.21 = (bf16[128,2048]{1,0:T(8,128)(2,1)}, bf16[128,2048]{1,0:T(8,128)(2,1)S(1)}, u32[]{:S(2)}, u32[]{:S(2)}) collective-permute-start(bf16[128,2048]{1,0:T(8,128)(2,1)} %get-tuple-element.66), channel_id=1, source_target_pairs={{0,2},{1,3},{2,0},{3,1},{4,6},{5,7},{6,4},{7,5},{8,10},{9,11},{10,... | collective-permute-start | bytes 1572872 | tf_op jit(solution)/shard_map/ppermute | solution.py:248
  125.8 20.3 %collective-permute-start.20 = (bf16[128,2048]{1,0:T(8,128)(2,1)}, bf16[128,2048]{1,0:T(8,128)(2,1)}, u32[]{:S(2)}, u32[]{:S(2)}) collective-permute-start(bf16[128,2048]{1,0:T(8,128)(2,1)} %get-tuple-element.64), channel_id=1, source_target_pairs={{0,1},{1,0},{2,3},{3,2},{4,5},{5,4},{6,7},{7,6},{8,9},{9,8},{10,11... | collective-permute-start | bytes 1572872 | tf_op jit(solution)/shard_map/ppermute | solution.py:248
  136.2 9.9 %copy-start.14 = (bf16[128,2048]{1,0:T(8,128)(2,1)}, bf16[128,2048]{1,0:T(8,128)(2,1)S(1)}, u32[]{:S(2)}) copy-start(bf16[128,2048]{1,0:T(8,128)(2,1)S(1)} %collective-permute-done.23.refs_7_) | copy-start | bytes 1572868
  146.1 0.8 copy-start.15
  146.1 1.0 copy-start.16
  152.9 6.3 %collective-permute-start.24 = (bf16[448,256]{1,0:T(8,128)(2,1)S(1)}, bf16[448,256]{1,0:T(8,128)(2,1)S(1)}, u32[]{:S(2)}, u32[]{:S(2)}) collective-permute-start(bf16[448,256]{1,0:T(8,128)(2,1)S(1)} %dynamic-slice_bitcast_fusion), channel_id=1, source_target_pairs={{0,128},{16,144},{32,160},{48,176},{64,192},{80,208},{96,224},{112... | collective-permute-start | bytes 688136 | tf_op jit(solution)/shard_map/ppermute | solution.py:265
  159.3 0.7 copy-start.10
Sparse Core Ops, SparseCore 0:
  65.7 51.1 reduce-scatter.1

commit v3 on v2

--- a/solution.py
+++ b/solution.py
@@ -9,9 +9,9 @@
 
 BLOCK = 64
 CHUNK = 256
-MAIN_STEP, BACK_STEP, FINAL_STEP = 512, 1024, 2048
+MAIN_STEP, FINAL_STEP = 512, 2048
 RING = 8
-VMEM = 60 << 20
+VMEM = 62 << 20
 F32 = jnp.float32
 BF16 = jnp.bfloat16
 
@@ -116,29 +116,33 @@
     ]
 
 
-def back_kernel(slope, sec, b1, b2, b4, b8):
+def back_kernel(low, high, sec, b1, *halves):
     mask = block_mask()
-    for c in range(slope.shape[1] // CHUNK):
-        cs = slice(c * CHUNK, (c + 1) * CHUNK)
-        for b, ref in enumerate((b1, b2, b4, b8)):
-            ref[:, cs] = dot(slope[:, cs], spread(sec[b, :, cs], mask), 1, 1).astype(BF16)
-
-
-def run_back(part, slope, section):
-    rows, width = slope.shape
-    steps = width // BACK_STEP
-    base = part * steps
-    local = pl.BlockSpec((rows, BACK_STEP), lambda i: (0, i))
+
+    def fill(slope, outs):
+        for c in range(slope.shape[1] // CHUNK):
+            cs = slice(c * CHUNK, (c + 1) * CHUNK)
+            for b, out in enumerate(outs):
+                out[:, cs] = dot(slope[:, cs], spread(sec[b, :, cs], mask), 1, 1).astype(BF16)
+
+    pl.when(pl.program_id(0) == 0)(lambda: fill(low, (b1, *halves[0::2])))
+    pl.when(pl.program_id(0) == 1)(lambda: fill(high, (b1, *halves[1::2])))
+
+
+def run_back(slopes, section):
+    rows, half = slopes[0].shape
+    fixed = pl.BlockSpec((rows, half), lambda i: (0, 0))
+    moving = pl.BlockSpec((rows, half), lambda i: (0, i))
     return pl.pallas_call(
         back_kernel,
-        grid=(steps,),
-        in_specs=[local, pl.BlockSpec((4, BLOCK, BACK_STEP), lambda i: (0, 0, base + i))],
-        out_specs=[local] * 4,
-        out_shape=[jax.ShapeDtypeStruct((rows, width), BF16)] * 4,
+        grid=(2,),
+        in_specs=[fixed, fixed, pl.BlockSpec((4, BLOCK, half), lambda i: (0, 0, i))],
+        out_specs=[moving] + [fixed] * 6,
+        out_shape=[jax.ShapeDtypeStruct((rows, 2 * half), BF16)] + [jax.ShapeDtypeStruct((rows, half), BF16)] * 6,
         compiler_params=pltpu.CompilerParams(vmem_limit_bytes=VMEM),
-        cost_estimate=pl.CostEstimate(flops=1_000_000_000, bytes_accessed=13 << 20, transcendentals=0),
+        cost_estimate=pl.CostEstimate(flops=2_000_000_000, bytes_accessed=20 << 20, transcendentals=0),
         name="back_products",
-    )(slope, section)
+    )(*slopes, section)
 
 
 def down_kernel(side, tok, lat, keep, send):
@@ -173,9 +177,9 @@
 
 
 def final_kernel(*refs):
-    pairs, (diag, down, lat, out) = refs[:8], refs[8:]
+    pairs, (r1, diag, down, lat, out) = refs[:6], refs[6:]
     mask = block_mask()
-    slope, r1, r2, r48 = (pick_half(pairs[2 * k], pairs[2 * k + 1]) for k in range(4))
+    slope, r2, r48 = (pick_half(pairs[2 * k], pairs[2 * k + 1]) for k in range(3))
     for c in range(FINAL_STEP // CHUNK):
         cs = slice(c * CHUNK, (c + 1) * CHUNK)
         total = dot(slope[:, cs], spread(diag[:, cs], mask), 1, 1)
@@ -185,7 +189,7 @@
         out[:, cs] = total.astype(BF16)
 
 
-def run_final(pairs, diag, low_down, latent_grad):
+def run_final(pairs, r1, diag, low_down, latent_grad):
     rows, half_width = pairs[0][0].shape
     width = 2 * half_width
     rank = latent_grad.shape[1]
@@ -194,8 +198,9 @@
     return pl.pallas_call(
         final_kernel,
         grid=(steps,),
-        in_specs=half_specs(rows, steps) * 4
+        in_specs=half_specs(rows, steps) * 3
         + [
+            col(rows),
             col(BLOCK),
             pl.BlockSpec((FINAL_STEP, rank), lambda i: (i, 0)),
             pl.BlockSpec((rows, rank), lambda i: (0, 0)),
@@ -205,7 +210,7 @@
         compiler_params=pltpu.CompilerParams(vmem_limit_bytes=VMEM),
         cost_estimate=pl.CostEstimate(flops=2_000_000_000, bytes_accessed=17 << 20, transcendentals=0),
         name="token_grad",
-    )(*[value for pair in pairs for value in pair], diag, low_down, latent_grad)
+    )(*[value for pair in pairs for value in pair], r1, diag, low_down, latent_grad)
 
 
 def finish_kernel(scale, side, summed, arrived, diag, section, up):
@@ -283,39 +288,37 @@
     part = part + flip(part, 2)
     m2_0 = flip(after(h0, part), 2)
     part = part + flip(part, 4)
-    m8_1 = flip(m4_1, 12)
+    m8_1 = flip(after(m4_1, part), 12)
     m2_1 = flip(after(h1, m2_0), 2)
     latent = part.astype(BF16)
 
     factors = (cotangent, diag_factor, section_factors, latent, low_up)
     slope0, lat0, grads = run_main(0, tokens, (m1, m2_0, m4_0, m8_0), *factors, None)
-    b1_0, b2_0, b4_0, b8_0 = run_back(0, slope0, section_factors)
-    moved1 = (m1, m2_1, m4_1, after(m8_1, b8_0))
-    slope1, lat1, grads = run_main(1, tokens, moved1, *factors, grads)
+    slope1, lat1, grads = run_main(1, tokens, (m1, m2_1, m4_1, m8_1), *factors, grads)
     summed = ring_sum(grads)
 
     part = lat0 + lat1
     arrived = flip(part, 2)
-    b1_1, b2_1, b4_1, b8_1 = run_back(1, slope1, section_factors)
-    part = part + after(arrived, b8_1)
-    r2_0, r1_0 = flip(after(b2_0, part), 2), flip(after(b1_0, part), 1)
-    part = part + flip(part, 4)
+    b1, b2_0, b2_1, b4_0, b4_1, b8_0, b8_1 = run_back((slope0, slope1), section_factors)
+    part = part + after(arrived, b1)
+    r2_0, r1 = flip(after(b2_0, part), 2), flip(after(b1, part), 1)
     part = part + flip(part, 12)
     q0, q1 = flip(after(b8_0, part), 12), flip(after(b8_1, part), 12)
-    part = part + after(flip(part, 1), r2_0, r1_0)
+    part = part + flip(part, 4)
+    part = part + after(flip(part, 1), r2_0, r1)
     latent_grad = part.astype(BF16)
 
     keep, send = run_down(x, tokens, latent_grad)
-    pair = (keep.astype(F32) + after(cross(send), q0, q1).astype(F32)).astype(BF16)
     s0 = flip(b4_0 + q0, 4)
-    r2_1, r1_1 = flip(after(b2_1, pair), 2), flip(after(b1_1, pair), 1)
+    pair = (keep.astype(F32) + after(cross(send), q1, s0).astype(F32)).astype(BF16)
+    r2_1 = flip(after(b2_1, send), 2)
     groups = [[side * RING + z for z in range(RING)] for side in range(2)]
     pair = lax.all_to_all(pair, "dp", 0, 0, axis_index_groups=groups, tiled=True)
     down_grad = (jnp.sum(pair.astype(F32), axis=0) * scale).T
     s1 = flip(b4_1 + q1, 4)
-    pairs = ((slope0, slope1), (r1_0, r1_1), (r2_0, r2_1), (s0, s1))
-    token_grad = run_final(pairs, diag_factor, low_down, latent_grad)
     arrived = cross(lax.dynamic_index_in_dim(summed, 1 - x, 0, keepdims=False))
+    pairs = ((slope0, slope1), (r2_0, r2_1), (s0, after(s1, arrived)))
+    token_grad = run_final(pairs, r1, diag_factor, low_down, latent_grad)
     diag_grad, section_grad, up_grad = run_finish(x, summed, arrived, scale)
     return token_grad, diag_grad, section_grad, down_grad, up_grad
 

time: 170 us -> 160 us (0.941)
  waiting for transfers between devices: 68.2 us -> 59.1 us
  local copies, waits for them, and re-layouts: 9.04 us -> 6.08 us
  starting transfers between devices: 39.4 us -> 41.8 us
    ppermute x23 -> x22, waiting for transfers between devices: 63.2 us -> 37.1 us  [flip(): return lax.ppermute(value, 'tensor', [(i, i ^ mask) for i in range(16)])]
    all_to_all x1, waiting for transfers between devices: 0.01 us -> 12.3 us  [per_device(): lax.all_to_all(pair, 'dp', 0, 0, axis_index_groups=groups, tiled=True)]
    ppermute x2, waiting for transfers between devices: 4.89 us -> 9.64 us  [cross(): return lax.ppermute(value, 'dp', [(i, i ^ RING) for i in range(2 * RING)])]
    unnamed x35 -> x21, local copies, waits for them, and re-layouts: 6.07 us -> 3.14 us
    ppermute x23 -> x22, starting transfers between devices: 29.6 us -> 31.8 us  [flip(): return lax.ppermute(value, 'tensor', [(i, i ^ mask) for i in range(16)])]
    pallas_call x2 -> x1, Pallas kernels: 7.35 us -> 6.42 us  [run_back(): pl.pallas_call(back_kernel, grid=(2,), in_specs=[fixed, fixed, pl.BlockSp...]
  transfers between devices with their start and end apart: 27 -> 26, of which waited for: 14 -> 12; matrix products, arithmetic and copies ran while one was open for 4% -> 6% of each run, Pallas kernels for 13% -> 12%
where the time goes in v3:
time: 160 us; the launch traced here: 159 us
  waiting for transfers between devices  59.1 us (37%)
  starting transfers between devices  41.8 us (26%)
  Pallas kernels  31.1 us (19%)
  between operations  14.2 us (9%)
  local copies, waits for them, and re-layouts  6.08 us (4%)
  other arithmetic  4.7 us (3%)
  matrix products  1.96 us (1%)
    ppermute x22, waiting for transfers between devices, flip(): return lax.ppermute(value, 'tensor', [(i, i ^ mask) for i in range(16)])  37.1 us
    ppermute x22, starting transfers between devices, flip(): return lax.ppermute(value, 'tensor', [(i, i ^ mask) for i in range(16)])  31.8 us
    pallas_call x2, Pallas kernels, run_main(): pl.pallas_call(main_kernel, grid=(steps,), in_specs=in_specs, out_specs=[...  15.5 us
    all_to_all x1, waiting for transfers between devices, per_device(): lax.all_to_all(pair, 'dp', 0, 0, axis_index_groups=groups, tiled=True)  12.3 us
    ppermute x2, waiting for transfers between devices, cross(): return lax.ppermute(value, 'dp', [(i, i ^ RING) for i in range(2 * RING)])  9.64 us
    all_to_all x1, starting transfers between devices, per_device(): lax.all_to_all(pair, 'dp', 0, 0, axis_index_groups=groups, tiled=True)  8.7 us
    pallas_call x1, Pallas kernels, run_back(): pl.pallas_call(back_kernel, grid=(2,), in_specs=[fixed, fixed, pl.BlockSp...  6.42 us
    pallas_call x1, Pallas kernels, run_final(): pl.pallas_call(final_kernel, grid=(steps,), in_specs=half_specs(rows, ste...  4.58 us
  transfers between devices with their start and end apart: 26, of which 12 were waited for; matrix products, arithmetic and copies ran while one was open for 6% of the time, Pallas kernels for 12%

profile of v3, /device:TPU:8, one launch (start us, length us, event | category | flops | bytes accessed | tf_op | source)
XLA Modules:
  0.0 159.0 jit_solution(2241273189993931479)
XLA Ops:
  7.2 0.0 copy-start
  7.2 0.0 reduce-scatter.2.cloned.1.call-start
  7.2 1.2 slice.6
  8.4 2.3 %collective-permute-start.5 = (bf16[128,2048]{1,0:T(8,128)(2,1)S(1)}, bf16[128,2048]{1,0:T(8,128)(2,1)S(1)}, u32[]{:S(2)}, u32[]{:S(2)}) collective-permute-start(bf16[128,2048]{1,0:T(8,128)(2,1)S(1)} %slice.6), channel_id=1, source_target_pairs={{0,4},{1,5},{2,6},{3,7},{4,0},{5,1},{6,2},{7,3},{8,12},{9,13},{10,... | collective-permute-start | bytes 1572872 | tf_op jit(solution)/shard_map/ppermute | solution.py:253
  10.7 2.0 %fusion = f32[128,128]{1,0:T(8,128)S(1)} fusion(bf16[128,4096]{1,0:T(8,128)(2,1)} %tok.5, bf16[4096,128]{1,0:T(8,128)(2,1)} %refs_8_.1), kind=kOutput, calls=%fused_computation.5 | convolution fusion | flops 134217728 | bytes 2162688 | tf_op jit(solution)/shard_map/dot_general | solution.py:282
  12.6 0.8 collective-permute-start.1
  13.4 0.0 collective-permute-start
  13.4 3.6 %collective-permute-done.1 = f32[128,128]{1,0:T(8,128)S(1)} collective-permute-done((f32[128,128]{1,0:T(8,128)S(1)}, f32[128,128]{1,0:T(8,128)S(1)}, u32[]{:S(2)}, u32[]{:S(2)}) %collective-permute-start.1) | collective-permute-done | bytes 65568 | tf_op jit(solution)/shard_map/ppermute | solution.py:253
  17.0 0.1 collective-permute-start.2
  17.1 1.2 collective-permute-done.2
  18.3 1.8 %collective-permute-start.3 = (f32[128,128]{1,0:T(8,128)S(1)}, f32[128,128]{1,0:T(8,128)S(1)}, u32[]{:S(2)}, u32[]{:S(2)}) collective-permute-start(f32[128,128]{1,0:T(8,128)S(1)} %add.45), channel_id=1, source_target_pairs={{0,2},{1,3},{2,0},{3,1},{4,6},{5,7},{6,4},{7,5},{8,10},{9,11},{10,... | collective-permute-start | bytes 196616 | tf_op jit(solution)/shard_map/ppermute | solution.py:253
  20.1 0.8 slice.7
  20.9 3.3 %collective-permute-done.3 = f32[128,128]{1,0:T(8,128)S(1)} collective-permute-done((f32[128,128]{1,0:T(8,128)S(1)}, f32[128,128]{1,0:T(8,128)S(1)}, u32[]{:S(2)}, u32[]{:S(2)}) %collective-permute-start.3) | collective-permute-done | bytes 65568 | tf_op jit(solution)/shard_map/ppermute | solution.py:253
  24.2 1.8 %collective-permute-start.4 = (bf16[128,2048]{1,0:T(8,128)(2,1)S(1)}, bf16[128,2048]{1,0:T(8,128)(2,1)S(1)}, u32[]{:S(2)}, u32[]{:S(2)}) collective-permute-start(bf16[128,2048]{1,0:T(8,128)(2,1)S(1)} %slice.6), channel_id=1, source_target_pairs={{0,2},{1,3},{2,0},{3,1},{4,6},{5,7},{6,4},{7,5},{8,10},{9,11},{10,... | collective-permute-start | bytes 1572872 | tf_op jit(solution)/shard_map/ppermute | solution.py:253
  26.0 2.4 %collective-permute-start.9 = (bf16[128,2048]{1,0:T(8,128)(2,1)}, bf16[128,2048]{1,0:T(8,128)(2,1)S(1)}, u32[]{:S(2)}, u32[]{:S(2)}) collective-permute-start(bf16[128,2048]{1,0:T(8,128)(2,1)} %slice.7), channel_id=1, source_target_pairs={{0,4},{1,5},{2,6},{3,7},{4,0},{5,1},{6,2},{7,3},{8,12},{9,13},{10,... | collective-permute-start | bytes 1572872 | tf_op jit(solution)/shard_map/ppermute | solution.py:253
  28.4 1.6 collective-permute-start.6
  30.0 0.7 collective-permute-start.7
  30.7 10.2 %collective-permute-done.7 = f32[128,128]{1,0:T(8,128)S(1)} collective-permute-done((f32[128,128]{1,0:T(8,128)S(1)}, f32[128,128]{1,0:T(8,128)S(1)}, u32[]{:S(2)}, u32[]{:S(2)}) %collective-permute-start.7) | collective-permute-done | bytes 65568 | tf_op jit(solution)/shard_map/ppermute | solution.py:253
  40.8 0.6 add.47.latent
  41.4 1.2 collective-permute-start.8
  42.6 0.0 collective-permute-done.9.m4
  42.6 0.9 collective-permute-start.10
  43.5 0.8 copy-done.5
  44.4 7.7 %main_part.2 = (bf16[128,2048]{1,0:T(8,128)(2,1)}, f32[128,128]{1,0:T(8,128)}, bf16[8,2,448,256]{3,2,1,0:T(8,128)(2,1)}) custom-call(bf16[128,4096]{1,0:T(8,128)(2,1)} %tok.5, bf16[128,4096]{1,0:T(8,128)(2,1)} %collective-permute-done.m1, bf16[128,2048]{1,0:T(8,128)(2,1)} %copy-done.4, bf16[128,2048]{1,0:T(8,128)(2,1)} %copy-done.2, ...), custom_call_target="tpu_custom_call" | custom-call | flops 2000000000 | bytes 29360128 | tf_op jit(solution)/shard_map/main_part/pallas_call | solution.py:89
  52.1 3.1 %collective-permute-done.8.m2 = bf16[128,2048]{1,0:T(8,128)(2,1)} collective-permute-done((bf16[128,2048]{1,0:T(8,128)(2,1)}, bf16[128,2048]{1,0:T(8,128)(2,1)}, u32[]{:S(2)}, u32[]{:S(2)}) %collective-permute-start.8) | collective-permute-done | bytes 524320 | tf_op jit(solution)/shard_map/ppermute | solution.py:253
  55.2 7.8 %main_part.3 = (bf16[128,2048]{1,0:T(8,128)(2,1)}, f32[128,128]{1,0:T(8,128)}, bf16[8,2,448,256]{3,2,1,0:T(8,128)(2,1)}) custom-call(bf16[128,4096]{1,0:T(8,128)(2,1)} %tok.5, bf16[128,4096]{1,0:T(8,128)(2,1)} %collective-permute-done.m1, bf16[128,2048]{1,0:T(8,128)(2,1)} %collective-permute-done.8.m2, ...), custom_call_target="tpu_custom_call", output_to_operand_aliasing={{2}: (10, {})} | custom-call | flops 2000000000 | bytes 29360128 | tf_op jit(solution)/shard_map/main_part/pallas_call | solution.py:89
  62.9 0.0 copy-start.8
  62.9 0.0 reduce-scatter.2.cloned.1.call-update
  63.0 0.8 copy-done.7
  63.8 0.0 copy-done.8
  63.8 1.6 %collective-permute-start.11 = (f32[128,128]{1,0:T(8,128)S(1)}, f32[128,128]{1,0:T(8,128)S(1)}, u32[]{:S(2)}, u32[]{:S(2)}) collective-permute-start(f32[128,128]{1,0:T(8,128)S(1)} %add.48), channel_id=1, source_target_pairs={{0,2},{1,3},{2,0},{3,1},{4,6},{5,7},{6,4},{7,5},{8,10},{9,11},{10,... | collective-permute-start | bytes 196616 | tf_op jit(solution)/shard_map/ppermute | solution.py:253
  65.4 6.4 %back_products.1 = (bf16[128,4096]{1,0:T(8,128)(2,1)}, bf16[128,2048]{1,0:T(8,128)(2,1)}, bf16[128,2048]{1,0:T(8,128)(2,1)}, bf16[128,2048]{1,0:T(8,128)(2,1)}, ...) custom-call(bf16[128,2048]{1,0:T(8,128)(2,1)} %get-tuple-element.40.low.refs_0_, ...), custom_call_target="tpu_custom_call" | custom-call | flops 2000000000 | bytes 20971520 | tf_op jit(solution)/shard_map/back_products/pallas_call | solution.py:136
  71.9 0.3 collective-permute-start.16
  72.2 1.6 %collective-permute-start.13 = (f32[128,128]{1,0:T(8,128)S(1)}, f32[128,128]{1,0:T(8,128)S(1)}, u32[]{:S(2)}, u32[]{:S(2)}) collective-permute-start(f32[128,128]{1,0:T(8,128)S(1)} %add.49), channel_id=1, source_target_pairs={{0,12},{1,13},{2,14},{3,15},{4,8},{5,9},{6,10},{7,11},{8,4},{9,5},... | collective-permute-start | bytes 196616 | tf_op jit(solution)/shard_map/ppermute | solution.py:253
  73.8 2.9 %collective-permute-done.13 = f32[128,128]{1,0:T(8,128)S(1)} collective-permute-done((f32[128,128]{1,0:T(8,128)S(1)}, f32[128,128]{1,0:T(8,128)S(1)}, u32[]{:S(2)}, u32[]{:S(2)}) %collective-permute-start.13) | collective-permute-done | bytes 65568 | tf_op jit(solution)/shard_map/ppermute | solution.py:253
  76.7 1.6 %collective-permute-start.18 = (bf16[128,2048]{1,0:T(8,128)(2,1)}, bf16[128,2048]{1,0:T(8,128)(2,1)S(1)}, u32[]{:S(2)}, u32[]{:S(2)}) collective-permute-start(bf16[128,2048]{1,0:T(8,128)(2,1)} %get-tuple-element.60), channel_id=1, source_target_pairs={{0,12},{1,13},{2,14},{3,15},{4,8},{5,9},{6,10},{7,11},{8,4},{9,5},... | collective-permute-start | bytes 1572872 | tf_op jit(solution)/shard_map/ppermute | solution.py:253
  78.3 2.0 %collective-permute-start.12 = (bf16[128,2048]{1,0:T(8,128)(2,1)}, bf16[128,2048]{1,0:T(8,128)(2,1)}, u32[]{:S(2)}, u32[]{:S(2)}) collective-permute-start(bf16[128,2048]{1,0:T(8,128)(2,1)} %get-tuple-element.52), channel_id=1, source_target_pairs={{0,2},{1,3},{2,0},{3,1},{4,6},{5,7},{6,4},{7,5},{8,10},{9,11},{10,... | collective-permute-start | bytes 1572872 | tf_op jit(solution)/shard_map/ppermute | solution.py:253
  80.3 3.3 %collective-permute-start.14 = (f32[128,128]{1,0:T(8,128)S(1)}, f32[128,128]{1,0:T(8,128)S(1)}, u32[]{:S(2)}, u32[]{:S(2)}) collective-permute-start(f32[128,128]{1,0:T(8,128)S(1)} %add.50), channel_id=1, source_target_pairs={{0,4},{1,5},{2,6},{3,7},{4,0},{5,1},{6,2},{7,3},{8,12},{9,13},{10,... | collective-permute-start | bytes 196616 | tf_op jit(solution)/shard_map/ppermute | solution.py:253
  83.6 2.2 %collective-permute-done.14 = f32[128,128]{1,0:T(8,128)S(1)} collective-permute-done((f32[128,128]{1,0:T(8,128)S(1)}, f32[128,128]{1,0:T(8,128)S(1)}, u32[]{:S(2)}, u32[]{:S(2)}) %collective-permute-start.14) | collective-permute-done | bytes 65568 | tf_op jit(solution)/shard_map/ppermute | solution.py:253
  85.9 0.1 collective-permute-start.15
  86.0 0.6 collective-permute-start.20
  86.6 5.0 %collective-permute-done.18 = bf16[128,2048]{1,0:T(8,128)(2,1)S(1)} collective-permute-done((bf16[128,2048]{1,0:T(8,128)(2,1)}, bf16[128,2048]{1,0:T(8,128)(2,1)S(1)}, u32[]{:S(2)}, u32[]{:S(2)}) %collective-permute-start.18) | collective-permute-done | bytes 524320 | tf_op jit(solution)/shard_map/ppermute | solution.py:253
  91.6 1.2 add.53
  92.8 5.4 %collective-permute-start.19 = (bf16[128,2048]{1,0:T(8,128)(2,1)S(1)}, bf16[128,2048]{1,0:T(8,128)(2,1)}, u32[]{:S(2)}, u32[]{:S(2)}) collective-permute-start(bf16[128,2048]{1,0:T(8,128)(2,1)S(1)} %add.53), channel_id=1, source_target_pairs={{0,4},{1,5},{2,6},{3,7},{4,0},{5,1},{6,2},{7,3},{8,12},{9,13},{10,... | collective-permute-start | bytes 1572872 | tf_op jit(solution)/shard_map/ppermute | solution.py:253
  98.2 0.7 add_convert_fusion.1.lat.refs_9_
  98.9 2.7 %down_part.1 = (bf16[8,128,256]{2,1,0:T(8,128)(2,1)}, bf16[8,128,256]{2,1,0:T(8,128)(2,1)}) custom-call(s32[1]{0:T(128)} %bitcast.side, bf16[128,4096]{1,0:T(8,128)(2,1)} %tok.5, bf16[128,128]{1,0:T(8,128)(2,1)} %add_convert_fusion.1.lat.refs_9_), custom_call_target="tpu_custom_call" | custom-call | flops 300000000 | bytes 10485760 | tf_op jit(solution)/shard_map/down_part/pallas_call | solution.py:162
  101.6 0.6 collective-permute-start.23
  102.2 5.6 %collective-permute-done.19.refs_4_ = bf16[128,2048]{1,0:T(8,128)(2,1)} collective-permute-done((bf16[128,2048]{1,0:T(8,128)(2,1)S(1)}, bf16[128,2048]{1,0:T(8,128)(2,1)}, u32[]{:S(2)}, u32[]{:S(2)}) %collective-permute-start.19) | collective-permute-done | bytes 524320 | tf_op jit(solution)/shard_map/ppermute | solution.py:253
  107.9 5.0 %collective-permute-done.23 = bf16[8,128,256]{2,1,0:T(8,128)(2,1)S(1)} collective-permute-done((bf16[8,128,256]{2,1,0:T(8,128)(2,1)}, bf16[8,128,256]{2,1,0:T(8,128)(2,1)S(1)}, u32[]{:S(2)}, u32[]{:S(2)}) %collective-permute-start.23) | collective-permute-done | bytes 524320 | tf_op jit(solution)/shard_map/ppermute | solution.py:270
  112.9 2.0 %add_convert_fusion = bf16[8,128,256]{2,1,0:T(8,128)(2,1)} fusion(bf16[8,128,256]{2,1,0:T(8,128)(2,1)S(1)} %collective-permute-done.23, bf16[8,128,256]{2,1,0:T(8,128)(2,1)} %get-tuple-element.68), kind=kLoop, calls=%fused_computation.1 | loop fusion | flops 1048576 | bytes 1572864 | tf_op jit(solution)/shard_map/convert_element_type | solution.py:313
  114.8 8.7 %all-to-all-start = ((bf16[8,128,256]{2,1,0:T(8,128)(2,1)}), bf16[8,128,256]{2,1,0:T(8,128)(2,1)S(1)}, u32[]{:S(2)}, u32[]{:S(2)}) async-start(bf16[8,128,256]{2,1,0:T(8,128)(2,1)} %add_convert_fusion), calls=%async_computation.1 | async-start | bytes 1048576 | tf_op jit(solution)/shard_map/all_to_all | solution.py:316
  123.5 0.1 add.54
  123.7 1.0 collective-permute-start.21
  124.6 0.9 collective-permute-start.17
  125.5 12.3 %all-to-all-done = bf16[8,128,256]{2,1,0:T(8,128)(2,1)S(1)} async-done(((bf16[8,128,256]{2,1,0:T(8,128)(2,1)}), bf16[8,128,256]{2,1,0:T(8,128)(2,1)S(1)}, u32[]{:S(2)}, u32[]{:S(2)}) %all-to-all-start) | async-done | bytes 524320 | tf_op jit(solution)/shard_map/all_to_all | solution.py:316
  137.8 0.1 convert_reduce_fusion
  137.9 0.0 reduce-scatter.2.cloned.1.call-done
  137.9 1.0 dynamic-slice_bitcast_fusion
  138.9 0.7 collective-permute-start.22
  139.6 0.8 copy.12
  140.3 4.6 %collective-permute-done.22.arrived = bf16[448,256]{1,0:T(8,128)(2,1)S(1)} collective-permute-done((bf16[448,256]{1,0:T(8,128)(2,1)S(1)}, bf16[448,256]{1,0:T(8,128)(2,1)S(1)}, u32[]{:S(2)}, u32[]{:S(2)}) %collective-permute-start.22) | collective-permute-done | bytes 229408 | tf_op jit(solution)/shard_map/ppermute | solution.py:270
  145.0 0.7 copy-done.6
  145.7 1.8 %finish.1 = (f32[64,256]{1,0:T(8,128)}, f32[4,64,256]{2,1,0:T(8,128)}, f32[128,256]{1,0:T(8,128)}) custom-call(s32[1]{0:T(128)} %bitcast.side, bf16[2,448,256]{2,1,0:T(8,128)(2,1)} %bitcast.11, bf16[448,256]{1,0:T(8,128)(2,1)} %copy-done.6), custom_call_target="tpu_custom_call" | custom-call | flops 300000 | bytes 4194304 | tf_op jit(solution)/shard_map/finish/pallas_call | solution.py:227
  147.5 4.6 %token_grad.1 = bf16[128,4096]{1,0:T(8,128)(2,1)} custom-call(bf16[128,2048]{1,0:T(8,128)(2,1)} %get-tuple-element.40.low.refs_0_, bf16[128,2048]{1,0:T(8,128)(2,1)} %get-tuple-element.46.high.refs_1_, bf16[128,2048]{1,0:T(8,128)(2,1)} %collective-permute-done.12.refs_2_, bf16[128,2048]{1,0:T(8,128)(2,1)} %collective-permute-done.17.refs_3_, ...), custom_call_target="tpu_custom_call" | custom-call | flops 2000000000 | bytes 17825792 | tf_op jit(solution)/shard_map/token_grad/pallas_call | solution.py:198
  (34 shorter events, 0.1 us)
Async XLA Ops:
  7.2 12.9 %copy-start = (bf16[128,4096]{1,0:T(8,128)(2,1)S(1)}, bf16[128,4096]{1,0:T(8,128)(2,1)}, u32[]{:S(2)}) copy-start(bf16[128,4096]{1,0:T(8,128)(2,1)} %tok.5) | copy-start | bytes 3145732
  7.2 130.7 %reduce-scatter.2.cloned.1.call-start = ((), (), s32[]{:S(2)}) async-start(), calls=%async_computation.2 | async-start | bytes 4128768 | tf_op jit(solution)/shard_map/reduce_scatter | solution.py:263
  8.4 17.6 %collective-permute-start.5 = (bf16[128,2048]{1,0:T(8,128)(2,1)S(1)}, bf16[128,2048]{1,0:T(8,128)(2,1)S(1)}, u32[]{:S(2)}, u32[]{:S(2)}) collective-permute-start(bf16[128,2048]{1,0:T(8,128)(2,1)S(1)} %slice.6), channel_id=1, source_target_pairs={{0,4},{1,5},{2,6},{3,7},{4,0},{5,1},{6,2},{7,3},{8,12},{9,13},{10,... | collective-permute-start | bytes 1572872 | tf_op jit(solution)/shard_map/ppermute | solution.py:253
  12.6 4.4 %collective-permute-start.1 = (f32[128,128]{1,0:T(8,128)S(1)}, f32[128,128]{1,0:T(8,128)S(1)}, u32[]{:S(2)}, u32[]{:S(2)}) collective-permute-start(f32[128,128]{1,0:T(8,128)S(1)} %fusion), channel_id=1, source_target_pairs={{0,12},{1,13},{2,14},{3,15},{4,8},{5,9},{6,10},{7,11},{8,4},{9,5},... | collective-permute-start | bytes 196616 | tf_op jit(solution)/shard_map/ppermute | solution.py:253
  13.4 31.0 %collective-permute-start = (bf16[128,4096]{1,0:T(8,128)(2,1)}, bf16[128,4096]{1,0:T(8,128)(2,1)}, u32[]{:S(2)}, u32[]{:S(2)}) collective-permute-start(bf16[128,4096]{1,0:T(8,128)(2,1)} %tok.5), channel_id=1, source_target_pairs={{0,1},{1,0},{2,3},{3,2},{4,5},{5,4},{6,7},{7,6},{8,9},{9,8},{10,11... | collective-permute-start | bytes 3145736 | tf_op jit(solution)/shard_map/ppermute | solution.py:253
  17.0 1.3 collective-permute-start.2
  18.3 5.9 %collective-permute-start.3 = (f32[128,128]{1,0:T(8,128)S(1)}, f32[128,128]{1,0:T(8,128)S(1)}, u32[]{:S(2)}, u32[]{:S(2)}) collective-permute-start(f32[128,128]{1,0:T(8,128)S(1)} %add.45), channel_id=1, source_target_pairs={{0,2},{1,3},{2,0},{3,1},{4,6},{5,7},{6,4},{7,5},{8,10},{9,11},{10,... | collective-permute-start | bytes 196616 | tf_op jit(solution)/shard_map/ppermute | solution.py:253
  24.2 17.2 %collective-permute-start.4 = (bf16[128,2048]{1,0:T(8,128)(2,1)S(1)}, bf16[128,2048]{1,0:T(8,128)(2,1)S(1)}, u32[]{:S(2)}, u32[]{:S(2)}) collective-permute-start(bf16[128,2048]{1,0:T(8,128)(2,1)S(1)} %slice.6), channel_id=1, source_target_pairs={{0,2},{1,3},{2,0},{3,1},{4,6},{5,7},{6,4},{7,5},{8,10},{9,11},{10,... | collective-permute-start | bytes 1572872 | tf_op jit(solution)/shard_map/ppermute | solution.py:253
  26.0 18.4 %copy-start.2 = (bf16[128,2048]{1,0:T(8,128)(2,1)}, bf16[128,2048]{1,0:T(8,128)(2,1)S(1)}, u32[]{:S(2)}) copy-start(bf16[128,2048]{1,0:T(8,128)(2,1)S(1)} %collective-permute-done.5.m4) | copy-start | bytes 1572868
  26.0 16.7 %collective-permute-start.9 = (bf16[128,2048]{1,0:T(8,128)(2,1)}, bf16[128,2048]{1,0:T(8,128)(2,1)S(1)}, u32[]{:S(2)}, u32[]{:S(2)}) collective-permute-start(bf16[128,2048]{1,0:T(8,128)(2,1)} %slice.7), channel_id=1, source_target_pairs={{0,4},{1,5},{2,6},{3,7},{4,0},{5,1},{6,2},{7,3},{8,12},{9,13},{10,... | collective-permute-start | bytes 1572872 | tf_op jit(solution)/shard_map/ppermute | solution.py:253
  28.4 15.2 %collective-permute-start.6 = (bf16[128,2048]{1,0:T(8,128)(2,1)S(1)}, bf16[128,2048]{1,0:T(8,128)(2,1)S(1)}, u32[]{:S(2)}, u32[]{:S(2)}) collective-permute-start(bf16[128,2048]{1,0:T(8,128)(2,1)S(1)} %collective-permute-done.5.m4), channel_id=1, source_target_pairs={{0,12},{1,13},{2,14},{3,15},{4,8},{5,9},{6,10},{7,11},{8,4},{9,5},... | collective-permute-start | bytes 1572872 | tf_op jit(solution)/shard_map/ppermute | solution.py:253
  30.0 10.9 %collective-permute-start.7 = (f32[128,128]{1,0:T(8,128)S(1)}, f32[128,128]{1,0:T(8,128)S(1)}, u32[]{:S(2)}, u32[]{:S(2)}) collective-permute-start(f32[128,128]{1,0:T(8,128)S(1)} %add.46), channel_id=1, source_target_pairs={{0,4},{1,5},{2,6},{3,7},{4,0},{5,1},{6,2},{7,3},{8,12},{9,13},{10,... | collective-permute-start | bytes 196616 | tf_op jit(solution)/shard_map/ppermute | solution.py:253
  41.4 2.9 %copy-start.4 = (bf16[128,2048]{1,0:T(8,128)(2,1)}, bf16[128,2048]{1,0:T(8,128)(2,1)S(1)}, u32[]{:S(2)}) copy-start(bf16[128,2048]{1,0:T(8,128)(2,1)S(1)} %collective-permute-done.4.m2) | copy-start | bytes 1572868
  41.4 13.7 %collective-permute-start.8 = (bf16[128,2048]{1,0:T(8,128)(2,1)}, bf16[128,2048]{1,0:T(8,128)(2,1)}, u32[]{:S(2)}, u32[]{:S(2)}) collective-permute-start(bf16[128,2048]{1,0:T(8,128)(2,1)} %slice.7), channel_id=1, source_target_pairs={{0,2},{1,3},{2,0},{3,1},{4,6},{5,7},{6,4},{7,5},{8,10},{9,11},{10,... | collective-permute-start | bytes 1572872 | tf_op jit(solution)/shard_map/ppermute | solution.py:253
  42.6 9.5 %copy-start.3 = (bf16[128,2048]{1,0:T(8,128)(2,1)}, bf16[128,2048]{1,0:T(8,128)(2,1)S(1)}, u32[]{:S(2)}) copy-start(bf16[128,2048]{1,0:T(8,128)(2,1)S(1)} %collective-permute-done.9.m4) | copy-start | bytes 1572868
  42.6 12.5 %collective-permute-start.10 = (bf16[128,2048]{1,0:T(8,128)(2,1)S(1)}, bf16[128,2048]{1,0:T(8,128)(2,1)}, u32[]{:S(2)}, u32[]{:S(2)}) collective-permute-start(bf16[128,2048]{1,0:T(8,128)(2,1)S(1)} %collective-permute-done.9.m4), channel_id=1, source_target_pairs={{0,12},{1,13},{2,14},{3,15},{4,8},{5,9},{6,10},{7,11},{8,4},{9,5},... | collective-permute-start | bytes 1572872 | tf_op jit(solution)/shard_map/ppermute | solution.py:253
  43.5 0.8 copy-start.5
  62.9 0.8 copy-start.7
  62.9 0.9 copy-start.8
  63.8 8.1 %collective-permute-start.11 = (f32[128,128]{1,0:T(8,128)S(1)}, f32[128,128]{1,0:T(8,128)S(1)}, u32[]{:S(2)}, u32[]{:S(2)}) collective-permute-start(f32[128,128]{1,0:T(8,128)S(1)} %add.48), channel_id=1, source_target_pairs={{0,2},{1,3},{2,0},{3,1},{4,6},{5,7},{6,4},{7,5},{8,10},{9,11},{10,... | collective-permute-start | bytes 196616 | tf_op jit(solution)/shard_map/ppermute | solution.py:253
  71.9 51.7 %copy-start.1 = (bf16[128,2048]{1,0:T(8,128)(2,1)S(1)}, bf16[128,2048]{1,0:T(8,128)(2,1)}, u32[]{:S(2)}) copy-start(bf16[128,2048]{1,0:T(8,128)(2,1)} %get-tuple-element.61) | copy-start | bytes 1572868
  71.9 26.3 %collective-permute-start.16 = (bf16[128,4096]{1,0:T(8,128)(2,1)}, bf16[128,4096]{1,0:T(8,128)(2,1)S(1)}, u32[]{:S(2)}, u32[]{:S(2)}) collective-permute-start(bf16[128,4096]{1,0:T(8,128)(2,1)} %get-tuple-element.54), channel_id=1, source_target_pairs={{0,1},{1,0},{2,3},{3,2},{4,5},{5,4},{6,7},{7,6},{8,9},{9,8},{10,11... | collective-permute-start | bytes 3145736 | tf_op jit(solution)/shard_map/ppermute | solution.py:253
  72.2 4.5 %collective-permute-start.13 = (f32[128,128]{1,0:T(8,128)S(1)}, f32[128,128]{1,0:T(8,128)S(1)}, u32[]{:S(2)}, u32[]{:S(2)}) collective-permute-start(f32[128,128]{1,0:T(8,128)S(1)} %add.49), channel_id=1, source_target_pairs={{0,12},{1,13},{2,14},{3,15},{4,8},{5,9},{6,10},{7,11},{8,4},{9,5},... | collective-permute-start | bytes 196616 | tf_op jit(solution)/shard_map/ppermute | solution.py:253
  76.7 14.9 %collective-permute-start.18 = (bf16[128,2048]{1,0:T(8,128)(2,1)}, bf16[128,2048]{1,0:T(8,128)(2,1)S(1)}, u32[]{:S(2)}, u32[]{:S(2)}) collective-permute-start(bf16[128,2048]{1,0:T(8,128)(2,1)} %get-tuple-element.60), channel_id=1, source_target_pairs={{0,12},{1,13},{2,14},{3,15},{4,8},{5,9},{6,10},{7,11},{8,4},{9,5},... | collective-permute-start | bytes 1572872 | tf_op jit(solution)/shard_map/ppermute | solution.py:253
  78.3 19.9 %collective-permute-start.12 = (bf16[128,2048]{1,0:T(8,128)(2,1)}, bf16[128,2048]{1,0:T(8,128)(2,1)}, u32[]{:S(2)}, u32[]{:S(2)}) collective-permute-start(bf16[128,2048]{1,0:T(8,128)(2,1)} %get-tuple-element.52), channel_id=1, source_target_pairs={{0,2},{1,3},{2,0},{3,1},{4,6},{5,7},{6,4},{7,5},{8,10},{9,11},{10,... | collective-permute-start | bytes 1572872 | tf_op jit(solution)/shard_map/ppermute | solution.py:253
  80.3 5.6 %collective-permute-start.14 = (f32[128,128]{1,0:T(8,128)S(1)}, f32[128,128]{1,0:T(8,128)S(1)}, u32[]{:S(2)}, u32[]{:S(2)}) collective-permute-start(f32[128,128]{1,0:T(8,128)S(1)} %add.50), channel_id=1, source_target_pairs={{0,4},{1,5},{2,6},{3,7},{4,0},{5,1},{6,2},{7,3},{8,12},{9,13},{10,... | collective-permute-start | bytes 196616 | tf_op jit(solution)/shard_map/ppermute | solution.py:253
  85.9 12.3 %collective-permute-start.15 = (f32[128,128]{1,0:T(8,128)S(1)}, f32[128,128]{1,0:T(8,128)S(1)}, u32[]{:S(2)}, u32[]{:S(2)}) collective-permute-start(f32[128,128]{1,0:T(8,128)S(1)} %add.51), channel_id=1, source_target_pairs={{0,1},{1,0},{2,3},{3,2},{4,5},{5,4},{6,7},{7,6},{8,9},{9,8},{10,11... | collective-permute-start | bytes 196616 | tf_op jit(solution)/shard_map/ppermute | solution.py:253
  86.0 16.2 %collective-permute-start.20 = (bf16[128,2048]{1,0:T(8,128)(2,1)}, bf16[128,2048]{1,0:T(8,128)(2,1)S(1)}, u32[]{:S(2)}, u32[]{:S(2)}) collective-permute-start(bf16[128,2048]{1,0:T(8,128)(2,1)} %get-tuple-element.63), channel_id=1, source_target_pairs={{0,12},{1,13},{2,14},{3,15},{4,8},{5,9},{6,10},{7,11},{8,4},{9,5},... | collective-permute-start | bytes 1572872 | tf_op jit(solution)/shard_map/ppermute | solution.py:253
  92.8 15.1 %collective-permute-start.19 = (bf16[128,2048]{1,0:T(8,128)(2,1)S(1)}, bf16[128,2048]{1,0:T(8,128)(2,1)}, u32[]{:S(2)}, u32[]{:S(2)}) collective-permute-start(bf16[128,2048]{1,0:T(8,128)(2,1)S(1)} %add.53), channel_id=1, source_target_pairs={{0,4},{1,5},{2,6},{3,7},{4,0},{5,1},{6,2},{7,3},{8,12},{9,13},{10,... | collective-permute-start | bytes 1572872 | tf_op jit(solution)/shard_map/ppermute | solution.py:253
  98.2 49.3 %copy-start.9 = (bf16[128,4096]{1,0:T(8,128)(2,1)}, bf16[128,4096]{1,0:T(8,128)(2,1)S(1)}, u32[]{:S(2)}) copy-start(bf16[128,4096]{1,0:T(8,128)(2,1)S(1)} %collective-permute-done.16.refs_6_) | copy-start | bytes 3145732
  101.6 11.2 %collective-permute-start.23 = (bf16[8,128,256]{2,1,0:T(8,128)(2,1)}, bf16[8,128,256]{2,1,0:T(8,128)(2,1)S(1)}, u32[]{:S(2)}, u32[]{:S(2)}) collective-permute-start(bf16[8,128,256]{2,1,0:T(8,128)(2,1)} %get-tuple-element.56), channel_id=1, source_target_pairs={{0,128},{16,144},{32,160},{48,176},{64,192},{80,208},{96,224},{112... | collective-permute-start | bytes 1572872 | tf_op jit(solution)/shard_map/ppermute | solution.py:270
  114.8 23.0 %all-to-all-start = ((bf16[8,128,256]{2,1,0:T(8,128)(2,1)}), bf16[8,128,256]{2,1,0:T(8,128)(2,1)S(1)}, u32[]{:S(2)}, u32[]{:S(2)}) async-start(bf16[8,128,256]{2,1,0:T(8,128)(2,1)} %add_convert_fusion), calls=%async_computation.1 | async-start | bytes 1048576 | tf_op jit(solution)/shard_map/all_to_all | solution.py:316
  123.7 23.9 %collective-permute-start.21 = (bf16[128,2048]{1,0:T(8,128)(2,1)S(1)}, bf16[128,2048]{1,0:T(8,128)(2,1)}, u32[]{:S(2)}, u32[]{:S(2)}) collective-permute-start(bf16[128,2048]{1,0:T(8,128)(2,1)S(1)} %add.54), channel_id=1, source_target_pairs={{0,4},{1,5},{2,6},{3,7},{4,0},{5,1},{6,2},{7,3},{8,12},{9,13},{10,... | collective-permute-start | bytes 1572872 | tf_op jit(solution)/shard_map/ppermute | solution.py:253
  124.6 22.9 %collective-permute-start.17 = (bf16[128,2048]{1,0:T(8,128)(2,1)}, bf16[128,2048]{1,0:T(8,128)(2,1)}, u32[]{:S(2)}, u32[]{:S(2)}) collective-permute-start(bf16[128,2048]{1,0:T(8,128)(2,1)} %get-tuple-element.57), channel_id=1, source_target_pairs={{0,2},{1,3},{2,0},{3,1},{4,6},{5,7},{6,4},{7,5},{8,10},{9,11},{10,... | collective-permute-start | bytes 1572872 | tf_op jit(solution)/shard_map/ppermute | solution.py:253
  138.9 6.1 %collective-permute-start.22 = (bf16[448,256]{1,0:T(8,128)(2,1)S(1)}, bf16[448,256]{1,0:T(8,128)(2,1)S(1)}, u32[]{:S(2)}, u32[]{:S(2)}) collective-permute-start(bf16[448,256]{1,0:T(8,128)(2,1)S(1)} %dynamic-slice_bitcast_fusion), channel_id=1, source_target_pairs={{0,128},{16,144},{32,160},{48,176},{64,192},{80,208},{96,224},{112... | collective-permute-start | bytes 688136 | tf_op jit(solution)/shard_map/ppermute | solution.py:270
  145.0 0.7 copy-start.6
Sparse Core Ops, SparseCore 0:
  63.1 52.9 reduce-scatter.1

commit v4 on v3

--- a/solution.py
+++ b/solution.py
@@ -277,19 +277,18 @@
     half = width // 2
 
     h0 = tokens[:, :half]
-    m4_0 = flip(h0, 4)
+    m4_0, m2_0 = flip(h0, 4), flip(h0, 2)
     m1 = flip(tokens, 1)
     part = jnp.dot(tokens, low_down, preferred_element_type=F32)
     part = part + flip(part, 12)
+    h1 = after(tokens, part)[:, half:]
+    part = part + flip(part, 4)
+    m8_0 = flip(after(m4_0, part), 12)
+    m4_1 = flip(after(h1, m4_0, part), 4)
     part = part + flip(part, 1)
-    h1 = after(tokens, part)[:, half:]
-    m4_1 = flip(after(h1, m4_0, part), 4)
-    m8_0 = flip(after(m4_0, part), 12)
     part = part + flip(part, 2)
-    m2_0 = flip(after(h0, part), 2)
-    part = part + flip(part, 4)
+    m2_1 = flip(after(h1, m2_0, part), 2)
     m8_1 = flip(after(m4_1, part), 12)
-    m2_1 = flip(after(h1, m2_0), 2)
     latent = part.astype(BF16)
 
     factors = (cotangent, diag_factor, section_factors, latent, low_up)
@@ -309,14 +308,14 @@
     latent_grad = part.astype(BF16)
 
     keep, send = run_down(x, tokens, latent_grad)
-    s0 = flip(b4_0 + q0, 4)
+    s0 = flip(b4_0 + after(q0, send), 4)
     pair = (keep.astype(F32) + after(cross(send), q1, s0).astype(F32)).astype(BF16)
     r2_1 = flip(after(b2_1, send), 2)
     groups = [[side * RING + z for z in range(RING)] for side in range(2)]
     pair = lax.all_to_all(pair, "dp", 0, 0, axis_index_groups=groups, tiled=True)
-    down_grad = (jnp.sum(pair.astype(F32), axis=0) * scale).T
     s1 = flip(b4_1 + q1, 4)
     arrived = cross(lax.dynamic_index_in_dim(summed, 1 - x, 0, keepdims=False))
+    down_grad = (jnp.sum(after(pair, arrived).astype(F32), axis=0) * scale).T
     pairs = ((slope0, slope1), (r2_0, r2_1), (s0, after(s1, arrived)))
     token_grad = run_final(pairs, r1, diag_factor, low_down, latent_grad)
     diag_grad, section_grad, up_grad = run_finish(x, summed, arrived, scale)

time: 160 us -> 145 us (0.906)
  waiting for transfers between devices: 59.1 us -> 40.8 us
  starting transfers between devices: 41.8 us -> 45.3 us
    all_to_all x1, waiting for transfers between devices: 12.3 us -> 1.38 us  [per_device(): lax.all_to_all(pair, 'dp', 0, 0, axis_index_groups=groups, tiled=True)]
    ppermute x22, starting transfers between devices: 31.8 us -> 36.1 us  [flip(): return lax.ppermute(value, 'tensor', [(i, i ^ mask) for i in range(16)])]
    ppermute x22, waiting for transfers between devices: 37.1 us -> 32.9 us  [flip(): return lax.ppermute(value, 'tensor', [(i, i ^ mask) for i in range(16)])]
    ppermute x2, waiting for transfers between devices: 9.64 us -> 6.53 us  [cross(): return lax.ppermute(value, 'dp', [(i, i ^ RING) for i in range(2 * RING)])]
  transfers between devices with their start and end apart: 26 -> 26, of which waited for: 12 -> 17; matrix products, arithmetic and copies ran while one was open for 6% -> 6% of each run, Pallas kernels for 12% -> 13%
where the time goes in v4:
time: 145 us; the launch traced here: 144 us
  starting transfers between devices  45.3 us (31%)
  waiting for transfers between devices  40.8 us (28%)
  Pallas kernels  31.1 us (21%)
  between operations  14.2 us (10%)
  local copies, waits for them, and re-layouts  6.07 us (4%)
  other arithmetic  4.7 us (3%)
  matrix products  1.96 us (1%)
    ppermute x22, starting transfers between devices, flip(): return lax.ppermute(value, 'tensor', [(i, i ^ mask) for i in range(16)])  36.1 us
    ppermute x22, waiting for transfers between devices, flip(): return lax.ppermute(value, 'tensor', [(i, i ^ mask) for i in range(16)])  32.9 us
    pallas_call x2, Pallas kernels, run_main(): pl.pallas_call(main_kernel, grid=(steps,), in_specs=in_specs, out_specs=[...  15.5 us
    all_to_all x1, starting transfers between devices, per_device(): lax.all_to_all(pair, 'dp', 0, 0, axis_index_groups=groups, tiled=True)  8.48 us
    ppermute x2, waiting for transfers between devices, cross(): return lax.ppermute(value, 'dp', [(i, i ^ RING) for i in range(2 * RING)])  6.53 us
    pallas_call x1, Pallas kernels, run_back(): pl.pallas_call(back_kernel, grid=(2,), in_specs=[fixed, fixed, pl.BlockSp...  6.41 us
    pallas_call x1, Pallas kernels, run_final(): pl.pallas_call(final_kernel, grid=(steps,), in_specs=half_specs(rows, ste...  4.57 us
    unnamed x27, local copies, waits for them, and re-layouts  3.14 us
  transfers between devices with their start and end apart: 26, of which 17 were waited for; matrix products, arithmetic and copies ran while one was open for 6% of the time, Pallas kernels for 13%

profile of v4, /device:TPU:8, one launch (start us, length us, event | category | flops | bytes accessed | tf_op | source)
XLA Modules:
  0.0 144.2 jit_solution(3959802601466627035)
XLA Ops:
  7.2 0.0 reduce-scatter.2.cloned.1.call-start
  7.2 1.2 slice.6
  8.4 2.3 %collective-permute-start.2 = (bf16[128,2048]{1,0:T(8,128)(2,1)S(1)}, bf16[128,2048]{1,0:T(8,128)(2,1)S(1)}, u32[]{:S(2)}, u32[]{:S(2)}) collective-permute-start(bf16[128,2048]{1,0:T(8,128)(2,1)S(1)} %slice.6), channel_id=1, source_target_pairs={{0,4},{1,5},{2,6},{3,7},{4,0},{5,1},{6,2},{7,3},{8,12},{9,13},{10,... | collective-permute-start | bytes 1572872 | tf_op jit(solution)/shard_map/ppermute | solution.py:253
  10.7 2.0 %fusion = f32[128,128]{1,0:T(8,128)S(1)} fusion(bf16[128,4096]{1,0:T(8,128)(2,1)} %tok.5, bf16[4096,128]{1,0:T(8,128)(2,1)} %refs_8_.1), kind=kOutput, calls=%fused_computation.5 | convolution fusion | flops 134217728 | bytes 2162688 | tf_op jit(solution)/shard_map/dot_general | solution.py:282
  12.6 0.8 collective-permute-start.3
  13.4 3.8 %collective-permute-done.3 = f32[128,128]{1,0:T(8,128)S(1)} collective-permute-done((f32[128,128]{1,0:T(8,128)S(1)}, f32[128,128]{1,0:T(8,128)S(1)}, u32[]{:S(2)}, u32[]{:S(2)}) %collective-permute-start.3) | collective-permute-done | bytes 65568 | tf_op jit(solution)/shard_map/ppermute | solution.py:253
  17.2 1.4 collective-permute-start.4
  18.6 2.8 %collective-permute-start.1 = (bf16[128,2048]{1,0:T(8,128)(2,1)S(1)}, bf16[128,2048]{1,0:T(8,128)(2,1)S(1)}, u32[]{:S(2)}, u32[]{:S(2)}) collective-permute-start(bf16[128,2048]{1,0:T(8,128)(2,1)S(1)} %slice.6), channel_id=1, source_target_pairs={{0,2},{1,3},{2,0},{3,1},{4,6},{5,7},{6,4},{7,5},{8,10},{9,11},{10,... | collective-permute-start | bytes 1572872 | tf_op jit(solution)/shard_map/ppermute | solution.py:253
  21.4 0.8 slice.7
  22.2 1.3 collective-permute-done.4
  23.6 0.4 collective-permute-start.9
  23.9 2.6 %collective-permute-start.5 = (bf16[128,2048]{1,0:T(8,128)(2,1)S(1)}, bf16[128,2048]{1,0:T(8,128)(2,1)S(1)}, u32[]{:S(2)}, u32[]{:S(2)}) collective-permute-start(bf16[128,2048]{1,0:T(8,128)(2,1)S(1)} %collective-permute-done.2.m4), channel_id=1, source_target_pairs={{0,12},{1,13},{2,14},{3,15},{4,8},{5,9},{6,10},{7,11},{8,4},{9,5},... | collective-permute-start | bytes 1572872 | tf_op jit(solution)/shard_map/ppermute | solution.py:253
  26.5 1.3 collective-permute-done.6
  27.8 3.1 %collective-permute-start.7 = (f32[128,128]{1,0:T(8,128)S(1)}, f32[128,128]{1,0:T(8,128)S(1)}, u32[]{:S(2)}, u32[]{:S(2)}) collective-permute-start(f32[128,128]{1,0:T(8,128)S(1)} %add.46), channel_id=1, source_target_pairs={{0,2},{1,3},{2,0},{3,1},{4,6},{5,7},{6,4},{7,5},{8,10},{9,11},{10,... | collective-permute-start | bytes 196616 | tf_op jit(solution)/shard_map/ppermute | solution.py:253
  30.9 3.9 %collective-permute-done.7 = f32[128,128]{1,0:T(8,128)S(1)} collective-permute-done((f32[128,128]{1,0:T(8,128)S(1)}, f32[128,128]{1,0:T(8,128)S(1)}, u32[]{:S(2)}, u32[]{:S(2)}) %collective-permute-start.7) | collective-permute-done | bytes 65568 | tf_op jit(solution)/shard_map/ppermute | solution.py:253
  34.8 0.6 add.47.latent
  35.4 2.8 %collective-permute-start.8 = (bf16[128,2048]{1,0:T(8,128)(2,1)}, bf16[128,2048]{1,0:T(8,128)(2,1)}, u32[]{:S(2)}, u32[]{:S(2)}) collective-permute-start(bf16[128,2048]{1,0:T(8,128)(2,1)} %slice.7), channel_id=1, source_target_pairs={{0,2},{1,3},{2,0},{3,1},{4,6},{5,7},{6,4},{7,5},{8,10},{9,11},{10,... | collective-permute-start | bytes 1572872 | tf_op jit(solution)/shard_map/ppermute | solution.py:253
  38.2 1.6 %collective-permute-start.10 = (bf16[128,2048]{1,0:T(8,128)(2,1)S(1)}, bf16[128,2048]{1,0:T(8,128)(2,1)}, u32[]{:S(2)}, u32[]{:S(2)}) collective-permute-start(bf16[128,2048]{1,0:T(8,128)(2,1)S(1)} %collective-permute-done.9.m4), channel_id=1, source_target_pairs={{0,12},{1,13},{2,14},{3,15},{4,8},{5,9},{6,10},{7,11},{8,4},{9,5},... | collective-permute-start | bytes 1572872 | tf_op jit(solution)/shard_map/ppermute | solution.py:253
  39.8 0.8 copy-done.5
  40.6 7.8 %main_part.2 = (bf16[128,2048]{1,0:T(8,128)(2,1)}, f32[128,128]{1,0:T(8,128)}, bf16[8,2,448,256]{3,2,1,0:T(8,128)(2,1)}) custom-call(bf16[128,4096]{1,0:T(8,128)(2,1)} %tok.5, bf16[128,4096]{1,0:T(8,128)(2,1)} %collective-permute-done.m1, bf16[128,2048]{1,0:T(8,128)(2,1)} %copy-done.3, bf16[128,2048]{1,0:T(8,128)(2,1)} %copy-done.2, ...), custom_call_target="tpu_custom_call" | custom-call | flops 2000000000 | bytes 29360128 | tf_op jit(solution)/shard_map/main_part/pallas_call | solution.py:89
  48.4 1.6 %collective-permute-done.8.m2 = bf16[128,2048]{1,0:T(8,128)(2,1)} collective-permute-done((bf16[128,2048]{1,0:T(8,128)(2,1)}, bf16[128,2048]{1,0:T(8,128)(2,1)}, u32[]{:S(2)}, u32[]{:S(2)}) %collective-permute-start.8) | collective-permute-done | bytes 524320 | tf_op jit(solution)/shard_map/ppermute | solution.py:253
  50.0 1.0 collective-permute-done.10.m8
  51.0 7.8 %main_part.3 = (bf16[128,2048]{1,0:T(8,128)(2,1)}, f32[128,128]{1,0:T(8,128)}, bf16[8,2,448,256]{3,2,1,0:T(8,128)(2,1)}) custom-call(bf16[128,4096]{1,0:T(8,128)(2,1)} %tok.5, bf16[128,4096]{1,0:T(8,128)(2,1)} %collective-permute-done.m1, bf16[128,2048]{1,0:T(8,128)(2,1)} %collective-permute-done.8.m2, ...), custom_call_target="tpu_custom_call", output_to_operand_aliasing={{2}: (10, {})} | custom-call | flops 2000000000 | bytes 29360128 | tf_op jit(solution)/shard_map/main_part/pallas_call | solution.py:89
  58.8 0.0 reduce-scatter.2.cloned.1.call-update
  58.8 0.8 copy-done.7
  59.6 0.0 copy-done.8
  59.7 2.1 %collective-permute-start.11 = (f32[128,128]{1,0:T(8,128)S(1)}, f32[128,128]{1,0:T(8,128)S(1)}, u32[]{:S(2)}, u32[]{:S(2)}) collective-permute-start(f32[128,128]{1,0:T(8,128)S(1)} %add.48), channel_id=1, source_target_pairs={{0,2},{1,3},{2,0},{3,1},{4,6},{5,7},{6,4},{7,5},{8,10},{9,11},{10,... | collective-permute-start | bytes 196616 | tf_op jit(solution)/shard_map/ppermute | solution.py:253
  61.7 6.4 %back_products.1 = (bf16[128,4096]{1,0:T(8,128)(2,1)}, bf16[128,2048]{1,0:T(8,128)(2,1)}, bf16[128,2048]{1,0:T(8,128)(2,1)}, bf16[128,2048]{1,0:T(8,128)(2,1)}, ...) custom-call(bf16[128,2048]{1,0:T(8,128)(2,1)} %get-tuple-element.40.low.refs_0_, ...), custom_call_target="tpu_custom_call" | custom-call | flops 2000000000 | bytes 20971520 | tf_op jit(solution)/shard_map/back_products/pallas_call | solution.py:136
  68.2 0.3 collective-permute-start.16
  68.5 1.6 %collective-permute-start.12 = (bf16[128,2048]{1,0:T(8,128)(2,1)}, bf16[128,2048]{1,0:T(8,128)(2,1)S(1)}, u32[]{:S(2)}, u32[]{:S(2)}) collective-permute-start(bf16[128,2048]{1,0:T(8,128)(2,1)} %get-tuple-element.52), channel_id=1, source_target_pairs={{0,2},{1,3},{2,0},{3,1},{4,6},{5,7},{6,4},{7,5},{8,10},{9,11},{10,... | collective-permute-start | bytes 1572872 | tf_op jit(solution)/shard_map/ppermute | solution.py:253
  70.1 0.9 collective-permute-start.13
  71.0 3.3 %collective-permute-done.13 = f32[128,128]{1,0:T(8,128)S(1)} collective-permute-done((f32[128,128]{1,0:T(8,128)S(1)}, f32[128,128]{1,0:T(8,128)S(1)}, u32[]{:S(2)}, u32[]{:S(2)}) %collective-permute-start.13) | collective-permute-done | bytes 65568 | tf_op jit(solution)/shard_map/ppermute | solution.py:253
  74.4 1.0 collective-permute-start.18
  75.4 3.9 %collective-permute-start.14 = (f32[128,128]{1,0:T(8,128)S(1)}, f32[128,128]{1,0:T(8,128)S(1)}, u32[]{:S(2)}, u32[]{:S(2)}) collective-permute-start(f32[128,128]{1,0:T(8,128)S(1)} %add.50), channel_id=1, source_target_pairs={{0,4},{1,5},{2,6},{3,7},{4,0},{5,1},{6,2},{7,3},{8,12},{9,13},{10,... | collective-permute-start | bytes 196616 | tf_op jit(solution)/shard_map/ppermute | solution.py:253
  79.3 2.2 %collective-permute-done.14 = f32[128,128]{1,0:T(8,128)S(1)} collective-permute-done((f32[128,128]{1,0:T(8,128)S(1)}, f32[128,128]{1,0:T(8,128)S(1)}, u32[]{:S(2)}, u32[]{:S(2)}) %collective-permute-start.14) | collective-permute-done | bytes 65568 | tf_op jit(solution)/shard_map/ppermute | solution.py:253
  81.5 0.1 collective-permute-start.15
  81.7 1.0 collective-permute-start.20
  82.7 0.2 collective-permute-done.15
  82.9 1.6 %collective-permute-done.12.refs_2_ = bf16[128,2048]{1,0:T(8,128)(2,1)S(1)} collective-permute-done((bf16[128,2048]{1,0:T(8,128)(2,1)}, bf16[128,2048]{1,0:T(8,128)(2,1)S(1)}, u32[]{:S(2)}, u32[]{:S(2)}) %collective-permute-start.12) | collective-permute-done | bytes 524320 | tf_op jit(solution)/shard_map/ppermute | solution.py:253
  84.5 0.7 add_convert_fusion.1.lat.refs_9_
  85.2 2.7 %down_part.1 = (bf16[8,128,256]{2,1,0:T(8,128)(2,1)}, bf16[8,128,256]{2,1,0:T(8,128)(2,1)}) custom-call(s32[1]{0:T(128)} %bitcast.side, bf16[128,4096]{1,0:T(8,128)(2,1)} %tok.5, bf16[128,128]{1,0:T(8,128)(2,1)} %add_convert_fusion.1.lat.refs_9_), custom_call_target="tpu_custom_call" | custom-call | flops 300000000 | bytes 10485760 | tf_op jit(solution)/shard_map/down_part/pallas_call | solution.py:162
  87.9 1.6 %collective-permute-done.18 = bf16[128,2048]{1,0:T(8,128)(2,1)S(1)} collective-permute-done((bf16[128,2048]{1,0:T(8,128)(2,1)}, bf16[128,2048]{1,0:T(8,128)(2,1)S(1)}, u32[]{:S(2)}, u32[]{:S(2)}) %collective-permute-start.18) | collective-permute-done | bytes 524320 | tf_op jit(solution)/shard_map/ppermute | solution.py:253
  89.5 1.2 add.53
  90.7 4.4 %collective-permute-start.19 = (bf16[128,2048]{1,0:T(8,128)(2,1)S(1)}, bf16[128,2048]{1,0:T(8,128)(2,1)S(1)}, u32[]{:S(2)}, u32[]{:S(2)}) collective-permute-start(bf16[128,2048]{1,0:T(8,128)(2,1)S(1)} %add.53), channel_id=1, source_target_pairs={{0,4},{1,5},{2,6},{3,7},{4,0},{5,1},{6,2},{7,3},{8,12},{9,13},{10,... | collective-permute-start | bytes 1572872 | tf_op jit(solution)/shard_map/ppermute | solution.py:253
  95.1 0.3 collective-permute-start.23
  95.4 3.4 %collective-permute-done.20 = bf16[128,2048]{1,0:T(8,128)(2,1)S(1)} collective-permute-done((bf16[128,2048]{1,0:T(8,128)(2,1)}, bf16[128,2048]{1,0:T(8,128)(2,1)S(1)}, u32[]{:S(2)}, u32[]{:S(2)}) %collective-permute-start.20) | collective-permute-done | bytes 524320 | tf_op jit(solution)/shard_map/ppermute | solution.py:253
  98.7 5.4 %collective-permute-done.19.refs_4_ = bf16[128,2048]{1,0:T(8,128)(2,1)S(1)} collective-permute-done((bf16[128,2048]{1,0:T(8,128)(2,1)S(1)}, bf16[128,2048]{1,0:T(8,128)(2,1)S(1)}, u32[]{:S(2)}, u32[]{:S(2)}) %collective-permute-start.19) | collective-permute-done | bytes 524320 | tf_op jit(solution)/shard_map/ppermute | solution.py:253
  104.1 1.7 %collective-permute-done.23 = bf16[8,128,256]{2,1,0:T(8,128)(2,1)S(1)} collective-permute-done((bf16[8,128,256]{2,1,0:T(8,128)(2,1)}, bf16[8,128,256]{2,1,0:T(8,128)(2,1)S(1)}, u32[]{:S(2)}, u32[]{:S(2)}) %collective-permute-start.23) | collective-permute-done | bytes 524320 | tf_op jit(solution)/shard_map/ppermute | solution.py:270
  105.8 2.0 %add_convert_fusion = bf16[8,128,256]{2,1,0:T(8,128)(2,1)} fusion(bf16[8,128,256]{2,1,0:T(8,128)(2,1)S(1)} %collective-permute-done.23, bf16[8,128,256]{2,1,0:T(8,128)(2,1)} %get-tuple-element.69), kind=kLoop, calls=%fused_computation.1 | loop fusion | flops 1048576 | bytes 1572864 | tf_op jit(solution)/shard_map/convert_element_type | solution.py:312
  107.7 8.5 %all-to-all-start = ((bf16[8,128,256]{2,1,0:T(8,128)(2,1)}), bf16[8,128,256]{2,1,0:T(8,128)(2,1)S(1)}, u32[]{:S(2)}, u32[]{:S(2)}) async-start(bf16[8,128,256]{2,1,0:T(8,128)(2,1)} %add_convert_fusion), calls=%async_computation.1 | async-start | bytes 1048576 | tf_op jit(solution)/shard_map/all_to_all | solution.py:315
  116.2 0.0 reduce-scatter.2.cloned.1.call-done
  116.3 1.0 dynamic-slice_bitcast_fusion
  117.2 0.4 collective-permute-start.22
  117.6 0.1 add.54
  117.7 0.9 collective-permute-start.21
  118.7 2.3 %collective-permute-start.17 = (bf16[128,2048]{1,0:T(8,128)(2,1)}, bf16[128,2048]{1,0:T(8,128)(2,1)}, u32[]{:S(2)}, u32[]{:S(2)}) collective-permute-start(bf16[128,2048]{1,0:T(8,128)(2,1)} %get-tuple-element.57), channel_id=1, source_target_pairs={{0,2},{1,3},{2,0},{3,1},{4,6},{5,7},{6,4},{7,5},{8,10},{9,11},{10,... | collective-permute-start | bytes 1572872 | tf_op jit(solution)/shard_map/ppermute | solution.py:253
  121.0 4.9 %collective-permute-done.22.arrived = bf16[448,256]{1,0:T(8,128)(2,1)S(1)} collective-permute-done((bf16[448,256]{1,0:T(8,128)(2,1)S(1)}, bf16[448,256]{1,0:T(8,128)(2,1)S(1)}, u32[]{:S(2)}, u32[]{:S(2)}) %collective-permute-start.22) | collective-permute-done | bytes 229408 | tf_op jit(solution)/shard_map/ppermute | solution.py:270
  125.9 0.7 copy-done.6
  126.5 1.8 %finish.1 = (f32[64,256]{1,0:T(8,128)}, f32[4,64,256]{2,1,0:T(8,128)}, f32[128,256]{1,0:T(8,128)}) custom-call(s32[1]{0:T(128)} %bitcast.side, bf16[2,448,256]{2,1,0:T(8,128)(2,1)} %bitcast.11, bf16[448,256]{1,0:T(8,128)(2,1)} %copy-done.6), custom_call_target="tpu_custom_call" | custom-call | flops 300000 | bytes 4194304 | tf_op jit(solution)/shard_map/finish/pallas_call | solution.py:227
  128.4 1.4 all-to-all-done
  129.8 0.1 convert_reduce_fusion
  129.9 0.8 copy.12
  130.6 2.1 %collective-permute-done.17.refs_3_ = bf16[128,2048]{1,0:T(8,128)(2,1)} collective-permute-done((bf16[128,2048]{1,0:T(8,128)(2,1)}, bf16[128,2048]{1,0:T(8,128)(2,1)}, u32[]{:S(2)}, u32[]{:S(2)}) %collective-permute-start.17) | collective-permute-done | bytes 524320 | tf_op jit(solution)/shard_map/ppermute | solution.py:253
  132.8 4.6 %token_grad.1 = bf16[128,4096]{1,0:T(8,128)(2,1)} custom-call(bf16[128,2048]{1,0:T(8,128)(2,1)} %get-tuple-element.40.low.refs_0_, bf16[128,2048]{1,0:T(8,128)(2,1)} %get-tuple-element.46.high.refs_1_, bf16[128,2048]{1,0:T(8,128)(2,1)} %copy-done.10, bf16[128,2048]{1,0:T(8,128)(2,1)} %collective-permute-done.17.refs_3_, bf16[128,2048]{1,0:T(8,128)(2,1)} %copy-done.11, ...), custom_call_target="tpu_custom_call" | custom-call | flops 2000000000 | bytes 17825792 | tf_op jit(solution)/shard_map/token_grad/pallas_call | solution.py:198
  (40 shorter events, 0.1 us)
Async XLA Ops:
  7.2 14.2 %copy-start = (bf16[128,4096]{1,0:T(8,128)(2,1)S(1)}, bf16[128,4096]{1,0:T(8,128)(2,1)}, u32[]{:S(2)}) copy-start(bf16[128,4096]{1,0:T(8,128)(2,1)} %tok.5) | copy-start | bytes 3145732
  7.2 109.1 %reduce-scatter.2.cloned.1.call-start = ((), (), s32[]{:S(2)}) async-start(), calls=%async_computation.2 | async-start | bytes 4128768 | tf_op jit(solution)/shard_map/reduce_scatter | solution.py:263
  8.4 15.2 %collective-permute-start.2 = (bf16[128,2048]{1,0:T(8,128)(2,1)S(1)}, bf16[128,2048]{1,0:T(8,128)(2,1)S(1)}, u32[]{:S(2)}, u32[]{:S(2)}) collective-permute-start(bf16[128,2048]{1,0:T(8,128)(2,1)S(1)} %slice.6), channel_id=1, source_target_pairs={{0,4},{1,5},{2,6},{3,7},{4,0},{5,1},{6,2},{7,3},{8,12},{9,13},{10,... | collective-permute-start | bytes 1572872 | tf_op jit(solution)/shard_map/ppermute | solution.py:253
  10.7 29.1 %collective-permute-start = (bf16[128,4096]{1,0:T(8,128)(2,1)}, bf16[128,4096]{1,0:T(8,128)(2,1)}, u32[]{:S(2)}, u32[]{:S(2)}) collective-permute-start(bf16[128,4096]{1,0:T(8,128)(2,1)} %tok.5), channel_id=1, source_target_pairs={{0,1},{1,0},{2,3},{3,2},{4,5},{5,4},{6,7},{7,6},{8,9},{9,8},{10,11... | collective-permute-start | bytes 3145736 | tf_op jit(solution)/shard_map/ppermute | solution.py:253
  12.6 4.6 %collective-permute-start.3 = (f32[128,128]{1,0:T(8,128)S(1)}, f32[128,128]{1,0:T(8,128)S(1)}, u32[]{:S(2)}, u32[]{:S(2)}) collective-permute-start(f32[128,128]{1,0:T(8,128)S(1)} %fusion), channel_id=1, source_target_pairs={{0,12},{1,13},{2,14},{3,15},{4,8},{5,9},{6,10},{7,11},{8,4},{9,5},... | collective-permute-start | bytes 196616 | tf_op jit(solution)/shard_map/ppermute | solution.py:253
  17.2 6.3 %collective-permute-start.4 = (f32[128,128]{1,0:T(8,128)S(1)}, f32[128,128]{1,0:T(8,128)S(1)}, u32[]{:S(2)}, u32[]{:S(2)}) collective-permute-start(f32[128,128]{1,0:T(8,128)S(1)} %add.44), channel_id=1, source_target_pairs={{0,4},{1,5},{2,6},{3,7},{4,0},{5,1},{6,2},{7,3},{8,12},{9,13},{10,... | collective-permute-start | bytes 196616 | tf_op jit(solution)/shard_map/ppermute | solution.py:253
  18.6 16.8 %collective-permute-start.1 = (bf16[128,2048]{1,0:T(8,128)(2,1)S(1)}, bf16[128,2048]{1,0:T(8,128)(2,1)S(1)}, u32[]{:S(2)}, u32[]{:S(2)}) collective-permute-start(bf16[128,2048]{1,0:T(8,128)(2,1)S(1)} %slice.6), channel_id=1, source_target_pairs={{0,2},{1,3},{2,0},{3,1},{4,6},{5,7},{6,4},{7,5},{8,10},{9,11},{10,... | collective-permute-start | bytes 1572872 | tf_op jit(solution)/shard_map/ppermute | solution.py:253
  23.6 16.2 %copy-start.2 = (bf16[128,2048]{1,0:T(8,128)(2,1)}, bf16[128,2048]{1,0:T(8,128)(2,1)S(1)}, u32[]{:S(2)}) copy-start(bf16[128,2048]{1,0:T(8,128)(2,1)S(1)} %collective-permute-done.2.m4) | copy-start | bytes 1572868
  23.6 14.6 %collective-permute-start.9 = (bf16[128,2048]{1,0:T(8,128)(2,1)}, bf16[128,2048]{1,0:T(8,128)(2,1)S(1)}, u32[]{:S(2)}, u32[]{:S(2)}) collective-permute-start(bf16[128,2048]{1,0:T(8,128)(2,1)} %slice.7), channel_id=1, source_target_pairs={{0,4},{1,5},{2,6},{3,7},{4,0},{5,1},{6,2},{7,3},{8,12},{9,13},{10,... | collective-permute-start | bytes 1572872 | tf_op jit(solution)/shard_map/ppermute | solution.py:253
  23.9 15.8 %collective-permute-start.5 = (bf16[128,2048]{1,0:T(8,128)(2,1)S(1)}, bf16[128,2048]{1,0:T(8,128)(2,1)S(1)}, u32[]{:S(2)}, u32[]{:S(2)}) collective-permute-start(bf16[128,2048]{1,0:T(8,128)(2,1)S(1)} %collective-permute-done.2.m4), channel_id=1, source_target_pairs={{0,12},{1,13},{2,14},{3,15},{4,8},{5,9},{6,10},{7,11},{8,4},{9,5},... | collective-permute-start | bytes 1572872 | tf_op jit(solution)/shard_map/ppermute | solution.py:253
  26.5 1.3 collective-permute-start.6
  27.8 7.0 %collective-permute-start.7 = (f32[128,128]{1,0:T(8,128)S(1)}, f32[128,128]{1,0:T(8,128)S(1)}, u32[]{:S(2)}, u32[]{:S(2)}) collective-permute-start(f32[128,128]{1,0:T(8,128)S(1)} %add.46), channel_id=1, source_target_pairs={{0,2},{1,3},{2,0},{3,1},{4,6},{5,7},{6,4},{7,5},{8,10},{9,11},{10,... | collective-permute-start | bytes 196616 | tf_op jit(solution)/shard_map/ppermute | solution.py:253
  35.4 4.4 %copy-start.3 = (bf16[128,2048]{1,0:T(8,128)(2,1)}, bf16[128,2048]{1,0:T(8,128)(2,1)S(1)}, u32[]{:S(2)}) copy-start(bf16[128,2048]{1,0:T(8,128)(2,1)S(1)} %collective-permute-done.1.m2) | copy-start | bytes 1572868
  35.4 14.6 %collective-permute-start.8 = (bf16[128,2048]{1,0:T(8,128)(2,1)}, bf16[128,2048]{1,0:T(8,128)(2,1)}, u32[]{:S(2)}, u32[]{:S(2)}) collective-permute-start(bf16[128,2048]{1,0:T(8,128)(2,1)} %slice.7), channel_id=1, source_target_pairs={{0,2},{1,3},{2,0},{3,1},{4,6},{5,7},{6,4},{7,5},{8,10},{9,11},{10,... | collective-permute-start | bytes 1572872 | tf_op jit(solution)/shard_map/ppermute | solution.py:253
  38.2 10.2 %copy-start.4 = (bf16[128,2048]{1,0:T(8,128)(2,1)}, bf16[128,2048]{1,0:T(8,128)(2,1)S(1)}, u32[]{:S(2)}) copy-start(bf16[128,2048]{1,0:T(8,128)(2,1)S(1)} %collective-permute-done.9.m4) | copy-start | bytes 1572868
  38.2 12.8 %collective-permute-start.10 = (bf16[128,2048]{1,0:T(8,128)(2,1)S(1)}, bf16[128,2048]{1,0:T(8,128)(2,1)}, u32[]{:S(2)}, u32[]{:S(2)}) collective-permute-start(bf16[128,2048]{1,0:T(8,128)(2,1)S(1)} %collective-permute-done.9.m4), channel_id=1, source_target_pairs={{0,12},{1,13},{2,14},{3,15},{4,8},{5,9},{6,10},{7,11},{8,4},{9,5},... | collective-permute-start | bytes 1572872 | tf_op jit(solution)/shard_map/ppermute | solution.py:253
  39.8 0.8 copy-start.5
  58.8 0.8 copy-start.7
  58.8 0.9 copy-start.8
  59.7 8.5 %collective-permute-start.11 = (f32[128,128]{1,0:T(8,128)S(1)}, f32[128,128]{1,0:T(8,128)S(1)}, u32[]{:S(2)}, u32[]{:S(2)}) collective-permute-start(f32[128,128]{1,0:T(8,128)S(1)} %add.48), channel_id=1, source_target_pairs={{0,2},{1,3},{2,0},{3,1},{4,6},{5,7},{6,4},{7,5},{8,10},{9,11},{10,... | collective-permute-start | bytes 196616 | tf_op jit(solution)/shard_map/ppermute | solution.py:253
  68.2 49.5 %copy-start.1 = (bf16[128,2048]{1,0:T(8,128)(2,1)S(1)}, bf16[128,2048]{1,0:T(8,128)(2,1)}, u32[]{:S(2)}) copy-start(bf16[128,2048]{1,0:T(8,128)(2,1)} %get-tuple-element.62) | copy-start | bytes 1572868
  68.2 16.3 %collective-permute-start.16 = (bf16[128,4096]{1,0:T(8,128)(2,1)}, bf16[128,4096]{1,0:T(8,128)(2,1)S(1)}, u32[]{:S(2)}, u32[]{:S(2)}) collective-permute-start(bf16[128,4096]{1,0:T(8,128)(2,1)} %get-tuple-element.54), channel_id=1, source_target_pairs={{0,1},{1,0},{2,3},{3,2},{4,5},{5,4},{6,7},{7,6},{8,9},{9,8},{10,11... | collective-permute-start | bytes 3145736 | tf_op jit(solution)/shard_map/ppermute | solution.py:253
  68.5 16.1 %collective-permute-start.12 = (bf16[128,2048]{1,0:T(8,128)(2,1)}, bf16[128,2048]{1,0:T(8,128)(2,1)S(1)}, u32[]{:S(2)}, u32[]{:S(2)}) collective-permute-start(bf16[128,2048]{1,0:T(8,128)(2,1)} %get-tuple-element.52), channel_id=1, source_target_pairs={{0,2},{1,3},{2,0},{3,1},{4,6},{5,7},{6,4},{7,5},{8,10},{9,11},{10,... | collective-permute-start | bytes 1572872 | tf_op jit(solution)/shard_map/ppermute | solution.py:253
  70.1 4.3 %collective-permute-start.13 = (f32[128,128]{1,0:T(8,128)S(1)}, f32[128,128]{1,0:T(8,128)S(1)}, u32[]{:S(2)}, u32[]{:S(2)}) collective-permute-start(f32[128,128]{1,0:T(8,128)S(1)} %add.49), channel_id=1, source_target_pairs={{0,12},{1,13},{2,14},{3,15},{4,8},{5,9},{6,10},{7,11},{8,4},{9,5},... | collective-permute-start | bytes 196616 | tf_op jit(solution)/shard_map/ppermute | solution.py:253
  74.4 15.2 %collective-permute-start.18 = (bf16[128,2048]{1,0:T(8,128)(2,1)}, bf16[128,2048]{1,0:T(8,128)(2,1)S(1)}, u32[]{:S(2)}, u32[]{:S(2)}) collective-permute-start(bf16[128,2048]{1,0:T(8,128)(2,1)} %get-tuple-element.60), channel_id=1, source_target_pairs={{0,12},{1,13},{2,14},{3,15},{4,8},{5,9},{6,10},{7,11},{8,4},{9,5},... | collective-permute-start | bytes 1572872 | tf_op jit(solution)/shard_map/ppermute | solution.py:253
  75.4 6.1 %collective-permute-start.14 = (f32[128,128]{1,0:T(8,128)S(1)}, f32[128,128]{1,0:T(8,128)S(1)}, u32[]{:S(2)}, u32[]{:S(2)}) collective-permute-start(f32[128,128]{1,0:T(8,128)S(1)} %add.50), channel_id=1, source_target_pairs={{0,4},{1,5},{2,6},{3,7},{4,0},{5,1},{6,2},{7,3},{8,12},{9,13},{10,... | collective-permute-start | bytes 196616 | tf_op jit(solution)/shard_map/ppermute | solution.py:253
  81.5 1.3 collective-permute-start.15
  81.7 17.1 %collective-permute-start.20 = (bf16[128,2048]{1,0:T(8,128)(2,1)}, bf16[128,2048]{1,0:T(8,128)(2,1)S(1)}, u32[]{:S(2)}, u32[]{:S(2)}) collective-permute-start(bf16[128,2048]{1,0:T(8,128)(2,1)} %get-tuple-element.64), channel_id=1, source_target_pairs={{0,12},{1,13},{2,14},{3,15},{4,8},{5,9},{6,10},{7,11},{8,4},{9,5},... | collective-permute-start | bytes 1572872 | tf_op jit(solution)/shard_map/ppermute | solution.py:253
  84.5 31.7 %copy-start.10 = (bf16[128,2048]{1,0:T(8,128)(2,1)}, bf16[128,2048]{1,0:T(8,128)(2,1)S(1)}, u32[]{:S(2)}) copy-start(bf16[128,2048]{1,0:T(8,128)(2,1)S(1)} %collective-permute-done.12.refs_2_) | copy-start | bytes 1572868
  84.5 33.2 %copy-start.9 = (bf16[128,4096]{1,0:T(8,128)(2,1)}, bf16[128,4096]{1,0:T(8,128)(2,1)S(1)}, u32[]{:S(2)}) copy-start(bf16[128,4096]{1,0:T(8,128)(2,1)S(1)} %collective-permute-done.16.refs_6_) | copy-start | bytes 3145732
  90.7 13.4 %collective-permute-start.19 = (bf16[128,2048]{1,0:T(8,128)(2,1)S(1)}, bf16[128,2048]{1,0:T(8,128)(2,1)S(1)}, u32[]{:S(2)}, u32[]{:S(2)}) collective-permute-start(bf16[128,2048]{1,0:T(8,128)(2,1)S(1)} %add.53), channel_id=1, source_target_pairs={{0,4},{1,5},{2,6},{3,7},{4,0},{5,1},{6,2},{7,3},{8,12},{9,13},{10,... | collective-permute-start | bytes 1572872 | tf_op jit(solution)/shard_map/ppermute | solution.py:253
  95.1 10.7 %collective-permute-start.23 = (bf16[8,128,256]{2,1,0:T(8,128)(2,1)}, bf16[8,128,256]{2,1,0:T(8,128)(2,1)S(1)}, u32[]{:S(2)}, u32[]{:S(2)}) collective-permute-start(bf16[8,128,256]{2,1,0:T(8,128)(2,1)} %get-tuple-element.56), channel_id=1, source_target_pairs={{0,128},{16,144},{32,160},{48,176},{64,192},{80,208},{96,224},{112... | collective-permute-start | bytes 1572872 | tf_op jit(solution)/shard_map/ppermute | solution.py:270
  104.1 1.7 %copy-start.11 = (bf16[128,2048]{1,0:T(8,128)(2,1)}, bf16[128,2048]{1,0:T(8,128)(2,1)S(1)}, u32[]{:S(2)}) copy-start(bf16[128,2048]{1,0:T(8,128)(2,1)S(1)} %collective-permute-done.19.refs_4_) | copy-start | bytes 1572868
  107.7 22.0 %all-to-all-start = ((bf16[8,128,256]{2,1,0:T(8,128)(2,1)}), bf16[8,128,256]{2,1,0:T(8,128)(2,1)S(1)}, u32[]{:S(2)}, u32[]{:S(2)}) async-start(bf16[8,128,256]{2,1,0:T(8,128)(2,1)} %add_convert_fusion), calls=%async_computation.1 | async-start | bytes 1048576 | tf_op jit(solution)/shard_map/all_to_all | solution.py:315
  117.2 8.6 %collective-permute-start.22 = (bf16[448,256]{1,0:T(8,128)(2,1)S(1)}, bf16[448,256]{1,0:T(8,128)(2,1)S(1)}, u32[]{:S(2)}, u32[]{:S(2)}) collective-permute-start(bf16[448,256]{1,0:T(8,128)(2,1)S(1)} %dynamic-slice_bitcast_fusion), channel_id=1, source_target_pairs={{0,128},{16,144},{32,160},{48,176},{64,192},{80,208},{96,224},{112... | collective-permute-start | bytes 688136 | tf_op jit(solution)/shard_map/ppermute | solution.py:270
  117.7 12.9 %collective-permute-start.21 = (bf16[128,2048]{1,0:T(8,128)(2,1)S(1)}, bf16[128,2048]{1,0:T(8,128)(2,1)S(1)}, u32[]{:S(2)}, u32[]{:S(2)}) collective-permute-start(bf16[128,2048]{1,0:T(8,128)(2,1)S(1)} %add.54), channel_id=1, source_target_pairs={{0,4},{1,5},{2,6},{3,7},{4,0},{5,1},{6,2},{7,3},{8,12},{9,13},{10,... | collective-permute-start | bytes 1572872 | tf_op jit(solution)/shard_map/ppermute | solution.py:253
  118.7 14.1 %collective-permute-start.17 = (bf16[128,2048]{1,0:T(8,128)(2,1)}, bf16[128,2048]{1,0:T(8,128)(2,1)}, u32[]{:S(2)}, u32[]{:S(2)}) collective-permute-start(bf16[128,2048]{1,0:T(8,128)(2,1)} %get-tuple-element.57), channel_id=1, source_target_pairs={{0,2},{1,3},{2,0},{3,1},{4,6},{5,7},{6,4},{7,5},{8,10},{9,11},{10,... | collective-permute-start | bytes 1572872 | tf_op jit(solution)/shard_map/ppermute | solution.py:253
  125.8 0.7 copy-start.6
  130.6 2.1 %copy-start.12 = (bf16[128,2048]{1,0:T(8,128)(2,1)}, bf16[128,2048]{1,0:T(8,128)(2,1)S(1)}, u32[]{:S(2)}) copy-start(bf16[128,2048]{1,0:T(8,128)(2,1)S(1)} %collective-permute-done.21.refs_5_) | copy-start | bytes 1572868
Sparse Core Ops, SparseCore 0:
  58.9 51.8 reduce-scatter.1

commit v5 on v4

--- a/solution.py
+++ b/solution.py
@@ -116,7 +116,7 @@
     ]
 
 
-def back_kernel(low, high, sec, b1, *halves):
+def back_kernel(low, high, sec, b1, b2, *halves):
     mask = block_mask()
 
     def fill(slope, outs):
@@ -125,8 +125,8 @@
             for b, out in enumerate(outs):
                 out[:, cs] = dot(slope[:, cs], spread(sec[b, :, cs], mask), 1, 1).astype(BF16)
 
-    pl.when(pl.program_id(0) == 0)(lambda: fill(low, (b1, *halves[0::2])))
-    pl.when(pl.program_id(0) == 1)(lambda: fill(high, (b1, *halves[1::2])))
+    pl.when(pl.program_id(0) == 0)(lambda: fill(low, (b1, b2, *halves[0::2])))
+    pl.when(pl.program_id(0) == 1)(lambda: fill(high, (b1, b2, *halves[1::2])))
 
 
 def run_back(slopes, section):
@@ -137,8 +137,8 @@
         back_kernel,
         grid=(2,),
         in_specs=[fixed, fixed, pl.BlockSpec((4, BLOCK, half), lambda i: (0, 0, i))],
-        out_specs=[moving] + [fixed] * 6,
-        out_shape=[jax.ShapeDtypeStruct((rows, 2 * half), BF16)] + [jax.ShapeDtypeStruct((rows, half), BF16)] * 6,
+        out_specs=[moving] * 2 + [fixed] * 4,
+        out_shape=[jax.ShapeDtypeStruct((rows, 2 * half), BF16)] * 2 + [jax.ShapeDtypeStruct((rows, half), BF16)] * 4,
         compiler_params=pltpu.CompilerParams(vmem_limit_bytes=VMEM),
         cost_estimate=pl.CostEstimate(flops=2_000_000_000, bytes_accessed=20 << 20, transcendentals=0),
         name="back_products",
@@ -177,9 +177,9 @@
 
 
 def final_kernel(*refs):
-    pairs, (r1, diag, down, lat, out) = refs[:6], refs[6:]
+    pairs, (r1, r2, diag, down, lat, out) = refs[:4], refs[4:]
     mask = block_mask()
-    slope, r2, r48 = (pick_half(pairs[2 * k], pairs[2 * k + 1]) for k in range(3))
+    slope, r48 = (pick_half(pairs[2 * k], pairs[2 * k + 1]) for k in range(2))
     for c in range(FINAL_STEP // CHUNK):
         cs = slice(c * CHUNK, (c + 1) * CHUNK)
         total = dot(slope[:, cs], spread(diag[:, cs], mask), 1, 1)
@@ -189,7 +189,7 @@
         out[:, cs] = total.astype(BF16)
 
 
-def run_final(pairs, r1, diag, low_down, latent_grad):
+def run_final(pairs, r1, r2, diag, low_down, latent_grad):
     rows, half_width = pairs[0][0].shape
     width = 2 * half_width
     rank = latent_grad.shape[1]
@@ -198,8 +198,9 @@
     return pl.pallas_call(
         final_kernel,
         grid=(steps,),
-        in_specs=half_specs(rows, steps) * 3
+        in_specs=half_specs(rows, steps) * 2
         + [
+            col(rows),
             col(rows),
             col(BLOCK),
             pl.BlockSpec((FINAL_STEP, rank), lambda i: (i, 0)),
@@ -210,7 +211,7 @@
         compiler_params=pltpu.CompilerParams(vmem_limit_bytes=VMEM),
         cost_estimate=pl.CostEstimate(flops=2_000_000_000, bytes_accessed=17 << 20, transcendentals=0),
         name="token_grad",
-    )(*[value for pair in pairs for value in pair], r1, diag, low_down, latent_grad)
+    )(*[value for pair in pairs for value in pair], r1, r2, diag, low_down, latent_grad)
 
 
 def finish_kernel(scale, side, summed, arrived, diag, section, up):
@@ -298,26 +299,26 @@
 
     part = lat0 + lat1
     arrived = flip(part, 2)
-    b1, b2_0, b2_1, b4_0, b4_1, b8_0, b8_1 = run_back((slope0, slope1), section_factors)
+    b1, b2, b4_0, b4_1, b8_0, b8_1 = run_back((slope0, slope1), section_factors)
     part = part + after(arrived, b1)
-    r2_0, r1 = flip(after(b2_0, part), 2), flip(after(b1, part), 1)
+    r2, r1 = flip(after(b2, part), 2), flip(after(b1, part), 1)
     part = part + flip(part, 12)
     q0, q1 = flip(after(b8_0, part), 12), flip(after(b8_1, part), 12)
     part = part + flip(part, 4)
-    part = part + after(flip(part, 1), r2_0, r1)
+    part = part + after(flip(part, 1), r1)
     latent_grad = part.astype(BF16)
 
     keep, send = run_down(x, tokens, latent_grad)
     s0 = flip(b4_0 + after(q0, send), 4)
-    pair = (keep.astype(F32) + after(cross(send), q1, s0).astype(F32)).astype(BF16)
-    r2_1 = flip(after(b2_1, send), 2)
+    pair = (keep.astype(F32) + after(cross(send), r2, q1, s0).astype(F32)).astype(BF16)
     groups = [[side * RING + z for z in range(RING)] for side in range(2)]
     pair = lax.all_to_all(pair, "dp", 0, 0, axis_index_groups=groups, tiled=True)
     s1 = flip(b4_1 + q1, 4)
-    arrived = cross(lax.dynamic_index_in_dim(summed, 1 - x, 0, keepdims=False))
+    other = lax.dynamic_index_in_dim(after(summed, s1), 1 - x, 0, keepdims=False)
+    arrived = cross(other)
     down_grad = (jnp.sum(after(pair, arrived).astype(F32), axis=0) * scale).T
-    pairs = ((slope0, slope1), (r2_0, r2_1), (s0, after(s1, arrived)))
-    token_grad = run_final(pairs, r1, diag_factor, low_down, latent_grad)
+    pairs = ((slope0, slope1), (s0, after(s1, other)))
+    token_grad = run_final(pairs, r1, r2, diag_factor, low_down, latent_grad)
     diag_grad, section_grad, up_grad = run_finish(x, summed, arrived, scale)
     return token_grad, diag_grad, section_grad, down_grad, up_grad
 

time: 145 us -> 154 us (1.062)
  waiting for transfers between devices: 40.8 us -> 47.6 us
  starting transfers between devices: 45.3 us -> 47 us
    ppermute x22 -> x21, waiting for transfers between devices: 32.9 us -> 39.8 us  [flip(): return lax.ppermute(value, 'tensor', [(i, i ^ mask) for i in range(16)])]
    ppermute x2, starting transfers between devices: 0.65 us -> 2.27 us  [cross(): return lax.ppermute(value, 'dp', [(i, i ^ RING) for i in range(2 * RING)])]
    unnamed x27 -> x23, local copies, waits for them, and re-layouts: 3.14 us -> 3.27 us
    ppermute x22 -> x21, starting transfers between devices: 36.1 us -> 36.2 us  [flip(): return lax.ppermute(value, 'tensor', [(i, i ^ mask) for i in range(16)])]
  transfers between devices with their start and end apart: 26 -> 25, of which waited for: 17 -> 16; matrix products, arithmetic and copies ran while one was open for 6% -> 5% of each run, Pallas kernels for 13% -> 14%
where the time goes in v5:
time: 154 us; the launch traced here: 153 us
  waiting for transfers between devices  47.6 us (31%)
  starting transfers between devices  47 us (31%)
  Pallas kernels  30.9 us (20%)
  between operations  14.2 us (9%)
  local copies, waits for them, and re-layouts  6.23 us (4%)
  other arithmetic  4.69 us (3%)
  matrix products  1.96 us (1%)
    ppermute x21, waiting for transfers between devices, flip(): return lax.ppermute(value, 'tensor', [(i, i ^ mask) for i in range(16)])  39.8 us
    ppermute x21, starting transfers between devices, flip(): return lax.ppermute(value, 'tensor', [(i, i ^ mask) for i in range(16)])  36.2 us
    pallas_call x2, Pallas kernels, run_main(): pl.pallas_call(main_kernel, grid=(steps,), in_specs=in_specs, out_specs=[...  15.4 us
    all_to_all x1, starting transfers between devices, per_device(): lax.all_to_all(pair, 'dp', 0, 0, axis_index_groups=groups, tiled=True)  8.46 us
    ppermute x2, waiting for transfers between devices, cross(): return lax.ppermute(value, 'dp', [(i, i ^ RING) for i in range(2 * RING)])  7.73 us
    pallas_call x1, Pallas kernels, run_back(): pl.pallas_call(back_kernel, grid=(2,), in_specs=[fixed, fixed, pl.BlockSp...  6.5 us
    pallas_call x1, Pallas kernels, run_final(): pl.pallas_call(final_kernel, grid=(steps,), in_specs=half_specs(rows, ste...  4.41 us
    unnamed x23, local copies, waits for them, and re-layouts  3.27 us
  transfers between devices with their start and end apart: 25, of which 16 were waited for; matrix products, arithmetic and copies ran while one was open for 5% of the time, Pallas kernels for 14%

profile of v5, /device:TPU:8, one launch (start us, length us, event | category | flops | bytes accessed | tf_op | source)
XLA Modules:
  0.0 152.6 jit_solution(7859755088825949572)
XLA Ops:
  7.2 0.0 copy-start
  7.2 0.0 reduce-scatter.2.cloned.1.call-start
  7.2 1.2 slice.6
  8.4 2.3 %collective-permute-start.2 = (bf16[128,2048]{1,0:T(8,128)(2,1)S(1)}, bf16[128,2048]{1,0:T(8,128)(2,1)S(1)}, u32[]{:S(2)}, u32[]{:S(2)}) collective-permute-start(bf16[128,2048]{1,0:T(8,128)(2,1)S(1)} %slice.6), channel_id=1, source_target_pairs={{0,4},{1,5},{2,6},{3,7},{4,0},{5,1},{6,2},{7,3},{8,12},{9,13},{10,... | collective-permute-start | bytes 1572872 | tf_op jit(solution)/shard_map/ppermute | solution.py:254
  10.7 2.0 %fusion = f32[128,128]{1,0:T(8,128)S(1)} fusion(bf16[128,4096]{1,0:T(8,128)(2,1)} %tok.5, bf16[4096,128]{1,0:T(8,128)(2,1)} %refs_7_.1), kind=kOutput, calls=%fused_computation.5 | convolution fusion | flops 134217728 | bytes 2162688 | tf_op jit(solution)/shard_map/dot_general | solution.py:283
  12.6 0.8 collective-permute-start.3
  13.4 3.8 %collective-permute-done.3 = f32[128,128]{1,0:T(8,128)S(1)} collective-permute-done((f32[128,128]{1,0:T(8,128)S(1)}, f32[128,128]{1,0:T(8,128)S(1)}, u32[]{:S(2)}, u32[]{:S(2)}) %collective-permute-start.3) | collective-permute-done | bytes 65568 | tf_op jit(solution)/shard_map/ppermute | solution.py:254
  17.2 1.4 collective-permute-start.4
  18.6 2.8 %collective-permute-start.1 = (bf16[128,2048]{1,0:T(8,128)(2,1)S(1)}, bf16[128,2048]{1,0:T(8,128)(2,1)S(1)}, u32[]{:S(2)}, u32[]{:S(2)}) collective-permute-start(bf16[128,2048]{1,0:T(8,128)(2,1)S(1)} %slice.6), channel_id=1, source_target_pairs={{0,2},{1,3},{2,0},{3,1},{4,6},{5,7},{6,4},{7,5},{8,10},{9,11},{10,... | collective-permute-start | bytes 1572872 | tf_op jit(solution)/shard_map/ppermute | solution.py:254
  21.4 0.8 slice.7
  22.2 1.3 collective-permute-done.4
  23.6 0.4 collective-permute-start.9
  23.9 2.6 %collective-permute-start.5 = (bf16[128,2048]{1,0:T(8,128)(2,1)S(1)}, bf16[128,2048]{1,0:T(8,128)(2,1)S(1)}, u32[]{:S(2)}, u32[]{:S(2)}) collective-permute-start(bf16[128,2048]{1,0:T(8,128)(2,1)S(1)} %collective-permute-done.2.m4), channel_id=1, source_target_pairs={{0,12},{1,13},{2,14},{3,15},{4,8},{5,9},{6,10},{7,11},{8,4},{9,5},... | collective-permute-start | bytes 1572872 | tf_op jit(solution)/shard_map/ppermute | solution.py:254
  26.5 0.0 collective-permute-start.6
  26.5 1.3 collective-permute-done.6
  27.8 3.1 %collective-permute-start.7 = (f32[128,128]{1,0:T(8,128)S(1)}, f32[128,128]{1,0:T(8,128)S(1)}, u32[]{:S(2)}, u32[]{:S(2)}) collective-permute-start(f32[128,128]{1,0:T(8,128)S(1)} %add.46), channel_id=1, source_target_pairs={{0,2},{1,3},{2,0},{3,1},{4,6},{5,7},{6,4},{7,5},{8,10},{9,11},{10,... | collective-permute-start | bytes 196616 | tf_op jit(solution)/shard_map/ppermute | solution.py:254
  30.9 3.9 %collective-permute-done.7 = f32[128,128]{1,0:T(8,128)S(1)} collective-permute-done((f32[128,128]{1,0:T(8,128)S(1)}, f32[128,128]{1,0:T(8,128)S(1)}, u32[]{:S(2)}, u32[]{:S(2)}) %collective-permute-start.7) | collective-permute-done | bytes 65568 | tf_op jit(solution)/shard_map/ppermute | solution.py:254
  34.8 0.6 add.47.latent
  35.4 2.8 %collective-permute-start.8 = (bf16[128,2048]{1,0:T(8,128)(2,1)}, bf16[128,2048]{1,0:T(8,128)(2,1)}, u32[]{:S(2)}, u32[]{:S(2)}) collective-permute-start(bf16[128,2048]{1,0:T(8,128)(2,1)} %slice.7), channel_id=1, source_target_pairs={{0,2},{1,3},{2,0},{3,1},{4,6},{5,7},{6,4},{7,5},{8,10},{9,11},{10,... | collective-permute-start | bytes 1572872 | tf_op jit(solution)/shard_map/ppermute | solution.py:254
  38.2 1.6 %collective-permute-start.10 = (bf16[128,2048]{1,0:T(8,128)(2,1)S(1)}, bf16[128,2048]{1,0:T(8,128)(2,1)}, u32[]{:S(2)}, u32[]{:S(2)}) collective-permute-start(bf16[128,2048]{1,0:T(8,128)(2,1)S(1)} %collective-permute-done.9.m4), channel_id=1, source_target_pairs={{0,12},{1,13},{2,14},{3,15},{4,8},{5,9},{6,10},{7,11},{8,4},{9,5},... | collective-permute-start | bytes 1572872 | tf_op jit(solution)/shard_map/ppermute | solution.py:254
  39.8 0.8 copy-done.5
  40.6 7.7 %main_part.2 = (bf16[128,2048]{1,0:T(8,128)(2,1)}, f32[128,128]{1,0:T(8,128)}, bf16[8,2,448,256]{3,2,1,0:T(8,128)(2,1)}) custom-call(bf16[128,4096]{1,0:T(8,128)(2,1)} %tok.5, bf16[128,4096]{1,0:T(8,128)(2,1)} %collective-permute-done.m1, bf16[128,2048]{1,0:T(8,128)(2,1)} %copy-done.3, bf16[128,2048]{1,0:T(8,128)(2,1)} %copy-done.2, ...), custom_call_target="tpu_custom_call" | custom-call | flops 2000000000 | bytes 29360128 | tf_op jit(solution)/shard_map/main_part/pallas_call | solution.py:89
  48.3 1.7 %collective-permute-done.8.m2 = bf16[128,2048]{1,0:T(8,128)(2,1)} collective-permute-done((bf16[128,2048]{1,0:T(8,128)(2,1)}, bf16[128,2048]{1,0:T(8,128)(2,1)}, u32[]{:S(2)}, u32[]{:S(2)}) %collective-permute-start.8) | collective-permute-done | bytes 524320 | tf_op jit(solution)/shard_map/ppermute | solution.py:254
  50.0 1.0 collective-permute-done.10.m8
  51.0 7.8 %main_part.3 = (bf16[128,2048]{1,0:T(8,128)(2,1)}, f32[128,128]{1,0:T(8,128)}, bf16[8,2,448,256]{3,2,1,0:T(8,128)(2,1)}) custom-call(bf16[128,4096]{1,0:T(8,128)(2,1)} %tok.5, bf16[128,4096]{1,0:T(8,128)(2,1)} %collective-permute-done.m1, bf16[128,2048]{1,0:T(8,128)(2,1)} %collective-permute-done.8.m2, ...), custom_call_target="tpu_custom_call", output_to_operand_aliasing={{2}: (10, {})} | custom-call | flops 2000000000 | bytes 29360128 | tf_op jit(solution)/shard_map/main_part/pallas_call | solution.py:89
  58.8 0.0 copy-start.8
  58.8 0.0 reduce-scatter.2.cloned.1.call-update
  58.8 0.8 copy-done.7
  59.6 0.0 copy-done.8
  59.7 2.1 %collective-permute-start.11 = (f32[128,128]{1,0:T(8,128)S(1)}, f32[128,128]{1,0:T(8,128)S(1)}, u32[]{:S(2)}, u32[]{:S(2)}) collective-permute-start(f32[128,128]{1,0:T(8,128)S(1)} %add.48), channel_id=1, source_target_pairs={{0,2},{1,3},{2,0},{3,1},{4,6},{5,7},{6,4},{7,5},{8,10},{9,11},{10,... | collective-permute-start | bytes 196616 | tf_op jit(solution)/shard_map/ppermute | solution.py:254
  61.7 6.5 %back_products.1 = (bf16[128,4096]{1,0:T(8,128)(2,1)}, bf16[128,4096]{1,0:T(8,128)(2,1)}, bf16[128,2048]{1,0:T(8,128)(2,1)}, bf16[128,2048]{1,0:T(8,128)(2,1)}, ...) custom-call(bf16[128,2048]{1,0:T(8,128)(2,1)} %get-tuple-element.39.low.refs_0_, ...), custom_call_target="tpu_custom_call" | custom-call | flops 2000000000 | bytes 20971520 | tf_op jit(solution)/shard_map/back_products/pallas_call | solution.py:136
  68.3 0.3 collective-permute-start.16
  68.6 1.0 collective-permute-start.12
  69.6 3.5 %collective-permute-done.12 = f32[128,128]{1,0:T(8,128)S(1)} collective-permute-done((f32[128,128]{1,0:T(8,128)S(1)}, f32[128,128]{1,0:T(8,128)S(1)}, u32[]{:S(2)}, u32[]{:S(2)}) %collective-permute-start.12) | collective-permute-done | bytes 65568 | tf_op jit(solution)/shard_map/ppermute | solution.py:254
  73.1 1.0 collective-permute-start.13
  74.1 1.5 %collective-permute-start.20 = (bf16[128,4096]{1,0:T(8,128)(2,1)}, bf16[128,4096]{1,0:T(8,128)(2,1)}, u32[]{:S(2)}, u32[]{:S(2)}) collective-permute-start(bf16[128,4096]{1,0:T(8,128)(2,1)} %get-tuple-element.64), channel_id=1, source_target_pairs={{0,2},{1,3},{2,0},{3,1},{4,6},{5,7},{6,4},{7,5},{8,10},{9,11},{10,... | collective-permute-start | bytes 3145736 | tf_op jit(solution)/shard_map/ppermute | solution.py:254
  75.7 3.9 %collective-permute-start.14 = (f32[128,128]{1,0:T(8,128)S(1)}, f32[128,128]{1,0:T(8,128)S(1)}, u32[]{:S(2)}, u32[]{:S(2)}) collective-permute-start(f32[128,128]{1,0:T(8,128)S(1)} %add.50), channel_id=1, source_target_pairs={{0,4},{1,5},{2,6},{3,7},{4,0},{5,1},{6,2},{7,3},{8,12},{9,13},{10,... | collective-permute-start | bytes 196616 | tf_op jit(solution)/shard_map/ppermute | solution.py:254
  79.6 2.2 %collective-permute-done.14 = f32[128,128]{1,0:T(8,128)S(1)} collective-permute-done((f32[128,128]{1,0:T(8,128)S(1)}, f32[128,128]{1,0:T(8,128)S(1)}, u32[]{:S(2)}, u32[]{:S(2)}) %collective-permute-start.14) | collective-permute-done | bytes 65568 | tf_op jit(solution)/shard_map/ppermute | solution.py:254
  81.8 0.1 collective-permute-start.15
  81.9 1.0 collective-permute-start.18
  82.9 0.2 collective-permute-done.15
  83.2 0.6 add_convert_fusion.1.lat.refs_8_
  83.8 2.7 %down_part.1 = (bf16[8,128,256]{2,1,0:T(8,128)(2,1)}, bf16[8,128,256]{2,1,0:T(8,128)(2,1)}) custom-call(s32[1]{0:T(128)} %bitcast.side, bf16[128,4096]{1,0:T(8,128)(2,1)} %tok.5, bf16[128,128]{1,0:T(8,128)(2,1)} %add_convert_fusion.1.lat.refs_8_), custom_call_target="tpu_custom_call" | custom-call | flops 300000000 | bytes 10485760 | tf_op jit(solution)/shard_map/down_part/pallas_call | solution.py:162
  86.5 1.7 %collective-permute-done.13 = bf16[128,2048]{1,0:T(8,128)(2,1)S(1)} collective-permute-done((bf16[128,2048]{1,0:T(8,128)(2,1)}, bf16[128,2048]{1,0:T(8,128)(2,1)S(1)}, u32[]{:S(2)}, u32[]{:S(2)}) %collective-permute-start.13) | collective-permute-done | bytes 524320 | tf_op jit(solution)/shard_map/ppermute | solution.py:254
  88.2 1.2 add.53
  89.4 3.6 %collective-permute-start.17 = (bf16[128,2048]{1,0:T(8,128)(2,1)S(1)}, bf16[128,2048]{1,0:T(8,128)(2,1)S(1)}, u32[]{:S(2)}, u32[]{:S(2)}) collective-permute-start(bf16[128,2048]{1,0:T(8,128)(2,1)S(1)} %add.53), channel_id=1, source_target_pairs={{0,4},{1,5},{2,6},{3,7},{4,0},{5,1},{6,2},{7,3},{8,12},{9,13},{10,... | collective-permute-start | bytes 1572872 | tf_op jit(solution)/shard_map/ppermute | solution.py:254
  93.0 0.8 collective-permute-start.22
  93.8 4.3 %collective-permute-done.18 = bf16[128,2048]{1,0:T(8,128)(2,1)S(1)} collective-permute-done((bf16[128,2048]{1,0:T(8,128)(2,1)}, bf16[128,2048]{1,0:T(8,128)(2,1)S(1)}, u32[]{:S(2)}, u32[]{:S(2)}) %collective-permute-start.18) | collective-permute-done | bytes 524320 | tf_op jit(solution)/shard_map/ppermute | solution.py:254
  98.1 3.9 %collective-permute-done.20.refs_5_ = bf16[128,4096]{1,0:T(8,128)(2,1)} collective-permute-done((bf16[128,4096]{1,0:T(8,128)(2,1)}, bf16[128,4096]{1,0:T(8,128)(2,1)}, u32[]{:S(2)}, u32[]{:S(2)}) %collective-permute-start.20) | collective-permute-done | bytes 1048608 | tf_op jit(solution)/shard_map/ppermute | solution.py:254
  102.0 0.5 collective-permute-done.17.refs_2_
  102.6 7.5 %collective-permute-done.22 = bf16[8,128,256]{2,1,0:T(8,128)(2,1)S(1)} collective-permute-done((bf16[8,128,256]{2,1,0:T(8,128)(2,1)}, bf16[8,128,256]{2,1,0:T(8,128)(2,1)S(1)}, u32[]{:S(2)}, u32[]{:S(2)}) %collective-permute-start.22) | collective-permute-done | bytes 524320 | tf_op jit(solution)/shard_map/ppermute | solution.py:271
  110.1 2.0 %add_convert_fusion = bf16[8,128,256]{2,1,0:T(8,128)(2,1)} fusion(bf16[8,128,256]{2,1,0:T(8,128)(2,1)S(1)} %collective-permute-done.22, bf16[8,128,256]{2,1,0:T(8,128)(2,1)} %get-tuple-element.67), kind=kLoop, calls=%fused_computation.1 | loop fusion | flops 1048576 | bytes 1572864 | tf_op jit(solution)/shard_map/convert_element_type | solution.py:313
  112.1 8.5 %all-to-all-start = ((bf16[8,128,256]{2,1,0:T(8,128)(2,1)}), bf16[8,128,256]{2,1,0:T(8,128)(2,1)S(1)}, u32[]{:S(2)}, u32[]{:S(2)}) async-start(bf16[8,128,256]{2,1,0:T(8,128)(2,1)} %add_convert_fusion), calls=%async_computation.1 | async-start | bytes 1048576 | tf_op jit(solution)/shard_map/all_to_all | solution.py:315
  120.6 0.1 add.54
  120.7 4.1 %collective-permute-start.19 = (bf16[128,2048]{1,0:T(8,128)(2,1)S(1)}, bf16[128,2048]{1,0:T(8,128)(2,1)S(1)}, u32[]{:S(2)}, u32[]{:S(2)}) collective-permute-start(bf16[128,2048]{1,0:T(8,128)(2,1)S(1)} %add.54), channel_id=1, source_target_pairs={{0,4},{1,5},{2,6},{3,7},{4,0},{5,1},{6,2},{7,3},{8,12},{9,13},{10,... | collective-permute-start | bytes 1572872 | tf_op jit(solution)/shard_map/ppermute | solution.py:254
  124.8 10.3 %collective-permute-done.19.refs_3_ = bf16[128,2048]{1,0:T(8,128)(2,1)S(1)} collective-permute-done((bf16[128,2048]{1,0:T(8,128)(2,1)S(1)}, bf16[128,2048]{1,0:T(8,128)(2,1)S(1)}, u32[]{:S(2)}, u32[]{:S(2)}) %collective-permute-start.19) | collective-permute-done | bytes 524320 | tf_op jit(solution)/shard_map/ppermute | solution.py:254
  135.1 0.8 copy-done.10
  136.0 1.0 dynamic-slice_bitcast_fusion
  136.9 1.5 collective-permute-start.21
  138.4 4.4 %token_grad.1 = bf16[128,4096]{1,0:T(8,128)(2,1)} custom-call(bf16[128,2048]{1,0:T(8,128)(2,1)} %get-tuple-element.39.low.refs_0_, bf16[128,2048]{1,0:T(8,128)(2,1)} %get-tuple-element.45.high.refs_1_, bf16[128,2048]{1,0:T(8,128)(2,1)} %copy-done.9, bf16[128,2048]{1,0:T(8,128)(2,1)} %copy-done.10, bf16[128,4096]{1,0:T(8,128)(2,1)} %collective-permute-done.16.refs_4_, ...), custom_call_target="tpu_custom_call" | custom-call | flops 2000000000 | bytes 17825792 | tf_op jit(solution)/shard_map/token_grad/pallas_call | solution.py:198
  142.8 0.2 collective-permute-done.21.arrived
  143.0 0.1 convert_reduce_fusion
  143.1 0.8 copy.12
  143.9 1.8 %finish.1 = (f32[64,256]{1,0:T(8,128)}, f32[4,64,256]{2,1,0:T(8,128)}, f32[128,256]{1,0:T(8,128)}) custom-call(s32[1]{0:T(128)} %bitcast.side, bf16[2,448,256]{2,1,0:T(8,128)(2,1)} %bitcast.11, bf16[448,256]{1,0:T(8,128)(2,1)} %copy-done.6), custom_call_target="tpu_custom_call" | custom-call | flops 300000 | bytes 4194304 | tf_op jit(solution)/shard_map/finish/pallas_call | solution.py:228
  (34 shorter events, 0.1 us)
Async XLA Ops:
  7.2 14.2 %copy-start = (bf16[128,4096]{1,0:T(8,128)(2,1)S(1)}, bf16[128,4096]{1,0:T(8,128)(2,1)}, u32[]{:S(2)}) copy-start(bf16[128,4096]{1,0:T(8,128)(2,1)} %tok.5) | copy-start | bytes 3145732
  7.2 128.0 %reduce-scatter.2.cloned.1.call-start = ((), (), s32[]{:S(2)}) async-start(), calls=%async_computation.2 | async-start | bytes 4128768 | tf_op jit(solution)/shard_map/reduce_scatter | solution.py:264
  8.4 15.2 %collective-permute-start.2 = (bf16[128,2048]{1,0:T(8,128)(2,1)S(1)}, bf16[128,2048]{1,0:T(8,128)(2,1)S(1)}, u32[]{:S(2)}, u32[]{:S(2)}) collective-permute-start(bf16[128,2048]{1,0:T(8,128)(2,1)S(1)} %slice.6), channel_id=1, source_target_pairs={{0,4},{1,5},{2,6},{3,7},{4,0},{5,1},{6,2},{7,3},{8,12},{9,13},{10,... | collective-permute-start | bytes 1572872 | tf_op jit(solution)/shard_map/ppermute | solution.py:254
  10.7 29.1 %collective-permute-start = (bf16[128,4096]{1,0:T(8,128)(2,1)}, bf16[128,4096]{1,0:T(8,128)(2,1)}, u32[]{:S(2)}, u32[]{:S(2)}) collective-permute-start(bf16[128,4096]{1,0:T(8,128)(2,1)} %tok.5), channel_id=1, source_target_pairs={{0,1},{1,0},{2,3},{3,2},{4,5},{5,4},{6,7},{7,6},{8,9},{9,8},{10,11... | collective-permute-start | bytes 3145736 | tf_op jit(solution)/shard_map/ppermute | solution.py:254
  12.6 4.6 %collective-permute-start.3 = (f32[128,128]{1,0:T(8,128)S(1)}, f32[128,128]{1,0:T(8,128)S(1)}, u32[]{:S(2)}, u32[]{:S(2)}) collective-permute-start(f32[128,128]{1,0:T(8,128)S(1)} %fusion), channel_id=1, source_target_pairs={{0,12},{1,13},{2,14},{3,15},{4,8},{5,9},{6,10},{7,11},{8,4},{9,5},... | collective-permute-start | bytes 196616 | tf_op jit(solution)/shard_map/ppermute | solution.py:254
  17.2 6.3 %collective-permute-start.4 = (f32[128,128]{1,0:T(8,128)S(1)}, f32[128,128]{1,0:T(8,128)S(1)}, u32[]{:S(2)}, u32[]{:S(2)}) collective-permute-start(f32[128,128]{1,0:T(8,128)S(1)} %add.44), channel_id=1, source_target_pairs={{0,4},{1,5},{2,6},{3,7},{4,0},{5,1},{6,2},{7,3},{8,12},{9,13},{10,... | collective-permute-start | bytes 196616 | tf_op jit(solution)/shard_map/ppermute | solution.py:254
  18.6 16.8 %collective-permute-start.1 = (bf16[128,2048]{1,0:T(8,128)(2,1)S(1)}, bf16[128,2048]{1,0:T(8,128)(2,1)S(1)}, u32[]{:S(2)}, u32[]{:S(2)}) collective-permute-start(bf16[128,2048]{1,0:T(8,128)(2,1)S(1)} %slice.6), channel_id=1, source_target_pairs={{0,2},{1,3},{2,0},{3,1},{4,6},{5,7},{6,4},{7,5},{8,10},{9,11},{10,... | collective-permute-start | bytes 1572872 | tf_op jit(solution)/shard_map/ppermute | solution.py:254
  23.6 16.2 %copy-start.2 = (bf16[128,2048]{1,0:T(8,128)(2,1)}, bf16[128,2048]{1,0:T(8,128)(2,1)S(1)}, u32[]{:S(2)}) copy-start(bf16[128,2048]{1,0:T(8,128)(2,1)S(1)} %collective-permute-done.2.m4) | copy-start | bytes 1572868
  23.6 14.6 %collective-permute-start.9 = (bf16[128,2048]{1,0:T(8,128)(2,1)}, bf16[128,2048]{1,0:T(8,128)(2,1)S(1)}, u32[]{:S(2)}, u32[]{:S(2)}) collective-permute-start(bf16[128,2048]{1,0:T(8,128)(2,1)} %slice.7), channel_id=1, source_target_pairs={{0,4},{1,5},{2,6},{3,7},{4,0},{5,1},{6,2},{7,3},{8,12},{9,13},{10,... | collective-permute-start | bytes 1572872 | tf_op jit(solution)/shard_map/ppermute | solution.py:254
  23.9 15.8 %collective-permute-start.5 = (bf16[128,2048]{1,0:T(8,128)(2,1)S(1)}, bf16[128,2048]{1,0:T(8,128)(2,1)S(1)}, u32[]{:S(2)}, u32[]{:S(2)}) collective-permute-start(bf16[128,2048]{1,0:T(8,128)(2,1)S(1)} %collective-permute-done.2.m4), channel_id=1, source_target_pairs={{0,12},{1,13},{2,14},{3,15},{4,8},{5,9},{6,10},{7,11},{8,4},{9,5},... | collective-permute-start | bytes 1572872 | tf_op jit(solution)/shard_map/ppermute | solution.py:254
  26.5 1.3 collective-permute-start.6
  27.8 7.0 %collective-permute-start.7 = (f32[128,128]{1,0:T(8,128)S(1)}, f32[128,128]{1,0:T(8,128)S(1)}, u32[]{:S(2)}, u32[]{:S(2)}) collective-permute-start(f32[128,128]{1,0:T(8,128)S(1)} %add.46), channel_id=1, source_target_pairs={{0,2},{1,3},{2,0},{3,1},{4,6},{5,7},{6,4},{7,5},{8,10},{9,11},{10,... | collective-permute-start | bytes 196616 | tf_op jit(solution)/shard_map/ppermute | solution.py:254
  35.4 4.4 %copy-start.3 = (bf16[128,2048]{1,0:T(8,128)(2,1)}, bf16[128,2048]{1,0:T(8,128)(2,1)S(1)}, u32[]{:S(2)}) copy-start(bf16[128,2048]{1,0:T(8,128)(2,1)S(1)} %collective-permute-done.1.m2) | copy-start | bytes 1572868
  35.4 14.6 %collective-permute-start.8 = (bf16[128,2048]{1,0:T(8,128)(2,1)}, bf16[128,2048]{1,0:T(8,128)(2,1)}, u32[]{:S(2)}, u32[]{:S(2)}) collective-permute-start(bf16[128,2048]{1,0:T(8,128)(2,1)} %slice.7), channel_id=1, source_target_pairs={{0,2},{1,3},{2,0},{3,1},{4,6},{5,7},{6,4},{7,5},{8,10},{9,11},{10,... | collective-permute-start | bytes 1572872 | tf_op jit(solution)/shard_map/ppermute | solution.py:254
  38.2 10.1 %copy-start.4 = (bf16[128,2048]{1,0:T(8,128)(2,1)}, bf16[128,2048]{1,0:T(8,128)(2,1)S(1)}, u32[]{:S(2)}) copy-start(bf16[128,2048]{1,0:T(8,128)(2,1)S(1)} %collective-permute-done.9.m4) | copy-start | bytes 1572868
  38.2 12.8 %collective-permute-start.10 = (bf16[128,2048]{1,0:T(8,128)(2,1)S(1)}, bf16[128,2048]{1,0:T(8,128)(2,1)}, u32[]{:S(2)}, u32[]{:S(2)}) collective-permute-start(bf16[128,2048]{1,0:T(8,128)(2,1)S(1)} %collective-permute-done.9.m4), channel_id=1, source_target_pairs={{0,12},{1,13},{2,14},{3,15},{4,8},{5,9},{6,10},{7,11},{8,4},{9,5},... | collective-permute-start | bytes 1572872 | tf_op jit(solution)/shard_map/ppermute | solution.py:254
  39.8 0.8 copy-start.5
  58.8 0.8 copy-start.7
  58.8 0.9 copy-start.8
  59.7 8.6 %collective-permute-start.11 = (f32[128,128]{1,0:T(8,128)S(1)}, f32[128,128]{1,0:T(8,128)S(1)}, u32[]{:S(2)}, u32[]{:S(2)}) collective-permute-start(f32[128,128]{1,0:T(8,128)S(1)} %add.48), channel_id=1, source_target_pairs={{0,2},{1,3},{2,0},{3,1},{4,6},{5,7},{6,4},{7,5},{8,10},{9,11},{10,... | collective-permute-start | bytes 196616 | tf_op jit(solution)/shard_map/ppermute | solution.py:254
  68.2 52.3 %copy-start.1 = (bf16[128,2048]{1,0:T(8,128)(2,1)S(1)}, bf16[128,2048]{1,0:T(8,128)(2,1)}, u32[]{:S(2)}) copy-start(bf16[128,2048]{1,0:T(8,128)(2,1)} %get-tuple-element.57) | copy-start | bytes 1572868
  68.3 14.9 %collective-permute-start.16 = (bf16[128,4096]{1,0:T(8,128)(2,1)}, bf16[128,4096]{1,0:T(8,128)(2,1)}, u32[]{:S(2)}, u32[]{:S(2)}) collective-permute-start(bf16[128,4096]{1,0:T(8,128)(2,1)} %get-tuple-element.53), channel_id=1, source_target_pairs={{0,1},{1,0},{2,3},{3,2},{4,5},{5,4},{6,7},{7,6},{8,9},{9,8},{10,11... | collective-permute-start | bytes 3145736 | tf_op jit(solution)/shard_map/ppermute | solution.py:254
  68.6 4.5 %collective-permute-start.12 = (f32[128,128]{1,0:T(8,128)S(1)}, f32[128,128]{1,0:T(8,128)S(1)}, u32[]{:S(2)}, u32[]{:S(2)}) collective-permute-start(f32[128,128]{1,0:T(8,128)S(1)} %add.49), channel_id=1, source_target_pairs={{0,12},{1,13},{2,14},{3,15},{4,8},{5,9},{6,10},{7,11},{8,4},{9,5},... | collective-permute-start | bytes 196616 | tf_op jit(solution)/shard_map/ppermute | solution.py:254
  73.1 15.1 %collective-permute-start.13 = (bf16[128,2048]{1,0:T(8,128)(2,1)}, bf16[128,2048]{1,0:T(8,128)(2,1)S(1)}, u32[]{:S(2)}, u32[]{:S(2)}) collective-permute-start(bf16[128,2048]{1,0:T(8,128)(2,1)} %get-tuple-element.52), channel_id=1, source_target_pairs={{0,12},{1,13},{2,14},{3,15},{4,8},{5,9},{6,10},{7,11},{8,4},{9,5},... | collective-permute-start | bytes 1572872 | tf_op jit(solution)/shard_map/ppermute | solution.py:254
  74.1 27.9 %collective-permute-start.20 = (bf16[128,4096]{1,0:T(8,128)(2,1)}, bf16[128,4096]{1,0:T(8,128)(2,1)}, u32[]{:S(2)}, u32[]{:S(2)}) collective-permute-start(bf16[128,4096]{1,0:T(8,128)(2,1)} %get-tuple-element.64), channel_id=1, source_target_pairs={{0,2},{1,3},{2,0},{3,1},{4,6},{5,7},{6,4},{7,5},{8,10},{9,11},{10,... | collective-permute-start | bytes 3145736 | tf_op jit(solution)/shard_map/ppermute | solution.py:254
  75.7 6.1 %collective-permute-start.14 = (f32[128,128]{1,0:T(8,128)S(1)}, f32[128,128]{1,0:T(8,128)S(1)}, u32[]{:S(2)}, u32[]{:S(2)}) collective-permute-start(f32[128,128]{1,0:T(8,128)S(1)} %add.50), channel_id=1, source_target_pairs={{0,4},{1,5},{2,6},{3,7},{4,0},{5,1},{6,2},{7,3},{8,12},{9,13},{10,... | collective-permute-start | bytes 196616 | tf_op jit(solution)/shard_map/ppermute | solution.py:254
  81.8 1.3 collective-permute-start.15
  81.9 16.2 %collective-permute-start.18 = (bf16[128,2048]{1,0:T(8,128)(2,1)}, bf16[128,2048]{1,0:T(8,128)(2,1)S(1)}, u32[]{:S(2)}, u32[]{:S(2)}) collective-permute-start(bf16[128,2048]{1,0:T(8,128)(2,1)} %get-tuple-element.59), channel_id=1, source_target_pairs={{0,12},{1,13},{2,14},{3,15},{4,8},{5,9},{6,10},{7,11},{8,4},{9,5},... | collective-permute-start | bytes 1572872 | tf_op jit(solution)/shard_map/ppermute | solution.py:254
  89.4 13.2 %collective-permute-start.17 = (bf16[128,2048]{1,0:T(8,128)(2,1)S(1)}, bf16[128,2048]{1,0:T(8,128)(2,1)S(1)}, u32[]{:S(2)}, u32[]{:S(2)}) collective-permute-start(bf16[128,2048]{1,0:T(8,128)(2,1)S(1)} %add.53), channel_id=1, source_target_pairs={{0,4},{1,5},{2,6},{3,7},{4,0},{5,1},{6,2},{7,3},{8,12},{9,13},{10,... | collective-permute-start | bytes 1572872 | tf_op jit(solution)/shard_map/ppermute | solution.py:254
  93.0 17.1 %collective-permute-start.22 = (bf16[8,128,256]{2,1,0:T(8,128)(2,1)}, bf16[8,128,256]{2,1,0:T(8,128)(2,1)S(1)}, u32[]{:S(2)}, u32[]{:S(2)}) collective-permute-start(bf16[8,128,256]{2,1,0:T(8,128)(2,1)} %get-tuple-element.55), channel_id=1, source_target_pairs={{0,128},{16,144},{32,160},{48,176},{64,192},{80,208},{96,224},{112... | collective-permute-start | bytes 1572872 | tf_op jit(solution)/shard_map/ppermute | solution.py:271
  102.6 35.9 %copy-start.9 = (bf16[128,2048]{1,0:T(8,128)(2,1)}, bf16[128,2048]{1,0:T(8,128)(2,1)S(1)}, u32[]{:S(2)}) copy-start(bf16[128,2048]{1,0:T(8,128)(2,1)S(1)} %collective-permute-done.17.refs_2_) | copy-start | bytes 1572868
  112.1 30.7 %all-to-all-start = ((bf16[8,128,256]{2,1,0:T(8,128)(2,1)}), bf16[8,128,256]{2,1,0:T(8,128)(2,1)S(1)}, u32[]{:S(2)}, u32[]{:S(2)}) async-start(bf16[8,128,256]{2,1,0:T(8,128)(2,1)} %add_convert_fusion), calls=%async_computation.1 | async-start | bytes 1048576 | tf_op jit(solution)/shard_map/all_to_all | solution.py:315
  120.7 14.4 %collective-permute-start.19 = (bf16[128,2048]{1,0:T(8,128)(2,1)S(1)}, bf16[128,2048]{1,0:T(8,128)(2,1)S(1)}, u32[]{:S(2)}, u32[]{:S(2)}) collective-permute-start(bf16[128,2048]{1,0:T(8,128)(2,1)S(1)} %add.54), channel_id=1, source_target_pairs={{0,4},{1,5},{2,6},{3,7},{4,0},{5,1},{6,2},{7,3},{8,12},{9,13},{10,... | collective-permute-start | bytes 1572872 | tf_op jit(solution)/shard_map/ppermute | solution.py:254
  135.1 0.8 copy-start.10
  136.9 6.1 %collective-permute-start.21 = (bf16[448,256]{1,0:T(8,128)(2,1)S(1)}, bf16[448,256]{1,0:T(8,128)(2,1)S(1)}, u32[]{:S(2)}, u32[]{:S(2)}) collective-permute-start(bf16[448,256]{1,0:T(8,128)(2,1)S(1)} %dynamic-slice_bitcast_fusion), channel_id=1, source_target_pairs={{0,128},{16,144},{32,160},{48,176},{64,192},{80,208},{96,224},{112... | collective-permute-start | bytes 688136 | tf_op jit(solution)/shard_map/ppermute | solution.py:271
  143.0 0.9 copy-start.6
Sparse Core Ops, SparseCore 0:
  58.9 51.8 reduce-scatter.1

commit v6 on v4

--- a/solution.py
+++ b/solution.py
@@ -9,7 +9,7 @@
 
 BLOCK = 64
 CHUNK = 256
-MAIN_STEP, FINAL_STEP = 512, 2048
+MAIN_STEP, FINAL_STEP = 512, 1024
 RING = 8
 VMEM = 62 << 20
 F32 = jnp.float32
@@ -103,19 +103,6 @@
     )(*args)
 
 
-def pick_half(low, high):
-    first = pl.program_id(0) < pl.num_programs(0) // 2
-    return jnp.where(first, low[...], high[...])
-
-
-def half_specs(rows, steps):
-    half = steps // 2
-    return [
-        pl.BlockSpec((rows, FINAL_STEP), lambda i: (0, jnp.minimum(i, half - 1))),
-        pl.BlockSpec((rows, FINAL_STEP), lambda i: (0, jnp.maximum(i - half, 0))),
-    ]
-
-
 def back_kernel(low, high, sec, b1, *halves):
     mask = block_mask()
 
@@ -176,41 +163,45 @@
     )(jnp.full((1,), x, jnp.int32), tokens, latent_grad)
 
 
-def final_kernel(*refs):
-    pairs, (r1, diag, down, lat, out) = refs[:6], refs[6:]
+def final_kernel(slope, r1, r2, r48, diag, down, lat, *refs):
+    out = refs[-1]
     mask = block_mask()
-    slope, r2, r48 = (pick_half(pairs[2 * k], pairs[2 * k + 1]) for k in range(3))
-    for c in range(FINAL_STEP // CHUNK):
+    for c in range(slope.shape[1] // CHUNK):
         cs = slice(c * CHUNK, (c + 1) * CHUNK)
         total = dot(slope[:, cs], spread(diag[:, cs], mask), 1, 1)
         total = total + dot(lat[...], down[cs, :], 1, 1)
-        for value in (r1, r2, r48):
-            total = total + value[:, cs].astype(F32)
+        for ref in (r1, r2, r48):
+            total = total + ref[:, cs].astype(F32)
         out[:, cs] = total.astype(BF16)
 
 
-def run_final(pairs, r1, diag, low_down, latent_grad):
-    rows, half_width = pairs[0][0].shape
-    width = 2 * half_width
+def run_final(part, slope, r1, r2, r48, diag, low_down, latent_grad, held):
+    rows, half = slope.shape
     rank = latent_grad.shape[1]
-    steps = width // FINAL_STEP
-    col = lambda r: pl.BlockSpec((r, FINAL_STEP), lambda i: (0, i))
+    steps = half // FINAL_STEP
+    base = part * steps
+    local = pl.BlockSpec((rows, FINAL_STEP), lambda i: (0, i))
+    whole = lambda r: pl.BlockSpec((r, FINAL_STEP), lambda i: (0, base + i))
+    in_specs = [
+        local, whole(rows), local, local, whole(BLOCK),
+        pl.BlockSpec((FINAL_STEP, rank), lambda i: (base + i, 0)),
+        pl.BlockSpec((rows, rank), lambda i: (0, 0)),
+    ]
+    args = [slope, r1, r2, r48, diag, low_down, latent_grad]
+    if held is not None:
+        in_specs.append(pl.BlockSpec(memory_space=pl.ANY))
+        args.append(held)
     return pl.pallas_call(
         final_kernel,
         grid=(steps,),
-        in_specs=half_specs(rows, steps) * 3
-        + [
-            col(rows),
-            col(BLOCK),
-            pl.BlockSpec((FINAL_STEP, rank), lambda i: (i, 0)),
-            pl.BlockSpec((rows, rank), lambda i: (0, 0)),
-        ],
-        out_specs=col(rows),
-        out_shape=jax.ShapeDtypeStruct((rows, width), BF16),
+        in_specs=in_specs,
+        out_specs=whole(rows),
+        out_shape=jax.ShapeDtypeStruct((rows, diag.shape[1]), BF16),
+        input_output_aliases={} if held is None else {7: 0},
         compiler_params=pltpu.CompilerParams(vmem_limit_bytes=VMEM),
-        cost_estimate=pl.CostEstimate(flops=2_000_000_000, bytes_accessed=17 << 20, transcendentals=0),
+        cost_estimate=pl.CostEstimate(flops=1_000_000_000, bytes_accessed=9 << 20, transcendentals=0),
         name="token_grad",
-    )(*[value for pair in pairs for value in pair], r1, diag, low_down, latent_grad)
+    )(*args)
 
 
 def finish_kernel(scale, side, summed, arrived, diag, section, up):
@@ -285,10 +276,10 @@
     part = part + flip(part, 4)
     m8_0 = flip(after(m4_0, part), 12)
     m4_1 = flip(after(h1, m4_0, part), 4)
-    part = part + flip(part, 1)
     part = part + flip(part, 2)
     m2_1 = flip(after(h1, m2_0, part), 2)
-    m8_1 = flip(after(m4_1, part), 12)
+    m8_1 = flip(m4_1, 12)
+    part = part + flip(part, 1)
     latent = part.astype(BF16)
 
     factors = (cotangent, diag_factor, section_factors, latent, low_up)
@@ -297,27 +288,25 @@
     summed = ring_sum(grads)
 
     part = lat0 + lat1
-    arrived = flip(part, 2)
+    arrived = flip(part, 2) + flip(part, 12) + flip(part, 14)
     b1, b2_0, b2_1, b4_0, b4_1, b8_0, b8_1 = run_back((slope0, slope1), section_factors)
     part = part + after(arrived, b1)
-    r2_0, r1 = flip(after(b2_0, part), 2), flip(after(b1, part), 1)
-    part = part + flip(part, 12)
-    q0, q1 = flip(after(b8_0, part), 12), flip(after(b8_1, part), 12)
-    part = part + flip(part, 4)
-    part = part + after(flip(part, 1), r2_0, r1)
+    r2_0, q0 = flip(after(b2_0, part), 2), flip(after(b8_0, part), 12)
+    part = part + after(flip(part, 4) + flip(part, 1) + flip(part, 5), r2_0)
+    r2_1, q1, r1 = flip(after(b2_1, part), 2), flip(after(b8_1, part), 12), flip(after(b1, part), 1)
     latent_grad = part.astype(BF16)
 
     keep, send = run_down(x, tokens, latent_grad)
     s0 = flip(b4_0 + after(q0, send), 4)
-    pair = (keep.astype(F32) + after(cross(send), q1, s0).astype(F32)).astype(BF16)
-    r2_1 = flip(after(b2_1, send), 2)
+    pair = (keep.astype(F32) + after(cross(after(send, r2_1)), q1, s0, r1).astype(F32)).astype(BF16)
     groups = [[side * RING + z for z in range(RING)] for side in range(2)]
     pair = lax.all_to_all(pair, "dp", 0, 0, axis_index_groups=groups, tiled=True)
     s1 = flip(b4_1 + q1, 4)
-    arrived = cross(lax.dynamic_index_in_dim(summed, 1 - x, 0, keepdims=False))
+    other = lax.dynamic_index_in_dim(summed, 1 - x, 0, keepdims=False)
+    arrived = cross(other)
     down_grad = (jnp.sum(after(pair, arrived).astype(F32), axis=0) * scale).T
-    pairs = ((slope0, slope1), (r2_0, r2_1), (s0, after(s1, arrived)))
-    token_grad = run_final(pairs, r1, diag_factor, low_down, latent_grad)
+    token_grad = run_final(0, slope0, r1, r2_0, after(s0, other), diag_factor, low_down, latent_grad, None)
+    token_grad = run_final(1, slope1, r1, r2_1, after(s1, other), diag_factor, low_down, latent_grad, token_grad)
     diag_grad, section_grad, up_grad = run_finish(x, summed, arrived, scale)
     return token_grad, diag_grad, section_grad, down_grad, up_grad
 

time: 145 us -> 153 us (1.055)
  starting transfers between devices: 45.3 us -> 49 us
  other arithmetic: 4.7 us -> 6.57 us
    ppermute x22 -> x24, waiting for transfers between devices: 32.9 us -> 39.7 us  [flip(): return lax.ppermute(value, 'tensor', [(i, i ^ mask) for i in range(16)])]
    ppermute x2, waiting for transfers between devices: 6.53 us -> 1.79 us  [cross(): return lax.ppermute(value, 'dp', [(i, i ^ RING) for i in range(2 * RING)])]
    ppermute x22 -> x24, starting transfers between devices: 36.1 us -> 38.2 us  [flip(): return lax.ppermute(value, 'tensor', [(i, i ^ mask) for i in range(16)])]
    add x1, other arithmetic: 0.12 us -> 1.96 us  [per_device(): s1 = flip(b4_1 + q1, 4)]
    ppermute x2, starting transfers between devices: 0.65 us -> 2.35 us  [cross(): return lax.ppermute(value, 'dp', [(i, i ^ RING) for i in range(2 * RING)])]
    pallas_call x1 -> x2, Pallas kernels: 4.57 us -> 6.03 us  [run_final(): pl.pallas_call(final_kernel, grid=(steps,), in_specs=in_specs, out_specs=...]
    unnamed x27 -> x29, local copies, waits for them, and re-layouts: 3.14 us -> 2.59 us
  transfers between devices with their start and end apart: 26 -> 28, of which waited for: 17 -> 13; matrix products, arithmetic and copies ran while one was open for 6% -> 7% of each run, Pallas kernels for 13% -> 15%
where the time goes in v6:
time: 153 us; the launch traced here: 151 us
  starting transfers between devices  49 us (32%)
  waiting for transfers between devices  41.5 us (27%)
  Pallas kernels  32.5 us (21%)
  between operations  14.3 us (9%)
  other arithmetic  6.57 us (4%)
  local copies, waits for them, and re-layouts  5.53 us (4%)
  matrix products  1.96 us (1%)
    ppermute x24, waiting for transfers between devices, flip(): return lax.ppermute(value, 'tensor', [(i, i ^ mask) for i in range(16)])  39.7 us
    ppermute x24, starting transfers between devices, flip(): return lax.ppermute(value, 'tensor', [(i, i ^ mask) for i in range(16)])  38.2 us
    pallas_call x2, Pallas kernels, run_main(): pl.pallas_call(main_kernel, grid=(steps,), in_specs=in_specs, out_specs=[...  15.5 us
    all_to_all x1, starting transfers between devices, per_device(): lax.all_to_all(pair, 'dp', 0, 0, axis_index_groups=groups, tiled=True)  8.46 us
    pallas_call x1, Pallas kernels, run_back(): pl.pallas_call(back_kernel, grid=(2,), in_specs=[fixed, fixed, pl.BlockSp...  6.37 us
    pallas_call x2, Pallas kernels, run_final(): pl.pallas_call(final_kernel, grid=(steps,), in_specs=in_specs, out_specs=...  6.03 us
  transfers between devices with their start and end apart: 28, of which 13 were waited for; matrix products, arithmetic and copies ran while one was open for 7% of the time, Pallas kernels for 15%

profile of v6, /device:TPU:8, one launch (start us, length us, event | category | flops | bytes accessed | tf_op | source)
XLA Modules:
  0.0 151.3 jit_solution(12014601281829058594)
XLA Ops:
  7.2 0.0 copy-start
  7.2 0.0 reduce-scatter.2.cloned.1.call-start
  7.2 1.2 slice.7
  8.4 2.3 %collective-permute-start.6 = (bf16[128,2048]{1,0:T(8,128)(2,1)S(1)}, bf16[128,2048]{1,0:T(8,128)(2,1)S(1)}, u32[]{:S(2)}, u32[]{:S(2)}) collective-permute-start(bf16[128,2048]{1,0:T(8,128)(2,1)S(1)} %slice.7), channel_id=1, source_target_pairs={{0,4},{1,5},{2,6},{3,7},{4,0},{5,1},{6,2},{7,3},{8,12},{9,13},{10,... | collective-permute-start | bytes 1572872 | tf_op jit(solution)/shard_map/ppermute | solution.py:244
  10.7 0.0 collective-permute-start
  10.7 2.0 %fusion = f32[128,128]{1,0:T(8,128)S(1)} fusion(bf16[128,4096]{1,0:T(8,128)(2,1)} %tok.5, bf16[4096,128]{1,0:T(8,128)(2,1)} %down.3), kind=kOutput, calls=%fused_computation.7 | convolution fusion | flops 134217728 | bytes 2162688 | tf_op jit(solution)/shard_map/dot_general | solution.py:273
  12.6 0.8 collective-permute-start.1
  13.4 3.8 %collective-permute-done.1 = f32[128,128]{1,0:T(8,128)S(1)} collective-permute-done((f32[128,128]{1,0:T(8,128)S(1)}, f32[128,128]{1,0:T(8,128)S(1)}, u32[]{:S(2)}, u32[]{:S(2)}) %collective-permute-start.1) | collective-permute-done | bytes 65568 | tf_op jit(solution)/shard_map/ppermute | solution.py:244
  17.2 1.4 collective-permute-start.3
  18.6 2.8 %collective-permute-start.2 = (bf16[128,2048]{1,0:T(8,128)(2,1)S(1)}, bf16[128,2048]{1,0:T(8,128)(2,1)S(1)}, u32[]{:S(2)}, u32[]{:S(2)}) collective-permute-start(bf16[128,2048]{1,0:T(8,128)(2,1)S(1)} %slice.7), channel_id=1, source_target_pairs={{0,2},{1,3},{2,0},{3,1},{4,6},{5,7},{6,4},{7,5},{8,10},{9,11},{10,... | collective-permute-start | bytes 1572872 | tf_op jit(solution)/shard_map/ppermute | solution.py:244
  21.4 0.8 slice.6
  22.2 1.3 collective-permute-done.3
  23.5 0.0 collective-permute-done.6.m4
  23.6 0.4 collective-permute-start.7
  23.9 2.6 %collective-permute-start.10 = (bf16[128,2048]{1,0:T(8,128)(2,1)S(1)}, bf16[128,2048]{1,0:T(8,128)(2,1)S(1)}, u32[]{:S(2)}, u32[]{:S(2)}) collective-permute-start(bf16[128,2048]{1,0:T(8,128)(2,1)S(1)} %collective-permute-done.6.m4), channel_id=1, source_target_pairs={{0,12},{1,13},{2,14},{3,15},{4,8},{5,9},{6,10},{7,11},{8,4},{9,5},... | collective-permute-start | bytes 1572872 | tf_op jit(solution)/shard_map/ppermute | solution.py:244
  26.5 3.0 %collective-permute-start.4 = (f32[128,128]{1,0:T(8,128)S(1)}, f32[128,128]{1,0:T(8,128)S(1)}, u32[]{:S(2)}, u32[]{:S(2)}) collective-permute-start(f32[128,128]{1,0:T(8,128)S(1)} %add.51), channel_id=1, source_target_pairs={{0,2},{1,3},{2,0},{3,1},{4,6},{5,7},{6,4},{7,5},{8,10},{9,11},{10,... | collective-permute-start | bytes 196616 | tf_op jit(solution)/shard_map/ppermute | solution.py:244
  29.5 5.3 %collective-permute-done.4 = f32[128,128]{1,0:T(8,128)S(1)} collective-permute-done((f32[128,128]{1,0:T(8,128)S(1)}, f32[128,128]{1,0:T(8,128)S(1)}, u32[]{:S(2)}, u32[]{:S(2)}) %collective-permute-start.4) | collective-permute-done | bytes 65568 | tf_op jit(solution)/shard_map/ppermute | solution.py:244
  34.8 2.9 %collective-permute-start.5 = (bf16[128,2048]{1,0:T(8,128)(2,1)}, bf16[128,2048]{1,0:T(8,128)(2,1)}, u32[]{:S(2)}, u32[]{:S(2)}) collective-permute-start(bf16[128,2048]{1,0:T(8,128)(2,1)} %slice.6), channel_id=1, source_target_pairs={{0,2},{1,3},{2,0},{3,1},{4,6},{5,7},{6,4},{7,5},{8,10},{9,11},{10,... | collective-permute-start | bytes 1572872 | tf_op jit(solution)/shard_map/ppermute | solution.py:244
  37.7 1.6 %collective-permute-start.8 = (bf16[128,2048]{1,0:T(8,128)(2,1)S(1)}, bf16[128,2048]{1,0:T(8,128)(2,1)}, u32[]{:S(2)}, u32[]{:S(2)}) collective-permute-start(bf16[128,2048]{1,0:T(8,128)(2,1)S(1)} %collective-permute-done.7.m4), channel_id=1, source_target_pairs={{0,12},{1,13},{2,14},{3,15},{4,8},{5,9},{6,10},{7,11},{8,4},{9,5},... | collective-permute-start | bytes 1572872 | tf_op jit(solution)/shard_map/ppermute | solution.py:244
  39.3 1.3 collective-permute-done.9
  40.5 0.6 add_convert_fusion.1.latent
  41.2 0.8 copy-done.9
  42.0 7.7 %main_part.2 = (bf16[128,2048]{1,0:T(8,128)(2,1)}, f32[128,128]{1,0:T(8,128)}, bf16[8,2,448,256]{3,2,1,0:T(8,128)(2,1)}) custom-call(bf16[128,4096]{1,0:T(8,128)(2,1)} %tok.5, bf16[128,4096]{1,0:T(8,128)(2,1)} %collective-permute-done.m1, bf16[128,2048]{1,0:T(8,128)(2,1)} %copy-done.7, bf16[128,2048]{1,0:T(8,128)(2,1)} %copy-done.5, ...), custom_call_target="tpu_custom_call" | custom-call | flops 2000000000 | bytes 29360128 | tf_op jit(solution)/shard_map/main_part/pallas_call | solution.py:89
  49.7 0.2 collective-permute-done.8.m8
  49.9 7.7 %main_part.3 = (bf16[128,2048]{1,0:T(8,128)(2,1)}, f32[128,128]{1,0:T(8,128)}, bf16[8,2,448,256]{3,2,1,0:T(8,128)(2,1)}) custom-call(bf16[128,4096]{1,0:T(8,128)(2,1)} %tok.5, bf16[128,4096]{1,0:T(8,128)(2,1)} %collective-permute-done.m1, bf16[128,2048]{1,0:T(8,128)(2,1)} %collective-permute-done.5.m2, ...), custom_call_target="tpu_custom_call", output_to_operand_aliasing={{2}: (10, {})} | custom-call | flops 2000000000 | bytes 29360128 | tf_op jit(solution)/shard_map/main_part/pallas_call | solution.py:89
  57.6 0.0 copy-start.13
  57.6 0.0 reduce-scatter.2.cloned.1.call-update
  57.7 0.8 copy-done.12
  58.5 0.0 copy-done.13
  58.5 2.1 %collective-permute-start.11 = (f32[128,128]{1,0:T(8,128)S(1)}, f32[128,128]{1,0:T(8,128)S(1)}, u32[]{:S(2)}, u32[]{:S(2)}) collective-permute-start(f32[128,128]{1,0:T(8,128)S(1)} %add.54), channel_id=1, source_target_pairs={{0,2},{1,3},{2,0},{3,1},{4,6},{5,7},{6,4},{7,5},{8,10},{9,11},{10,... | collective-permute-start | bytes 196616 | tf_op jit(solution)/shard_map/ppermute | solution.py:244
  60.6 1.6 %collective-permute-start.12 = (f32[128,128]{1,0:T(8,128)S(1)}, f32[128,128]{1,0:T(8,128)S(1)}, u32[]{:S(2)}, u32[]{:S(2)}) collective-permute-start(f32[128,128]{1,0:T(8,128)S(1)} %add.54), channel_id=1, source_target_pairs={{0,12},{1,13},{2,14},{3,15},{4,8},{5,9},{6,10},{7,11},{8,4},{9,5},... | collective-permute-start | bytes 196616 | tf_op jit(solution)/shard_map/ppermute | solution.py:244
  62.2 1.4 collective-permute-start.13
  63.6 6.4 %back_products.1 = (bf16[128,4096]{1,0:T(8,128)(2,1)}, bf16[128,2048]{1,0:T(8,128)(2,1)}, bf16[128,2048]{1,0:T(8,128)(2,1)}, bf16[128,2048]{1,0:T(8,128)(2,1)}, ...) custom-call(bf16[128,2048]{1,0:T(8,128)(2,1)} %get-tuple-element.46.low.slope, ...), custom_call_target="tpu_custom_call" | custom-call | flops 2000000000 | bytes 20971520 | tf_op jit(solution)/shard_map/back_products/pallas_call | solution.py:123
  70.0 2.1 %collective-permute-start.17 = (bf16[128,2048]{1,0:T(8,128)(2,1)}, bf16[128,2048]{1,0:T(8,128)(2,1)S(1)}, u32[]{:S(2)}, u32[]{:S(2)}) collective-permute-start(bf16[128,2048]{1,0:T(8,128)(2,1)} %get-tuple-element.52), channel_id=1, source_target_pairs={{0,2},{1,3},{2,0},{3,1},{4,6},{5,7},{6,4},{7,5},{8,10},{9,11},{10,... | collective-permute-start | bytes 1572872 | tf_op jit(solution)/shard_map/ppermute | solution.py:244
  72.1 3.1 %collective-permute-start.14 = (f32[128,128]{1,0:T(8,128)S(1)}, f32[128,128]{1,0:T(8,128)S(1)}, u32[]{:S(2)}, u32[]{:S(2)}) collective-permute-start(f32[128,128]{1,0:T(8,128)S(1)} %add.57), channel_id=1, source_target_pairs={{0,4},{1,5},{2,6},{3,7},{4,0},{5,1},{6,2},{7,3},{8,12},{9,13},{10,... | collective-permute-start | bytes 196616 | tf_op jit(solution)/shard_map/ppermute | solution.py:244
  75.2 0.1 collective-permute-start.16
  75.4 2.0 %collective-permute-start.22 = (bf16[128,2048]{1,0:T(8,128)(2,1)}, bf16[128,2048]{1,0:T(8,128)(2,1)S(1)}, u32[]{:S(2)}, u32[]{:S(2)}) collective-permute-start(bf16[128,2048]{1,0:T(8,128)(2,1)} %get-tuple-element.64), channel_id=1, source_target_pairs={{0,12},{1,13},{2,14},{3,15},{4,8},{5,9},{6,10},{7,11},{8,4},{9,5},... | collective-permute-start | bytes 1572872 | tf_op jit(solution)/shard_map/ppermute | solution.py:244
  77.3 0.2 collective-permute-done.14
  77.5 1.4 collective-permute-done.16
  79.0 5.9 %collective-permute-done.17.r2 = bf16[128,2048]{1,0:T(8,128)(2,1)S(1)} collective-permute-done((bf16[128,2048]{1,0:T(8,128)(2,1)}, bf16[128,2048]{1,0:T(8,128)(2,1)S(1)}, u32[]{:S(2)}, u32[]{:S(2)}) %collective-permute-start.17) | collective-permute-done | bytes 524320 | tf_op jit(solution)/shard_map/ppermute | solution.py:244
  84.9 0.7 add.60.lat
  85.5 0.2 copy-done.2
  85.7 2.0 %collective-permute-start.19 = (bf16[128,2048]{1,0:T(8,128)(2,1)}, bf16[128,2048]{1,0:T(8,128)(2,1)S(1)}, u32[]{:S(2)}, u32[]{:S(2)}) collective-permute-start(bf16[128,2048]{1,0:T(8,128)(2,1)} %get-tuple-element.56), channel_id=1, source_target_pairs={{0,2},{1,3},{2,0},{3,1},{4,6},{5,7},{6,4},{7,5},{8,10},{9,11},{10,... | collective-permute-start | bytes 1572872 | tf_op jit(solution)/shard_map/ppermute | solution.py:244
  87.7 2.8 %down_part.1 = (bf16[8,128,256]{2,1,0:T(8,128)(2,1)}, bf16[8,128,256]{2,1,0:T(8,128)(2,1)}) custom-call(s32[1]{0:T(128)} %bitcast.3.side, bf16[128,4096]{1,0:T(8,128)(2,1)} %tok.5, bf16[128,128]{1,0:T(8,128)(2,1)} %add.60.lat), custom_call_target="tpu_custom_call" | custom-call | flops 300000000 | bytes 10485760 | tf_op jit(solution)/shard_map/down_part/pallas_call | solution.py:149
  90.5 1.2 add.63
  91.6 3.2 %collective-permute-start.23 = (bf16[128,2048]{1,0:T(8,128)(2,1)S(1)}, bf16[128,2048]{1,0:T(8,128)(2,1)S(1)}, u32[]{:S(2)}, u32[]{:S(2)}) collective-permute-start(bf16[128,2048]{1,0:T(8,128)(2,1)S(1)} %add.63), channel_id=1, source_target_pairs={{0,4},{1,5},{2,6},{3,7},{4,0},{5,1},{6,2},{7,3},{8,12},{9,13},{10,... | collective-permute-start | bytes 1572872 | tf_op jit(solution)/shard_map/ppermute | solution.py:244
  94.8 1.1 collective-permute-start.20
  95.9 3.6 %collective-permute-done.19.r2 = bf16[128,2048]{1,0:T(8,128)(2,1)S(1)} collective-permute-done((bf16[128,2048]{1,0:T(8,128)(2,1)}, bf16[128,2048]{1,0:T(8,128)(2,1)S(1)}, u32[]{:S(2)}, u32[]{:S(2)}) %collective-permute-start.19) | collective-permute-done | bytes 524320 | tf_op jit(solution)/shard_map/ppermute | solution.py:244
  99.5 0.7 collective-permute-start.25
  100.2 7.2 %collective-permute-done.23.r48 = bf16[128,2048]{1,0:T(8,128)(2,1)S(1)} collective-permute-done((bf16[128,2048]{1,0:T(8,128)(2,1)S(1)}, bf16[128,2048]{1,0:T(8,128)(2,1)S(1)}, u32[]{:S(2)}, u32[]{:S(2)}) %collective-permute-start.23) | collective-permute-done | bytes 524320 | tf_op jit(solution)/shard_map/ppermute | solution.py:244
  107.4 1.7 %collective-permute-done.20 = bf16[128,2048]{1,0:T(8,128)(2,1)S(1)} collective-permute-done((bf16[128,2048]{1,0:T(8,128)(2,1)}, bf16[128,2048]{1,0:T(8,128)(2,1)S(1)}, u32[]{:S(2)}, u32[]{:S(2)}) %collective-permute-start.20) | collective-permute-done | bytes 524320 | tf_op jit(solution)/shard_map/ppermute | solution.py:244
  109.1 1.8 %collective-permute-done.25 = bf16[8,128,256]{2,1,0:T(8,128)(2,1)S(1)} collective-permute-done((bf16[8,128,256]{2,1,0:T(8,128)(2,1)}, bf16[8,128,256]{2,1,0:T(8,128)(2,1)S(1)}, u32[]{:S(2)}, u32[]{:S(2)}) %collective-permute-start.25) | collective-permute-done | bytes 524320 | tf_op jit(solution)/shard_map/ppermute | solution.py:261
  110.9 2.0 %add_convert_fusion = bf16[8,128,256]{2,1,0:T(8,128)(2,1)} fusion(bf16[8,128,256]{2,1,0:T(8,128)(2,1)S(1)} %collective-permute-done.25, bf16[8,128,256]{2,1,0:T(8,128)(2,1)} %get-tuple-element.70), kind=kLoop, calls=%fused_computation.1 | loop fusion | flops 1048576 | bytes 1572864 | tf_op jit(solution)/shard_map/convert_element_type | solution.py:301
  112.9 8.5 %all-to-all-start = ((bf16[8,128,256]{2,1,0:T(8,128)(2,1)}), bf16[8,128,256]{2,1,0:T(8,128)(2,1)S(1)}, u32[]{:S(2)}, u32[]{:S(2)}) async-start(bf16[8,128,256]{2,1,0:T(8,128)(2,1)} %add_convert_fusion), calls=%async_computation.1 | async-start | bytes 1048576 | tf_op jit(solution)/shard_map/all_to_all | solution.py:303
  121.4 2.0 %add.61 = bf16[128,2048]{1,0:T(8,128)(2,1)} add(bf16[128,2048]{1,0:T(8,128)(2,1)S(1)} %copy-done.3, bf16[128,2048]{1,0:T(8,128)(2,1)} %copy-done.10) | non-fusion elementwise | flops 262144 | bytes 1572864 | tf_op jit(solution)/shard_map/add | solution.py:304
  123.3 2.0 %collective-permute-start.21 = (bf16[128,2048]{1,0:T(8,128)(2,1)}, bf16[128,2048]{1,0:T(8,128)(2,1)}, u32[]{:S(2)}, u32[]{:S(2)}) collective-permute-start(bf16[128,2048]{1,0:T(8,128)(2,1)} %add.61), channel_id=1, source_target_pairs={{0,4},{1,5},{2,6},{3,7},{4,0},{5,1},{6,2},{7,3},{8,12},{9,13},{10,... | collective-permute-start | bytes 1572872 | tf_op jit(solution)/shard_map/ppermute | solution.py:244
  125.3 1.0 dynamic-slice_bitcast_fusion
  126.3 1.7 %collective-permute-start.24 = (bf16[448,256]{1,0:T(8,128)(2,1)S(1)}, bf16[448,256]{1,0:T(8,128)(2,1)S(1)}, u32[]{:S(2)}, u32[]{:S(2)}) collective-permute-start(bf16[448,256]{1,0:T(8,128)(2,1)S(1)} %dynamic-slice_bitcast_fusion), channel_id=1, source_target_pairs={{0,128},{16,144},{32,160},{48,176},{64,192},{80,208},{96,224},{112... | collective-permute-start | bytes 688136 | tf_op jit(solution)/shard_map/ppermute | solution.py:261
  128.0 7.8 %collective-permute-done.21.r48 = bf16[128,2048]{1,0:T(8,128)(2,1)} collective-permute-done((bf16[128,2048]{1,0:T(8,128)(2,1)}, bf16[128,2048]{1,0:T(8,128)(2,1)}, u32[]{:S(2)}, u32[]{:S(2)}) %collective-permute-start.21) | collective-permute-done | bytes 524320 | tf_op jit(solution)/shard_map/ppermute | solution.py:244
  135.7 3.1 %token_grad.2.refs_0_ = bf16[128,4096]{1,0:T(8,128)(2,1)} custom-call(bf16[128,2048]{1,0:T(8,128)(2,1)} %get-tuple-element.46.low.slope, bf16[128,4096]{1,0:T(8,128)(2,1)} %copy-done.1, bf16[128,2048]{1,0:T(8,128)(2,1)} %copy-done.2, bf16[128,2048]{1,0:T(8,128)(2,1)} %copy-done.6, bf16[64,4096]{1,0:T(8,128)(2,1)} %diag.7, bf16[4096,128]{1,0:T(8,128)(2,1)} %down.3, ...), custom_call_target="tpu_custom_call" | custom-call | flops 1000000000 | bytes 9437184 | tf_op jit(solution)/shard_map/token_grad/pallas_call | solution.py:194
  138.8 3.0 %token_grad.3 = bf16[128,4096]{1,0:T(8,128)(2,1)} custom-call(bf16[128,2048]{1,0:T(8,128)(2,1)} %get-tuple-element.45.high.slope, bf16[128,4096]{1,0:T(8,128)(2,1)} %copy-done.1, bf16[128,2048]{1,0:T(8,128)(2,1)} %copy-done.4, bf16[128,2048]{1,0:T(8,128)(2,1)} %collective-permute-done.21.r48, bf16[64,4096]{1,0:T(8,128)(2,1)} %diag.7, ...), custom_call_target="tpu_custom_call", output_to_operand_aliasing={{}: (7, {})} | custom-call | flops 1000000000 | bytes 9437184 | tf_op jit(solution)/shard_map/token_grad/pallas_call | solution.py:194
  141.8 0.1 convert_reduce_fusion
  141.9 0.8 copy.13
  142.7 1.8 %finish.1 = (f32[64,256]{1,0:T(8,128)}, f32[4,64,256]{2,1,0:T(8,128)}, f32[128,256]{1,0:T(8,128)}) custom-call(s32[1]{0:T(128)} %bitcast.3.side, bf16[2,448,256]{2,1,0:T(8,128)(2,1)} %bitcast.11, bf16[448,256]{1,0:T(8,128)(2,1)} %copy-done.11), custom_call_target="tpu_custom_call" | custom-call | flops 300000 | bytes 4194304 | tf_op jit(solution)/shard_map/finish/pallas_call | solution.py:218
  (47 shorter events, 0.2 us)
Async XLA Ops:
  7.2 14.2 %copy-start = (bf16[128,4096]{1,0:T(8,128)(2,1)S(1)}, bf16[128,4096]{1,0:T(8,128)(2,1)}, u32[]{:S(2)}) copy-start(bf16[128,4096]{1,0:T(8,128)(2,1)} %tok.5) | copy-start | bytes 3145732
  7.2 118.1 %reduce-scatter.2.cloned.1.call-start = ((), (), s32[]{:S(2)}) async-start(), calls=%async_computation.2 | async-start | bytes 4128768 | tf_op jit(solution)/shard_map/reduce_scatter | solution.py:254
  8.4 15.2 %collective-permute-start.6 = (bf16[128,2048]{1,0:T(8,128)(2,1)S(1)}, bf16[128,2048]{1,0:T(8,128)(2,1)S(1)}, u32[]{:S(2)}, u32[]{:S(2)}) collective-permute-start(bf16[128,2048]{1,0:T(8,128)(2,1)S(1)} %slice.7), channel_id=1, source_target_pairs={{0,4},{1,5},{2,6},{3,7},{4,0},{5,1},{6,2},{7,3},{8,12},{9,13},{10,... | collective-permute-start | bytes 1572872 | tf_op jit(solution)/shard_map/ppermute | solution.py:244
  10.7 30.5 %collective-permute-start = (bf16[128,4096]{1,0:T(8,128)(2,1)}, bf16[128,4096]{1,0:T(8,128)(2,1)}, u32[]{:S(2)}, u32[]{:S(2)}) collective-permute-start(bf16[128,4096]{1,0:T(8,128)(2,1)} %tok.5), channel_id=1, source_target_pairs={{0,1},{1,0},{2,3},{3,2},{4,5},{5,4},{6,7},{7,6},{8,9},{9,8},{10,11... | collective-permute-start | bytes 3145736 | tf_op jit(solution)/shard_map/ppermute | solution.py:244
  12.6 4.6 %collective-permute-start.1 = (f32[128,128]{1,0:T(8,128)S(1)}, f32[128,128]{1,0:T(8,128)S(1)}, u32[]{:S(2)}, u32[]{:S(2)}) collective-permute-start(f32[128,128]{1,0:T(8,128)S(1)} %fusion), channel_id=1, source_target_pairs={{0,12},{1,13},{2,14},{3,15},{4,8},{5,9},{6,10},{7,11},{8,4},{9,5},... | collective-permute-start | bytes 196616 | tf_op jit(solution)/shard_map/ppermute | solution.py:244
  17.2 6.3 %collective-permute-start.3 = (f32[128,128]{1,0:T(8,128)S(1)}, f32[128,128]{1,0:T(8,128)S(1)}, u32[]{:S(2)}, u32[]{:S(2)}) collective-permute-start(f32[128,128]{1,0:T(8,128)S(1)} %add.50), channel_id=1, source_target_pairs={{0,4},{1,5},{2,6},{3,7},{4,0},{5,1},{6,2},{7,3},{8,12},{9,13},{10,... | collective-permute-start | bytes 196616 | tf_op jit(solution)/shard_map/ppermute | solution.py:244
  18.6 16.2 %collective-permute-start.2 = (bf16[128,2048]{1,0:T(8,128)(2,1)S(1)}, bf16[128,2048]{1,0:T(8,128)(2,1)S(1)}, u32[]{:S(2)}, u32[]{:S(2)}) collective-permute-start(bf16[128,2048]{1,0:T(8,128)(2,1)S(1)} %slice.7), channel_id=1, source_target_pairs={{0,2},{1,3},{2,0},{3,1},{4,6},{5,7},{6,4},{7,5},{8,10},{9,11},{10,... | collective-permute-start | bytes 1572872 | tf_op jit(solution)/shard_map/ppermute | solution.py:244
  23.6 17.6 %copy-start.5 = (bf16[128,2048]{1,0:T(8,128)(2,1)}, bf16[128,2048]{1,0:T(8,128)(2,1)S(1)}, u32[]{:S(2)}) copy-start(bf16[128,2048]{1,0:T(8,128)(2,1)S(1)} %collective-permute-done.6.m4) | copy-start | bytes 1572868
  23.6 14.1 %collective-permute-start.7 = (bf16[128,2048]{1,0:T(8,128)(2,1)}, bf16[128,2048]{1,0:T(8,128)(2,1)S(1)}, u32[]{:S(2)}, u32[]{:S(2)}) collective-permute-start(bf16[128,2048]{1,0:T(8,128)(2,1)} %slice.6), channel_id=1, source_target_pairs={{0,4},{1,5},{2,6},{3,7},{4,0},{5,1},{6,2},{7,3},{8,12},{9,13},{10,... | collective-permute-start | bytes 1572872 | tf_op jit(solution)/shard_map/ppermute | solution.py:244
  23.9 17.2 %collective-permute-start.10 = (bf16[128,2048]{1,0:T(8,128)(2,1)S(1)}, bf16[128,2048]{1,0:T(8,128)(2,1)S(1)}, u32[]{:S(2)}, u32[]{:S(2)}) collective-permute-start(bf16[128,2048]{1,0:T(8,128)(2,1)S(1)} %collective-permute-done.6.m4), channel_id=1, source_target_pairs={{0,12},{1,13},{2,14},{3,15},{4,8},{5,9},{6,10},{7,11},{8,4},{9,5},... | collective-permute-start | bytes 1572872 | tf_op jit(solution)/shard_map/ppermute | solution.py:244
  26.5 8.3 %collective-permute-start.4 = (f32[128,128]{1,0:T(8,128)S(1)}, f32[128,128]{1,0:T(8,128)S(1)}, u32[]{:S(2)}, u32[]{:S(2)}) collective-permute-start(f32[128,128]{1,0:T(8,128)S(1)} %add.51), channel_id=1, source_target_pairs={{0,2},{1,3},{2,0},{3,1},{4,6},{5,7},{6,4},{7,5},{8,10},{9,11},{10,... | collective-permute-start | bytes 196616 | tf_op jit(solution)/shard_map/ppermute | solution.py:244
  34.8 6.3 %copy-start.7 = (bf16[128,2048]{1,0:T(8,128)(2,1)}, bf16[128,2048]{1,0:T(8,128)(2,1)S(1)}, u32[]{:S(2)}) copy-start(bf16[128,2048]{1,0:T(8,128)(2,1)S(1)} %collective-permute-done.2.m2) | copy-start | bytes 1572868
  34.8 14.9 %collective-permute-start.5 = (bf16[128,2048]{1,0:T(8,128)(2,1)}, bf16[128,2048]{1,0:T(8,128)(2,1)}, u32[]{:S(2)}, u32[]{:S(2)}) collective-permute-start(bf16[128,2048]{1,0:T(8,128)(2,1)} %slice.6), channel_id=1, source_target_pairs={{0,2},{1,3},{2,0},{3,1},{4,6},{5,7},{6,4},{7,5},{8,10},{9,11},{10,... | collective-permute-start | bytes 1572872 | tf_op jit(solution)/shard_map/ppermute | solution.py:244
  37.7 12.0 %copy-start.8 = (bf16[128,2048]{1,0:T(8,128)(2,1)}, bf16[128,2048]{1,0:T(8,128)(2,1)S(1)}, u32[]{:S(2)}) copy-start(bf16[128,2048]{1,0:T(8,128)(2,1)S(1)} %collective-permute-done.7.m4) | copy-start | bytes 1572868
  37.7 12.2 %collective-permute-start.8 = (bf16[128,2048]{1,0:T(8,128)(2,1)S(1)}, bf16[128,2048]{1,0:T(8,128)(2,1)}, u32[]{:S(2)}, u32[]{:S(2)}) collective-permute-start(bf16[128,2048]{1,0:T(8,128)(2,1)S(1)} %collective-permute-done.7.m4), channel_id=1, source_target_pairs={{0,12},{1,13},{2,14},{3,15},{4,8},{5,9},{6,10},{7,11},{8,4},{9,5},... | collective-permute-start | bytes 1572872 | tf_op jit(solution)/shard_map/ppermute | solution.py:244
  39.3 1.3 collective-permute-start.9
  41.2 0.8 copy-start.9
  57.6 0.8 copy-start.12
  57.6 0.9 copy-start.13
  58.5 11.5 %collective-permute-start.11 = (f32[128,128]{1,0:T(8,128)S(1)}, f32[128,128]{1,0:T(8,128)S(1)}, u32[]{:S(2)}, u32[]{:S(2)}) collective-permute-start(f32[128,128]{1,0:T(8,128)S(1)} %add.54), channel_id=1, source_target_pairs={{0,2},{1,3},{2,0},{3,1},{4,6},{5,7},{6,4},{7,5},{8,10},{9,11},{10,... | collective-permute-start | bytes 196616 | tf_op jit(solution)/shard_map/ppermute | solution.py:244
  60.6 9.4 %collective-permute-start.12 = (f32[128,128]{1,0:T(8,128)S(1)}, f32[128,128]{1,0:T(8,128)S(1)}, u32[]{:S(2)}, u32[]{:S(2)}) collective-permute-start(f32[128,128]{1,0:T(8,128)S(1)} %add.54), channel_id=1, source_target_pairs={{0,12},{1,13},{2,14},{3,15},{4,8},{5,9},{6,10},{7,11},{8,4},{9,5},... | collective-permute-start | bytes 196616 | tf_op jit(solution)/shard_map/ppermute | solution.py:244
  62.2 7.8 %collective-permute-start.13 = (f32[128,128]{1,0:T(8,128)S(1)}, f32[128,128]{1,0:T(8,128)S(1)}, u32[]{:S(2)}, u32[]{:S(2)}) collective-permute-start(f32[128,128]{1,0:T(8,128)S(1)} %add.54), channel_id=1, source_target_pairs={{0,14},{1,15},{2,12},{3,13},{4,10},{5,11},{6,8},{7,9},{8,6},{9,7},... | collective-permute-start | bytes 196616 | tf_op jit(solution)/shard_map/ppermute | solution.py:244
  70.0 51.4 %copy-start.3 = (bf16[128,2048]{1,0:T(8,128)(2,1)S(1)}, bf16[128,2048]{1,0:T(8,128)(2,1)}, u32[]{:S(2)}) copy-start(bf16[128,2048]{1,0:T(8,128)(2,1)} %get-tuple-element.57) | copy-start | bytes 1572868
  70.0 14.8 %collective-permute-start.17 = (bf16[128,2048]{1,0:T(8,128)(2,1)}, bf16[128,2048]{1,0:T(8,128)(2,1)S(1)}, u32[]{:S(2)}, u32[]{:S(2)}) collective-permute-start(bf16[128,2048]{1,0:T(8,128)(2,1)} %get-tuple-element.52), channel_id=1, source_target_pairs={{0,2},{1,3},{2,0},{3,1},{4,6},{5,7},{6,4},{7,5},{8,10},{9,11},{10,... | collective-permute-start | bytes 1572872 | tf_op jit(solution)/shard_map/ppermute | solution.py:244
  72.1 5.4 %collective-permute-start.14 = (f32[128,128]{1,0:T(8,128)S(1)}, f32[128,128]{1,0:T(8,128)S(1)}, u32[]{:S(2)}, u32[]{:S(2)}) collective-permute-start(f32[128,128]{1,0:T(8,128)S(1)} %add.57), channel_id=1, source_target_pairs={{0,4},{1,5},{2,6},{3,7},{4,0},{5,1},{6,2},{7,3},{8,12},{9,13},{10,... | collective-permute-start | bytes 196616 | tf_op jit(solution)/shard_map/ppermute | solution.py:244
  75.2 2.3 %collective-permute-start.15 = (f32[128,128]{1,0:T(8,128)S(1)}, f32[128,128]{1,0:T(8,128)S(1)}, u32[]{:S(2)}, u32[]{:S(2)}) collective-permute-start(f32[128,128]{1,0:T(8,128)S(1)} %add.57), channel_id=1, source_target_pairs={{0,1},{1,0},{2,3},{3,2},{4,5},{5,4},{6,7},{7,6},{8,9},{9,8},{10,11... | collective-permute-start | bytes 196616 | tf_op jit(solution)/shard_map/ppermute | solution.py:244
  75.2 3.7 %collective-permute-start.16 = (f32[128,128]{1,0:T(8,128)S(1)}, f32[128,128]{1,0:T(8,128)S(1)}, u32[]{:S(2)}, u32[]{:S(2)}) collective-permute-start(f32[128,128]{1,0:T(8,128)S(1)} %add.57), channel_id=1, source_target_pairs={{0,5},{1,4},{2,7},{3,6},{4,1},{5,0},{6,3},{7,2},{8,13},{9,12},{10,... | collective-permute-start | bytes 196616 | tf_op jit(solution)/shard_map/ppermute | solution.py:244
  75.4 15.1 %collective-permute-start.22 = (bf16[128,2048]{1,0:T(8,128)(2,1)}, bf16[128,2048]{1,0:T(8,128)(2,1)S(1)}, u32[]{:S(2)}, u32[]{:S(2)}) collective-permute-start(bf16[128,2048]{1,0:T(8,128)(2,1)} %get-tuple-element.64), channel_id=1, source_target_pairs={{0,12},{1,13},{2,14},{3,15},{4,8},{5,9},{6,10},{7,11},{8,4},{9,5},... | collective-permute-start | bytes 1572872 | tf_op jit(solution)/shard_map/ppermute | solution.py:244
  84.9 0.8 copy-start.2
  85.7 13.8 %collective-permute-start.19 = (bf16[128,2048]{1,0:T(8,128)(2,1)}, bf16[128,2048]{1,0:T(8,128)(2,1)S(1)}, u32[]{:S(2)}, u32[]{:S(2)}) collective-permute-start(bf16[128,2048]{1,0:T(8,128)(2,1)} %get-tuple-element.56), channel_id=1, source_target_pairs={{0,2},{1,3},{2,0},{3,1},{4,6},{5,7},{6,4},{7,5},{8,10},{9,11},{10,... | collective-permute-start | bytes 1572872 | tf_op jit(solution)/shard_map/ppermute | solution.py:244
  87.7 21.4 %collective-permute-start.18 = (bf16[128,4096]{1,0:T(8,128)(2,1)}, bf16[128,4096]{1,0:T(8,128)(2,1)S(1)}, u32[]{:S(2)}, u32[]{:S(2)}) collective-permute-start(bf16[128,4096]{1,0:T(8,128)(2,1)} %get-tuple-element.54), channel_id=1, source_target_pairs={{0,1},{1,0},{2,3},{3,2},{4,5},{5,4},{6,7},{7,6},{8,9},{9,8},{10,11... | collective-permute-start | bytes 3145736 | tf_op jit(solution)/shard_map/ppermute | solution.py:244
  91.6 15.8 %collective-permute-start.23 = (bf16[128,2048]{1,0:T(8,128)(2,1)S(1)}, bf16[128,2048]{1,0:T(8,128)(2,1)S(1)}, u32[]{:S(2)}, u32[]{:S(2)}) collective-permute-start(bf16[128,2048]{1,0:T(8,128)(2,1)S(1)} %add.63), channel_id=1, source_target_pairs={{0,4},{1,5},{2,6},{3,7},{4,0},{5,1},{6,2},{7,3},{8,12},{9,13},{10,... | collective-permute-start | bytes 1572872 | tf_op jit(solution)/shard_map/ppermute | solution.py:244
  94.8 14.3 %collective-permute-start.20 = (bf16[128,2048]{1,0:T(8,128)(2,1)}, bf16[128,2048]{1,0:T(8,128)(2,1)S(1)}, u32[]{:S(2)}, u32[]{:S(2)}) collective-permute-start(bf16[128,2048]{1,0:T(8,128)(2,1)} %get-tuple-element.59), channel_id=1, source_target_pairs={{0,12},{1,13},{2,14},{3,15},{4,8},{5,9},{6,10},{7,11},{8,4},{9,5},... | collective-permute-start | bytes 1572872 | tf_op jit(solution)/shard_map/ppermute | solution.py:244
  99.5 23.8 %copy-start.4 = (bf16[128,2048]{1,0:T(8,128)(2,1)}, bf16[128,2048]{1,0:T(8,128)(2,1)S(1)}, u32[]{:S(2)}) copy-start(bf16[128,2048]{1,0:T(8,128)(2,1)S(1)} %collective-permute-done.19.r2) | copy-start | bytes 1572868
  99.5 11.4 %collective-permute-start.25 = (bf16[8,128,256]{2,1,0:T(8,128)(2,1)}, bf16[8,128,256]{2,1,0:T(8,128)(2,1)S(1)}, u32[]{:S(2)}, u32[]{:S(2)}) collective-permute-start(bf16[8,128,256]{2,1,0:T(8,128)(2,1)} %get-tuple-element.71), channel_id=1, source_target_pairs={{0,128},{16,144},{32,160},{48,176},{64,192},{80,208},{96,224},{112... | collective-permute-start | bytes 1572872 | tf_op jit(solution)/shard_map/ppermute | solution.py:261
  107.4 1.7 %copy-start.6 = (bf16[128,2048]{1,0:T(8,128)(2,1)}, bf16[128,2048]{1,0:T(8,128)(2,1)S(1)}, u32[]{:S(2)}) copy-start(bf16[128,2048]{1,0:T(8,128)(2,1)S(1)} %collective-permute-done.23.r48) | copy-start | bytes 1572868
  109.1 1.8 %copy-start.10 = (bf16[128,2048]{1,0:T(8,128)(2,1)}, bf16[128,2048]{1,0:T(8,128)(2,1)S(1)}, u32[]{:S(2)}) copy-start(bf16[128,2048]{1,0:T(8,128)(2,1)S(1)} %collective-permute-done.20) | copy-start | bytes 1572868
  109.1 26.6 %copy-start.1 = (bf16[128,4096]{1,0:T(8,128)(2,1)}, bf16[128,4096]{1,0:T(8,128)(2,1)S(1)}, u32[]{:S(2)}) copy-start(bf16[128,4096]{1,0:T(8,128)(2,1)S(1)} %collective-permute-done.18.r1) | copy-start | bytes 3145732
  112.9 28.9 %all-to-all-start = ((bf16[8,128,256]{2,1,0:T(8,128)(2,1)}), bf16[8,128,256]{2,1,0:T(8,128)(2,1)S(1)}, u32[]{:S(2)}, u32[]{:S(2)}) async-start(bf16[8,128,256]{2,1,0:T(8,128)(2,1)} %add_convert_fusion), calls=%async_computation.1 | async-start | bytes 1048576 | tf_op jit(solution)/shard_map/all_to_all | solution.py:303
  123.3 12.4 %collective-permute-start.21 = (bf16[128,2048]{1,0:T(8,128)(2,1)}, bf16[128,2048]{1,0:T(8,128)(2,1)}, u32[]{:S(2)}, u32[]{:S(2)}) collective-permute-start(bf16[128,2048]{1,0:T(8,128)(2,1)} %add.61), channel_id=1, source_target_pairs={{0,4},{1,5},{2,6},{3,7},{4,0},{5,1},{6,2},{7,3},{8,12},{9,13},{10,... | collective-permute-start | bytes 1572872 | tf_op jit(solution)/shard_map/ppermute | solution.py:244
  126.3 15.5 %collective-permute-start.24 = (bf16[448,256]{1,0:T(8,128)(2,1)S(1)}, bf16[448,256]{1,0:T(8,128)(2,1)S(1)}, u32[]{:S(2)}, u32[]{:S(2)}) collective-permute-start(bf16[448,256]{1,0:T(8,128)(2,1)S(1)} %dynamic-slice_bitcast_fusion), channel_id=1, source_target_pairs={{0,128},{16,144},{32,160},{48,176},{64,192},{80,208},{96,224},{112... | collective-permute-start | bytes 688136 | tf_op jit(solution)/shard_map/ppermute | solution.py:261
  141.8 0.9 copy-start.11
Sparse Core Ops, SparseCore 0:
  57.8 53.0 reduce-scatter.1

commit v7 on v4

--- a/solution.py
+++ b/solution.py
@@ -145,35 +145,35 @@
     )(*slopes, section)
 
 
-def down_kernel(side, tok, lat, keep, send):
-    def fill(out):
-        for c in range(tok.shape[1] // CHUNK):
-            out[c] = dot(lat[...], tok[:, c * CHUNK : (c + 1) * CHUNK], 0, 0).astype(BF16)
-
-    pl.when(pl.program_id(0) == 0)(lambda: fill(send))
-    pl.when(pl.program_id(0) == 1)(lambda: fill(keep))
-
-
-def run_down(x, tokens, latent_grad):
-    rows, width = tokens.shape
+def down_kernel(side, tok, others, lat, lat_others, out):
+    both = jnp.concatenate([lat[...], lat_others[...]], axis=0)
+    for c in range(tok.shape[1] // CHUNK):
+        cs = slice(c * CHUNK, (c + 1) * CHUNK)
+        out[c] = dot(both, jnp.concatenate([tok[:, cs], others[:, cs]], axis=0), 0, 0).astype(BF16)
+
+
+def run_down(x, tokens, others, latent_grad, latent_others):
+    rows, half = others.shape
     rank = latent_grad.shape[1]
-    half = width // 2
-    block = pl.BlockSpec((RING, rank, CHUNK), lambda i, side: (0, 0, 0))
+    step = half // 2
+    square = pl.BlockSpec((rows, rank), lambda i, side: (0, 0))
     return pl.pallas_call(
         down_kernel,
         grid_spec=pltpu.PrefetchScalarGridSpec(
             num_scalar_prefetch=1,
             grid=(2,),
             in_specs=[
-                pl.BlockSpec((rows, half), lambda i, side: (0, (1 + i + side[0]) % 2)),
-                pl.BlockSpec((rows, rank), lambda i, side: (0, 0)),
+                pl.BlockSpec((rows, step), lambda i, side: (0, 2 * side[0] + i)),
+                pl.BlockSpec((rows, step), lambda i, side: (0, i)),
+                square,
+                square,
             ],
-            out_specs=[block, block],
+            out_specs=pl.BlockSpec((RING // 2, rank, CHUNK), lambda i, side: (i, 0, 0)),
         ),
-        out_shape=[jax.ShapeDtypeStruct((RING, rank, CHUNK), BF16)] * 2,
+        out_shape=jax.ShapeDtypeStruct((RING, rank, CHUNK), BF16),
         cost_estimate=pl.CostEstimate(flops=300_000_000, bytes_accessed=10 << 20, transcendentals=0),
         name="down_part",
-    )(jnp.full((1,), x, jnp.int32), tokens, latent_grad)
+    )(jnp.full((1,), x, jnp.int32), tokens, others, latent_grad, latent_others)
 
 
 def final_kernel(*refs):
@@ -285,11 +285,12 @@
     part = part + flip(part, 4)
     m8_0 = flip(after(m4_0, part), 12)
     m4_1 = flip(after(h1, m4_0, part), 4)
-    part = part + flip(part, 1)
     part = part + flip(part, 2)
     m2_1 = flip(after(h1, m2_0, part), 2)
-    m8_1 = flip(after(m4_1, part), 12)
+    m8_1 = flip(m4_1, 12)
+    part = part + flip(part, 1)
     latent = part.astype(BF16)
+    others = cross(lax.dynamic_slice_in_dim(after(tokens, m2_1), (1 - x) * half, half, axis=1))
 
     factors = (cotangent, diag_factor, section_factors, latent, low_up)
     slope0, lat0, grads = run_main(0, tokens, (m1, m2_0, m4_0, m8_0), *factors, None)
@@ -297,26 +298,27 @@
     summed = ring_sum(grads)
 
     part = lat0 + lat1
-    arrived = flip(part, 2)
+    arrived = flip(part, 12)
     b1, b2_0, b2_1, b4_0, b4_1, b8_0, b8_1 = run_back((slope0, slope1), section_factors)
-    part = part + after(arrived, b1)
+    part = part + after(arrived, b1, others)
+    q0, q1 = flip(after(b8_0, part), 12), flip(after(b8_1, part), 12)
+    part = part + flip(part, 2)
     r2_0, r1 = flip(after(b2_0, part), 2), flip(after(b1, part), 1)
-    part = part + flip(part, 12)
-    q0, q1 = flip(after(b8_0, part), 12), flip(after(b8_1, part), 12)
     part = part + flip(part, 4)
-    part = part + after(flip(part, 1), r2_0, r1)
+    part = part + after(flip(part, 1), r1)
     latent_grad = part.astype(BF16)
 
-    keep, send = run_down(x, tokens, latent_grad)
-    s0 = flip(b4_0 + after(q0, send), 4)
-    pair = (keep.astype(F32) + after(cross(send), q1, s0).astype(F32)).astype(BF16)
-    r2_1 = flip(after(b2_1, send), 2)
+    pair = run_down(x, tokens, others, latent_grad, after(cross(latent_grad), r2_0))
+    s0 = flip(b4_0 + after(q0, pair), 4)
+    r2_1 = flip(after(b2_1, pair), 2)
+    pair = after(pair, q0)
     groups = [[side * RING + z for z in range(RING)] for side in range(2)]
     pair = lax.all_to_all(pair, "dp", 0, 0, axis_index_groups=groups, tiled=True)
     s1 = flip(b4_1 + q1, 4)
-    arrived = cross(lax.dynamic_index_in_dim(summed, 1 - x, 0, keepdims=False))
+    other = lax.dynamic_index_in_dim(summed, 1 - x, 0, keepdims=False)
+    arrived = cross(other)
     down_grad = (jnp.sum(after(pair, arrived).astype(F32), axis=0) * scale).T
-    pairs = ((slope0, slope1), (r2_0, r2_1), (s0, after(s1, arrived)))
+    pairs = ((slope0, slope1), (r2_0, r2_1), (s0, after(s1, other)))
     token_grad = run_final(pairs, r1, diag_factor, low_down, latent_grad)
     diag_grad, section_grad, up_grad = run_finish(x, summed, arrived, scale)
     return token_grad, diag_grad, section_grad, down_grad, up_grad

time: 145 us -> 150 us (1.034)
  waiting for transfers between devices: 40.8 us -> 49 us
  other arithmetic: 4.7 us -> 1.83 us
  starting transfers between devices: 45.3 us -> 42.7 us
  local copies, waits for them, and re-layouts: 6.07 us -> 7.98 us
    ppermute x22, waiting for transfers between devices: 32.9 us -> 43.9 us  [flip(): return lax.ppermute(value, 'tensor', [(i, i ^ mask) for i in range(16)])]
    ppermute x22, starting transfers between devices: 36.1 us -> 32.1 us  [flip(): return lax.ppermute(value, 'tensor', [(i, i ^ mask) for i in range(16)])]
    unnamed x27 -> x37, local copies, waits for them, and re-layouts: 3.14 us -> 4.99 us
    ppermute x2 -> x3, waiting for transfers between devices: 6.53 us -> 5.05 us  [cross(): return lax.ppermute(value, 'dp', [(i, i ^ RING) for i in range(2 * RING)])]
  transfers between devices with their start and end apart: 26 -> 27, of which waited for: 17 -> 11; matrix products, arithmetic and copies ran while one was open for 6% -> 4% of each run, Pallas kernels for 13% -> 14%
where the time goes in v7:
time: 150 us; the launch traced here: 148 us
  waiting for transfers between devices  49 us (33%)
  starting transfers between devices  42.7 us (28%)
  Pallas kernels  30.6 us (20%)
  between operations  14.3 us (10%)
  local copies, waits for them, and re-layouts  7.98 us (5%)
  matrix products  1.96 us (1%)
  other arithmetic  1.83 us (1%)
    ppermute x22, waiting for transfers between devices, flip(): return lax.ppermute(value, 'tensor', [(i, i ^ mask) for i in range(16)])  43.9 us
    ppermute x22, starting transfers between devices, flip(): return lax.ppermute(value, 'tensor', [(i, i ^ mask) for i in range(16)])  32.1 us
    pallas_call x2, Pallas kernels, run_main(): pl.pallas_call(main_kernel, grid=(steps,), in_specs=in_specs, out_specs=[...  15.5 us
    all_to_all x1, starting transfers between devices, per_device(): lax.all_to_all(pair, 'dp', 0, 0, axis_index_groups=groups, tiled=True)  8.47 us
    pallas_call x1, Pallas kernels, run_back(): pl.pallas_call(back_kernel, grid=(2,), in_specs=[fixed, fixed, pl.BlockSp...  6.38 us
    ppermute x3, waiting for transfers between devices, cross(): return lax.ppermute(value, 'dp', [(i, i ^ RING) for i in range(2 * RING)])  5.05 us
    unnamed x37, local copies, waits for them, and re-layouts  4.99 us
    pallas_call x1, Pallas kernels, run_final(): pl.pallas_call(final_kernel, grid=(steps,), in_specs=half_specs(rows, ste...  4.57 us
  transfers between devices with their start and end apart: 27, of which 11 were waited for; matrix products, arithmetic and copies ran while one was open for 4% of the time, Pallas kernels for 14%

profile of v7, /device:TPU:8, one launch (start us, length us, event | category | flops | bytes accessed | tf_op | source)
XLA Modules:
  0.0 148.3 jit_solution(16905219280875298912)
XLA Ops:
  7.2 0.0 copy-start
  7.2 0.0 reduce-scatter.2.cloned.1.call-start
  7.2 1.2 slice.6
  8.4 2.3 %collective-permute-start.2 = (bf16[128,2048]{1,0:T(8,128)(2,1)S(1)}, bf16[128,2048]{1,0:T(8,128)(2,1)S(1)}, u32[]{:S(2)}, u32[]{:S(2)}) collective-permute-start(bf16[128,2048]{1,0:T(8,128)(2,1)S(1)} %slice.6), channel_id=1, source_target_pairs={{0,4},{1,5},{2,6},{3,7},{4,0},{5,1},{6,2},{7,3},{8,12},{9,13},{10,... | collective-permute-start | bytes 1572872 | tf_op jit(solution)/shard_map/ppermute | solution.py:253
  10.7 0.0 collective-permute-start
  10.7 2.0 %fusion = f32[128,128]{1,0:T(8,128)S(1)} fusion(bf16[128,4096]{1,0:T(8,128)(2,1)} %tok.5, bf16[4096,128]{1,0:T(8,128)(2,1)} %refs_8_.1), kind=kOutput, calls=%fused_computation.6 | convolution fusion | flops 134217728 | bytes 2162688 | tf_op jit(solution)/shard_map/dot_general | solution.py:282
  12.6 0.8 collective-permute-start.3
  13.4 3.8 %collective-permute-done.3 = f32[128,128]{1,0:T(8,128)S(1)} collective-permute-done((f32[128,128]{1,0:T(8,128)S(1)}, f32[128,128]{1,0:T(8,128)S(1)}, u32[]{:S(2)}, u32[]{:S(2)}) %collective-permute-start.3) | collective-permute-done | bytes 65568 | tf_op jit(solution)/shard_map/ppermute | solution.py:253
  17.2 1.4 collective-permute-start.4
  18.6 2.8 %collective-permute-start.1 = (bf16[128,2048]{1,0:T(8,128)(2,1)S(1)}, bf16[128,2048]{1,0:T(8,128)(2,1)S(1)}, u32[]{:S(2)}, u32[]{:S(2)}) collective-permute-start(bf16[128,2048]{1,0:T(8,128)(2,1)S(1)} %slice.6), channel_id=1, source_target_pairs={{0,2},{1,3},{2,0},{3,1},{4,6},{5,7},{6,4},{7,5},{8,10},{9,11},{10,... | collective-permute-start | bytes 1572872 | tf_op jit(solution)/shard_map/ppermute | solution.py:253
  21.4 0.8 slice.7
  22.2 1.3 collective-permute-done.4
  23.5 0.0 collective-permute-done.2.m4
  23.6 0.4 collective-permute-start.9
  23.9 2.6 %collective-permute-start.5 = (bf16[128,2048]{1,0:T(8,128)(2,1)S(1)}, bf16[128,2048]{1,0:T(8,128)(2,1)S(1)}, u32[]{:S(2)}, u32[]{:S(2)}) collective-permute-start(bf16[128,2048]{1,0:T(8,128)(2,1)S(1)} %collective-permute-done.2.m4), channel_id=1, source_target_pairs={{0,12},{1,13},{2,14},{3,15},{4,8},{5,9},{6,10},{7,11},{8,4},{9,5},... | collective-permute-start | bytes 1572872 | tf_op jit(solution)/shard_map/ppermute | solution.py:253
  26.5 3.0 %collective-permute-start.6 = (f32[128,128]{1,0:T(8,128)S(1)}, f32[128,128]{1,0:T(8,128)S(1)}, u32[]{:S(2)}, u32[]{:S(2)}) collective-permute-start(f32[128,128]{1,0:T(8,128)S(1)} %add.45), channel_id=1, source_target_pairs={{0,2},{1,3},{2,0},{3,1},{4,6},{5,7},{6,4},{7,5},{8,10},{9,11},{10,... | collective-permute-start | bytes 196616 | tf_op jit(solution)/shard_map/ppermute | solution.py:253
  29.5 5.3 %collective-permute-done.6 = f32[128,128]{1,0:T(8,128)S(1)} collective-permute-done((f32[128,128]{1,0:T(8,128)S(1)}, f32[128,128]{1,0:T(8,128)S(1)}, u32[]{:S(2)}, u32[]{:S(2)}) %collective-permute-start.6) | collective-permute-done | bytes 65568 | tf_op jit(solution)/shard_map/ppermute | solution.py:253
  34.8 0.0 copy-start.6
  34.8 2.9 %collective-permute-start.8 = (bf16[128,2048]{1,0:T(8,128)(2,1)}, bf16[128,2048]{1,0:T(8,128)(2,1)}, u32[]{:S(2)}, u32[]{:S(2)}) collective-permute-start(bf16[128,2048]{1,0:T(8,128)(2,1)} %slice.7), channel_id=1, source_target_pairs={{0,2},{1,3},{2,0},{3,1},{4,6},{5,7},{6,4},{7,5},{8,10},{9,11},{10,... | collective-permute-start | bytes 1572872 | tf_op jit(solution)/shard_map/ppermute | solution.py:253
  37.7 1.6 %collective-permute-start.10 = (bf16[128,2048]{1,0:T(8,128)(2,1)S(1)}, bf16[128,2048]{1,0:T(8,128)(2,1)}, u32[]{:S(2)}, u32[]{:S(2)}) collective-permute-start(bf16[128,2048]{1,0:T(8,128)(2,1)S(1)} %collective-permute-done.9.m4), channel_id=1, source_target_pairs={{0,12},{1,13},{2,14},{3,15},{4,8},{5,9},{6,10},{7,11},{8,4},{9,5},... | collective-permute-start | bytes 1572872 | tf_op jit(solution)/shard_map/ppermute | solution.py:253
  39.3 1.3 collective-permute-done.7
  40.5 0.6 add_convert_fusion.1.latent
  41.2 0.8 copy-done.8
  42.0 7.7 %main_part.2 = (bf16[128,2048]{1,0:T(8,128)(2,1)}, f32[128,128]{1,0:T(8,128)}, bf16[8,2,448,256]{3,2,1,0:T(8,128)(2,1)}) custom-call(bf16[128,4096]{1,0:T(8,128)(2,1)} %tok.5, bf16[128,4096]{1,0:T(8,128)(2,1)} %collective-permute-done.m1, bf16[128,2048]{1,0:T(8,128)(2,1)} %copy-done.6, bf16[128,2048]{1,0:T(8,128)(2,1)} %copy-done.5, ...), custom_call_target="tpu_custom_call" | custom-call | flops 2000000000 | bytes 29360128 | tf_op jit(solution)/shard_map/main_part/pallas_call | solution.py:89
  49.8 0.1 collective-permute-done.10.m8
  49.9 7.7 %main_part.3 = (bf16[128,2048]{1,0:T(8,128)(2,1)}, f32[128,128]{1,0:T(8,128)}, bf16[8,2,448,256]{3,2,1,0:T(8,128)(2,1)}) custom-call(bf16[128,4096]{1,0:T(8,128)(2,1)} %tok.5, bf16[128,4096]{1,0:T(8,128)(2,1)} %collective-permute-done.m1, bf16[128,2048]{1,0:T(8,128)(2,1)} %collective-permute-done.8.m2, ...), custom_call_target="tpu_custom_call", output_to_operand_aliasing={{2}: (10, {})} | custom-call | flops 2000000000 | bytes 29360128 | tf_op jit(solution)/shard_map/main_part/pallas_call | solution.py:89
  57.6 0.0 copy-start.11
  57.6 0.0 copy-start.12
  57.7 0.0 reduce-scatter.2.cloned.1.call-update
  57.7 1.1 copy-done.1
  58.9 0.7 collective-permute-start.12
  59.6 1.8 %collective-permute-start.11 = (f32[128,128]{1,0:T(8,128)S(1)}, f32[128,128]{1,0:T(8,128)S(1)}, u32[]{:S(2)}, u32[]{:S(2)}) collective-permute-start(f32[128,128]{1,0:T(8,128)S(1)} %add.48), channel_id=1, source_target_pairs={{0,12},{1,13},{2,14},{3,15},{4,8},{5,9},{6,10},{7,11},{8,4},{9,5},... | collective-permute-start | bytes 196616 | tf_op jit(solution)/shard_map/ppermute | solution.py:253
  61.4 6.4 %back_products.1 = (bf16[128,4096]{1,0:T(8,128)(2,1)}, bf16[128,2048]{1,0:T(8,128)(2,1)}, bf16[128,2048]{1,0:T(8,128)(2,1)}, bf16[128,2048]{1,0:T(8,128)(2,1)}, ...) custom-call(bf16[128,2048]{1,0:T(8,128)(2,1)} %get-tuple-element.39.low.refs_0_, ...), custom_call_target="tpu_custom_call" | custom-call | flops 2000000000 | bytes 20971520 | tf_op jit(solution)/shard_map/back_products/pallas_call | solution.py:136
  67.8 5.0 %collective-permute-done.12.others = bf16[128,2048]{1,0:T(8,128)(2,1)S(1)} collective-permute-done((bf16[128,2048]{1,0:T(8,128)(2,1)S(1)}, bf16[128,2048]{1,0:T(8,128)(2,1)S(1)}, u32[]{:S(2)}, u32[]{:S(2)}) %collective-permute-start.12) | collective-permute-done | bytes 524320 | tf_op jit(solution)/shard_map/ppermute | solution.py:270
  72.9 2.1 %collective-permute-start.13 = (f32[128,128]{1,0:T(8,128)S(1)}, f32[128,128]{1,0:T(8,128)S(1)}, u32[]{:S(2)}, u32[]{:S(2)}) collective-permute-start(f32[128,128]{1,0:T(8,128)S(1)} %add.50), channel_id=1, source_target_pairs={{0,2},{1,3},{2,0},{3,1},{4,6},{5,7},{6,4},{7,5},{8,10},{9,11},{10,... | collective-permute-start | bytes 196616 | tf_op jit(solution)/shard_map/ppermute | solution.py:253
  75.0 3.8 %collective-permute-done.13 = f32[128,128]{1,0:T(8,128)S(1)} collective-permute-done((f32[128,128]{1,0:T(8,128)S(1)}, f32[128,128]{1,0:T(8,128)S(1)}, u32[]{:S(2)}, u32[]{:S(2)}) %collective-permute-start.13) | collective-permute-done | bytes 65568 | tf_op jit(solution)/shard_map/ppermute | solution.py:253
  78.8 0.1 collective-permute-start.17
  78.9 2.1 %collective-permute-start.14 = (bf16[128,2048]{1,0:T(8,128)(2,1)}, bf16[128,2048]{1,0:T(8,128)(2,1)S(1)}, u32[]{:S(2)}, u32[]{:S(2)}) collective-permute-start(bf16[128,2048]{1,0:T(8,128)(2,1)} %get-tuple-element.51), channel_id=1, source_target_pairs={{0,2},{1,3},{2,0},{3,1},{4,6},{5,7},{6,4},{7,5},{8,10},{9,11},{10,... | collective-permute-start | bytes 1572872 | tf_op jit(solution)/shard_map/ppermute | solution.py:253
  80.9 0.4 collective-permute-start.20
  81.4 1.7 %collective-permute-start.15 = (f32[128,128]{1,0:T(8,128)S(1)}, f32[128,128]{1,0:T(8,128)S(1)}, u32[]{:S(2)}, u32[]{:S(2)}) collective-permute-start(f32[128,128]{1,0:T(8,128)S(1)} %add.51), channel_id=1, source_target_pairs={{0,4},{1,5},{2,6},{3,7},{4,0},{5,1},{6,2},{7,3},{8,12},{9,13},{10,... | collective-permute-start | bytes 196616 | tf_op jit(solution)/shard_map/ppermute | solution.py:253
  83.0 2.6 %collective-permute-done.15 = f32[128,128]{1,0:T(8,128)S(1)} collective-permute-done((f32[128,128]{1,0:T(8,128)S(1)}, f32[128,128]{1,0:T(8,128)S(1)}, u32[]{:S(2)}, u32[]{:S(2)}) %collective-permute-start.15) | collective-permute-done | bytes 65568 | tf_op jit(solution)/shard_map/ppermute | solution.py:253
  85.7 0.1 collective-permute-start.16
  85.8 2.1 %collective-permute-start.22 = (bf16[128,2048]{1,0:T(8,128)(2,1)}, bf16[128,2048]{1,0:T(8,128)(2,1)S(1)}, u32[]{:S(2)}, u32[]{:S(2)}) collective-permute-start(bf16[128,2048]{1,0:T(8,128)(2,1)} %get-tuple-element.63), channel_id=1, source_target_pairs={{0,12},{1,13},{2,14},{3,15},{4,8},{5,9},{6,10},{7,11},{8,4},{9,5},... | collective-permute-start | bytes 1572872 | tf_op jit(solution)/shard_map/ppermute | solution.py:253
  87.9 0.0 copy-start.10
  87.9 0.7 collective-permute-start.18
  88.6 6.6 %collective-permute-done.14.refs_2_ = bf16[128,2048]{1,0:T(8,128)(2,1)S(1)} collective-permute-done((bf16[128,2048]{1,0:T(8,128)(2,1)}, bf16[128,2048]{1,0:T(8,128)(2,1)S(1)}, u32[]{:S(2)}, u32[]{:S(2)}) %collective-permute-start.14) | collective-permute-done | bytes 524320 | tf_op jit(solution)/shard_map/ppermute | solution.py:253
  95.3 0.8 copy-done.15
  96.1 0.6 copy-done.13
  96.7 2.3 %down_part.1 = bf16[8,128,256]{2,1,0:T(8,128)(2,1)} custom-call(s32[1]{0:T(128)} %bitcast.side, bf16[128,4096]{1,0:T(8,128)(2,1)} %tok.5, bf16[128,2048]{1,0:T(8,128)(2,1)} %copy-done.4, bf16[128,128]{1,0:T(8,128)(2,1)} %copy-done.10, bf16[128,128]{1,0:T(8,128)(2,1)} %copy-done.13), custom_call_target="tpu_custom_call" | custom-call | flops 300000000 | bytes 10485760 | tf_op jit(solution)/shard_map/down_part/pallas_call | solution.py:160
  99.0 8.5 %all-to-all-start = ((bf16[8,128,256]{2,1,0:T(8,128)(2,1)}), bf16[8,128,256]{2,1,0:T(8,128)(2,1)S(1)}, u32[]{:S(2)}, u32[]{:S(2)}) async-start(bf16[8,128,256]{2,1,0:T(8,128)(2,1)} %down_part.1), calls=%async_computation.1 | async-start | bytes 1048576 | tf_op jit(solution)/shard_map/all_to_all | solution.py:316
  107.5 0.9 add.55
  108.4 2.0 %collective-permute-start.23 = (bf16[128,2048]{1,0:T(8,128)(2,1)}, bf16[128,2048]{1,0:T(8,128)(2,1)S(1)}, u32[]{:S(2)}, u32[]{:S(2)}) collective-permute-start(bf16[128,2048]{1,0:T(8,128)(2,1)} %add.55), channel_id=1, source_target_pairs={{0,4},{1,5},{2,6},{3,7},{4,0},{5,1},{6,2},{7,3},{8,12},{9,13},{10,... | collective-permute-start | bytes 1572872 | tf_op jit(solution)/shard_map/ppermute | solution.py:253
  110.4 0.1 add.54
  110.5 0.1 collective-permute-start.21
  110.6 2.0 %collective-permute-start.19 = (bf16[128,2048]{1,0:T(8,128)(2,1)}, bf16[128,2048]{1,0:T(8,128)(2,1)}, u32[]{:S(2)}, u32[]{:S(2)}) collective-permute-start(bf16[128,2048]{1,0:T(8,128)(2,1)} %get-tuple-element.56), channel_id=1, source_target_pairs={{0,2},{1,3},{2,0},{3,1},{4,6},{5,7},{6,4},{7,5},{8,10},{9,11},{10,... | collective-permute-start | bytes 1572872 | tf_op jit(solution)/shard_map/ppermute | solution.py:253
  112.6 1.0 dynamic-slice_bitcast_fusion
  113.6 0.7 collective-permute-start.24
  114.3 9.2 %collective-permute-done.23.refs_5_ = bf16[128,2048]{1,0:T(8,128)(2,1)S(1)} collective-permute-done((bf16[128,2048]{1,0:T(8,128)(2,1)}, bf16[128,2048]{1,0:T(8,128)(2,1)S(1)}, u32[]{:S(2)}, u32[]{:S(2)}) %collective-permute-start.23) | collective-permute-done | bytes 524320 | tf_op jit(solution)/shard_map/ppermute | solution.py:253
  123.4 9.9 %collective-permute-done.21.refs_4_ = bf16[128,2048]{1,0:T(8,128)(2,1)S(1)} collective-permute-done((bf16[128,2048]{1,0:T(8,128)(2,1)S(1)}, bf16[128,2048]{1,0:T(8,128)(2,1)S(1)}, u32[]{:S(2)}, u32[]{:S(2)}) %collective-permute-start.21) | collective-permute-done | bytes 524320 | tf_op jit(solution)/shard_map/ppermute | solution.py:253
  133.3 0.8 copy-done.17
  134.1 4.6 %token_grad.1 = bf16[128,4096]{1,0:T(8,128)(2,1)} custom-call(bf16[128,2048]{1,0:T(8,128)(2,1)} %get-tuple-element.39.low.refs_0_, bf16[128,2048]{1,0:T(8,128)(2,1)} %get-tuple-element.44.high.refs_1_, bf16[128,2048]{1,0:T(8,128)(2,1)} %copy-done.15, bf16[128,2048]{1,0:T(8,128)(2,1)} %collective-permute-done.19.refs_3_, bf16[128,2048]{1,0:T(8,128)(2,1)} %copy-done.17, ...), custom_call_target="tpu_custom_call" | custom-call | flops 2000000000 | bytes 17825792 | tf_op jit(solution)/shard_map/token_grad/pallas_call | solution.py:198
  138.7 0.1 convert_reduce_fusion
  138.8 0.8 copy.12
  139.6 1.8 %finish.1 = (f32[64,256]{1,0:T(8,128)}, f32[4,64,256]{2,1,0:T(8,128)}, f32[128,256]{1,0:T(8,128)}) custom-call(s32[1]{0:T(128)} %bitcast.side, bf16[2,448,256]{2,1,0:T(8,128)(2,1)} %bitcast.11, bf16[448,256]{1,0:T(8,128)(2,1)} %copy-done.9), custom_call_target="tpu_custom_call" | custom-call | flops 300000 | bytes 4194304 | tf_op jit(solution)/shard_map/finish/pallas_call | solution.py:227
  (52 shorter events, 0.2 us)
Async XLA Ops:
  7.2 14.2 %copy-start = (bf16[128,4096]{1,0:T(8,128)(2,1)S(1)}, bf16[128,4096]{1,0:T(8,128)(2,1)}, u32[]{:S(2)}) copy-start(bf16[128,4096]{1,0:T(8,128)(2,1)} %tok.5) | copy-start | bytes 3145732
  7.2 105.5 %reduce-scatter.2.cloned.1.call-start = ((), (), s32[]{:S(2)}) async-start(), calls=%async_computation.2 | async-start | bytes 4128768 | tf_op jit(solution)/shard_map/reduce_scatter | solution.py:263
  8.4 15.2 %collective-permute-start.2 = (bf16[128,2048]{1,0:T(8,128)(2,1)S(1)}, bf16[128,2048]{1,0:T(8,128)(2,1)S(1)}, u32[]{:S(2)}, u32[]{:S(2)}) collective-permute-start(bf16[128,2048]{1,0:T(8,128)(2,1)S(1)} %slice.6), channel_id=1, source_target_pairs={{0,4},{1,5},{2,6},{3,7},{4,0},{5,1},{6,2},{7,3},{8,12},{9,13},{10,... | collective-permute-start | bytes 1572872 | tf_op jit(solution)/shard_map/ppermute | solution.py:253
  10.7 31.3 %collective-permute-start = (bf16[128,4096]{1,0:T(8,128)(2,1)}, bf16[128,4096]{1,0:T(8,128)(2,1)}, u32[]{:S(2)}, u32[]{:S(2)}) collective-permute-start(bf16[128,4096]{1,0:T(8,128)(2,1)} %tok.5), channel_id=1, source_target_pairs={{0,1},{1,0},{2,3},{3,2},{4,5},{5,4},{6,7},{7,6},{8,9},{9,8},{10,11... | collective-permute-start | bytes 3145736 | tf_op jit(solution)/shard_map/ppermute | solution.py:253
  12.6 4.6 %collective-permute-start.3 = (f32[128,128]{1,0:T(8,128)S(1)}, f32[128,128]{1,0:T(8,128)S(1)}, u32[]{:S(2)}, u32[]{:S(2)}) collective-permute-start(f32[128,128]{1,0:T(8,128)S(1)} %fusion), channel_id=1, source_target_pairs={{0,12},{1,13},{2,14},{3,15},{4,8},{5,9},{6,10},{7,11},{8,4},{9,5},... | collective-permute-start | bytes 196616 | tf_op jit(solution)/shard_map/ppermute | solution.py:253
  17.2 6.3 %collective-permute-start.4 = (f32[128,128]{1,0:T(8,128)S(1)}, f32[128,128]{1,0:T(8,128)S(1)}, u32[]{:S(2)}, u32[]{:S(2)}) collective-permute-start(f32[128,128]{1,0:T(8,128)S(1)} %add.44), channel_id=1, source_target_pairs={{0,4},{1,5},{2,6},{3,7},{4,0},{5,1},{6,2},{7,3},{8,12},{9,13},{10,... | collective-permute-start | bytes 196616 | tf_op jit(solution)/shard_map/ppermute | solution.py:253
  18.6 16.2 %collective-permute-start.1 = (bf16[128,2048]{1,0:T(8,128)(2,1)S(1)}, bf16[128,2048]{1,0:T(8,128)(2,1)S(1)}, u32[]{:S(2)}, u32[]{:S(2)}) collective-permute-start(bf16[128,2048]{1,0:T(8,128)(2,1)S(1)} %slice.6), channel_id=1, source_target_pairs={{0,2},{1,3},{2,0},{3,1},{4,6},{5,7},{6,4},{7,5},{8,10},{9,11},{10,... | collective-permute-start | bytes 1572872 | tf_op jit(solution)/shard_map/ppermute | solution.py:253
  23.6 18.4 %copy-start.5 = (bf16[128,2048]{1,0:T(8,128)(2,1)}, bf16[128,2048]{1,0:T(8,128)(2,1)S(1)}, u32[]{:S(2)}) copy-start(bf16[128,2048]{1,0:T(8,128)(2,1)S(1)} %collective-permute-done.2.m4) | copy-start | bytes 1572868
  23.6 14.1 %collective-permute-start.9 = (bf16[128,2048]{1,0:T(8,128)(2,1)}, bf16[128,2048]{1,0:T(8,128)(2,1)S(1)}, u32[]{:S(2)}, u32[]{:S(2)}) collective-permute-start(bf16[128,2048]{1,0:T(8,128)(2,1)} %slice.7), channel_id=1, source_target_pairs={{0,4},{1,5},{2,6},{3,7},{4,0},{5,1},{6,2},{7,3},{8,12},{9,13},{10,... | collective-permute-start | bytes 1572872 | tf_op jit(solution)/shard_map/ppermute | solution.py:253
  23.9 17.2 %collective-permute-start.5 = (bf16[128,2048]{1,0:T(8,128)(2,1)S(1)}, bf16[128,2048]{1,0:T(8,128)(2,1)S(1)}, u32[]{:S(2)}, u32[]{:S(2)}) collective-permute-start(bf16[128,2048]{1,0:T(8,128)(2,1)S(1)} %collective-permute-done.2.m4), channel_id=1, source_target_pairs={{0,12},{1,13},{2,14},{3,15},{4,8},{5,9},{6,10},{7,11},{8,4},{9,5},... | collective-permute-start | bytes 1572872 | tf_op jit(solution)/shard_map/ppermute | solution.py:253
  26.5 8.3 %collective-permute-start.6 = (f32[128,128]{1,0:T(8,128)S(1)}, f32[128,128]{1,0:T(8,128)S(1)}, u32[]{:S(2)}, u32[]{:S(2)}) collective-permute-start(f32[128,128]{1,0:T(8,128)S(1)} %add.45), channel_id=1, source_target_pairs={{0,2},{1,3},{2,0},{3,1},{4,6},{5,7},{6,4},{7,5},{8,10},{9,11},{10,... | collective-permute-start | bytes 196616 | tf_op jit(solution)/shard_map/ppermute | solution.py:253
  34.8 7.2 %copy-start.6 = (bf16[128,2048]{1,0:T(8,128)(2,1)}, bf16[128,2048]{1,0:T(8,128)(2,1)S(1)}, u32[]{:S(2)}) copy-start(bf16[128,2048]{1,0:T(8,128)(2,1)S(1)} %collective-permute-done.1.m2) | copy-start | bytes 1572868
  34.8 14.9 %collective-permute-start.8 = (bf16[128,2048]{1,0:T(8,128)(2,1)}, bf16[128,2048]{1,0:T(8,128)(2,1)}, u32[]{:S(2)}, u32[]{:S(2)}) collective-permute-start(bf16[128,2048]{1,0:T(8,128)(2,1)} %slice.7), channel_id=1, source_target_pairs={{0,2},{1,3},{2,0},{3,1},{4,6},{5,7},{6,4},{7,5},{8,10},{9,11},{10,... | collective-permute-start | bytes 1572872 | tf_op jit(solution)/shard_map/ppermute | solution.py:253
  37.7 12.0 %copy-start.7 = (bf16[128,2048]{1,0:T(8,128)(2,1)}, bf16[128,2048]{1,0:T(8,128)(2,1)S(1)}, u32[]{:S(2)}) copy-start(bf16[128,2048]{1,0:T(8,128)(2,1)S(1)} %collective-permute-done.9.m4) | copy-start | bytes 1572868
  37.7 12.2 %collective-permute-start.10 = (bf16[128,2048]{1,0:T(8,128)(2,1)S(1)}, bf16[128,2048]{1,0:T(8,128)(2,1)}, u32[]{:S(2)}, u32[]{:S(2)}) collective-permute-start(bf16[128,2048]{1,0:T(8,128)(2,1)S(1)} %collective-permute-done.9.m4), channel_id=1, source_target_pairs={{0,12},{1,13},{2,14},{3,15},{4,8},{5,9},{6,10},{7,11},{8,4},{9,5},... | collective-permute-start | bytes 1572872 | tf_op jit(solution)/shard_map/ppermute | solution.py:253
  39.3 1.3 collective-permute-start.7
  41.2 0.8 copy-start.8
  57.6 1.2 copy-start.1
  57.6 1.9 %copy-start.11 = (f32[128,128]{1,0:T(8,128)S(1)}, f32[128,128]{1,0:T(8,128)}, u32[]{:S(2)}) copy-start(f32[128,128]{1,0:T(8,128)} %get-tuple-element.46) | copy-start | bytes 196612
  57.6 1.9 %copy-start.12 = (f32[128,128]{1,0:T(8,128)S(1)}, f32[128,128]{1,0:T(8,128)}, u32[]{:S(2)}) copy-start(f32[128,128]{1,0:T(8,128)} %get-tuple-element.47) | copy-start | bytes 196612
  58.9 14.0 %collective-permute-start.12 = (bf16[128,2048]{1,0:T(8,128)(2,1)S(1)}, bf16[128,2048]{1,0:T(8,128)(2,1)S(1)}, u32[]{:S(2)}, u32[]{:S(2)}) collective-permute-start(bf16[128,2048]{1,0:T(8,128)(2,1)S(1)} %constant_dynamic-slice_fusion), channel_id=1, source_target_pairs={{0,128},{16,144},{32,160},{48,176},{64,192},{80,208},{96,224},{112... | collective-permute-start | bytes 1572872 | tf_op jit(solution)/shard_map/ppermute | solution.py:270
  59.6 13.3 %collective-permute-start.11 = (f32[128,128]{1,0:T(8,128)S(1)}, f32[128,128]{1,0:T(8,128)S(1)}, u32[]{:S(2)}, u32[]{:S(2)}) collective-permute-start(f32[128,128]{1,0:T(8,128)S(1)} %add.48), channel_id=1, source_target_pairs={{0,12},{1,13},{2,14},{3,15},{4,8},{5,9},{6,10},{7,11},{8,4},{9,5},... | collective-permute-start | bytes 196616 | tf_op jit(solution)/shard_map/ppermute | solution.py:253
  67.8 39.6 %copy-start.3 = (bf16[128,2048]{1,0:T(8,128)(2,1)S(1)}, bf16[128,2048]{1,0:T(8,128)(2,1)}, u32[]{:S(2)}) copy-start(bf16[128,2048]{1,0:T(8,128)(2,1)} %get-tuple-element.61) | copy-start | bytes 1572868
  67.8 42.6 %copy-start.2 = (bf16[128,2048]{1,0:T(8,128)(2,1)S(1)}, bf16[128,2048]{1,0:T(8,128)(2,1)}, u32[]{:S(2)}) copy-start(bf16[128,2048]{1,0:T(8,128)(2,1)} %get-tuple-element.57) | copy-start | bytes 1572868
  72.9 23.2 %copy-start.4 = (bf16[128,2048]{1,0:T(8,128)(2,1)}, bf16[128,2048]{1,0:T(8,128)(2,1)S(1)}, u32[]{:S(2)}) copy-start(bf16[128,2048]{1,0:T(8,128)(2,1)S(1)} %collective-permute-done.12.others) | copy-start | bytes 1572868
  72.9 5.9 %collective-permute-start.13 = (f32[128,128]{1,0:T(8,128)S(1)}, f32[128,128]{1,0:T(8,128)S(1)}, u32[]{:S(2)}, u32[]{:S(2)}) collective-permute-start(f32[128,128]{1,0:T(8,128)S(1)} %add.50), channel_id=1, source_target_pairs={{0,2},{1,3},{2,0},{3,1},{4,6},{5,7},{6,4},{7,5},{8,10},{9,11},{10,... | collective-permute-start | bytes 196616 | tf_op jit(solution)/shard_map/ppermute | solution.py:253
  78.8 9.1 %collective-permute-start.17 = (bf16[128,4096]{1,0:T(8,128)(2,1)}, bf16[128,4096]{1,0:T(8,128)(2,1)S(1)}, u32[]{:S(2)}, u32[]{:S(2)}) collective-permute-start(bf16[128,4096]{1,0:T(8,128)(2,1)} %get-tuple-element.53), channel_id=1, source_target_pairs={{0,1},{1,0},{2,3},{3,2},{4,5},{5,4},{6,7},{7,6},{8,9},{9,8},{10,11... | collective-permute-start | bytes 3145736 | tf_op jit(solution)/shard_map/ppermute | solution.py:253
  78.9 16.4 %collective-permute-start.14 = (bf16[128,2048]{1,0:T(8,128)(2,1)}, bf16[128,2048]{1,0:T(8,128)(2,1)S(1)}, u32[]{:S(2)}, u32[]{:S(2)}) collective-permute-start(bf16[128,2048]{1,0:T(8,128)(2,1)} %get-tuple-element.51), channel_id=1, source_target_pairs={{0,2},{1,3},{2,0},{3,1},{4,6},{5,7},{6,4},{7,5},{8,10},{9,11},{10,... | collective-permute-start | bytes 1572872 | tf_op jit(solution)/shard_map/ppermute | solution.py:253
  80.9 18.1 %collective-permute-start.20 = (bf16[128,2048]{1,0:T(8,128)(2,1)}, bf16[128,2048]{1,0:T(8,128)(2,1)S(1)}, u32[]{:S(2)}, u32[]{:S(2)}) collective-permute-start(bf16[128,2048]{1,0:T(8,128)(2,1)} %get-tuple-element.59), channel_id=1, source_target_pairs={{0,12},{1,13},{2,14},{3,15},{4,8},{5,9},{6,10},{7,11},{8,4},{9,5},... | collective-permute-start | bytes 1572872 | tf_op jit(solution)/shard_map/ppermute | solution.py:253
  81.4 4.3 %collective-permute-start.15 = (f32[128,128]{1,0:T(8,128)S(1)}, f32[128,128]{1,0:T(8,128)S(1)}, u32[]{:S(2)}, u32[]{:S(2)}) collective-permute-start(f32[128,128]{1,0:T(8,128)S(1)} %add.51), channel_id=1, source_target_pairs={{0,4},{1,5},{2,6},{3,7},{4,0},{5,1},{6,2},{7,3},{8,12},{9,13},{10,... | collective-permute-start | bytes 196616 | tf_op jit(solution)/shard_map/ppermute | solution.py:253
  85.7 2.2 %collective-permute-start.16 = (f32[128,128]{1,0:T(8,128)S(1)}, f32[128,128]{1,0:T(8,128)S(1)}, u32[]{:S(2)}, u32[]{:S(2)}) collective-permute-start(f32[128,128]{1,0:T(8,128)S(1)} %add.52), channel_id=1, source_target_pairs={{0,1},{1,0},{2,3},{3,2},{4,5},{5,4},{6,7},{7,6},{8,9},{9,8},{10,11... | collective-permute-start | bytes 196616 | tf_op jit(solution)/shard_map/ppermute | solution.py:253
  85.8 21.7 %collective-permute-start.22 = (bf16[128,2048]{1,0:T(8,128)(2,1)}, bf16[128,2048]{1,0:T(8,128)(2,1)S(1)}, u32[]{:S(2)}, u32[]{:S(2)}) collective-permute-start(bf16[128,2048]{1,0:T(8,128)(2,1)} %get-tuple-element.63), channel_id=1, source_target_pairs={{0,12},{1,13},{2,14},{3,15},{4,8},{5,9},{6,10},{7,11},{8,4},{9,5},... | collective-permute-start | bytes 1572872 | tf_op jit(solution)/shard_map/ppermute | solution.py:253
  87.9 7.4 %copy-start.14 = (bf16[128,4096]{1,0:T(8,128)(2,1)}, bf16[128,4096]{1,0:T(8,128)(2,1)S(1)}, u32[]{:S(2)}) copy-start(bf16[128,4096]{1,0:T(8,128)(2,1)S(1)} %collective-permute-done.17.refs_6_) | copy-start | bytes 3145732
  87.9 8.2 %copy-start.10 = (bf16[128,128]{1,0:T(8,128)(2,1)}, bf16[128,128]{1,0:T(8,128)(2,1)S(1)}, u32[]{:S(2)}) copy-start(bf16[128,128]{1,0:T(8,128)(2,1)S(1)} %add_convert_fusion.lat.refs_9_) | copy-start | bytes 98308
  87.9 7.3 %collective-permute-start.18 = (bf16[128,128]{1,0:T(8,128)(2,1)S(1)}, bf16[128,128]{1,0:T(8,128)(2,1)S(1)}, u32[]{:S(2)}, u32[]{:S(2)}) collective-permute-start(bf16[128,128]{1,0:T(8,128)(2,1)S(1)} %add_convert_fusion.lat.refs_9_), channel_id=1, source_target_pairs={{0,128},{16,144},{32,160},{48,176},{64,192},{80,208},{96,224},{112... | collective-permute-start | bytes 98312 | tf_op jit(solution)/shard_map/ppermute | solution.py:270
  95.3 0.8 copy-start.15
  96.1 0.6 copy-start.13
  99.0 39.7 %all-to-all-start = ((bf16[8,128,256]{2,1,0:T(8,128)(2,1)}), bf16[8,128,256]{2,1,0:T(8,128)(2,1)S(1)}, u32[]{:S(2)}, u32[]{:S(2)}) async-start(bf16[8,128,256]{2,1,0:T(8,128)(2,1)} %down_part.1), calls=%async_computation.1 | async-start | bytes 1048576 | tf_op jit(solution)/shard_map/all_to_all | solution.py:316
  108.4 15.0 %collective-permute-start.23 = (bf16[128,2048]{1,0:T(8,128)(2,1)}, bf16[128,2048]{1,0:T(8,128)(2,1)S(1)}, u32[]{:S(2)}, u32[]{:S(2)}) collective-permute-start(bf16[128,2048]{1,0:T(8,128)(2,1)} %add.55), channel_id=1, source_target_pairs={{0,4},{1,5},{2,6},{3,7},{4,0},{5,1},{6,2},{7,3},{8,12},{9,13},{10,... | collective-permute-start | bytes 1572872 | tf_op jit(solution)/shard_map/ppermute | solution.py:253
  110.5 22.8 %collective-permute-start.21 = (bf16[128,2048]{1,0:T(8,128)(2,1)S(1)}, bf16[128,2048]{1,0:T(8,128)(2,1)S(1)}, u32[]{:S(2)}, u32[]{:S(2)}) collective-permute-start(bf16[128,2048]{1,0:T(8,128)(2,1)S(1)} %add.54), channel_id=1, source_target_pairs={{0,4},{1,5},{2,6},{3,7},{4,0},{5,1},{6,2},{7,3},{8,12},{9,13},{10,... | collective-permute-start | bytes 1572872 | tf_op jit(solution)/shard_map/ppermute | solution.py:253
  110.6 23.5 %collective-permute-start.19 = (bf16[128,2048]{1,0:T(8,128)(2,1)}, bf16[128,2048]{1,0:T(8,128)(2,1)}, u32[]{:S(2)}, u32[]{:S(2)}) collective-permute-start(bf16[128,2048]{1,0:T(8,128)(2,1)} %get-tuple-element.56), channel_id=1, source_target_pairs={{0,2},{1,3},{2,0},{3,1},{4,6},{5,7},{6,4},{7,5},{8,10},{9,11},{10,... | collective-permute-start | bytes 1572872 | tf_op jit(solution)/shard_map/ppermute | solution.py:253
  113.6 25.1 %collective-permute-start.24 = (bf16[448,256]{1,0:T(8,128)(2,1)S(1)}, bf16[448,256]{1,0:T(8,128)(2,1)S(1)}, u32[]{:S(2)}, u32[]{:S(2)}) collective-permute-start(bf16[448,256]{1,0:T(8,128)(2,1)S(1)} %dynamic-slice_bitcast_fusion), channel_id=1, source_target_pairs={{0,128},{16,144},{32,160},{48,176},{64,192},{80,208},{96,224},{112... | collective-permute-start | bytes 688136 | tf_op jit(solution)/shard_map/ppermute | solution.py:270
  123.4 10.7 %copy-start.16 = (bf16[128,2048]{1,0:T(8,128)(2,1)}, bf16[128,2048]{1,0:T(8,128)(2,1)S(1)}, u32[]{:S(2)}) copy-start(bf16[128,2048]{1,0:T(8,128)(2,1)S(1)} %collective-permute-done.23.refs_5_) | copy-start | bytes 1572868
  133.3 0.8 copy-start.17
  138.7 0.9 copy-start.9
Sparse Core Ops, SparseCore 0:
  57.8 53.0 reduce-scatter.1

commit v8 on v7

--- a/solution.py
+++ b/solution.py
@@ -302,16 +302,15 @@
     b1, b2_0, b2_1, b4_0, b4_1, b8_0, b8_1 = run_back((slope0, slope1), section_factors)
     part = part + after(arrived, b1, others)
     q0, q1 = flip(after(b8_0, part), 12), flip(after(b8_1, part), 12)
+    part = part + flip(part, 4)
+    s0 = flip(b4_0 + after(q0, part), 4)
     part = part + flip(part, 2)
     r2_0, r1 = flip(after(b2_0, part), 2), flip(after(b1, part), 1)
-    part = part + flip(part, 4)
     part = part + after(flip(part, 1), r1)
     latent_grad = part.astype(BF16)
 
-    pair = run_down(x, tokens, others, latent_grad, after(cross(latent_grad), r2_0))
-    s0 = flip(b4_0 + after(q0, pair), 4)
+    pair = run_down(x, tokens, others, latent_grad, after(cross(latent_grad), r2_0, s0, q1))
     r2_1 = flip(after(b2_1, pair), 2)
-    pair = after(pair, q0)
     groups = [[side * RING + z for z in range(RING)] for side in range(2)]
     pair = lax.all_to_all(pair, "dp", 0, 0, axis_index_groups=groups, tiled=True)
     s1 = flip(b4_1 + q1, 4)

time: 150 us -> 158 us (1.053)
  waiting for transfers between devices: 49 us -> 55.1 us
  starting transfers between devices: 42.7 us -> 45.1 us
    ppermute x22, waiting for transfers between devices: 43.9 us -> 50 us  [flip(): return lax.ppermute(value, 'tensor', [(i, i ^ mask) for i in range(16)])]
    ppermute x22, starting transfers between devices: 32.1 us -> 33.8 us  [flip(): return lax.ppermute(value, 'tensor', [(i, i ^ mask) for i in range(16)])]
  transfers between devices with their start and end apart: 27 -> 27, of which waited for: 11 -> 14; matrix products, arithmetic and copies ran while one was open for 4% -> 4% of each run, Pallas kernels for 14% -> 13%
where the time goes in v8:
time: 158 us; the launch traced here: 157 us
  waiting for transfers between devices  55.1 us (35%)
  starting transfers between devices  45.1 us (29%)
  Pallas kernels  30.6 us (19%)
  between operations  14.3 us (9%)
  local copies, waits for them, and re-layouts  8 us (5%)
  other arithmetic  2.08 us (1%)
  matrix products  1.96 us (1%)
    ppermute x22, waiting for transfers between devices, flip(): return lax.ppermute(value, 'tensor', [(i, i ^ mask) for i in range(16)])  50 us
    ppermute x22, starting transfers between devices, flip(): return lax.ppermute(value, 'tensor', [(i, i ^ mask) for i in range(16)])  33.8 us
    pallas_call x2, Pallas kernels, run_main(): pl.pallas_call(main_kernel, grid=(steps,), in_specs=in_specs, out_specs=[...  15.5 us
    all_to_all x1, starting transfers between devices, per_device(): lax.all_to_all(pair, 'dp', 0, 0, axis_index_groups=groups, tiled=True)  8.47 us
    pallas_call x1, Pallas kernels, run_back(): pl.pallas_call(back_kernel, grid=(2,), in_specs=[fixed, fixed, pl.BlockSp...  6.41 us
    ppermute x3, waiting for transfers between devices, cross(): return lax.ppermute(value, 'dp', [(i, i ^ RING) for i in range(2 * RING)])  5.02 us
    unnamed x37, local copies, waits for them, and re-layouts  5.01 us
    pallas_call x1, Pallas kernels, run_final(): pl.pallas_call(final_kernel, grid=(steps,), in_specs=half_specs(rows, ste...  4.57 us
  transfers between devices with their start and end apart: 27, of which 14 were waited for; matrix products, arithmetic and copies ran while one was open for 4% of the time, Pallas kernels for 13%

profile of v8, /device:TPU:8, one launch (start us, length us, event | category | flops | bytes accessed | tf_op | source)
XLA Modules:
  0.0 157.1 jit_solution(15277747614853620144)
XLA Ops:
  7.2 0.0 copy-start
  7.2 0.0 reduce-scatter.2.cloned.1.call-start
  7.2 1.2 slice.6
  8.4 2.3 %collective-permute-start.2 = (bf16[128,2048]{1,0:T(8,128)(2,1)S(1)}, bf16[128,2048]{1,0:T(8,128)(2,1)S(1)}, u32[]{:S(2)}, u32[]{:S(2)}) collective-permute-start(bf16[128,2048]{1,0:T(8,128)(2,1)S(1)} %slice.6), channel_id=1, source_target_pairs={{0,4},{1,5},{2,6},{3,7},{4,0},{5,1},{6,2},{7,3},{8,12},{9,13},{10,... | collective-permute-start | bytes 1572872 | tf_op jit(solution)/shard_map/ppermute | solution.py:253
  10.7 2.0 %fusion = f32[128,128]{1,0:T(8,128)S(1)} fusion(bf16[128,4096]{1,0:T(8,128)(2,1)} %tok.5, bf16[4096,128]{1,0:T(8,128)(2,1)} %refs_8_.1), kind=kOutput, calls=%fused_computation.6 | convolution fusion | flops 134217728 | bytes 2162688 | tf_op jit(solution)/shard_map/dot_general | solution.py:282
  12.6 0.8 collective-permute-start.3
  13.4 3.8 %collective-permute-done.3 = f32[128,128]{1,0:T(8,128)S(1)} collective-permute-done((f32[128,128]{1,0:T(8,128)S(1)}, f32[128,128]{1,0:T(8,128)S(1)}, u32[]{:S(2)}, u32[]{:S(2)}) %collective-permute-start.3) | collective-permute-done | bytes 65568 | tf_op jit(solution)/shard_map/ppermute | solution.py:253
  17.2 1.4 collective-permute-start.4
  18.6 2.8 %collective-permute-start.1 = (bf16[128,2048]{1,0:T(8,128)(2,1)S(1)}, bf16[128,2048]{1,0:T(8,128)(2,1)S(1)}, u32[]{:S(2)}, u32[]{:S(2)}) collective-permute-start(bf16[128,2048]{1,0:T(8,128)(2,1)S(1)} %slice.6), channel_id=1, source_target_pairs={{0,2},{1,3},{2,0},{3,1},{4,6},{5,7},{6,4},{7,5},{8,10},{9,11},{10,... | collective-permute-start | bytes 1572872 | tf_op jit(solution)/shard_map/ppermute | solution.py:253
  21.4 0.8 slice.7
  22.2 1.3 collective-permute-done.4
  23.6 0.4 collective-permute-start.9
  23.9 2.6 %collective-permute-start.5 = (bf16[128,2048]{1,0:T(8,128)(2,1)S(1)}, bf16[128,2048]{1,0:T(8,128)(2,1)S(1)}, u32[]{:S(2)}, u32[]{:S(2)}) collective-permute-start(bf16[128,2048]{1,0:T(8,128)(2,1)S(1)} %collective-permute-done.2.m4), channel_id=1, source_target_pairs={{0,12},{1,13},{2,14},{3,15},{4,8},{5,9},{6,10},{7,11},{8,4},{9,5},... | collective-permute-start | bytes 1572872 | tf_op jit(solution)/shard_map/ppermute | solution.py:253
  26.5 3.0 %collective-permute-start.6 = (f32[128,128]{1,0:T(8,128)S(1)}, f32[128,128]{1,0:T(8,128)S(1)}, u32[]{:S(2)}, u32[]{:S(2)}) collective-permute-start(f32[128,128]{1,0:T(8,128)S(1)} %add.45), channel_id=1, source_target_pairs={{0,2},{1,3},{2,0},{3,1},{4,6},{5,7},{6,4},{7,5},{8,10},{9,11},{10,... | collective-permute-start | bytes 196616 | tf_op jit(solution)/shard_map/ppermute | solution.py:253
  29.5 5.3 %collective-permute-done.6 = f32[128,128]{1,0:T(8,128)S(1)} collective-permute-done((f32[128,128]{1,0:T(8,128)S(1)}, f32[128,128]{1,0:T(8,128)S(1)}, u32[]{:S(2)}, u32[]{:S(2)}) %collective-permute-start.6) | collective-permute-done | bytes 65568 | tf_op jit(solution)/shard_map/ppermute | solution.py:253
  34.8 0.0 copy-start.5
  34.8 2.9 %collective-permute-start.8 = (bf16[128,2048]{1,0:T(8,128)(2,1)}, bf16[128,2048]{1,0:T(8,128)(2,1)}, u32[]{:S(2)}, u32[]{:S(2)}) collective-permute-start(bf16[128,2048]{1,0:T(8,128)(2,1)} %slice.7), channel_id=1, source_target_pairs={{0,2},{1,3},{2,0},{3,1},{4,6},{5,7},{6,4},{7,5},{8,10},{9,11},{10,... | collective-permute-start | bytes 1572872 | tf_op jit(solution)/shard_map/ppermute | solution.py:253
  37.7 1.6 %collective-permute-start.10 = (bf16[128,2048]{1,0:T(8,128)(2,1)S(1)}, bf16[128,2048]{1,0:T(8,128)(2,1)}, u32[]{:S(2)}, u32[]{:S(2)}) collective-permute-start(bf16[128,2048]{1,0:T(8,128)(2,1)S(1)} %collective-permute-done.9.m4), channel_id=1, source_target_pairs={{0,12},{1,13},{2,14},{3,15},{4,8},{5,9},{6,10},{7,11},{8,4},{9,5},... | collective-permute-start | bytes 1572872 | tf_op jit(solution)/shard_map/ppermute | solution.py:253
  39.3 1.3 collective-permute-done.7
  40.5 0.6 add_convert_fusion.1.latent
  41.2 0.8 copy-done.7
  42.0 7.7 %main_part.2 = (bf16[128,2048]{1,0:T(8,128)(2,1)}, f32[128,128]{1,0:T(8,128)}, bf16[8,2,448,256]{3,2,1,0:T(8,128)(2,1)}) custom-call(bf16[128,4096]{1,0:T(8,128)(2,1)} %tok.5, bf16[128,4096]{1,0:T(8,128)(2,1)} %collective-permute-done.m1, bf16[128,2048]{1,0:T(8,128)(2,1)} %copy-done.5, bf16[128,2048]{1,0:T(8,128)(2,1)} %copy-done.4, ...), custom_call_target="tpu_custom_call" | custom-call | flops 2000000000 | bytes 29360128 | tf_op jit(solution)/shard_map/main_part/pallas_call | solution.py:89
  49.8 0.1 collective-permute-done.10.m8
  49.9 7.7 %main_part.3 = (bf16[128,2048]{1,0:T(8,128)(2,1)}, f32[128,128]{1,0:T(8,128)}, bf16[8,2,448,256]{3,2,1,0:T(8,128)(2,1)}) custom-call(bf16[128,4096]{1,0:T(8,128)(2,1)} %tok.5, bf16[128,4096]{1,0:T(8,128)(2,1)} %collective-permute-done.m1, bf16[128,2048]{1,0:T(8,128)(2,1)} %collective-permute-done.8.m2, ...), custom_call_target="tpu_custom_call", output_to_operand_aliasing={{2}: (10, {})} | custom-call | flops 2000000000 | bytes 29360128 | tf_op jit(solution)/shard_map/main_part/pallas_call | solution.py:89
  57.6 0.0 copy-start.10
  57.6 0.0 copy-start.11
  57.7 0.0 reduce-scatter.2.cloned.1.call-update
  57.7 1.1 copy-done.1
  58.9 0.7 collective-permute-start.12
  59.6 1.8 %collective-permute-start.11 = (f32[128,128]{1,0:T(8,128)S(1)}, f32[128,128]{1,0:T(8,128)S(1)}, u32[]{:S(2)}, u32[]{:S(2)}) collective-permute-start(f32[128,128]{1,0:T(8,128)S(1)} %add.48), channel_id=1, source_target_pairs={{0,12},{1,13},{2,14},{3,15},{4,8},{5,9},{6,10},{7,11},{8,4},{9,5},... | collective-permute-start | bytes 196616 | tf_op jit(solution)/shard_map/ppermute | solution.py:253
  61.4 6.4 %back_products.1 = (bf16[128,4096]{1,0:T(8,128)(2,1)}, bf16[128,2048]{1,0:T(8,128)(2,1)}, bf16[128,2048]{1,0:T(8,128)(2,1)}, bf16[128,2048]{1,0:T(8,128)(2,1)}, ...) custom-call(bf16[128,2048]{1,0:T(8,128)(2,1)} %get-tuple-element.38.low.refs_0_, ...), custom_call_target="tpu_custom_call" | custom-call | flops 2000000000 | bytes 20971520 | tf_op jit(solution)/shard_map/back_products/pallas_call | solution.py:136
  67.9 5.0 %collective-permute-done.12.others = bf16[128,2048]{1,0:T(8,128)(2,1)S(1)} collective-permute-done((bf16[128,2048]{1,0:T(8,128)(2,1)S(1)}, bf16[128,2048]{1,0:T(8,128)(2,1)S(1)}, u32[]{:S(2)}, u32[]{:S(2)}) %collective-permute-start.12) | collective-permute-done | bytes 524320 | tf_op jit(solution)/shard_map/ppermute | solution.py:270
  72.9 1.1 collective-permute-start.13
  74.0 3.3 %collective-permute-done.13 = f32[128,128]{1,0:T(8,128)S(1)} collective-permute-done((f32[128,128]{1,0:T(8,128)S(1)}, f32[128,128]{1,0:T(8,128)S(1)}, u32[]{:S(2)}, u32[]{:S(2)}) %collective-permute-start.13) | collective-permute-done | bytes 65568 | tf_op jit(solution)/shard_map/ppermute | solution.py:253
  77.3 2.1 %collective-permute-start.14 = (f32[128,128]{1,0:T(8,128)S(1)}, f32[128,128]{1,0:T(8,128)S(1)}, u32[]{:S(2)}, u32[]{:S(2)}) collective-permute-start(f32[128,128]{1,0:T(8,128)S(1)} %add.51), channel_id=1, source_target_pairs={{0,2},{1,3},{2,0},{3,1},{4,6},{5,7},{6,4},{7,5},{8,10},{9,11},{10,... | collective-permute-start | bytes 196616 | tf_op jit(solution)/shard_map/ppermute | solution.py:253
  79.3 3.8 %collective-permute-done.14 = f32[128,128]{1,0:T(8,128)S(1)} collective-permute-done((f32[128,128]{1,0:T(8,128)S(1)}, f32[128,128]{1,0:T(8,128)S(1)}, u32[]{:S(2)}, u32[]{:S(2)}) %collective-permute-start.14) | collective-permute-done | bytes 65568 | tf_op jit(solution)/shard_map/ppermute | solution.py:253
  83.1 0.1 collective-permute-start.17
  83.2 0.5 collective-permute-start.19
  83.8 1.6 collective-permute-start.21
  85.3 2.0 %collective-permute-start.15 = (bf16[128,2048]{1,0:T(8,128)(2,1)}, bf16[128,2048]{1,0:T(8,128)(2,1)S(1)}, u32[]{:S(2)}, u32[]{:S(2)}) collective-permute-start(bf16[128,2048]{1,0:T(8,128)(2,1)} %get-tuple-element.50), channel_id=1, source_target_pairs={{0,2},{1,3},{2,0},{3,1},{4,6},{5,7},{6,4},{7,5},{8,10},{9,11},{10,... | collective-permute-start | bytes 1572872 | tf_op jit(solution)/shard_map/ppermute | solution.py:253
  87.3 10.9 %collective-permute-done.19 = bf16[128,2048]{1,0:T(8,128)(2,1)S(1)} collective-permute-done((bf16[128,2048]{1,0:T(8,128)(2,1)}, bf16[128,2048]{1,0:T(8,128)(2,1)S(1)}, u32[]{:S(2)}, u32[]{:S(2)}) %collective-permute-start.19) | collective-permute-done | bytes 524320 | tf_op jit(solution)/shard_map/ppermute | solution.py:253
  98.3 1.2 add.54
  99.4 2.3 %collective-permute-start.20 = (bf16[128,2048]{1,0:T(8,128)(2,1)S(1)}, bf16[128,2048]{1,0:T(8,128)(2,1)S(1)}, u32[]{:S(2)}, u32[]{:S(2)}) collective-permute-start(bf16[128,2048]{1,0:T(8,128)(2,1)S(1)} %add.54), channel_id=1, source_target_pairs={{0,4},{1,5},{2,6},{3,7},{4,0},{5,1},{6,2},{7,3},{8,12},{9,13},{10,... | collective-permute-start | bytes 1572872 | tf_op jit(solution)/shard_map/ppermute | solution.py:253
  101.7 1.3 collective-permute-done.16
  103.0 0.0 copy-start.9
  103.0 1.4 collective-permute-start.18
  104.4 4.6 %collective-permute-done.21 = bf16[128,2048]{1,0:T(8,128)(2,1)S(1)} collective-permute-done((bf16[128,2048]{1,0:T(8,128)(2,1)}, bf16[128,2048]{1,0:T(8,128)(2,1)S(1)}, u32[]{:S(2)}, u32[]{:S(2)}) %collective-permute-start.21) | collective-permute-done | bytes 524320 | tf_op jit(solution)/shard_map/ppermute | solution.py:253
  109.0 4.0 %collective-permute-done.20.refs_4_ = bf16[128,2048]{1,0:T(8,128)(2,1)S(1)} collective-permute-done((bf16[128,2048]{1,0:T(8,128)(2,1)S(1)}, bf16[128,2048]{1,0:T(8,128)(2,1)S(1)}, u32[]{:S(2)}, u32[]{:S(2)}) %collective-permute-start.20) | collective-permute-done | bytes 524320 | tf_op jit(solution)/shard_map/ppermute | solution.py:253
  113.1 0.8 copy-done.16
  113.9 0.6 copy-done.12
  114.5 2.3 %down_part.1 = bf16[8,128,256]{2,1,0:T(8,128)(2,1)} custom-call(s32[1]{0:T(128)} %bitcast.side, bf16[128,4096]{1,0:T(8,128)(2,1)} %tok.5, bf16[128,2048]{1,0:T(8,128)(2,1)} %copy-done.2, bf16[128,128]{1,0:T(8,128)(2,1)} %copy-done.9, bf16[128,128]{1,0:T(8,128)(2,1)} %copy-done.12), custom_call_target="tpu_custom_call" | custom-call | flops 300000000 | bytes 10485760 | tf_op jit(solution)/shard_map/down_part/pallas_call | solution.py:160
  116.8 8.5 %all-to-all-start = ((bf16[8,128,256]{2,1,0:T(8,128)(2,1)}), bf16[8,128,256]{2,1,0:T(8,128)(2,1)S(1)}, u32[]{:S(2)}, u32[]{:S(2)}) async-start(bf16[8,128,256]{2,1,0:T(8,128)(2,1)} %down_part.1), calls=%async_computation.1 | async-start | bytes 1048576 | tf_op jit(solution)/shard_map/all_to_all | solution.py:315
  125.3 0.1 add.55
  125.4 1.8 %collective-permute-start.23 = (bf16[128,2048]{1,0:T(8,128)(2,1)S(1)}, bf16[128,2048]{1,0:T(8,128)(2,1)S(1)}, u32[]{:S(2)}, u32[]{:S(2)}) collective-permute-start(bf16[128,2048]{1,0:T(8,128)(2,1)S(1)} %add.55), channel_id=1, source_target_pairs={{0,4},{1,5},{2,6},{3,7},{4,0},{5,1},{6,2},{7,3},{8,12},{9,13},{10,... | collective-permute-start | bytes 1572872 | tf_op jit(solution)/shard_map/ppermute | solution.py:253
  127.2 2.9 %collective-permute-start.22 = (bf16[128,2048]{1,0:T(8,128)(2,1)S(1)}, bf16[128,2048]{1,0:T(8,128)(2,1)}, u32[]{:S(2)}, u32[]{:S(2)}) collective-permute-start(bf16[128,2048]{1,0:T(8,128)(2,1)S(1)} %copy-done.14), channel_id=1, source_target_pairs={{0,2},{1,3},{2,0},{3,1},{4,6},{5,7},{6,4},{7,5},{8,10},{9,11},{10,... | collective-permute-start | bytes 1572872 | tf_op jit(solution)/shard_map/ppermute | solution.py:253
  130.1 1.0 dynamic-slice_bitcast_fusion
  131.1 0.7 collective-permute-start.24
  131.8 5.9 %collective-permute-done.23.refs_5_ = bf16[128,2048]{1,0:T(8,128)(2,1)S(1)} collective-permute-done((bf16[128,2048]{1,0:T(8,128)(2,1)S(1)}, bf16[128,2048]{1,0:T(8,128)(2,1)S(1)}, u32[]{:S(2)}, u32[]{:S(2)}) %collective-permute-start.23) | collective-permute-done | bytes 524320 | tf_op jit(solution)/shard_map/ppermute | solution.py:253
  137.7 0.8 copy-done.17
  138.5 4.4 %collective-permute-done.22.refs_3_ = bf16[128,2048]{1,0:T(8,128)(2,1)} collective-permute-done((bf16[128,2048]{1,0:T(8,128)(2,1)S(1)}, bf16[128,2048]{1,0:T(8,128)(2,1)}, u32[]{:S(2)}, u32[]{:S(2)}) %collective-permute-start.22) | collective-permute-done | bytes 524320 | tf_op jit(solution)/shard_map/ppermute | solution.py:253
  142.9 4.6 %token_grad.1 = bf16[128,4096]{1,0:T(8,128)(2,1)} custom-call(bf16[128,2048]{1,0:T(8,128)(2,1)} %get-tuple-element.38.low.refs_0_, bf16[128,2048]{1,0:T(8,128)(2,1)} %get-tuple-element.43.high.refs_1_, bf16[128,2048]{1,0:T(8,128)(2,1)} %copy-done.15, bf16[128,2048]{1,0:T(8,128)(2,1)} %collective-permute-done.22.refs_3_, bf16[128,2048]{1,0:T(8,128)(2,1)} %copy-done.16, ...), custom_call_target="tpu_custom_call" | custom-call | flops 2000000000 | bytes 17825792 | tf_op jit(solution)/shard_map/token_grad/pallas_call | solution.py:198
  147.5 0.1 convert_reduce_fusion
  147.6 0.8 copy.12
  148.4 1.8 %finish.1 = (f32[64,256]{1,0:T(8,128)}, f32[4,64,256]{2,1,0:T(8,128)}, f32[128,256]{1,0:T(8,128)}) custom-call(s32[1]{0:T(128)} %bitcast.side, bf16[2,448,256]{2,1,0:T(8,128)(2,1)} %bitcast.11, bf16[448,256]{1,0:T(8,128)(2,1)} %copy-done.8), custom_call_target="tpu_custom_call" | custom-call | flops 300000 | bytes 4194304 | tf_op jit(solution)/shard_map/finish/pallas_call | solution.py:227
  (52 shorter events, 0.2 us)
Async XLA Ops:
  7.2 14.2 %copy-start = (bf16[128,4096]{1,0:T(8,128)(2,1)S(1)}, bf16[128,4096]{1,0:T(8,128)(2,1)}, u32[]{:S(2)}) copy-start(bf16[128,4096]{1,0:T(8,128)(2,1)} %tok.5) | copy-start | bytes 3145732
  7.2 123.0 %reduce-scatter.2.cloned.1.call-start = ((), (), s32[]{:S(2)}) async-start(), calls=%async_computation.2 | async-start | bytes 4128768 | tf_op jit(solution)/shard_map/reduce_scatter | solution.py:263
  8.4 15.2 %collective-permute-start.2 = (bf16[128,2048]{1,0:T(8,128)(2,1)S(1)}, bf16[128,2048]{1,0:T(8,128)(2,1)S(1)}, u32[]{:S(2)}, u32[]{:S(2)}) collective-permute-start(bf16[128,2048]{1,0:T(8,128)(2,1)S(1)} %slice.6), channel_id=1, source_target_pairs={{0,4},{1,5},{2,6},{3,7},{4,0},{5,1},{6,2},{7,3},{8,12},{9,13},{10,... | collective-permute-start | bytes 1572872 | tf_op jit(solution)/shard_map/ppermute | solution.py:253
  10.7 31.3 %collective-permute-start = (bf16[128,4096]{1,0:T(8,128)(2,1)}, bf16[128,4096]{1,0:T(8,128)(2,1)}, u32[]{:S(2)}, u32[]{:S(2)}) collective-permute-start(bf16[128,4096]{1,0:T(8,128)(2,1)} %tok.5), channel_id=1, source_target_pairs={{0,1},{1,0},{2,3},{3,2},{4,5},{5,4},{6,7},{7,6},{8,9},{9,8},{10,11... | collective-permute-start | bytes 3145736 | tf_op jit(solution)/shard_map/ppermute | solution.py:253
  12.6 4.6 %collective-permute-start.3 = (f32[128,128]{1,0:T(8,128)S(1)}, f32[128,128]{1,0:T(8,128)S(1)}, u32[]{:S(2)}, u32[]{:S(2)}) collective-permute-start(f32[128,128]{1,0:T(8,128)S(1)} %fusion), channel_id=1, source_target_pairs={{0,12},{1,13},{2,14},{3,15},{4,8},{5,9},{6,10},{7,11},{8,4},{9,5},... | collective-permute-start | bytes 196616 | tf_op jit(solution)/shard_map/ppermute | solution.py:253
  17.2 6.3 %collective-permute-start.4 = (f32[128,128]{1,0:T(8,128)S(1)}, f32[128,128]{1,0:T(8,128)S(1)}, u32[]{:S(2)}, u32[]{:S(2)}) collective-permute-start(f32[128,128]{1,0:T(8,128)S(1)} %add.44), channel_id=1, source_target_pairs={{0,4},{1,5},{2,6},{3,7},{4,0},{5,1},{6,2},{7,3},{8,12},{9,13},{10,... | collective-permute-start | bytes 196616 | tf_op jit(solution)/shard_map/ppermute | solution.py:253
  18.6 16.2 %collective-permute-start.1 = (bf16[128,2048]{1,0:T(8,128)(2,1)S(1)}, bf16[128,2048]{1,0:T(8,128)(2,1)S(1)}, u32[]{:S(2)}, u32[]{:S(2)}) collective-permute-start(bf16[128,2048]{1,0:T(8,128)(2,1)S(1)} %slice.6), channel_id=1, source_target_pairs={{0,2},{1,3},{2,0},{3,1},{4,6},{5,7},{6,4},{7,5},{8,10},{9,11},{10,... | collective-permute-start | bytes 1572872 | tf_op jit(solution)/shard_map/ppermute | solution.py:253
  23.6 18.4 %copy-start.4 = (bf16[128,2048]{1,0:T(8,128)(2,1)}, bf16[128,2048]{1,0:T(8,128)(2,1)S(1)}, u32[]{:S(2)}) copy-start(bf16[128,2048]{1,0:T(8,128)(2,1)S(1)} %collective-permute-done.2.m4) | copy-start | bytes 1572868
  23.6 14.1 %collective-permute-start.9 = (bf16[128,2048]{1,0:T(8,128)(2,1)}, bf16[128,2048]{1,0:T(8,128)(2,1)S(1)}, u32[]{:S(2)}, u32[]{:S(2)}) collective-permute-start(bf16[128,2048]{1,0:T(8,128)(2,1)} %slice.7), channel_id=1, source_target_pairs={{0,4},{1,5},{2,6},{3,7},{4,0},{5,1},{6,2},{7,3},{8,12},{9,13},{10,... | collective-permute-start | bytes 1572872 | tf_op jit(solution)/shard_map/ppermute | solution.py:253
  23.9 17.2 %collective-permute-start.5 = (bf16[128,2048]{1,0:T(8,128)(2,1)S(1)}, bf16[128,2048]{1,0:T(8,128)(2,1)S(1)}, u32[]{:S(2)}, u32[]{:S(2)}) collective-permute-start(bf16[128,2048]{1,0:T(8,128)(2,1)S(1)} %collective-permute-done.2.m4), channel_id=1, source_target_pairs={{0,12},{1,13},{2,14},{3,15},{4,8},{5,9},{6,10},{7,11},{8,4},{9,5},... | collective-permute-start | bytes 1572872 | tf_op jit(solution)/shard_map/ppermute | solution.py:253
  26.5 8.3 %collective-permute-start.6 = (f32[128,128]{1,0:T(8,128)S(1)}, f32[128,128]{1,0:T(8,128)S(1)}, u32[]{:S(2)}, u32[]{:S(2)}) collective-permute-start(f32[128,128]{1,0:T(8,128)S(1)} %add.45), channel_id=1, source_target_pairs={{0,2},{1,3},{2,0},{3,1},{4,6},{5,7},{6,4},{7,5},{8,10},{9,11},{10,... | collective-permute-start | bytes 196616 | tf_op jit(solution)/shard_map/ppermute | solution.py:253
  34.8 7.2 %copy-start.5 = (bf16[128,2048]{1,0:T(8,128)(2,1)}, bf16[128,2048]{1,0:T(8,128)(2,1)S(1)}, u32[]{:S(2)}) copy-start(bf16[128,2048]{1,0:T(8,128)(2,1)S(1)} %collective-permute-done.1.m2) | copy-start | bytes 1572868
  34.8 14.9 %collective-permute-start.8 = (bf16[128,2048]{1,0:T(8,128)(2,1)}, bf16[128,2048]{1,0:T(8,128)(2,1)}, u32[]{:S(2)}, u32[]{:S(2)}) collective-permute-start(bf16[128,2048]{1,0:T(8,128)(2,1)} %slice.7), channel_id=1, source_target_pairs={{0,2},{1,3},{2,0},{3,1},{4,6},{5,7},{6,4},{7,5},{8,10},{9,11},{10,... | collective-permute-start | bytes 1572872 | tf_op jit(solution)/shard_map/ppermute | solution.py:253
  37.7 12.0 %copy-start.6 = (bf16[128,2048]{1,0:T(8,128)(2,1)}, bf16[128,2048]{1,0:T(8,128)(2,1)S(1)}, u32[]{:S(2)}) copy-start(bf16[128,2048]{1,0:T(8,128)(2,1)S(1)} %collective-permute-done.9.m4) | copy-start | bytes 1572868
  37.7 12.2 %collective-permute-start.10 = (bf16[128,2048]{1,0:T(8,128)(2,1)S(1)}, bf16[128,2048]{1,0:T(8,128)(2,1)}, u32[]{:S(2)}, u32[]{:S(2)}) collective-permute-start(bf16[128,2048]{1,0:T(8,128)(2,1)S(1)} %collective-permute-done.9.m4), channel_id=1, source_target_pairs={{0,12},{1,13},{2,14},{3,15},{4,8},{5,9},{6,10},{7,11},{8,4},{9,5},... | collective-permute-start | bytes 1572872 | tf_op jit(solution)/shard_map/ppermute | solution.py:253
  39.3 1.3 collective-permute-start.7
  41.2 0.8 copy-start.7
  57.6 1.2 copy-start.1
  57.6 1.9 %copy-start.10 = (f32[128,128]{1,0:T(8,128)S(1)}, f32[128,128]{1,0:T(8,128)}, u32[]{:S(2)}) copy-start(f32[128,128]{1,0:T(8,128)} %get-tuple-element.45) | copy-start | bytes 196612
  57.6 1.9 %copy-start.11 = (f32[128,128]{1,0:T(8,128)S(1)}, f32[128,128]{1,0:T(8,128)}, u32[]{:S(2)}) copy-start(f32[128,128]{1,0:T(8,128)} %get-tuple-element.46) | copy-start | bytes 196612
  58.9 14.0 %collective-permute-start.12 = (bf16[128,2048]{1,0:T(8,128)(2,1)S(1)}, bf16[128,2048]{1,0:T(8,128)(2,1)S(1)}, u32[]{:S(2)}, u32[]{:S(2)}) collective-permute-start(bf16[128,2048]{1,0:T(8,128)(2,1)S(1)} %constant_dynamic-slice_fusion), channel_id=1, source_target_pairs={{0,128},{16,144},{32,160},{48,176},{64,192},{80,208},{96,224},{112... | collective-permute-start | bytes 1572872 | tf_op jit(solution)/shard_map/ppermute | solution.py:270
  59.6 13.3 %collective-permute-start.11 = (f32[128,128]{1,0:T(8,128)S(1)}, f32[128,128]{1,0:T(8,128)S(1)}, u32[]{:S(2)}, u32[]{:S(2)}) collective-permute-start(f32[128,128]{1,0:T(8,128)S(1)} %add.48), channel_id=1, source_target_pairs={{0,12},{1,13},{2,14},{3,15},{4,8},{5,9},{6,10},{7,11},{8,4},{9,5},... | collective-permute-start | bytes 196616 | tf_op jit(solution)/shard_map/ppermute | solution.py:253
  67.8 57.4 %copy-start.3 = (bf16[128,2048]{1,0:T(8,128)(2,1)S(1)}, bf16[128,2048]{1,0:T(8,128)(2,1)}, u32[]{:S(2)}) copy-start(bf16[128,2048]{1,0:T(8,128)(2,1)} %get-tuple-element.62) | copy-start | bytes 1572868
  67.8 59.4 %copy-start.14 = (bf16[128,2048]{1,0:T(8,128)(2,1)S(1)}, bf16[128,2048]{1,0:T(8,128)(2,1)}, u32[]{:S(2)}) copy-start(bf16[128,2048]{1,0:T(8,128)(2,1)} %get-tuple-element.61) | copy-start | bytes 1572868
  72.9 41.0 %copy-start.2 = (bf16[128,2048]{1,0:T(8,128)(2,1)}, bf16[128,2048]{1,0:T(8,128)(2,1)S(1)}, u32[]{:S(2)}) copy-start(bf16[128,2048]{1,0:T(8,128)(2,1)S(1)} %collective-permute-done.12.others) | copy-start | bytes 1572868
  72.9 4.4 %collective-permute-start.13 = (f32[128,128]{1,0:T(8,128)S(1)}, f32[128,128]{1,0:T(8,128)S(1)}, u32[]{:S(2)}, u32[]{:S(2)}) collective-permute-start(f32[128,128]{1,0:T(8,128)S(1)} %add.50), channel_id=1, source_target_pairs={{0,4},{1,5},{2,6},{3,7},{4,0},{5,1},{6,2},{7,3},{8,12},{9,13},{10,... | collective-permute-start | bytes 196616 | tf_op jit(solution)/shard_map/ppermute | solution.py:253
  77.3 5.9 %collective-permute-start.14 = (f32[128,128]{1,0:T(8,128)S(1)}, f32[128,128]{1,0:T(8,128)S(1)}, u32[]{:S(2)}, u32[]{:S(2)}) collective-permute-start(f32[128,128]{1,0:T(8,128)S(1)} %add.51), channel_id=1, source_target_pairs={{0,2},{1,3},{2,0},{3,1},{4,6},{5,7},{6,4},{7,5},{8,10},{9,11},{10,... | collective-permute-start | bytes 196616 | tf_op jit(solution)/shard_map/ppermute | solution.py:253
  83.1 19.8 %collective-permute-start.17 = (bf16[128,4096]{1,0:T(8,128)(2,1)}, bf16[128,4096]{1,0:T(8,128)(2,1)S(1)}, u32[]{:S(2)}, u32[]{:S(2)}) collective-permute-start(bf16[128,4096]{1,0:T(8,128)(2,1)} %get-tuple-element.52), channel_id=1, source_target_pairs={{0,1},{1,0},{2,3},{3,2},{4,5},{5,4},{6,7},{7,6},{8,9},{9,8},{10,11... | collective-permute-start | bytes 3145736 | tf_op jit(solution)/shard_map/ppermute | solution.py:253
  83.2 15.0 %collective-permute-start.19 = (bf16[128,2048]{1,0:T(8,128)(2,1)}, bf16[128,2048]{1,0:T(8,128)(2,1)S(1)}, u32[]{:S(2)}, u32[]{:S(2)}) collective-permute-start(bf16[128,2048]{1,0:T(8,128)(2,1)} %get-tuple-element.56), channel_id=1, source_target_pairs={{0,12},{1,13},{2,14},{3,15},{4,8},{5,9},{6,10},{7,11},{8,4},{9,5},... | collective-permute-start | bytes 1572872 | tf_op jit(solution)/shard_map/ppermute | solution.py:253
  83.8 25.2 %collective-permute-start.21 = (bf16[128,2048]{1,0:T(8,128)(2,1)}, bf16[128,2048]{1,0:T(8,128)(2,1)S(1)}, u32[]{:S(2)}, u32[]{:S(2)}) collective-permute-start(bf16[128,2048]{1,0:T(8,128)(2,1)} %get-tuple-element.59), channel_id=1, source_target_pairs={{0,12},{1,13},{2,14},{3,15},{4,8},{5,9},{6,10},{7,11},{8,4},{9,5},... | collective-permute-start | bytes 1572872 | tf_op jit(solution)/shard_map/ppermute | solution.py:253
  85.3 23.7 %collective-permute-start.15 = (bf16[128,2048]{1,0:T(8,128)(2,1)}, bf16[128,2048]{1,0:T(8,128)(2,1)S(1)}, u32[]{:S(2)}, u32[]{:S(2)}) collective-permute-start(bf16[128,2048]{1,0:T(8,128)(2,1)} %get-tuple-element.50), channel_id=1, source_target_pairs={{0,2},{1,3},{2,0},{3,1},{4,6},{5,7},{6,4},{7,5},{8,10},{9,11},{10,... | collective-permute-start | bytes 1572872 | tf_op jit(solution)/shard_map/ppermute | solution.py:253
  99.4 13.6 %collective-permute-start.20 = (bf16[128,2048]{1,0:T(8,128)(2,1)S(1)}, bf16[128,2048]{1,0:T(8,128)(2,1)S(1)}, u32[]{:S(2)}, u32[]{:S(2)}) collective-permute-start(bf16[128,2048]{1,0:T(8,128)(2,1)S(1)} %add.54), channel_id=1, source_target_pairs={{0,4},{1,5},{2,6},{3,7},{4,0},{5,1},{6,2},{7,3},{8,12},{9,13},{10,... | collective-permute-start | bytes 1572872 | tf_op jit(solution)/shard_map/ppermute | solution.py:253
  101.7 1.3 collective-permute-start.16
  103.0 10.1 %copy-start.13 = (bf16[128,4096]{1,0:T(8,128)(2,1)}, bf16[128,4096]{1,0:T(8,128)(2,1)S(1)}, u32[]{:S(2)}) copy-start(bf16[128,4096]{1,0:T(8,128)(2,1)S(1)} %collective-permute-done.17.refs_6_) | copy-start | bytes 3145732
  103.0 10.9 %copy-start.9 = (bf16[128,128]{1,0:T(8,128)(2,1)}, bf16[128,128]{1,0:T(8,128)(2,1)S(1)}, u32[]{:S(2)}) copy-start(bf16[128,128]{1,0:T(8,128)(2,1)S(1)} %add_convert_fusion.lat.refs_9_) | copy-start | bytes 98308
  103.0 10.1 %collective-permute-start.18 = (bf16[128,128]{1,0:T(8,128)(2,1)S(1)}, bf16[128,128]{1,0:T(8,128)(2,1)S(1)}, u32[]{:S(2)}, u32[]{:S(2)}) collective-permute-start(bf16[128,128]{1,0:T(8,128)(2,1)S(1)} %add_convert_fusion.lat.refs_9_), channel_id=1, source_target_pairs={{0,128},{16,144},{32,160},{48,176},{64,192},{80,208},{96,224},{112... | collective-permute-start | bytes 98312 | tf_op jit(solution)/shard_map/ppermute | solution.py:270
  109.0 16.2 %copy-start.15 = (bf16[128,2048]{1,0:T(8,128)(2,1)}, bf16[128,2048]{1,0:T(8,128)(2,1)S(1)}, u32[]{:S(2)}) copy-start(bf16[128,2048]{1,0:T(8,128)(2,1)S(1)} %collective-permute-done.15.refs_2_) | copy-start | bytes 1572868
  113.1 0.8 copy-start.16
  113.9 0.6 copy-start.12
  116.8 30.7 %all-to-all-start = ((bf16[8,128,256]{2,1,0:T(8,128)(2,1)}), bf16[8,128,256]{2,1,0:T(8,128)(2,1)S(1)}, u32[]{:S(2)}, u32[]{:S(2)}) async-start(bf16[8,128,256]{2,1,0:T(8,128)(2,1)} %down_part.1), calls=%async_computation.1 | async-start | bytes 1048576 | tf_op jit(solution)/shard_map/all_to_all | solution.py:315
  125.4 12.3 %collective-permute-start.23 = (bf16[128,2048]{1,0:T(8,128)(2,1)S(1)}, bf16[128,2048]{1,0:T(8,128)(2,1)S(1)}, u32[]{:S(2)}, u32[]{:S(2)}) collective-permute-start(bf16[128,2048]{1,0:T(8,128)(2,1)S(1)} %add.55), channel_id=1, source_target_pairs={{0,4},{1,5},{2,6},{3,7},{4,0},{5,1},{6,2},{7,3},{8,12},{9,13},{10,... | collective-permute-start | bytes 1572872 | tf_op jit(solution)/shard_map/ppermute | solution.py:253
  127.2 15.7 %collective-permute-start.22 = (bf16[128,2048]{1,0:T(8,128)(2,1)S(1)}, bf16[128,2048]{1,0:T(8,128)(2,1)}, u32[]{:S(2)}, u32[]{:S(2)}) collective-permute-start(bf16[128,2048]{1,0:T(8,128)(2,1)S(1)} %copy-done.14), channel_id=1, source_target_pairs={{0,2},{1,3},{2,0},{3,1},{4,6},{5,7},{6,4},{7,5},{8,10},{9,11},{10,... | collective-permute-start | bytes 1572872 | tf_op jit(solution)/shard_map/ppermute | solution.py:253
  131.1 16.4 %collective-permute-start.24 = (bf16[448,256]{1,0:T(8,128)(2,1)S(1)}, bf16[448,256]{1,0:T(8,128)(2,1)S(1)}, u32[]{:S(2)}, u32[]{:S(2)}) collective-permute-start(bf16[448,256]{1,0:T(8,128)(2,1)S(1)} %dynamic-slice_bitcast_fusion), channel_id=1, source_target_pairs={{0,128},{16,144},{32,160},{48,176},{64,192},{80,208},{96,224},{112... | collective-permute-start | bytes 688136 | tf_op jit(solution)/shard_map/ppermute | solution.py:270
  137.7 0.8 copy-start.17
  147.5 0.9 copy-start.8
Sparse Core Ops, SparseCore 0:
  57.8 53.0 reduce-scatter.1

commit v9 on v7

--- a/solution.py
+++ b/solution.py
@@ -145,35 +145,38 @@
     )(*slopes, section)
 
 
-def down_kernel(side, tok, others, lat, lat_others, out):
+def down_kernel(place, tok, others, lat, lat_others, out):
     both = jnp.concatenate([lat[...], lat_others[...]], axis=0)
-    for c in range(tok.shape[1] // CHUNK):
+    count = tok.shape[1] // CHUNK
+    for c in range(count):
         cs = slice(c * CHUNK, (c + 1) * CHUNK)
-        out[c] = dot(both, jnp.concatenate([tok[:, cs], others[:, cs]], axis=0), 0, 0).astype(BF16)
-
-
-def run_down(x, tokens, others, latent_grad, latent_others):
+        bits = (pl.program_id(0) * count + c) ^ place[1]
+        slot = (bits & 1) * 4 + (bits & 2) + bits // 4
+        out[slot] = dot(both, jnp.concatenate([tok[:, cs], others[:, cs]], axis=0), 0, 0).astype(BF16)
+
+
+def run_down(x, z, tokens, others, latent_grad, latent_others):
     rows, half = others.shape
     rank = latent_grad.shape[1]
     step = half // 2
-    square = pl.BlockSpec((rows, rank), lambda i, side: (0, 0))
+    square = pl.BlockSpec((rows, rank), lambda i, place: (0, 0))
     return pl.pallas_call(
         down_kernel,
         grid_spec=pltpu.PrefetchScalarGridSpec(
             num_scalar_prefetch=1,
             grid=(2,),
             in_specs=[
-                pl.BlockSpec((rows, step), lambda i, side: (0, 2 * side[0] + i)),
-                pl.BlockSpec((rows, step), lambda i, side: (0, i)),
+                pl.BlockSpec((rows, step), lambda i, place: (0, 2 * place[0] + i)),
+                pl.BlockSpec((rows, step), lambda i, place: (0, i)),
                 square,
                 square,
             ],
-            out_specs=pl.BlockSpec((RING // 2, rank, CHUNK), lambda i, side: (i, 0, 0)),
+            out_specs=pl.BlockSpec((RING, rank, CHUNK), lambda i, place: (0, 0, 0)),
         ),
         out_shape=jax.ShapeDtypeStruct((RING, rank, CHUNK), BF16),
         cost_estimate=pl.CostEstimate(flops=300_000_000, bytes_accessed=10 << 20, transcendentals=0),
         name="down_part",
-    )(jnp.full((1,), x, jnp.int32), tokens, others, latent_grad, latent_others)
+    )(jnp.stack([x, z]).astype(jnp.int32), tokens, others, latent_grad, latent_others)
 
 
 def final_kernel(*refs):
@@ -308,16 +311,20 @@
     part = part + after(flip(part, 1), r1)
     latent_grad = part.astype(BF16)
 
-    pair = run_down(x, tokens, others, latent_grad, after(cross(latent_grad), r2_0))
-    s0 = flip(b4_0 + after(q0, pair), 4)
-    r2_1 = flip(after(b2_1, pair), 2)
-    pair = after(pair, q0)
-    groups = [[side * RING + z for z in range(RING)] for side in range(2)]
-    pair = lax.all_to_all(pair, "dp", 0, 0, axis_index_groups=groups, tiled=True)
-    s1 = flip(b4_1 + q1, 4)
+    z = lax.axis_index("dp") % RING
+    left = run_down(x, z, tokens, others, latent_grad, after(cross(latent_grad), r2_0))
+    s0 = flip(b4_0 + after(q0, left), 4)
+    r2_1 = flip(after(b2_1, left), 2)
+    s1 = flip(b4_1 + after(q1, left), 4)
     other = lax.dynamic_index_in_dim(summed, 1 - x, 0, keepdims=False)
     arrived = cross(other)
-    down_grad = (jnp.sum(after(pair, arrived).astype(F32), axis=0) * scale).T
+    for mask, events in ((1, (q1,)), (2, (s0,)), (4, (s1, r2_1, arrived))):
+        count = left.shape[0] // 2
+        got = lax.ppermute(left[count:], "dp", [(i, i ^ mask) for i in range(2 * RING)])
+        left = left[:count].astype(F32) + after(got, *events).astype(F32)
+        if mask < 4:
+            left = left.astype(BF16)
+    down_grad = (left[0] * scale).T
     pairs = ((slope0, slope1), (r2_0, r2_1), (s0, after(s1, other)))
     token_grad = run_final(pairs, r1, diag_factor, low_down, latent_grad)
     diag_grad, section_grad, up_grad = run_finish(x, summed, arrived, scale)

time: 150 us -> 150 us (level)
  waiting for transfers between devices: 49 us -> 42.7 us
  starting transfers between devices: 42.7 us -> 47.8 us
  local copies, waits for them, and re-layouts: 7.98 us -> 9.85 us
    ppermute x0 -> x3, starting transfers between devices: none -> 12 us  [per_device(): lax.ppermute(left[count:], 'dp', [(i, i ^ mask) for i in range(2 * RING)])]
    ppermute x22, waiting for transfers between devices: 43.9 us -> 32.1 us  [flip(): return lax.ppermute(value, 'tensor', [(i, i ^ mask) for i in range(16)])]
    all_to_all x1 -> x0, starting transfers between devices: 8.47 us -> none  [per_device(): lax.all_to_all(pair, 'dp', 0, 0, axis_index_groups=groups, tiled=True)]
    ppermute x0 -> x3, waiting for transfers between devices: none -> 5.55 us  [per_device(): lax.ppermute(left[count:], 'dp', [(i, i ^ mask) for i in range(2 * RING)])]
  transfers between devices with their start and end apart: 27 -> 29, of which waited for: 11 -> 11; matrix products, arithmetic and copies ran while one was open for 4% -> 4% of each run, Pallas kernels for 14% -> 15%
where the time goes in v9:
time: 150 us
  starting transfers between devices  47.8 us (32%)
  waiting for transfers between devices  42.7 us (28%)
  Pallas kernels  31.3 us (21%)
  between operations  14.3 us (10%)
  local copies, waits for them, and re-layouts  9.85 us (7%)
  matrix products  1.96 us (1%)
  other arithmetic  1.65 us (1%)
    ppermute x22, starting transfers between devices, flip(): return lax.ppermute(value, 'tensor', [(i, i ^ mask) for i in range(16)])  33 us
    ppermute x22, waiting for transfers between devices, flip(): return lax.ppermute(value, 'tensor', [(i, i ^ mask) for i in range(16)])  32.1 us
    pallas_call x2, Pallas kernels, run_main(): pl.pallas_call(main_kernel, grid=(steps,), in_specs=in_specs, out_specs=[...  15.4 us
    ppermute x3, starting transfers between devices, per_device(): lax.ppermute(left[count:], 'dp', [(i, i ^ mask) for i in range(2 * RING)])  12 us
    pallas_call x1, Pallas kernels, run_back(): pl.pallas_call(back_kernel, grid=(2,), in_specs=[fixed, fixed, pl.BlockSp...  6.4 us
    unnamed x37, local copies, waits for them, and re-layouts  5.8 us
    ppermute x3, waiting for transfers between devices, per_device(): lax.ppermute(left[count:], 'dp', [(i, i ^ mask) for i in range(2 * RING)])  5.55 us
    ppermute x3, waiting for transfers between devices, cross(): return lax.ppermute(value, 'dp', [(i, i ^ RING) for i in range(2 * RING)])  5.03 us
  transfers between devices with their start and end apart: 29, of which 11 were waited for; matrix products, arithmetic and copies ran while one was open for 4% of the time, Pallas kernels for 15%

profile of v9, /device:TPU:8, one launch (start us, length us, event | category | flops | bytes accessed | tf_op | source)
XLA Modules:
  0.0 149.6 jit_solution(17615024781901724733)
XLA Ops:
  7.2 0.0 copy-start
  7.2 0.0 reduce-scatter.2.cloned.1.call-start
  7.2 1.2 slice.24
  8.4 2.3 %collective-permute-start.2 = (bf16[128,2048]{1,0:T(8,128)(2,1)S(1)}, bf16[128,2048]{1,0:T(8,128)(2,1)S(1)}, u32[]{:S(2)}, u32[]{:S(2)}) collective-permute-start(bf16[128,2048]{1,0:T(8,128)(2,1)S(1)} %slice.24), channel_id=1, source_target_pairs={{0,4},{1,5},{2,6},{3,7},{4,0},{5,1},{6,2},{7,3},{8,12},{9,13},{10,... | collective-permute-start | bytes 1572872 | tf_op jit(solution)/shard_map/ppermute | solution.py:256
  10.7 2.0 %fusion = f32[128,128]{1,0:T(8,128)S(1)} fusion(bf16[128,4096]{1,0:T(8,128)(2,1)} %tok.5, bf16[4096,128]{1,0:T(8,128)(2,1)} %refs_8_.1), kind=kOutput, calls=%fused_computation.8 | convolution fusion | flops 134217728 | bytes 2162688 | tf_op jit(solution)/shard_map/dot_general | solution.py:285
  12.6 0.8 collective-permute-start.3
  13.4 3.8 %collective-permute-done.3 = f32[128,128]{1,0:T(8,128)S(1)} collective-permute-done((f32[128,128]{1,0:T(8,128)S(1)}, f32[128,128]{1,0:T(8,128)S(1)}, u32[]{:S(2)}, u32[]{:S(2)}) %collective-permute-start.3) | collective-permute-done | bytes 65568 | tf_op jit(solution)/shard_map/ppermute | solution.py:256
  17.2 1.4 collective-permute-start.4
  18.6 2.8 %collective-permute-start.1 = (bf16[128,2048]{1,0:T(8,128)(2,1)S(1)}, bf16[128,2048]{1,0:T(8,128)(2,1)S(1)}, u32[]{:S(2)}, u32[]{:S(2)}) collective-permute-start(bf16[128,2048]{1,0:T(8,128)(2,1)S(1)} %slice.24), channel_id=1, source_target_pairs={{0,2},{1,3},{2,0},{3,1},{4,6},{5,7},{6,4},{7,5},{8,10},{9,11},{10,... | collective-permute-start | bytes 1572872 | tf_op jit(solution)/shard_map/ppermute | solution.py:256
  21.4 0.8 slice.25
  22.2 1.3 collective-permute-done.4
  23.6 0.4 collective-permute-start.9
  23.9 2.6 %collective-permute-start.5 = (bf16[128,2048]{1,0:T(8,128)(2,1)S(1)}, bf16[128,2048]{1,0:T(8,128)(2,1)S(1)}, u32[]{:S(2)}, u32[]{:S(2)}) collective-permute-start(bf16[128,2048]{1,0:T(8,128)(2,1)S(1)} %collective-permute-done.2.m4), channel_id=1, source_target_pairs={{0,12},{1,13},{2,14},{3,15},{4,8},{5,9},{6,10},{7,11},{8,4},{9,5},... | collective-permute-start | bytes 1572872 | tf_op jit(solution)/shard_map/ppermute | solution.py:256
  26.5 3.0 %collective-permute-start.6 = (f32[128,128]{1,0:T(8,128)S(1)}, f32[128,128]{1,0:T(8,128)S(1)}, u32[]{:S(2)}, u32[]{:S(2)}) collective-permute-start(f32[128,128]{1,0:T(8,128)S(1)} %add.58), channel_id=1, source_target_pairs={{0,2},{1,3},{2,0},{3,1},{4,6},{5,7},{6,4},{7,5},{8,10},{9,11},{10,... | collective-permute-start | bytes 196616 | tf_op jit(solution)/shard_map/ppermute | solution.py:256
  29.5 5.3 %collective-permute-done.6 = f32[128,128]{1,0:T(8,128)S(1)} collective-permute-done((f32[128,128]{1,0:T(8,128)S(1)}, f32[128,128]{1,0:T(8,128)S(1)}, u32[]{:S(2)}, u32[]{:S(2)}) %collective-permute-start.6) | collective-permute-done | bytes 65568 | tf_op jit(solution)/shard_map/ppermute | solution.py:256
  34.8 2.9 %collective-permute-start.8 = (bf16[128,2048]{1,0:T(8,128)(2,1)}, bf16[128,2048]{1,0:T(8,128)(2,1)}, u32[]{:S(2)}, u32[]{:S(2)}) collective-permute-start(bf16[128,2048]{1,0:T(8,128)(2,1)} %slice.25), channel_id=1, source_target_pairs={{0,2},{1,3},{2,0},{3,1},{4,6},{5,7},{6,4},{7,5},{8,10},{9,11},{10,... | collective-permute-start | bytes 1572872 | tf_op jit(solution)/shard_map/ppermute | solution.py:256
  37.7 1.6 %collective-permute-start.10 = (bf16[128,2048]{1,0:T(8,128)(2,1)S(1)}, bf16[128,2048]{1,0:T(8,128)(2,1)}, u32[]{:S(2)}, u32[]{:S(2)}) collective-permute-start(bf16[128,2048]{1,0:T(8,128)(2,1)S(1)} %collective-permute-done.9.m4), channel_id=1, source_target_pairs={{0,12},{1,13},{2,14},{3,15},{4,8},{5,9},{6,10},{7,11},{8,4},{9,5},... | collective-permute-start | bytes 1572872 | tf_op jit(solution)/shard_map/ppermute | solution.py:256
  39.3 1.3 collective-permute-done.7
  40.5 0.6 add_convert_fusion.3.latent
  41.2 0.8 copy-done.9
  42.0 7.7 %main_part.2 = (bf16[128,2048]{1,0:T(8,128)(2,1)}, f32[128,128]{1,0:T(8,128)}, bf16[8,2,448,256]{3,2,1,0:T(8,128)(2,1)}) custom-call(bf16[128,4096]{1,0:T(8,128)(2,1)} %tok.5, bf16[128,4096]{1,0:T(8,128)(2,1)} %collective-permute-done.m1, bf16[128,2048]{1,0:T(8,128)(2,1)} %copy-done.7, bf16[128,2048]{1,0:T(8,128)(2,1)} %copy-done.6, ...), custom_call_target="tpu_custom_call" | custom-call | flops 2000000000 | bytes 29360128 | tf_op jit(solution)/shard_map/main_part/pallas_call | solution.py:89
  49.7 0.1 collective-permute-done.10.m8
  49.9 7.7 %main_part.3 = (bf16[128,2048]{1,0:T(8,128)(2,1)}, f32[128,128]{1,0:T(8,128)}, bf16[8,2,448,256]{3,2,1,0:T(8,128)(2,1)}) custom-call(bf16[128,4096]{1,0:T(8,128)(2,1)} %tok.5, bf16[128,4096]{1,0:T(8,128)(2,1)} %collective-permute-done.m1, bf16[128,2048]{1,0:T(8,128)(2,1)} %collective-permute-done.8.m2, ...), custom_call_target="tpu_custom_call", output_to_operand_aliasing={{2}: (10, {})} | custom-call | flops 2000000000 | bytes 29360128 | tf_op jit(solution)/shard_map/main_part/pallas_call | solution.py:89
  57.6 0.0 copy-start.13
  57.6 0.0 reduce-scatter.2.cloned.1.call-update
  57.7 1.1 copy-done.1
  58.9 0.7 collective-permute-start.12
  59.6 1.8 %collective-permute-start.11 = (f32[128,128]{1,0:T(8,128)S(1)}, f32[128,128]{1,0:T(8,128)S(1)}, u32[]{:S(2)}, u32[]{:S(2)}) collective-permute-start(f32[128,128]{1,0:T(8,128)S(1)} %add.61), channel_id=1, source_target_pairs={{0,12},{1,13},{2,14},{3,15},{4,8},{5,9},{6,10},{7,11},{8,4},{9,5},... | collective-permute-start | bytes 196616 | tf_op jit(solution)/shard_map/ppermute | solution.py:256
  61.4 6.4 %back_products.1 = (bf16[128,4096]{1,0:T(8,128)(2,1)}, bf16[128,2048]{1,0:T(8,128)(2,1)}, bf16[128,2048]{1,0:T(8,128)(2,1)}, bf16[128,2048]{1,0:T(8,128)(2,1)}, ...) custom-call(bf16[128,2048]{1,0:T(8,128)(2,1)} %get-tuple-element.41.low.refs_0_, ...), custom_call_target="tpu_custom_call" | custom-call | flops 2000000000 | bytes 20971520 | tf_op jit(solution)/shard_map/back_products/pallas_call | solution.py:136
  67.8 5.0 %collective-permute-done.12.others = bf16[128,2048]{1,0:T(8,128)(2,1)S(1)} collective-permute-done((bf16[128,2048]{1,0:T(8,128)(2,1)S(1)}, bf16[128,2048]{1,0:T(8,128)(2,1)S(1)}, u32[]{:S(2)}, u32[]{:S(2)}) %collective-permute-start.12) | collective-permute-done | bytes 524320 | tf_op jit(solution)/shard_map/ppermute | solution.py:273
  72.9 2.1 %collective-permute-start.13 = (f32[128,128]{1,0:T(8,128)S(1)}, f32[128,128]{1,0:T(8,128)S(1)}, u32[]{:S(2)}, u32[]{:S(2)}) collective-permute-start(f32[128,128]{1,0:T(8,128)S(1)} %add.63), channel_id=1, source_target_pairs={{0,2},{1,3},{2,0},{3,1},{4,6},{5,7},{6,4},{7,5},{8,10},{9,11},{10,... | collective-permute-start | bytes 196616 | tf_op jit(solution)/shard_map/ppermute | solution.py:256
  75.0 3.8 %collective-permute-done.13 = f32[128,128]{1,0:T(8,128)S(1)} collective-permute-done((f32[128,128]{1,0:T(8,128)S(1)}, f32[128,128]{1,0:T(8,128)S(1)}, u32[]{:S(2)}, u32[]{:S(2)}) %collective-permute-start.13) | collective-permute-done | bytes 65568 | tf_op jit(solution)/shard_map/ppermute | solution.py:256
  78.8 0.1 collective-permute-start.17
  78.9 2.1 %collective-permute-start.14 = (bf16[128,2048]{1,0:T(8,128)(2,1)}, bf16[128,2048]{1,0:T(8,128)(2,1)}, u32[]{:S(2)}, u32[]{:S(2)}) collective-permute-start(bf16[128,2048]{1,0:T(8,128)(2,1)} %get-tuple-element.53), channel_id=1, source_target_pairs={{0,2},{1,3},{2,0},{3,1},{4,6},{5,7},{6,4},{7,5},{8,10},{9,11},{10,... | collective-permute-start | bytes 1572872 | tf_op jit(solution)/shard_map/ppermute | solution.py:256
  80.9 1.9 %collective-permute-start.15 = (f32[128,128]{1,0:T(8,128)S(1)}, f32[128,128]{1,0:T(8,128)S(1)}, u32[]{:S(2)}, u32[]{:S(2)}) collective-permute-start(f32[128,128]{1,0:T(8,128)S(1)} %add.64), channel_id=1, source_target_pairs={{0,4},{1,5},{2,6},{3,7},{4,0},{5,1},{6,2},{7,3},{8,12},{9,13},{10,... | collective-permute-start | bytes 196616 | tf_op jit(solution)/shard_map/ppermute | solution.py:256
  82.8 2.4 %collective-permute-done.15 = f32[128,128]{1,0:T(8,128)S(1)} collective-permute-done((f32[128,128]{1,0:T(8,128)S(1)}, f32[128,128]{1,0:T(8,128)S(1)}, u32[]{:S(2)}, u32[]{:S(2)}) %collective-permute-start.15) | collective-permute-done | bytes 65568 | tf_op jit(solution)/shard_map/ppermute | solution.py:256
  85.2 0.1 collective-permute-start.16
  85.3 0.5 collective-permute-start.20
  85.8 1.6 %collective-permute-start.22 = (bf16[128,2048]{1,0:T(8,128)(2,1)}, bf16[128,2048]{1,0:T(8,128)(2,1)S(1)}, u32[]{:S(2)}, u32[]{:S(2)}) collective-permute-start(bf16[128,2048]{1,0:T(8,128)(2,1)} %get-tuple-element.65), channel_id=1, source_target_pairs={{0,12},{1,13},{2,14},{3,15},{4,8},{5,9},{6,10},{7,11},{8,4},{9,5},... | collective-permute-start | bytes 1572872 | tf_op jit(solution)/shard_map/ppermute | solution.py:256
  87.5 0.7 collective-permute-start.18
  88.2 0.6 pad_add_fusion.place
  88.7 6.6 %collective-permute-done.14.refs_2_ = bf16[128,2048]{1,0:T(8,128)(2,1)} collective-permute-done((bf16[128,2048]{1,0:T(8,128)(2,1)}, bf16[128,2048]{1,0:T(8,128)(2,1)}, u32[]{:S(2)}, u32[]{:S(2)}) %collective-permute-start.14) | collective-permute-done | bytes 524320 | tf_op jit(solution)/shard_map/ppermute | solution.py:256
  95.4 0.6 copy-done.14
  96.0 3.1 %down_part.1 = bf16[8,128,256]{2,1,0:T(8,128)(2,1)} custom-call(s32[2]{0:T(128)} %pad_add_fusion.place, bf16[128,4096]{1,0:T(8,128)(2,1)} %tok.5, bf16[128,2048]{1,0:T(8,128)(2,1)} %copy-done.4, bf16[128,128]{1,0:T(8,128)(2,1)} %copy-done.11, bf16[128,128]{1,0:T(8,128)(2,1)} %copy-done.14), custom_call_target="tpu_custom_call" | custom-call | flops 300000000 | bytes 10485760 | tf_op jit(solution)/shard_map/down_part/pallas_call | solution.py:163
  99.1 1.0 slice.33
  100.1 2.0 %collective-permute-start.25 = (bf16[4,128,256]{2,1,0:T(8,128)(2,1)S(1)}, bf16[4,128,256]{2,1,0:T(8,128)(2,1)S(1)}, u32[]{:S(2)}, u32[]{:S(2)}) collective-permute-start(bf16[4,128,256]{2,1,0:T(8,128)(2,1)S(1)} %slice.33), channel_id=1, source_target_pairs={{0,16},{16,0},{32,48},{48,32},{64,80},{80,64},{96,112},{112,96},{1... | collective-permute-start | bytes 786440 | tf_op jit(solution)/shard_map/ppermute | solution.py:323
  102.1 0.1 add.68
  102.3 1.4 collective-permute-start.21
  103.7 7.5 %collective-permute-done.22 = bf16[128,2048]{1,0:T(8,128)(2,1)S(1)} collective-permute-done((bf16[128,2048]{1,0:T(8,128)(2,1)}, bf16[128,2048]{1,0:T(8,128)(2,1)S(1)}, u32[]{:S(2)}, u32[]{:S(2)}) %collective-permute-start.22) | collective-permute-done | bytes 524320 | tf_op jit(solution)/shard_map/ppermute | solution.py:256
  111.1 0.1 add.69
  111.3 3.2 %collective-permute-start.23 = (bf16[128,2048]{1,0:T(8,128)(2,1)S(1)}, bf16[128,2048]{1,0:T(8,128)(2,1)S(1)}, u32[]{:S(2)}, u32[]{:S(2)}) collective-permute-start(bf16[128,2048]{1,0:T(8,128)(2,1)S(1)} %add.69), channel_id=1, source_target_pairs={{0,4},{1,5},{2,6},{3,7},{4,0},{5,1},{6,2},{7,3},{8,12},{9,13},{10,... | collective-permute-start | bytes 1572872 | tf_op jit(solution)/shard_map/ppermute | solution.py:256
  114.4 0.6 collective-permute-start.19
  115.1 0.1 add_convert_fusion
  115.2 3.4 %collective-permute-start.26 = (bf16[2,128,256]{2,1,0:T(8,128)(2,1)S(1)}, bf16[2,128,256]{2,1,0:T(8,128)(2,1)S(1)}, u32[]{:S(2)}, u32[]{:S(2)}) collective-permute-start(bf16[2,128,256]{2,1,0:T(8,128)(2,1)S(1)} %slice.35), channel_id=1, source_target_pairs={{0,32},{16,48},{32,0},{48,16},{64,96},{80,112},{96,64},{112,80},{1... | collective-permute-start | bytes 393224 | tf_op jit(solution)/shard_map/ppermute | solution.py:323
  118.5 5.5 %collective-permute-done.26 = bf16[2,128,256]{2,1,0:T(8,128)(2,1)S(1)} collective-permute-done((bf16[2,128,256]{2,1,0:T(8,128)(2,1)S(1)}, bf16[2,128,256]{2,1,0:T(8,128)(2,1)S(1)}, u32[]{:S(2)}, u32[]{:S(2)}) %collective-permute-start.26) | collective-permute-done | bytes 131104 | tf_op jit(solution)/shard_map/ppermute | solution.py:323
  124.1 0.8 copy-done.15
  124.9 1.0 dynamic-slice_bitcast_fusion
  125.8 1.4 collective-permute-start.24
  127.3 6.7 %collective-permute-start.27 = (bf16[1,128,256]{2,1,0:T(8,128)(2,1)S(1)}, bf16[1,128,256]{2,1,0:T(8,128)(2,1)S(1)}, u32[]{:S(2)}, u32[]{:S(2)}) collective-permute-start(bf16[1,128,256]{2,1,0:T(8,128)(2,1)S(1)} %slice.37), channel_id=1, source_target_pairs={{0,64},{16,80},{32,96},{48,112},{64,0},{80,16},{96,32},{112,48},{1... | collective-permute-start | bytes 196616 | tf_op jit(solution)/shard_map/ppermute | solution.py:323
  134.0 0.8 copy-done.16
  134.8 0.8 copy-done.17
  135.6 4.6 %token_grad.1 = bf16[128,4096]{1,0:T(8,128)(2,1)} custom-call(bf16[128,2048]{1,0:T(8,128)(2,1)} %get-tuple-element.41.low.refs_0_, bf16[128,2048]{1,0:T(8,128)(2,1)} %get-tuple-element.46.high.refs_1_, bf16[128,2048]{1,0:T(8,128)(2,1)} %collective-permute-done.14.refs_2_, bf16[128,2048]{1,0:T(8,128)(2,1)} %copy-done.17, bf16[128,2048]{1,0:T(8,128)(2,1)} %copy-done.15, ...), custom_call_target="tpu_custom_call" | custom-call | flops 2000000000 | bytes 17825792 | tf_op jit(solution)/shard_map/token_grad/pallas_call | solution.py:201
  140.2 0.8 copy.12
  140.9 1.8 %finish.1 = (f32[64,256]{1,0:T(8,128)}, f32[4,64,256]{2,1,0:T(8,128)}, f32[128,256]{1,0:T(8,128)}) custom-call(s32[1]{0:T(128)} %bitcast.side, bf16[2,448,256]{2,1,0:T(8,128)(2,1)} %bitcast.14, bf16[448,256]{1,0:T(8,128)(2,1)} %copy-done.10), custom_call_target="tpu_custom_call" | custom-call | flops 300000 | bytes 4194304 | tf_op jit(solution)/shard_map/finish/pallas_call | solution.py:230
  (61 shorter events, 0.3 us)
Async XLA Ops:
  7.2 14.2 %copy-start = (bf16[128,4096]{1,0:T(8,128)(2,1)S(1)}, bf16[128,4096]{1,0:T(8,128)(2,1)}, u32[]{:S(2)}) copy-start(bf16[128,4096]{1,0:T(8,128)(2,1)} %tok.5) | copy-start | bytes 3145732
  7.2 116.9 %reduce-scatter.2.cloned.1.call-start = ((), (), s32[]{:S(2)}) async-start(), calls=%async_computation.1 | async-start | bytes 4128768 | tf_op jit(solution)/shard_map/reduce_scatter | solution.py:266
  8.4 15.2 %collective-permute-start.2 = (bf16[128,2048]{1,0:T(8,128)(2,1)S(1)}, bf16[128,2048]{1,0:T(8,128)(2,1)S(1)}, u32[]{:S(2)}, u32[]{:S(2)}) collective-permute-start(bf16[128,2048]{1,0:T(8,128)(2,1)S(1)} %slice.24), channel_id=1, source_target_pairs={{0,4},{1,5},{2,6},{3,7},{4,0},{5,1},{6,2},{7,3},{8,12},{9,13},{10,... | collective-permute-start | bytes 1572872 | tf_op jit(solution)/shard_map/ppermute | solution.py:256
  10.7 31.4 %collective-permute-start = (bf16[128,4096]{1,0:T(8,128)(2,1)}, bf16[128,4096]{1,0:T(8,128)(2,1)}, u32[]{:S(2)}, u32[]{:S(2)}) collective-permute-start(bf16[128,4096]{1,0:T(8,128)(2,1)} %tok.5), channel_id=1, source_target_pairs={{0,1},{1,0},{2,3},{3,2},{4,5},{5,4},{6,7},{7,6},{8,9},{9,8},{10,11... | collective-permute-start | bytes 3145736 | tf_op jit(solution)/shard_map/ppermute | solution.py:256
  12.6 4.6 %collective-permute-start.3 = (f32[128,128]{1,0:T(8,128)S(1)}, f32[128,128]{1,0:T(8,128)S(1)}, u32[]{:S(2)}, u32[]{:S(2)}) collective-permute-start(f32[128,128]{1,0:T(8,128)S(1)} %fusion), channel_id=1, source_target_pairs={{0,12},{1,13},{2,14},{3,15},{4,8},{5,9},{6,10},{7,11},{8,4},{9,5},... | collective-permute-start | bytes 196616 | tf_op jit(solution)/shard_map/ppermute | solution.py:256
  17.2 6.3 %collective-permute-start.4 = (f32[128,128]{1,0:T(8,128)S(1)}, f32[128,128]{1,0:T(8,128)S(1)}, u32[]{:S(2)}, u32[]{:S(2)}) collective-permute-start(f32[128,128]{1,0:T(8,128)S(1)} %add.57), channel_id=1, source_target_pairs={{0,4},{1,5},{2,6},{3,7},{4,0},{5,1},{6,2},{7,3},{8,12},{9,13},{10,... | collective-permute-start | bytes 196616 | tf_op jit(solution)/shard_map/ppermute | solution.py:256
  18.6 16.2 %collective-permute-start.1 = (bf16[128,2048]{1,0:T(8,128)(2,1)S(1)}, bf16[128,2048]{1,0:T(8,128)(2,1)S(1)}, u32[]{:S(2)}, u32[]{:S(2)}) collective-permute-start(bf16[128,2048]{1,0:T(8,128)(2,1)S(1)} %slice.24), channel_id=1, source_target_pairs={{0,2},{1,3},{2,0},{3,1},{4,6},{5,7},{6,4},{7,5},{8,10},{9,11},{10,... | collective-permute-start | bytes 1572872 | tf_op jit(solution)/shard_map/ppermute | solution.py:256
  23.6 18.4 %copy-start.6 = (bf16[128,2048]{1,0:T(8,128)(2,1)}, bf16[128,2048]{1,0:T(8,128)(2,1)S(1)}, u32[]{:S(2)}) copy-start(bf16[128,2048]{1,0:T(8,128)(2,1)S(1)} %collective-permute-done.2.m4) | copy-start | bytes 1572868
  23.6 14.1 %collective-permute-start.9 = (bf16[128,2048]{1,0:T(8,128)(2,1)}, bf16[128,2048]{1,0:T(8,128)(2,1)S(1)}, u32[]{:S(2)}, u32[]{:S(2)}) collective-permute-start(bf16[128,2048]{1,0:T(8,128)(2,1)} %slice.25), channel_id=1, source_target_pairs={{0,4},{1,5},{2,6},{3,7},{4,0},{5,1},{6,2},{7,3},{8,12},{9,13},{10,... | collective-permute-start | bytes 1572872 | tf_op jit(solution)/shard_map/ppermute | solution.py:256
  23.9 17.2 %collective-permute-start.5 = (bf16[128,2048]{1,0:T(8,128)(2,1)S(1)}, bf16[128,2048]{1,0:T(8,128)(2,1)S(1)}, u32[]{:S(2)}, u32[]{:S(2)}) collective-permute-start(bf16[128,2048]{1,0:T(8,128)(2,1)S(1)} %collective-permute-done.2.m4), channel_id=1, source_target_pairs={{0,12},{1,13},{2,14},{3,15},{4,8},{5,9},{6,10},{7,11},{8,4},{9,5},... | collective-permute-start | bytes 1572872 | tf_op jit(solution)/shard_map/ppermute | solution.py:256
  26.5 8.3 %collective-permute-start.6 = (f32[128,128]{1,0:T(8,128)S(1)}, f32[128,128]{1,0:T(8,128)S(1)}, u32[]{:S(2)}, u32[]{:S(2)}) collective-permute-start(f32[128,128]{1,0:T(8,128)S(1)} %add.58), channel_id=1, source_target_pairs={{0,2},{1,3},{2,0},{3,1},{4,6},{5,7},{6,4},{7,5},{8,10},{9,11},{10,... | collective-permute-start | bytes 196616 | tf_op jit(solution)/shard_map/ppermute | solution.py:256
  34.8 7.2 %copy-start.7 = (bf16[128,2048]{1,0:T(8,128)(2,1)}, bf16[128,2048]{1,0:T(8,128)(2,1)S(1)}, u32[]{:S(2)}) copy-start(bf16[128,2048]{1,0:T(8,128)(2,1)S(1)} %collective-permute-done.1.m2) | copy-start | bytes 1572868
  34.8 14.9 %collective-permute-start.8 = (bf16[128,2048]{1,0:T(8,128)(2,1)}, bf16[128,2048]{1,0:T(8,128)(2,1)}, u32[]{:S(2)}, u32[]{:S(2)}) collective-permute-start(bf16[128,2048]{1,0:T(8,128)(2,1)} %slice.25), channel_id=1, source_target_pairs={{0,2},{1,3},{2,0},{3,1},{4,6},{5,7},{6,4},{7,5},{8,10},{9,11},{10,... | collective-permute-start | bytes 1572872 | tf_op jit(solution)/shard_map/ppermute | solution.py:256
  37.7 12.0 %copy-start.8 = (bf16[128,2048]{1,0:T(8,128)(2,1)}, bf16[128,2048]{1,0:T(8,128)(2,1)S(1)}, u32[]{:S(2)}) copy-start(bf16[128,2048]{1,0:T(8,128)(2,1)S(1)} %collective-permute-done.9.m4) | copy-start | bytes 1572868
  37.7 12.2 %collective-permute-start.10 = (bf16[128,2048]{1,0:T(8,128)(2,1)S(1)}, bf16[128,2048]{1,0:T(8,128)(2,1)}, u32[]{:S(2)}, u32[]{:S(2)}) collective-permute-start(bf16[128,2048]{1,0:T(8,128)(2,1)S(1)} %collective-permute-done.9.m4), channel_id=1, source_target_pairs={{0,12},{1,13},{2,14},{3,15},{4,8},{5,9},{6,10},{7,11},{8,4},{9,5},... | collective-permute-start | bytes 1572872 | tf_op jit(solution)/shard_map/ppermute | solution.py:256
  39.3 1.3 collective-permute-start.7
  41.2 0.8 copy-start.9
  57.6 1.2 copy-start.1
  57.6 1.9 %copy-start.12 = (f32[128,128]{1,0:T(8,128)S(1)}, f32[128,128]{1,0:T(8,128)}, u32[]{:S(2)}) copy-start(f32[128,128]{1,0:T(8,128)} %get-tuple-element.48) | copy-start | bytes 196612
  57.6 1.9 %copy-start.13 = (f32[128,128]{1,0:T(8,128)S(1)}, f32[128,128]{1,0:T(8,128)}, u32[]{:S(2)}) copy-start(f32[128,128]{1,0:T(8,128)} %get-tuple-element.49) | copy-start | bytes 196612
  58.9 14.0 %collective-permute-start.12 = (bf16[128,2048]{1,0:T(8,128)(2,1)S(1)}, bf16[128,2048]{1,0:T(8,128)(2,1)S(1)}, u32[]{:S(2)}, u32[]{:S(2)}) collective-permute-start(bf16[128,2048]{1,0:T(8,128)(2,1)S(1)} %constant_dynamic-slice_fusion), channel_id=1, source_target_pairs={{0,128},{16,144},{32,160},{48,176},{64,192},{80,208},{96,224},{112... | collective-permute-start | bytes 1572872 | tf_op jit(solution)/shard_map/ppermute | solution.py:273
  59.6 13.3 %collective-permute-start.11 = (f32[128,128]{1,0:T(8,128)S(1)}, f32[128,128]{1,0:T(8,128)S(1)}, u32[]{:S(2)}, u32[]{:S(2)}) collective-permute-start(f32[128,128]{1,0:T(8,128)S(1)} %add.61), channel_id=1, source_target_pairs={{0,12},{1,13},{2,14},{3,15},{4,8},{5,9},{6,10},{7,11},{8,4},{9,5},... | collective-permute-start | bytes 196616 | tf_op jit(solution)/shard_map/ppermute | solution.py:256
  67.8 34.3 %copy-start.5 = (bf16[128,2048]{1,0:T(8,128)(2,1)S(1)}, bf16[128,2048]{1,0:T(8,128)(2,1)}, u32[]{:S(2)}) copy-start(bf16[128,2048]{1,0:T(8,128)(2,1)} %get-tuple-element.59) | copy-start | bytes 1572868
  67.8 43.3 %copy-start.3 = (bf16[128,2048]{1,0:T(8,128)(2,1)S(1)}, bf16[128,2048]{1,0:T(8,128)(2,1)}, u32[]{:S(2)}) copy-start(bf16[128,2048]{1,0:T(8,128)(2,1)} %get-tuple-element.63) | copy-start | bytes 1572868
  72.9 22.5 %copy-start.4 = (bf16[128,2048]{1,0:T(8,128)(2,1)}, bf16[128,2048]{1,0:T(8,128)(2,1)S(1)}, u32[]{:S(2)}) copy-start(bf16[128,2048]{1,0:T(8,128)(2,1)S(1)} %collective-permute-done.12.others) | copy-start | bytes 1572868
  72.9 5.9 %collective-permute-start.13 = (f32[128,128]{1,0:T(8,128)S(1)}, f32[128,128]{1,0:T(8,128)S(1)}, u32[]{:S(2)}, u32[]{:S(2)}) collective-permute-start(f32[128,128]{1,0:T(8,128)S(1)} %add.63), channel_id=1, source_target_pairs={{0,2},{1,3},{2,0},{3,1},{4,6},{5,7},{6,4},{7,5},{8,10},{9,11},{10,... | collective-permute-start | bytes 196616 | tf_op jit(solution)/shard_map/ppermute | solution.py:256
  78.8 8.7 %collective-permute-start.17 = (bf16[128,4096]{1,0:T(8,128)(2,1)}, bf16[128,4096]{1,0:T(8,128)(2,1)}, u32[]{:S(2)}, u32[]{:S(2)}) collective-permute-start(bf16[128,4096]{1,0:T(8,128)(2,1)} %get-tuple-element.55), channel_id=1, source_target_pairs={{0,1},{1,0},{2,3},{3,2},{4,5},{5,4},{6,7},{7,6},{8,9},{9,8},{10,11... | collective-permute-start | bytes 3145736 | tf_op jit(solution)/shard_map/ppermute | solution.py:256
  78.9 16.5 %collective-permute-start.14 = (bf16[128,2048]{1,0:T(8,128)(2,1)}, bf16[128,2048]{1,0:T(8,128)(2,1)}, u32[]{:S(2)}, u32[]{:S(2)}) collective-permute-start(bf16[128,2048]{1,0:T(8,128)(2,1)} %get-tuple-element.53), channel_id=1, source_target_pairs={{0,2},{1,3},{2,0},{3,1},{4,6},{5,7},{6,4},{7,5},{8,10},{9,11},{10,... | collective-permute-start | bytes 1572872 | tf_op jit(solution)/shard_map/ppermute | solution.py:256
  80.9 4.3 %collective-permute-start.15 = (f32[128,128]{1,0:T(8,128)S(1)}, f32[128,128]{1,0:T(8,128)S(1)}, u32[]{:S(2)}, u32[]{:S(2)}) collective-permute-start(f32[128,128]{1,0:T(8,128)S(1)} %add.64), channel_id=1, source_target_pairs={{0,4},{1,5},{2,6},{3,7},{4,0},{5,1},{6,2},{7,3},{8,12},{9,13},{10,... | collective-permute-start | bytes 196616 | tf_op jit(solution)/shard_map/ppermute | solution.py:256
  85.2 2.2 %collective-permute-start.16 = (f32[128,128]{1,0:T(8,128)S(1)}, f32[128,128]{1,0:T(8,128)S(1)}, u32[]{:S(2)}, u32[]{:S(2)}) collective-permute-start(f32[128,128]{1,0:T(8,128)S(1)} %add.66), channel_id=1, source_target_pairs={{0,1},{1,0},{2,3},{3,2},{4,5},{5,4},{6,7},{7,6},{8,9},{9,8},{10,11... | collective-permute-start | bytes 196616 | tf_op jit(solution)/shard_map/ppermute | solution.py:256
  85.3 16.8 %collective-permute-start.20 = (bf16[128,2048]{1,0:T(8,128)(2,1)}, bf16[128,2048]{1,0:T(8,128)(2,1)S(1)}, u32[]{:S(2)}, u32[]{:S(2)}) collective-permute-start(bf16[128,2048]{1,0:T(8,128)(2,1)} %get-tuple-element.61), channel_id=1, source_target_pairs={{0,12},{1,13},{2,14},{3,15},{4,8},{5,9},{6,10},{7,11},{8,4},{9,5},... | collective-permute-start | bytes 1572872 | tf_op jit(solution)/shard_map/ppermute | solution.py:256
  85.8 25.3 %collective-permute-start.22 = (bf16[128,2048]{1,0:T(8,128)(2,1)}, bf16[128,2048]{1,0:T(8,128)(2,1)S(1)}, u32[]{:S(2)}, u32[]{:S(2)}) collective-permute-start(bf16[128,2048]{1,0:T(8,128)(2,1)} %get-tuple-element.65), channel_id=1, source_target_pairs={{0,12},{1,13},{2,14},{3,15},{4,8},{5,9},{6,10},{7,11},{8,4},{9,5},... | collective-permute-start | bytes 1572872 | tf_op jit(solution)/shard_map/ppermute | solution.py:256
  87.5 7.9 %copy-start.11 = (bf16[128,128]{1,0:T(8,128)(2,1)}, bf16[128,128]{1,0:T(8,128)(2,1)S(1)}, u32[]{:S(2)}) copy-start(bf16[128,128]{1,0:T(8,128)(2,1)S(1)} %add_convert_fusion.2.lat.refs_9_) | copy-start | bytes 98308
  87.5 7.9 %collective-permute-start.18 = (bf16[128,128]{1,0:T(8,128)(2,1)S(1)}, bf16[128,128]{1,0:T(8,128)(2,1)S(1)}, u32[]{:S(2)}, u32[]{:S(2)}) collective-permute-start(bf16[128,128]{1,0:T(8,128)(2,1)S(1)} %add_convert_fusion.2.lat.refs_9_), channel_id=1, source_target_pairs={{0,128},{16,144},{32,160},{48,176},{64,192},{80,208},{96,224},{112... | collective-permute-start | bytes 98312 | tf_op jit(solution)/shard_map/ppermute | solution.py:273
  95.4 0.6 copy-start.14
  99.1 16.0 %copy-start.2 = (bf16[8,128,256]{2,1,0:T(8,128)(2,1)S(1)}, bf16[8,128,256]{2,1,0:T(8,128)(2,1)}, u32[]{:S(2)}) copy-start(bf16[8,128,256]{2,1,0:T(8,128)(2,1)} %down_part.1) | copy-start | bytes 1572868
  100.1 15.0 %collective-permute-start.25 = (bf16[4,128,256]{2,1,0:T(8,128)(2,1)S(1)}, bf16[4,128,256]{2,1,0:T(8,128)(2,1)S(1)}, u32[]{:S(2)}, u32[]{:S(2)}) collective-permute-start(bf16[4,128,256]{2,1,0:T(8,128)(2,1)S(1)} %slice.33), channel_id=1, source_target_pairs={{0,16},{16,0},{32,48},{48,32},{64,80},{80,64},{96,112},{112,96},{1... | collective-permute-start | bytes 786440 | tf_op jit(solution)/shard_map/ppermute | solution.py:323
  102.3 21.8 %collective-permute-start.21 = (bf16[128,2048]{1,0:T(8,128)(2,1)S(1)}, bf16[128,2048]{1,0:T(8,128)(2,1)S(1)}, u32[]{:S(2)}, u32[]{:S(2)}) collective-permute-start(bf16[128,2048]{1,0:T(8,128)(2,1)S(1)} %add.68), channel_id=1, source_target_pairs={{0,4},{1,5},{2,6},{3,7},{4,0},{5,1},{6,2},{7,3},{8,12},{9,13},{10,... | collective-permute-start | bytes 1572872 | tf_op jit(solution)/shard_map/ppermute | solution.py:256
  111.3 22.7 %collective-permute-start.23 = (bf16[128,2048]{1,0:T(8,128)(2,1)S(1)}, bf16[128,2048]{1,0:T(8,128)(2,1)S(1)}, u32[]{:S(2)}, u32[]{:S(2)}) collective-permute-start(bf16[128,2048]{1,0:T(8,128)(2,1)S(1)} %add.69), channel_id=1, source_target_pairs={{0,4},{1,5},{2,6},{3,7},{4,0},{5,1},{6,2},{7,3},{8,12},{9,13},{10,... | collective-permute-start | bytes 1572872 | tf_op jit(solution)/shard_map/ppermute | solution.py:256
  114.4 19.6 %collective-permute-start.19 = (bf16[128,2048]{1,0:T(8,128)(2,1)}, bf16[128,2048]{1,0:T(8,128)(2,1)S(1)}, u32[]{:S(2)}, u32[]{:S(2)}) collective-permute-start(bf16[128,2048]{1,0:T(8,128)(2,1)} %get-tuple-element.58), channel_id=1, source_target_pairs={{0,2},{1,3},{2,0},{3,1},{4,6},{5,7},{6,4},{7,5},{8,10},{9,11},{10,... | collective-permute-start | bytes 1572872 | tf_op jit(solution)/shard_map/ppermute | solution.py:256
  115.2 8.9 %collective-permute-start.26 = (bf16[2,128,256]{2,1,0:T(8,128)(2,1)S(1)}, bf16[2,128,256]{2,1,0:T(8,128)(2,1)S(1)}, u32[]{:S(2)}, u32[]{:S(2)}) collective-permute-start(bf16[2,128,256]{2,1,0:T(8,128)(2,1)S(1)} %slice.35), channel_id=1, source_target_pairs={{0,32},{16,48},{32,0},{48,16},{64,96},{80,112},{96,64},{112,80},{1... | collective-permute-start | bytes 393224 | tf_op jit(solution)/shard_map/ppermute | solution.py:323
  124.1 0.8 copy-start.15
  125.8 14.3 %collective-permute-start.24 = (bf16[448,256]{1,0:T(8,128)(2,1)S(1)}, bf16[448,256]{1,0:T(8,128)(2,1)S(1)}, u32[]{:S(2)}, u32[]{:S(2)}) collective-permute-start(bf16[448,256]{1,0:T(8,128)(2,1)S(1)} %dynamic-slice_bitcast_fusion), channel_id=1, source_target_pairs={{0,128},{16,144},{32,160},{48,176},{64,192},{80,208},{96,224},{112... | collective-permute-start | bytes 688136 | tf_op jit(solution)/shard_map/ppermute | solution.py:273
  127.3 12.8 %collective-permute-start.27 = (bf16[1,128,256]{2,1,0:T(8,128)(2,1)S(1)}, bf16[1,128,256]{2,1,0:T(8,128)(2,1)S(1)}, u32[]{:S(2)}, u32[]{:S(2)}) collective-permute-start(bf16[1,128,256]{2,1,0:T(8,128)(2,1)S(1)} %slice.37), channel_id=1, source_target_pairs={{0,64},{16,80},{32,96},{48,112},{64,0},{80,16},{96,32},{112,48},{1... | collective-permute-start | bytes 196616 | tf_op jit(solution)/shard_map/ppermute | solution.py:323
  134.0 0.8 copy-start.16
  134.8 0.8 copy-start.17
  140.1 0.8 copy-start.10
Sparse Core Ops, SparseCore 0:
  57.8 56.6 reduce-scatter.1

commit v10 on v9

--- a/solution.py
+++ b/solution.py
@@ -308,7 +308,7 @@
     part = part + flip(part, 2)
     r2_0, r1 = flip(after(b2_0, part), 2), flip(after(b1, part), 1)
     part = part + flip(part, 4)
-    part = part + after(flip(part, 1), r1)
+    part = part + after(flip(part, 1), r1, q0)
     latent_grad = part.astype(BF16)
 
     z = lax.axis_index("dp") % RING

time: 150 us -> 147 us (0.980)
  waiting for transfers between devices: 42.7 us -> 41 us
  starting transfers between devices: 47.8 us -> 46.1 us
    ppermute x22, waiting for transfers between devices: 32.1 us -> 24.2 us  [flip(): return lax.ppermute(value, 'tensor', [(i, i ^ mask) for i in range(16)])]
    ppermute x3, waiting for transfers between devices: 5.55 us -> 9.06 us  [per_device(): lax.ppermute(left[count:], 'dp', [(i, i ^ mask) for i in range(2 * RING)])]
    ppermute x3, waiting for transfers between devices: 5.03 us -> 7.71 us  [cross(): return lax.ppermute(value, 'dp', [(i, i ^ RING) for i in range(2 * RING)])]
    ppermute x3, starting transfers between devices: 12 us -> 9.7 us  [per_device(): lax.ppermute(left[count:], 'dp', [(i, i ^ mask) for i in range(2 * RING)])]
  transfers between devices with their start and end apart: 29 -> 29, of which waited for: 11 -> 12; matrix products, arithmetic and copies ran while one was open for 4% -> 4% of each run, Pallas kernels for 15% -> 15%
where the time goes in v10:
time: 147 us; the launch traced here: 146 us
  starting transfers between devices  46.1 us (31%)
  waiting for transfers between devices  41 us (28%)
  Pallas kernels  31.3 us (21%)
  between operations  14.3 us (10%)
  local copies, waits for them, and re-layouts  9.86 us (7%)
  matrix products  1.96 us (1%)
  other arithmetic  1.65 us (1%)
    ppermute x22, starting transfers between devices, flip(): return lax.ppermute(value, 'tensor', [(i, i ^ mask) for i in range(16)])  33.4 us
    ppermute x22, waiting for transfers between devices, flip(): return lax.ppermute(value, 'tensor', [(i, i ^ mask) for i in range(16)])  24.2 us
    pallas_call x2, Pallas kernels, run_main(): pl.pallas_call(main_kernel, grid=(steps,), in_specs=in_specs, out_specs=[...  15.4 us
    ppermute x3, starting transfers between devices, per_device(): lax.ppermute(left[count:], 'dp', [(i, i ^ mask) for i in range(2 * RING)])  9.7 us
    ppermute x3, waiting for transfers between devices, per_device(): lax.ppermute(left[count:], 'dp', [(i, i ^ mask) for i in range(2 * RING)])  9.06 us
    ppermute x3, waiting for transfers between devices, cross(): return lax.ppermute(value, 'dp', [(i, i ^ RING) for i in range(2 * RING)])  7.71 us
    pallas_call x1, Pallas kernels, run_back(): pl.pallas_call(back_kernel, grid=(2,), in_specs=[fixed, fixed, pl.BlockSp...  6.43 us
    unnamed x37, local copies, waits for them, and re-layouts  5.81 us
  transfers between devices with their start and end apart: 29, of which 12 were waited for; matrix products, arithmetic and copies ran while one was open for 4% of the time, Pallas kernels for 15%

profile of v10, /device:TPU:8, one launch (start us, length us, event | category | flops | bytes accessed | tf_op | source)
XLA Modules:
  0.0 146.2 jit_solution(15172939997021021743)
XLA Ops:
  7.2 0.0 copy-start
  7.2 0.0 reduce-scatter.2.cloned.1.call-start
  7.2 1.2 slice.24
  8.4 2.3 %collective-permute-start.2 = (bf16[128,2048]{1,0:T(8,128)(2,1)S(1)}, bf16[128,2048]{1,0:T(8,128)(2,1)S(1)}, u32[]{:S(2)}, u32[]{:S(2)}) collective-permute-start(bf16[128,2048]{1,0:T(8,128)(2,1)S(1)} %slice.24), channel_id=1, source_target_pairs={{0,4},{1,5},{2,6},{3,7},{4,0},{5,1},{6,2},{7,3},{8,12},{9,13},{10,... | collective-permute-start | bytes 1572872 | tf_op jit(solution)/shard_map/ppermute | solution.py:256
  10.7 2.0 %fusion = f32[128,128]{1,0:T(8,128)S(1)} fusion(bf16[128,4096]{1,0:T(8,128)(2,1)} %tok.5, bf16[4096,128]{1,0:T(8,128)(2,1)} %refs_8_.1), kind=kOutput, calls=%fused_computation.8 | convolution fusion | flops 134217728 | bytes 2162688 | tf_op jit(solution)/shard_map/dot_general | solution.py:285
  12.6 0.8 collective-permute-start.3
  13.4 3.8 %collective-permute-done.3 = f32[128,128]{1,0:T(8,128)S(1)} collective-permute-done((f32[128,128]{1,0:T(8,128)S(1)}, f32[128,128]{1,0:T(8,128)S(1)}, u32[]{:S(2)}, u32[]{:S(2)}) %collective-permute-start.3) | collective-permute-done | bytes 65568 | tf_op jit(solution)/shard_map/ppermute | solution.py:256
  17.2 1.4 collective-permute-start.4
  18.6 2.8 %collective-permute-start.1 = (bf16[128,2048]{1,0:T(8,128)(2,1)S(1)}, bf16[128,2048]{1,0:T(8,128)(2,1)S(1)}, u32[]{:S(2)}, u32[]{:S(2)}) collective-permute-start(bf16[128,2048]{1,0:T(8,128)(2,1)S(1)} %slice.24), channel_id=1, source_target_pairs={{0,2},{1,3},{2,0},{3,1},{4,6},{5,7},{6,4},{7,5},{8,10},{9,11},{10,... | collective-permute-start | bytes 1572872 | tf_op jit(solution)/shard_map/ppermute | solution.py:256
  21.4 0.8 slice.25
  22.2 1.3 collective-permute-done.4
  23.6 0.4 collective-permute-start.9
  23.9 2.6 %collective-permute-start.5 = (bf16[128,2048]{1,0:T(8,128)(2,1)S(1)}, bf16[128,2048]{1,0:T(8,128)(2,1)S(1)}, u32[]{:S(2)}, u32[]{:S(2)}) collective-permute-start(bf16[128,2048]{1,0:T(8,128)(2,1)S(1)} %collective-permute-done.2.m4), channel_id=1, source_target_pairs={{0,12},{1,13},{2,14},{3,15},{4,8},{5,9},{6,10},{7,11},{8,4},{9,5},... | collective-permute-start | bytes 1572872 | tf_op jit(solution)/shard_map/ppermute | solution.py:256
  26.5 3.0 %collective-permute-start.6 = (f32[128,128]{1,0:T(8,128)S(1)}, f32[128,128]{1,0:T(8,128)S(1)}, u32[]{:S(2)}, u32[]{:S(2)}) collective-permute-start(f32[128,128]{1,0:T(8,128)S(1)} %add.58), channel_id=1, source_target_pairs={{0,2},{1,3},{2,0},{3,1},{4,6},{5,7},{6,4},{7,5},{8,10},{9,11},{10,... | collective-permute-start | bytes 196616 | tf_op jit(solution)/shard_map/ppermute | solution.py:256
  29.5 5.3 %collective-permute-done.6 = f32[128,128]{1,0:T(8,128)S(1)} collective-permute-done((f32[128,128]{1,0:T(8,128)S(1)}, f32[128,128]{1,0:T(8,128)S(1)}, u32[]{:S(2)}, u32[]{:S(2)}) %collective-permute-start.6) | collective-permute-done | bytes 65568 | tf_op jit(solution)/shard_map/ppermute | solution.py:256
  34.8 2.9 %collective-permute-start.8 = (bf16[128,2048]{1,0:T(8,128)(2,1)}, bf16[128,2048]{1,0:T(8,128)(2,1)}, u32[]{:S(2)}, u32[]{:S(2)}) collective-permute-start(bf16[128,2048]{1,0:T(8,128)(2,1)} %slice.25), channel_id=1, source_target_pairs={{0,2},{1,3},{2,0},{3,1},{4,6},{5,7},{6,4},{7,5},{8,10},{9,11},{10,... | collective-permute-start | bytes 1572872 | tf_op jit(solution)/shard_map/ppermute | solution.py:256
  37.7 1.6 %collective-permute-start.10 = (bf16[128,2048]{1,0:T(8,128)(2,1)S(1)}, bf16[128,2048]{1,0:T(8,128)(2,1)}, u32[]{:S(2)}, u32[]{:S(2)}) collective-permute-start(bf16[128,2048]{1,0:T(8,128)(2,1)S(1)} %collective-permute-done.9.m4), channel_id=1, source_target_pairs={{0,12},{1,13},{2,14},{3,15},{4,8},{5,9},{6,10},{7,11},{8,4},{9,5},... | collective-permute-start | bytes 1572872 | tf_op jit(solution)/shard_map/ppermute | solution.py:256
  39.3 1.3 collective-permute-done.7
  40.5 0.6 add_convert_fusion.3.latent
  41.2 0.8 copy-done.9
  42.0 7.7 %main_part.2 = (bf16[128,2048]{1,0:T(8,128)(2,1)}, f32[128,128]{1,0:T(8,128)}, bf16[8,2,448,256]{3,2,1,0:T(8,128)(2,1)}) custom-call(bf16[128,4096]{1,0:T(8,128)(2,1)} %tok.5, bf16[128,4096]{1,0:T(8,128)(2,1)} %collective-permute-done.m1, bf16[128,2048]{1,0:T(8,128)(2,1)} %copy-done.7, bf16[128,2048]{1,0:T(8,128)(2,1)} %copy-done.6, ...), custom_call_target="tpu_custom_call" | custom-call | flops 2000000000 | bytes 29360128 | tf_op jit(solution)/shard_map/main_part/pallas_call | solution.py:89
  49.7 0.1 collective-permute-done.10.m8
  49.9 7.7 %main_part.3 = (bf16[128,2048]{1,0:T(8,128)(2,1)}, f32[128,128]{1,0:T(8,128)}, bf16[8,2,448,256]{3,2,1,0:T(8,128)(2,1)}) custom-call(bf16[128,4096]{1,0:T(8,128)(2,1)} %tok.5, bf16[128,4096]{1,0:T(8,128)(2,1)} %collective-permute-done.m1, bf16[128,2048]{1,0:T(8,128)(2,1)} %collective-permute-done.8.m2, ...), custom_call_target="tpu_custom_call", output_to_operand_aliasing={{2}: (10, {})} | custom-call | flops 2000000000 | bytes 29360128 | tf_op jit(solution)/shard_map/main_part/pallas_call | solution.py:89
  57.6 0.0 reduce-scatter.2.cloned.1.call-update
  57.7 1.1 copy-done.1
  58.9 0.7 collective-permute-start.12
  59.6 1.8 %collective-permute-start.11 = (f32[128,128]{1,0:T(8,128)S(1)}, f32[128,128]{1,0:T(8,128)S(1)}, u32[]{:S(2)}, u32[]{:S(2)}) collective-permute-start(f32[128,128]{1,0:T(8,128)S(1)} %add.61), channel_id=1, source_target_pairs={{0,12},{1,13},{2,14},{3,15},{4,8},{5,9},{6,10},{7,11},{8,4},{9,5},... | collective-permute-start | bytes 196616 | tf_op jit(solution)/shard_map/ppermute | solution.py:256
  61.4 6.4 %back_products.1 = (bf16[128,4096]{1,0:T(8,128)(2,1)}, bf16[128,2048]{1,0:T(8,128)(2,1)}, bf16[128,2048]{1,0:T(8,128)(2,1)}, bf16[128,2048]{1,0:T(8,128)(2,1)}, ...) custom-call(bf16[128,2048]{1,0:T(8,128)(2,1)} %get-tuple-element.41.low.refs_0_, ...), custom_call_target="tpu_custom_call" | custom-call | flops 2000000000 | bytes 20971520 | tf_op jit(solution)/shard_map/back_products/pallas_call | solution.py:136
  67.9 5.0 %collective-permute-done.12.others = bf16[128,2048]{1,0:T(8,128)(2,1)S(1)} collective-permute-done((bf16[128,2048]{1,0:T(8,128)(2,1)S(1)}, bf16[128,2048]{1,0:T(8,128)(2,1)S(1)}, u32[]{:S(2)}, u32[]{:S(2)}) %collective-permute-start.12) | collective-permute-done | bytes 524320 | tf_op jit(solution)/shard_map/ppermute | solution.py:273
  72.9 2.1 %collective-permute-start.13 = (f32[128,128]{1,0:T(8,128)S(1)}, f32[128,128]{1,0:T(8,128)S(1)}, u32[]{:S(2)}, u32[]{:S(2)}) collective-permute-start(f32[128,128]{1,0:T(8,128)S(1)} %add.63), channel_id=1, source_target_pairs={{0,2},{1,3},{2,0},{3,1},{4,6},{5,7},{6,4},{7,5},{8,10},{9,11},{10,... | collective-permute-start | bytes 196616 | tf_op jit(solution)/shard_map/ppermute | solution.py:256
  75.0 3.8 %collective-permute-done.13 = f32[128,128]{1,0:T(8,128)S(1)} collective-permute-done((f32[128,128]{1,0:T(8,128)S(1)}, f32[128,128]{1,0:T(8,128)S(1)}, u32[]{:S(2)}, u32[]{:S(2)}) %collective-permute-start.13) | collective-permute-done | bytes 65568 | tf_op jit(solution)/shard_map/ppermute | solution.py:256
  78.8 0.1 collective-permute-start.17
  78.9 0.5 collective-permute-start.18
  79.4 2.0 %collective-permute-start.14 = (bf16[128,2048]{1,0:T(8,128)(2,1)}, bf16[128,2048]{1,0:T(8,128)(2,1)}, u32[]{:S(2)}, u32[]{:S(2)}) collective-permute-start(bf16[128,2048]{1,0:T(8,128)(2,1)} %get-tuple-element.53), channel_id=1, source_target_pairs={{0,2},{1,3},{2,0},{3,1},{4,6},{5,7},{6,4},{7,5},{8,10},{9,11},{10,... | collective-permute-start | bytes 1572872 | tf_op jit(solution)/shard_map/ppermute | solution.py:256
  81.4 1.7 %collective-permute-start.15 = (f32[128,128]{1,0:T(8,128)S(1)}, f32[128,128]{1,0:T(8,128)S(1)}, u32[]{:S(2)}, u32[]{:S(2)}) collective-permute-start(f32[128,128]{1,0:T(8,128)S(1)} %add.64), channel_id=1, source_target_pairs={{0,4},{1,5},{2,6},{3,7},{4,0},{5,1},{6,2},{7,3},{8,12},{9,13},{10,... | collective-permute-start | bytes 196616 | tf_op jit(solution)/shard_map/ppermute | solution.py:256
  83.0 2.6 %collective-permute-done.15 = f32[128,128]{1,0:T(8,128)S(1)} collective-permute-done((f32[128,128]{1,0:T(8,128)S(1)}, f32[128,128]{1,0:T(8,128)S(1)}, u32[]{:S(2)}, u32[]{:S(2)}) %collective-permute-start.15) | collective-permute-done | bytes 65568 | tf_op jit(solution)/shard_map/ppermute | solution.py:256
  85.7 0.1 collective-permute-start.16
  85.8 2.1 %collective-permute-start.22 = (bf16[128,2048]{1,0:T(8,128)(2,1)}, bf16[128,2048]{1,0:T(8,128)(2,1)S(1)}, u32[]{:S(2)}, u32[]{:S(2)}) collective-permute-start(bf16[128,2048]{1,0:T(8,128)(2,1)} %get-tuple-element.65), channel_id=1, source_target_pairs={{0,12},{1,13},{2,14},{3,15},{4,8},{5,9},{6,10},{7,11},{8,4},{9,5},... | collective-permute-start | bytes 1572872 | tf_op jit(solution)/shard_map/ppermute | solution.py:256
  87.9 6.0 %collective-permute-done.18 = bf16[128,2048]{1,0:T(8,128)(2,1)S(1)} collective-permute-done((bf16[128,2048]{1,0:T(8,128)(2,1)}, bf16[128,2048]{1,0:T(8,128)(2,1)S(1)}, u32[]{:S(2)}, u32[]{:S(2)}) %collective-permute-start.18) | collective-permute-done | bytes 524320 | tf_op jit(solution)/shard_map/ppermute | solution.py:256
  93.9 0.7 collective-permute-start.19
  94.6 0.6 pad_add_fusion.place
  95.2 2.7 %collective-permute-done.19.lat_others = bf16[128,128]{1,0:T(8,128)(2,1)S(1)} collective-permute-done((bf16[128,128]{1,0:T(8,128)(2,1)S(1)}, bf16[128,128]{1,0:T(8,128)(2,1)S(1)}, u32[]{:S(2)}, u32[]{:S(2)}) %collective-permute-start.19) | collective-permute-done | bytes 32800 | tf_op jit(solution)/shard_map/ppermute | solution.py:273
  97.9 0.6 copy-done.14
  98.5 3.1 %down_part.1 = bf16[8,128,256]{2,1,0:T(8,128)(2,1)} custom-call(s32[2]{0:T(128)} %pad_add_fusion.place, bf16[128,4096]{1,0:T(8,128)(2,1)} %tok.5, bf16[128,2048]{1,0:T(8,128)(2,1)} %copy-done.4, bf16[128,128]{1,0:T(8,128)(2,1)} %copy-done.11, bf16[128,128]{1,0:T(8,128)(2,1)} %copy-done.14), custom_call_target="tpu_custom_call" | custom-call | flops 300000000 | bytes 10485760 | tf_op jit(solution)/shard_map/down_part/pallas_call | solution.py:163
  101.6 1.0 slice.33
  102.6 2.0 %collective-permute-start.25 = (bf16[4,128,256]{2,1,0:T(8,128)(2,1)S(1)}, bf16[4,128,256]{2,1,0:T(8,128)(2,1)S(1)}, u32[]{:S(2)}, u32[]{:S(2)}) collective-permute-start(bf16[4,128,256]{2,1,0:T(8,128)(2,1)S(1)} %slice.33), channel_id=1, source_target_pairs={{0,16},{16,0},{32,48},{48,32},{64,80},{80,64},{96,112},{112,96},{1... | collective-permute-start | bytes 786440 | tf_op jit(solution)/shard_map/ppermute | solution.py:323
  104.7 0.1 add.68
  104.8 2.3 %collective-permute-start.21 = (bf16[128,2048]{1,0:T(8,128)(2,1)S(1)}, bf16[128,2048]{1,0:T(8,128)(2,1)S(1)}, u32[]{:S(2)}, u32[]{:S(2)}) collective-permute-start(bf16[128,2048]{1,0:T(8,128)(2,1)S(1)} %add.68), channel_id=1, source_target_pairs={{0,4},{1,5},{2,6},{3,7},{4,0},{5,1},{6,2},{7,3},{8,12},{9,13},{10,... | collective-permute-start | bytes 1572872 | tf_op jit(solution)/shard_map/ppermute | solution.py:256
  107.1 0.1 add.69
  107.2 0.1 collective-permute-start.23
  107.3 3.0 %collective-permute-start.20 = (bf16[128,2048]{1,0:T(8,128)(2,1)}, bf16[128,2048]{1,0:T(8,128)(2,1)S(1)}, u32[]{:S(2)}, u32[]{:S(2)}) collective-permute-start(bf16[128,2048]{1,0:T(8,128)(2,1)} %get-tuple-element.60), channel_id=1, source_target_pairs={{0,2},{1,3},{2,0},{3,1},{4,6},{5,7},{6,4},{7,5},{8,10},{9,11},{10,... | collective-permute-start | bytes 1572872 | tf_op jit(solution)/shard_map/ppermute | solution.py:256
  110.3 3.4 %collective-permute-done.25 = bf16[4,128,256]{2,1,0:T(8,128)(2,1)S(1)} collective-permute-done((bf16[4,128,256]{2,1,0:T(8,128)(2,1)S(1)}, bf16[4,128,256]{2,1,0:T(8,128)(2,1)S(1)}, u32[]{:S(2)}, u32[]{:S(2)}) %collective-permute-start.25) | collective-permute-done | bytes 262176 | tf_op jit(solution)/shard_map/ppermute | solution.py:323
  113.6 0.1 add_convert_fusion
  113.7 3.2 %collective-permute-start.26 = (bf16[2,128,256]{2,1,0:T(8,128)(2,1)S(1)}, bf16[2,128,256]{2,1,0:T(8,128)(2,1)S(1)}, u32[]{:S(2)}, u32[]{:S(2)}) collective-permute-start(bf16[2,128,256]{2,1,0:T(8,128)(2,1)S(1)} %slice.35), channel_id=1, source_target_pairs={{0,32},{16,48},{32,0},{48,16},{64,96},{80,112},{96,64},{112,80},{1... | collective-permute-start | bytes 393224 | tf_op jit(solution)/shard_map/ppermute | solution.py:323
  116.9 5.7 %collective-permute-done.26 = bf16[2,128,256]{2,1,0:T(8,128)(2,1)S(1)} collective-permute-done((bf16[2,128,256]{2,1,0:T(8,128)(2,1)S(1)}, bf16[2,128,256]{2,1,0:T(8,128)(2,1)S(1)}, u32[]{:S(2)}, u32[]{:S(2)}) %collective-permute-start.26) | collective-permute-done | bytes 131104 | tf_op jit(solution)/shard_map/ppermute | solution.py:323
  122.6 0.8 copy-done.15
  123.4 1.0 dynamic-slice_bitcast_fusion
  124.4 1.6 %collective-permute-start.24 = (bf16[448,256]{1,0:T(8,128)(2,1)S(1)}, bf16[448,256]{1,0:T(8,128)(2,1)S(1)}, u32[]{:S(2)}, u32[]{:S(2)}) collective-permute-start(bf16[448,256]{1,0:T(8,128)(2,1)S(1)} %dynamic-slice_bitcast_fusion), channel_id=1, source_target_pairs={{0,128},{16,144},{32,160},{48,176},{64,192},{80,208},{96,224},{112... | collective-permute-start | bytes 688136 | tf_op jit(solution)/shard_map/ppermute | solution.py:273
  126.0 4.5 %collective-permute-start.27 = (bf16[1,128,256]{2,1,0:T(8,128)(2,1)S(1)}, bf16[1,128,256]{2,1,0:T(8,128)(2,1)S(1)}, u32[]{:S(2)}, u32[]{:S(2)}) collective-permute-start(bf16[1,128,256]{2,1,0:T(8,128)(2,1)S(1)} %slice.37), channel_id=1, source_target_pairs={{0,64},{16,80},{32,96},{48,112},{64,0},{80,16},{96,32},{112,48},{1... | collective-permute-start | bytes 196616 | tf_op jit(solution)/shard_map/ppermute | solution.py:323
  130.5 0.8 copy-done.16
  131.3 0.8 copy-done.17
  132.1 4.6 %token_grad.1 = bf16[128,4096]{1,0:T(8,128)(2,1)} custom-call(bf16[128,2048]{1,0:T(8,128)(2,1)} %get-tuple-element.41.low.refs_0_, bf16[128,2048]{1,0:T(8,128)(2,1)} %get-tuple-element.46.high.refs_1_, bf16[128,2048]{1,0:T(8,128)(2,1)} %collective-permute-done.14.refs_2_, bf16[128,2048]{1,0:T(8,128)(2,1)} %copy-done.17, bf16[128,2048]{1,0:T(8,128)(2,1)} %copy-done.15, ...), custom_call_target="tpu_custom_call" | custom-call | flops 2000000000 | bytes 17825792 | tf_op jit(solution)/shard_map/token_grad/pallas_call | solution.py:201
  136.7 0.8 copy.12
  137.5 1.8 %finish.1 = (f32[64,256]{1,0:T(8,128)}, f32[4,64,256]{2,1,0:T(8,128)}, f32[128,256]{1,0:T(8,128)}) custom-call(s32[1]{0:T(128)} %bitcast.side, bf16[2,448,256]{2,1,0:T(8,128)(2,1)} %bitcast.14, bf16[448,256]{1,0:T(8,128)(2,1)} %copy-done.10), custom_call_target="tpu_custom_call" | custom-call | flops 300000 | bytes 4194304 | tf_op jit(solution)/shard_map/finish/pallas_call | solution.py:230
  (61 shorter events, 0.3 us)
Async XLA Ops:
  7.2 14.2 %copy-start = (bf16[128,4096]{1,0:T(8,128)(2,1)S(1)}, bf16[128,4096]{1,0:T(8,128)(2,1)}, u32[]{:S(2)}) copy-start(bf16[128,4096]{1,0:T(8,128)(2,1)} %tok.5) | copy-start | bytes 3145732
  7.2 115.5 %reduce-scatter.2.cloned.1.call-start = ((), (), s32[]{:S(2)}) async-start(), calls=%async_computation.1 | async-start | bytes 4128768 | tf_op jit(solution)/shard_map/reduce_scatter | solution.py:266
  8.4 15.2 %collective-permute-start.2 = (bf16[128,2048]{1,0:T(8,128)(2,1)S(1)}, bf16[128,2048]{1,0:T(8,128)(2,1)S(1)}, u32[]{:S(2)}, u32[]{:S(2)}) collective-permute-start(bf16[128,2048]{1,0:T(8,128)(2,1)S(1)} %slice.24), channel_id=1, source_target_pairs={{0,4},{1,5},{2,6},{3,7},{4,0},{5,1},{6,2},{7,3},{8,12},{9,13},{10,... | collective-permute-start | bytes 1572872 | tf_op jit(solution)/shard_map/ppermute | solution.py:256
  10.7 31.4 %collective-permute-start = (bf16[128,4096]{1,0:T(8,128)(2,1)}, bf16[128,4096]{1,0:T(8,128)(2,1)}, u32[]{:S(2)}, u32[]{:S(2)}) collective-permute-start(bf16[128,4096]{1,0:T(8,128)(2,1)} %tok.5), channel_id=1, source_target_pairs={{0,1},{1,0},{2,3},{3,2},{4,5},{5,4},{6,7},{7,6},{8,9},{9,8},{10,11... | collective-permute-start | bytes 3145736 | tf_op jit(solution)/shard_map/ppermute | solution.py:256
  12.6 4.6 %collective-permute-start.3 = (f32[128,128]{1,0:T(8,128)S(1)}, f32[128,128]{1,0:T(8,128)S(1)}, u32[]{:S(2)}, u32[]{:S(2)}) collective-permute-start(f32[128,128]{1,0:T(8,128)S(1)} %fusion), channel_id=1, source_target_pairs={{0,12},{1,13},{2,14},{3,15},{4,8},{5,9},{6,10},{7,11},{8,4},{9,5},... | collective-permute-start | bytes 196616 | tf_op jit(solution)/shard_map/ppermute | solution.py:256
  17.2 6.3 %collective-permute-start.4 = (f32[128,128]{1,0:T(8,128)S(1)}, f32[128,128]{1,0:T(8,128)S(1)}, u32[]{:S(2)}, u32[]{:S(2)}) collective-permute-start(f32[128,128]{1,0:T(8,128)S(1)} %add.57), channel_id=1, source_target_pairs={{0,4},{1,5},{2,6},{3,7},{4,0},{5,1},{6,2},{7,3},{8,12},{9,13},{10,... | collective-permute-start | bytes 196616 | tf_op jit(solution)/shard_map/ppermute | solution.py:256
  18.6 16.2 %collective-permute-start.1 = (bf16[128,2048]{1,0:T(8,128)(2,1)S(1)}, bf16[128,2048]{1,0:T(8,128)(2,1)S(1)}, u32[]{:S(2)}, u32[]{:S(2)}) collective-permute-start(bf16[128,2048]{1,0:T(8,128)(2,1)S(1)} %slice.24), channel_id=1, source_target_pairs={{0,2},{1,3},{2,0},{3,1},{4,6},{5,7},{6,4},{7,5},{8,10},{9,11},{10,... | collective-permute-start | bytes 1572872 | tf_op jit(solution)/shard_map/ppermute | solution.py:256
  23.6 18.4 %copy-start.6 = (bf16[128,2048]{1,0:T(8,128)(2,1)}, bf16[128,2048]{1,0:T(8,128)(2,1)S(1)}, u32[]{:S(2)}) copy-start(bf16[128,2048]{1,0:T(8,128)(2,1)S(1)} %collective-permute-done.2.m4) | copy-start | bytes 1572868
  23.6 14.1 %collective-permute-start.9 = (bf16[128,2048]{1,0:T(8,128)(2,1)}, bf16[128,2048]{1,0:T(8,128)(2,1)S(1)}, u32[]{:S(2)}, u32[]{:S(2)}) collective-permute-start(bf16[128,2048]{1,0:T(8,128)(2,1)} %slice.25), channel_id=1, source_target_pairs={{0,4},{1,5},{2,6},{3,7},{4,0},{5,1},{6,2},{7,3},{8,12},{9,13},{10,... | collective-permute-start | bytes 1572872 | tf_op jit(solution)/shard_map/ppermute | solution.py:256
  23.9 17.2 %collective-permute-start.5 = (bf16[128,2048]{1,0:T(8,128)(2,1)S(1)}, bf16[128,2048]{1,0:T(8,128)(2,1)S(1)}, u32[]{:S(2)}, u32[]{:S(2)}) collective-permute-start(bf16[128,2048]{1,0:T(8,128)(2,1)S(1)} %collective-permute-done.2.m4), channel_id=1, source_target_pairs={{0,12},{1,13},{2,14},{3,15},{4,8},{5,9},{6,10},{7,11},{8,4},{9,5},... | collective-permute-start | bytes 1572872 | tf_op jit(solution)/shard_map/ppermute | solution.py:256
  26.5 8.3 %collective-permute-start.6 = (f32[128,128]{1,0:T(8,128)S(1)}, f32[128,128]{1,0:T(8,128)S(1)}, u32[]{:S(2)}, u32[]{:S(2)}) collective-permute-start(f32[128,128]{1,0:T(8,128)S(1)} %add.58), channel_id=1, source_target_pairs={{0,2},{1,3},{2,0},{3,1},{4,6},{5,7},{6,4},{7,5},{8,10},{9,11},{10,... | collective-permute-start | bytes 196616 | tf_op jit(solution)/shard_map/ppermute | solution.py:256
  34.8 7.2 %copy-start.7 = (bf16[128,2048]{1,0:T(8,128)(2,1)}, bf16[128,2048]{1,0:T(8,128)(2,1)S(1)}, u32[]{:S(2)}) copy-start(bf16[128,2048]{1,0:T(8,128)(2,1)S(1)} %collective-permute-done.1.m2) | copy-start | bytes 1572868
  34.8 14.9 %collective-permute-start.8 = (bf16[128,2048]{1,0:T(8,128)(2,1)}, bf16[128,2048]{1,0:T(8,128)(2,1)}, u32[]{:S(2)}, u32[]{:S(2)}) collective-permute-start(bf16[128,2048]{1,0:T(8,128)(2,1)} %slice.25), channel_id=1, source_target_pairs={{0,2},{1,3},{2,0},{3,1},{4,6},{5,7},{6,4},{7,5},{8,10},{9,11},{10,... | collective-permute-start | bytes 1572872 | tf_op jit(solution)/shard_map/ppermute | solution.py:256
  37.7 12.0 %copy-start.8 = (bf16[128,2048]{1,0:T(8,128)(2,1)}, bf16[128,2048]{1,0:T(8,128)(2,1)S(1)}, u32[]{:S(2)}) copy-start(bf16[128,2048]{1,0:T(8,128)(2,1)S(1)} %collective-permute-done.9.m4) | copy-start | bytes 1572868
  37.7 12.2 %collective-permute-start.10 = (bf16[128,2048]{1,0:T(8,128)(2,1)S(1)}, bf16[128,2048]{1,0:T(8,128)(2,1)}, u32[]{:S(2)}, u32[]{:S(2)}) collective-permute-start(bf16[128,2048]{1,0:T(8,128)(2,1)S(1)} %collective-permute-done.9.m4), channel_id=1, source_target_pairs={{0,12},{1,13},{2,14},{3,15},{4,8},{5,9},{6,10},{7,11},{8,4},{9,5},... | collective-permute-start | bytes 1572872 | tf_op jit(solution)/shard_map/ppermute | solution.py:256
  39.3 1.3 collective-permute-start.7
  41.2 0.8 copy-start.9
  57.6 1.2 copy-start.1
  57.6 1.9 %copy-start.12 = (f32[128,128]{1,0:T(8,128)S(1)}, f32[128,128]{1,0:T(8,128)}, u32[]{:S(2)}) copy-start(f32[128,128]{1,0:T(8,128)} %get-tuple-element.48) | copy-start | bytes 196612
  57.6 1.9 %copy-start.13 = (f32[128,128]{1,0:T(8,128)S(1)}, f32[128,128]{1,0:T(8,128)}, u32[]{:S(2)}) copy-start(f32[128,128]{1,0:T(8,128)} %get-tuple-element.49) | copy-start | bytes 196612
  58.9 14.0 %collective-permute-start.12 = (bf16[128,2048]{1,0:T(8,128)(2,1)S(1)}, bf16[128,2048]{1,0:T(8,128)(2,1)S(1)}, u32[]{:S(2)}, u32[]{:S(2)}) collective-permute-start(bf16[128,2048]{1,0:T(8,128)(2,1)S(1)} %constant_dynamic-slice_fusion), channel_id=1, source_target_pairs={{0,128},{16,144},{32,160},{48,176},{64,192},{80,208},{96,224},{112... | collective-permute-start | bytes 1572872 | tf_op jit(solution)/shard_map/ppermute | solution.py:273
  59.6 13.3 %collective-permute-start.11 = (f32[128,128]{1,0:T(8,128)S(1)}, f32[128,128]{1,0:T(8,128)S(1)}, u32[]{:S(2)}, u32[]{:S(2)}) collective-permute-start(f32[128,128]{1,0:T(8,128)S(1)} %add.61), channel_id=1, source_target_pairs={{0,12},{1,13},{2,14},{3,15},{4,8},{5,9},{6,10},{7,11},{8,4},{9,5},... | collective-permute-start | bytes 196616 | tf_op jit(solution)/shard_map/ppermute | solution.py:256
  67.9 36.8 %copy-start.5 = (bf16[128,2048]{1,0:T(8,128)(2,1)S(1)}, bf16[128,2048]{1,0:T(8,128)(2,1)}, u32[]{:S(2)}) copy-start(bf16[128,2048]{1,0:T(8,128)(2,1)} %get-tuple-element.61) | copy-start | bytes 1572868
  67.9 39.2 %copy-start.3 = (bf16[128,2048]{1,0:T(8,128)(2,1)S(1)}, bf16[128,2048]{1,0:T(8,128)(2,1)}, u32[]{:S(2)}) copy-start(bf16[128,2048]{1,0:T(8,128)(2,1)} %get-tuple-element.63) | copy-start | bytes 1572868
  72.9 25.1 %copy-start.4 = (bf16[128,2048]{1,0:T(8,128)(2,1)}, bf16[128,2048]{1,0:T(8,128)(2,1)S(1)}, u32[]{:S(2)}) copy-start(bf16[128,2048]{1,0:T(8,128)(2,1)S(1)} %collective-permute-done.12.others) | copy-start | bytes 1572868
  72.9 5.9 %collective-permute-start.13 = (f32[128,128]{1,0:T(8,128)S(1)}, f32[128,128]{1,0:T(8,128)S(1)}, u32[]{:S(2)}, u32[]{:S(2)}) collective-permute-start(f32[128,128]{1,0:T(8,128)S(1)} %add.63), channel_id=1, source_target_pairs={{0,2},{1,3},{2,0},{3,1},{4,6},{5,7},{6,4},{7,5},{8,10},{9,11},{10,... | collective-permute-start | bytes 196616 | tf_op jit(solution)/shard_map/ppermute | solution.py:256
  78.8 15.1 %collective-permute-start.17 = (bf16[128,4096]{1,0:T(8,128)(2,1)}, bf16[128,4096]{1,0:T(8,128)(2,1)}, u32[]{:S(2)}, u32[]{:S(2)}) collective-permute-start(bf16[128,4096]{1,0:T(8,128)(2,1)} %get-tuple-element.55), channel_id=1, source_target_pairs={{0,1},{1,0},{2,3},{3,2},{4,5},{5,4},{6,7},{7,6},{8,9},{9,8},{10,11... | collective-permute-start | bytes 3145736 | tf_op jit(solution)/shard_map/ppermute | solution.py:256
  78.9 15.0 %collective-permute-start.18 = (bf16[128,2048]{1,0:T(8,128)(2,1)}, bf16[128,2048]{1,0:T(8,128)(2,1)S(1)}, u32[]{:S(2)}, u32[]{:S(2)}) collective-permute-start(bf16[128,2048]{1,0:T(8,128)(2,1)} %get-tuple-element.57), channel_id=1, source_target_pairs={{0,12},{1,13},{2,14},{3,15},{4,8},{5,9},{6,10},{7,11},{8,4},{9,5},... | collective-permute-start | bytes 1572872 | tf_op jit(solution)/shard_map/ppermute | solution.py:256
  79.4 15.8 %collective-permute-start.14 = (bf16[128,2048]{1,0:T(8,128)(2,1)}, bf16[128,2048]{1,0:T(8,128)(2,1)}, u32[]{:S(2)}, u32[]{:S(2)}) collective-permute-start(bf16[128,2048]{1,0:T(8,128)(2,1)} %get-tuple-element.53), channel_id=1, source_target_pairs={{0,2},{1,3},{2,0},{3,1},{4,6},{5,7},{6,4},{7,5},{8,10},{9,11},{10,... | collective-permute-start | bytes 1572872 | tf_op jit(solution)/shard_map/ppermute | solution.py:256
  81.4 4.3 %collective-permute-start.15 = (f32[128,128]{1,0:T(8,128)S(1)}, f32[128,128]{1,0:T(8,128)S(1)}, u32[]{:S(2)}, u32[]{:S(2)}) collective-permute-start(f32[128,128]{1,0:T(8,128)S(1)} %add.64), channel_id=1, source_target_pairs={{0,4},{1,5},{2,6},{3,7},{4,0},{5,1},{6,2},{7,3},{8,12},{9,13},{10,... | collective-permute-start | bytes 196616 | tf_op jit(solution)/shard_map/ppermute | solution.py:256
  85.7 2.3 %collective-permute-start.16 = (f32[128,128]{1,0:T(8,128)S(1)}, f32[128,128]{1,0:T(8,128)S(1)}, u32[]{:S(2)}, u32[]{:S(2)}) collective-permute-start(f32[128,128]{1,0:T(8,128)S(1)} %add.66), channel_id=1, source_target_pairs={{0,1},{1,0},{2,3},{3,2},{4,5},{5,4},{6,7},{7,6},{8,9},{9,8},{10,11... | collective-permute-start | bytes 196616 | tf_op jit(solution)/shard_map/ppermute | solution.py:256
  85.8 21.3 %collective-permute-start.22 = (bf16[128,2048]{1,0:T(8,128)(2,1)}, bf16[128,2048]{1,0:T(8,128)(2,1)S(1)}, u32[]{:S(2)}, u32[]{:S(2)}) collective-permute-start(bf16[128,2048]{1,0:T(8,128)(2,1)} %get-tuple-element.65), channel_id=1, source_target_pairs={{0,12},{1,13},{2,14},{3,15},{4,8},{5,9},{6,10},{7,11},{8,4},{9,5},... | collective-permute-start | bytes 1572872 | tf_op jit(solution)/shard_map/ppermute | solution.py:256
  93.9 4.0 %copy-start.11 = (bf16[128,128]{1,0:T(8,128)(2,1)}, bf16[128,128]{1,0:T(8,128)(2,1)S(1)}, u32[]{:S(2)}) copy-start(bf16[128,128]{1,0:T(8,128)(2,1)S(1)} %add_convert_fusion.2.lat.refs_9_) | copy-start | bytes 98308
  93.9 4.0 %collective-permute-start.19 = (bf16[128,128]{1,0:T(8,128)(2,1)S(1)}, bf16[128,128]{1,0:T(8,128)(2,1)S(1)}, u32[]{:S(2)}, u32[]{:S(2)}) collective-permute-start(bf16[128,128]{1,0:T(8,128)(2,1)S(1)} %add_convert_fusion.2.lat.refs_9_), channel_id=1, source_target_pairs={{0,128},{16,144},{32,160},{48,176},{64,192},{80,208},{96,224},{112... | collective-permute-start | bytes 98312 | tf_op jit(solution)/shard_map/ppermute | solution.py:273
  97.9 0.6 copy-start.14
  101.6 12.0 %copy-start.2 = (bf16[8,128,256]{2,1,0:T(8,128)(2,1)S(1)}, bf16[8,128,256]{2,1,0:T(8,128)(2,1)}, u32[]{:S(2)}) copy-start(bf16[8,128,256]{2,1,0:T(8,128)(2,1)} %down_part.1) | copy-start | bytes 1572868
  102.6 11.0 %collective-permute-start.25 = (bf16[4,128,256]{2,1,0:T(8,128)(2,1)S(1)}, bf16[4,128,256]{2,1,0:T(8,128)(2,1)S(1)}, u32[]{:S(2)}, u32[]{:S(2)}) collective-permute-start(bf16[4,128,256]{2,1,0:T(8,128)(2,1)S(1)} %slice.33), channel_id=1, source_target_pairs={{0,16},{16,0},{32,48},{48,32},{64,80},{80,64},{96,112},{112,96},{1... | collective-permute-start | bytes 786440 | tf_op jit(solution)/shard_map/ppermute | solution.py:323
  104.8 17.9 %collective-permute-start.21 = (bf16[128,2048]{1,0:T(8,128)(2,1)S(1)}, bf16[128,2048]{1,0:T(8,128)(2,1)S(1)}, u32[]{:S(2)}, u32[]{:S(2)}) collective-permute-start(bf16[128,2048]{1,0:T(8,128)(2,1)S(1)} %add.68), channel_id=1, source_target_pairs={{0,4},{1,5},{2,6},{3,7},{4,0},{5,1},{6,2},{7,3},{8,12},{9,13},{10,... | collective-permute-start | bytes 1572872 | tf_op jit(solution)/shard_map/ppermute | solution.py:256
  107.2 23.3 %collective-permute-start.23 = (bf16[128,2048]{1,0:T(8,128)(2,1)S(1)}, bf16[128,2048]{1,0:T(8,128)(2,1)S(1)}, u32[]{:S(2)}, u32[]{:S(2)}) collective-permute-start(bf16[128,2048]{1,0:T(8,128)(2,1)S(1)} %add.69), channel_id=1, source_target_pairs={{0,4},{1,5},{2,6},{3,7},{4,0},{5,1},{6,2},{7,3},{8,12},{9,13},{10,... | collective-permute-start | bytes 1572872 | tf_op jit(solution)/shard_map/ppermute | solution.py:256
  107.3 23.2 %collective-permute-start.20 = (bf16[128,2048]{1,0:T(8,128)(2,1)}, bf16[128,2048]{1,0:T(8,128)(2,1)S(1)}, u32[]{:S(2)}, u32[]{:S(2)}) collective-permute-start(bf16[128,2048]{1,0:T(8,128)(2,1)} %get-tuple-element.60), channel_id=1, source_target_pairs={{0,2},{1,3},{2,0},{3,1},{4,6},{5,7},{6,4},{7,5},{8,10},{9,11},{10,... | collective-permute-start | bytes 1572872 | tf_op jit(solution)/shard_map/ppermute | solution.py:256
  113.7 8.9 %collective-permute-start.26 = (bf16[2,128,256]{2,1,0:T(8,128)(2,1)S(1)}, bf16[2,128,256]{2,1,0:T(8,128)(2,1)S(1)}, u32[]{:S(2)}, u32[]{:S(2)}) collective-permute-start(bf16[2,128,256]{2,1,0:T(8,128)(2,1)S(1)} %slice.35), channel_id=1, source_target_pairs={{0,32},{16,48},{32,0},{48,16},{64,96},{80,112},{96,64},{112,80},{1... | collective-permute-start | bytes 393224 | tf_op jit(solution)/shard_map/ppermute | solution.py:323
  122.6 0.8 copy-start.15
  124.4 12.3 %collective-permute-start.24 = (bf16[448,256]{1,0:T(8,128)(2,1)S(1)}, bf16[448,256]{1,0:T(8,128)(2,1)S(1)}, u32[]{:S(2)}, u32[]{:S(2)}) collective-permute-start(bf16[448,256]{1,0:T(8,128)(2,1)S(1)} %dynamic-slice_bitcast_fusion), channel_id=1, source_target_pairs={{0,128},{16,144},{32,160},{48,176},{64,192},{80,208},{96,224},{112... | collective-permute-start | bytes 688136 | tf_op jit(solution)/shard_map/ppermute | solution.py:273
  126.0 10.6 %collective-permute-start.27 = (bf16[1,128,256]{2,1,0:T(8,128)(2,1)S(1)}, bf16[1,128,256]{2,1,0:T(8,128)(2,1)S(1)}, u32[]{:S(2)}, u32[]{:S(2)}) collective-permute-start(bf16[1,128,256]{2,1,0:T(8,128)(2,1)S(1)} %slice.37), channel_id=1, source_target_pairs={{0,64},{16,80},{32,96},{48,112},{64,0},{80,16},{96,32},{112,48},{1... | collective-permute-start | bytes 196616 | tf_op jit(solution)/shard_map/ppermute | solution.py:323
  130.5 0.8 copy-start.16
  131.3 0.8 copy-start.17
  136.7 0.8 copy-start.10
Sparse Core Ops, SparseCore 0:
  57.8 54.9 reduce-scatter.1

commit v11 on v9

--- a/solution.py
+++ b/solution.py
@@ -312,13 +312,13 @@
     latent_grad = part.astype(BF16)
 
     z = lax.axis_index("dp") % RING
-    left = run_down(x, z, tokens, others, latent_grad, after(cross(latent_grad), r2_0))
+    left = run_down(x, z, tokens, others, latent_grad, after(cross(latent_grad), r2_0, q0))
     s0 = flip(b4_0 + after(q0, left), 4)
     r2_1 = flip(after(b2_1, left), 2)
     s1 = flip(b4_1 + after(q1, left), 4)
     other = lax.dynamic_index_in_dim(summed, 1 - x, 0, keepdims=False)
     arrived = cross(other)
-    for mask, events in ((1, (q1,)), (2, (s0,)), (4, (s1, r2_1, arrived))):
+    for mask, events in ((1, (q1, other)), (2, (s0,)), (4, (s1, r2_1, arrived))):
         count = left.shape[0] // 2
         got = lax.ppermute(left[count:], "dp", [(i, i ^ mask) for i in range(2 * RING)])
         left = left[:count].astype(F32) + after(got, *events).astype(F32)

time: 150 us -> 154 us (1.027)
  waiting for transfers between devices: 42.7 us -> 45 us
  local copies, waits for them, and re-layouts: 9.85 us -> 8.24 us
    ppermute x3, waiting for transfers between devices: 5.55 us -> 0.01 us  [per_device(): lax.ppermute(left[count:], 'dp', [(i, i ^ mask) for i in range(2 * RING)])]
    ppermute x22, waiting for transfers between devices: 32.1 us -> 37.4 us  [flip(): return lax.ppermute(value, 'tensor', [(i, i ^ mask) for i in range(16)])]
    reduce_scatter x1, waiting for transfers between devices: 0.01 us -> 2.65 us  [ring_sum(): lax.psum_scatter(grads.reshape(ring * sides * rows, width), 'dp', scatter...]
    unnamed x37 -> x35, local copies, waits for them, and re-layouts: 5.8 us -> 3.49 us
  transfers between devices with their start and end apart: 29 -> 29, of which waited for: 11 -> 14; matrix products, arithmetic and copies ran while one was open for 4% -> 5% of each run, Pallas kernels for 15% -> 14%
where the time goes in v11:
time: 154 us; the launch traced here: 153 us
  starting transfers between devices  48.9 us (32%)
  waiting for transfers between devices  45 us (29%)
  Pallas kernels  31.4 us (20%)
  between operations  14.4 us (9%)
  local copies, waits for them, and re-layouts  8.24 us (5%)
  other arithmetic  2.7 us (2%)
  matrix products  1.96 us (1%)
    ppermute x22, waiting for transfers between devices, flip(): return lax.ppermute(value, 'tensor', [(i, i ^ mask) for i in range(16)])  37.4 us
    ppermute x22, starting transfers between devices, flip(): return lax.ppermute(value, 'tensor', [(i, i ^ mask) for i in range(16)])  33.4 us
    pallas_call x2, Pallas kernels, run_main(): pl.pallas_call(main_kernel, grid=(steps,), in_specs=in_specs, out_specs=[...  15.4 us
    ppermute x3, starting transfers between devices, per_device(): lax.ppermute(left[count:], 'dp', [(i, i ^ mask) for i in range(2 * RING)])  12.4 us
    pallas_call x1, Pallas kernels, run_back(): pl.pallas_call(back_kernel, grid=(2,), in_specs=[fixed, fixed, pl.BlockSp...  6.44 us
    ppermute x3, waiting for transfers between devices, cross(): return lax.ppermute(value, 'dp', [(i, i ^ RING) for i in range(2 * RING)])  4.98 us
    pallas_call x1, Pallas kernels, run_final(): pl.pallas_call(final_kernel, grid=(steps,), in_specs=half_specs(rows, ste...  4.57 us
    unnamed x35, local copies, waits for them, and re-layouts  3.49 us
  transfers between devices with their start and end apart: 29, of which 14 were waited for; matrix products, arithmetic and copies ran while one was open for 5% of the time, Pallas kernels for 14%

profile of v11, /device:TPU:8, one launch (start us, length us, event | category | flops | bytes accessed | tf_op | source)
XLA Modules:
  0.0 152.6 jit_solution(10360672488994865622)
XLA Ops:
  7.2 0.0 copy-start
  7.2 0.0 reduce-scatter.2.cloned.1.call-start
  7.2 1.2 slice.24
  8.4 2.3 %collective-permute-start.2 = (bf16[128,2048]{1,0:T(8,128)(2,1)S(1)}, bf16[128,2048]{1,0:T(8,128)(2,1)S(1)}, u32[]{:S(2)}, u32[]{:S(2)}) collective-permute-start(bf16[128,2048]{1,0:T(8,128)(2,1)S(1)} %slice.24), channel_id=1, source_target_pairs={{0,4},{1,5},{2,6},{3,7},{4,0},{5,1},{6,2},{7,3},{8,12},{9,13},{10,... | collective-permute-start | bytes 1572872 | tf_op jit(solution)/shard_map/ppermute | solution.py:256
  10.7 2.0 %fusion = f32[128,128]{1,0:T(8,128)S(1)} fusion(bf16[128,4096]{1,0:T(8,128)(2,1)} %tok.5, bf16[4096,128]{1,0:T(8,128)(2,1)} %refs_8_.1), kind=kOutput, calls=%fused_computation.8 | convolution fusion | flops 134217728 | bytes 2162688 | tf_op jit(solution)/shard_map/dot_general | solution.py:285
  12.6 0.8 collective-permute-start.3
  13.4 3.8 %collective-permute-done.3 = f32[128,128]{1,0:T(8,128)S(1)} collective-permute-done((f32[128,128]{1,0:T(8,128)S(1)}, f32[128,128]{1,0:T(8,128)S(1)}, u32[]{:S(2)}, u32[]{:S(2)}) %collective-permute-start.3) | collective-permute-done | bytes 65568 | tf_op jit(solution)/shard_map/ppermute | solution.py:256
  17.2 1.4 collective-permute-start.4
  18.6 2.8 %collective-permute-start.1 = (bf16[128,2048]{1,0:T(8,128)(2,1)S(1)}, bf16[128,2048]{1,0:T(8,128)(2,1)S(1)}, u32[]{:S(2)}, u32[]{:S(2)}) collective-permute-start(bf16[128,2048]{1,0:T(8,128)(2,1)S(1)} %slice.24), channel_id=1, source_target_pairs={{0,2},{1,3},{2,0},{3,1},{4,6},{5,7},{6,4},{7,5},{8,10},{9,11},{10,... | collective-permute-start | bytes 1572872 | tf_op jit(solution)/shard_map/ppermute | solution.py:256
  21.4 0.8 slice.25
  22.2 1.3 collective-permute-done.4
  23.6 0.4 collective-permute-start.9
  23.9 2.6 %collective-permute-start.5 = (bf16[128,2048]{1,0:T(8,128)(2,1)S(1)}, bf16[128,2048]{1,0:T(8,128)(2,1)S(1)}, u32[]{:S(2)}, u32[]{:S(2)}) collective-permute-start(bf16[128,2048]{1,0:T(8,128)(2,1)S(1)} %collective-permute-done.2.m4), channel_id=1, source_target_pairs={{0,12},{1,13},{2,14},{3,15},{4,8},{5,9},{6,10},{7,11},{8,4},{9,5},... | collective-permute-start | bytes 1572872 | tf_op jit(solution)/shard_map/ppermute | solution.py:256
  26.5 3.0 %collective-permute-start.6 = (f32[128,128]{1,0:T(8,128)S(1)}, f32[128,128]{1,0:T(8,128)S(1)}, u32[]{:S(2)}, u32[]{:S(2)}) collective-permute-start(f32[128,128]{1,0:T(8,128)S(1)} %add.58), channel_id=1, source_target_pairs={{0,2},{1,3},{2,0},{3,1},{4,6},{5,7},{6,4},{7,5},{8,10},{9,11},{10,... | collective-permute-start | bytes 196616 | tf_op jit(solution)/shard_map/ppermute | solution.py:256
  29.5 5.3 %collective-permute-done.6 = f32[128,128]{1,0:T(8,128)S(1)} collective-permute-done((f32[128,128]{1,0:T(8,128)S(1)}, f32[128,128]{1,0:T(8,128)S(1)}, u32[]{:S(2)}, u32[]{:S(2)}) %collective-permute-start.6) | collective-permute-done | bytes 65568 | tf_op jit(solution)/shard_map/ppermute | solution.py:256
  34.8 2.9 %collective-permute-start.8 = (bf16[128,2048]{1,0:T(8,128)(2,1)}, bf16[128,2048]{1,0:T(8,128)(2,1)}, u32[]{:S(2)}, u32[]{:S(2)}) collective-permute-start(bf16[128,2048]{1,0:T(8,128)(2,1)} %slice.25), channel_id=1, source_target_pairs={{0,2},{1,3},{2,0},{3,1},{4,6},{5,7},{6,4},{7,5},{8,10},{9,11},{10,... | collective-permute-start | bytes 1572872 | tf_op jit(solution)/shard_map/ppermute | solution.py:256
  37.7 1.6 %collective-permute-start.10 = (bf16[128,2048]{1,0:T(8,128)(2,1)S(1)}, bf16[128,2048]{1,0:T(8,128)(2,1)}, u32[]{:S(2)}, u32[]{:S(2)}) collective-permute-start(bf16[128,2048]{1,0:T(8,128)(2,1)S(1)} %collective-permute-done.9.m4), channel_id=1, source_target_pairs={{0,12},{1,13},{2,14},{3,15},{4,8},{5,9},{6,10},{7,11},{8,4},{9,5},... | collective-permute-start | bytes 1572872 | tf_op jit(solution)/shard_map/ppermute | solution.py:256
  39.3 1.3 collective-permute-done.7
  40.5 0.6 add_convert_fusion.3.latent
  41.2 0.8 copy-done.9
  42.0 7.7 %main_part.2 = (bf16[128,2048]{1,0:T(8,128)(2,1)}, f32[128,128]{1,0:T(8,128)}, bf16[8,2,448,256]{3,2,1,0:T(8,128)(2,1)}) custom-call(bf16[128,4096]{1,0:T(8,128)(2,1)} %tok.5, bf16[128,4096]{1,0:T(8,128)(2,1)} %collective-permute-done.m1, bf16[128,2048]{1,0:T(8,128)(2,1)} %copy-done.7, bf16[128,2048]{1,0:T(8,128)(2,1)} %copy-done.6, ...), custom_call_target="tpu_custom_call" | custom-call | flops 2000000000 | bytes 29360128 | tf_op jit(solution)/shard_map/main_part/pallas_call | solution.py:89
  49.8 0.1 collective-permute-done.10.m8
  49.9 7.7 %main_part.3 = (bf16[128,2048]{1,0:T(8,128)(2,1)}, f32[128,128]{1,0:T(8,128)}, bf16[8,2,448,256]{3,2,1,0:T(8,128)(2,1)}) custom-call(bf16[128,4096]{1,0:T(8,128)(2,1)} %tok.5, bf16[128,4096]{1,0:T(8,128)(2,1)} %collective-permute-done.m1, bf16[128,2048]{1,0:T(8,128)(2,1)} %collective-permute-done.8.m2, ...), custom_call_target="tpu_custom_call", output_to_operand_aliasing={{2}: (10, {})} | custom-call | flops 2000000000 | bytes 29360128 | tf_op jit(solution)/shard_map/main_part/pallas_call | solution.py:89
  57.6 0.0 copy-start.12
  57.6 0.0 reduce-scatter.2.cloned.1.call-update
  57.7 1.1 copy-done.1
  58.9 0.7 collective-permute-start.12
  59.6 1.8 %collective-permute-start.11 = (f32[128,128]{1,0:T(8,128)S(1)}, f32[128,128]{1,0:T(8,128)S(1)}, u32[]{:S(2)}, u32[]{:S(2)}) collective-permute-start(f32[128,128]{1,0:T(8,128)S(1)} %add.61), channel_id=1, source_target_pairs={{0,12},{1,13},{2,14},{3,15},{4,8},{5,9},{6,10},{7,11},{8,4},{9,5},... | collective-permute-start | bytes 196616 | tf_op jit(solution)/shard_map/ppermute | solution.py:256
  61.4 6.4 %back_products.1 = (bf16[128,4096]{1,0:T(8,128)(2,1)}, bf16[128,2048]{1,0:T(8,128)(2,1)}, bf16[128,2048]{1,0:T(8,128)(2,1)}, bf16[128,2048]{1,0:T(8,128)(2,1)}, ...) custom-call(bf16[128,2048]{1,0:T(8,128)(2,1)} %get-tuple-element.41.low.refs_0_, ...), custom_call_target="tpu_custom_call" | custom-call | flops 2000000000 | bytes 20971520 | tf_op jit(solution)/shard_map/back_products/pallas_call | solution.py:136
  67.9 5.0 %collective-permute-done.12.others = bf16[128,2048]{1,0:T(8,128)(2,1)S(1)} collective-permute-done((bf16[128,2048]{1,0:T(8,128)(2,1)S(1)}, bf16[128,2048]{1,0:T(8,128)(2,1)S(1)}, u32[]{:S(2)}, u32[]{:S(2)}) %collective-permute-start.12) | collective-permute-done | bytes 524320 | tf_op jit(solution)/shard_map/ppermute | solution.py:273
  72.9 2.1 %collective-permute-start.13 = (f32[128,128]{1,0:T(8,128)S(1)}, f32[128,128]{1,0:T(8,128)S(1)}, u32[]{:S(2)}, u32[]{:S(2)}) collective-permute-start(f32[128,128]{1,0:T(8,128)S(1)} %add.63), channel_id=1, source_target_pairs={{0,2},{1,3},{2,0},{3,1},{4,6},{5,7},{6,4},{7,5},{8,10},{9,11},{10,... | collective-permute-start | bytes 196616 | tf_op jit(solution)/shard_map/ppermute | solution.py:256
  74.9 3.8 %collective-permute-done.13 = f32[128,128]{1,0:T(8,128)S(1)} collective-permute-done((f32[128,128]{1,0:T(8,128)S(1)}, f32[128,128]{1,0:T(8,128)S(1)}, u32[]{:S(2)}, u32[]{:S(2)}) %collective-permute-start.13) | collective-permute-done | bytes 65568 | tf_op jit(solution)/shard_map/ppermute | solution.py:256
  78.7 0.1 collective-permute-start.17
  78.8 0.5 collective-permute-start.19
  79.4 2.0 %collective-permute-start.14 = (bf16[128,2048]{1,0:T(8,128)(2,1)}, bf16[128,2048]{1,0:T(8,128)(2,1)S(1)}, u32[]{:S(2)}, u32[]{:S(2)}) collective-permute-start(bf16[128,2048]{1,0:T(8,128)(2,1)} %get-tuple-element.53), channel_id=1, source_target_pairs={{0,2},{1,3},{2,0},{3,1},{4,6},{5,7},{6,4},{7,5},{8,10},{9,11},{10,... | collective-permute-start | bytes 1572872 | tf_op jit(solution)/shard_map/ppermute | solution.py:256
  81.4 1.7 %collective-permute-start.15 = (f32[128,128]{1,0:T(8,128)S(1)}, f32[128,128]{1,0:T(8,128)S(1)}, u32[]{:S(2)}, u32[]{:S(2)}) collective-permute-start(f32[128,128]{1,0:T(8,128)S(1)} %add.64), channel_id=1, source_target_pairs={{0,4},{1,5},{2,6},{3,7},{4,0},{5,1},{6,2},{7,3},{8,12},{9,13},{10,... | collective-permute-start | bytes 196616 | tf_op jit(solution)/shard_map/ppermute | solution.py:256
  83.0 2.6 %collective-permute-done.15 = f32[128,128]{1,0:T(8,128)S(1)} collective-permute-done((f32[128,128]{1,0:T(8,128)S(1)}, f32[128,128]{1,0:T(8,128)S(1)}, u32[]{:S(2)}, u32[]{:S(2)}) %collective-permute-start.15) | collective-permute-done | bytes 65568 | tf_op jit(solution)/shard_map/ppermute | solution.py:256
  85.6 0.1 collective-permute-start.16
  85.7 2.1 %collective-permute-start.22 = (bf16[128,2048]{1,0:T(8,128)(2,1)}, bf16[128,2048]{1,0:T(8,128)(2,1)}, u32[]{:S(2)}, u32[]{:S(2)}) collective-permute-start(bf16[128,2048]{1,0:T(8,128)(2,1)} %get-tuple-element.65), channel_id=1, source_target_pairs={{0,12},{1,13},{2,14},{3,15},{4,8},{5,9},{6,10},{7,11},{8,4},{9,5},... | collective-permute-start | bytes 1572872 | tf_op jit(solution)/shard_map/ppermute | solution.py:256
  87.9 0.7 collective-permute-start.18
  88.6 0.6 pad_add_fusion.place
  89.2 4.7 %collective-permute-done.19 = bf16[128,2048]{1,0:T(8,128)(2,1)S(1)} collective-permute-done((bf16[128,2048]{1,0:T(8,128)(2,1)}, bf16[128,2048]{1,0:T(8,128)(2,1)S(1)}, u32[]{:S(2)}, u32[]{:S(2)}) %collective-permute-start.19) | collective-permute-done | bytes 524320 | tf_op jit(solution)/shard_map/ppermute | solution.py:256
  93.9 1.6 %collective-permute-done.14.refs_2_ = bf16[128,2048]{1,0:T(8,128)(2,1)S(1)} collective-permute-done((bf16[128,2048]{1,0:T(8,128)(2,1)}, bf16[128,2048]{1,0:T(8,128)(2,1)S(1)}, u32[]{:S(2)}, u32[]{:S(2)}) %collective-permute-start.14) | collective-permute-done | bytes 524320 | tf_op jit(solution)/shard_map/ppermute | solution.py:256
  95.5 0.7 copy-done.14
  96.1 3.1 %down_part.1 = bf16[8,128,256]{2,1,0:T(8,128)(2,1)} custom-call(s32[2]{0:T(128)} %pad_add_fusion.place, bf16[128,4096]{1,0:T(8,128)(2,1)} %tok.5, bf16[128,2048]{1,0:T(8,128)(2,1)} %copy-done.4, bf16[128,128]{1,0:T(8,128)(2,1)} %copy-done.11, bf16[128,128]{1,0:T(8,128)(2,1)} %copy-done.14), custom_call_target="tpu_custom_call" | custom-call | flops 300000000 | bytes 10485760 | tf_op jit(solution)/shard_map/down_part/pallas_call | solution.py:163
  99.2 1.7 %slice.33 = bf16[4,128,256]{2,1,0:T(8,128)(2,1)} slice(bf16[8,128,256]{2,1,0:T(8,128)(2,1)} %down_part.1), slice={[4:8], [0:128], [0:256]} | slice | bytes 524288 | tf_op jit(solution)/shard_map/slice | solution.py:323
  100.9 1.9 %collective-permute-start.25 = (bf16[4,128,256]{2,1,0:T(8,128)(2,1)}, bf16[4,128,256]{2,1,0:T(8,128)(2,1)S(1)}, u32[]{:S(2)}, u32[]{:S(2)}) collective-permute-start(bf16[4,128,256]{2,1,0:T(8,128)(2,1)} %slice.33), channel_id=1, source_target_pairs={{0,16},{16,0},{32,48},{48,32},{64,80},{80,64},{96,112},{112,96},{1... | collective-permute-start | bytes 786440 | tf_op jit(solution)/shard_map/ppermute | solution.py:323
  102.9 1.9 %collective-permute-done.22 = bf16[128,2048]{1,0:T(8,128)(2,1)} collective-permute-done((bf16[128,2048]{1,0:T(8,128)(2,1)}, bf16[128,2048]{1,0:T(8,128)(2,1)}, u32[]{:S(2)}, u32[]{:S(2)}) %collective-permute-start.22) | collective-permute-done | bytes 524320 | tf_op jit(solution)/shard_map/ppermute | solution.py:256
  104.7 1.2 add.69
  105.9 2.3 %collective-permute-start.23 = (bf16[128,2048]{1,0:T(8,128)(2,1)S(1)}, bf16[128,2048]{1,0:T(8,128)(2,1)}, u32[]{:S(2)}, u32[]{:S(2)}) collective-permute-start(bf16[128,2048]{1,0:T(8,128)(2,1)S(1)} %add.69), channel_id=1, source_target_pairs={{0,4},{1,5},{2,6},{3,7},{4,0},{5,1},{6,2},{7,3},{8,12},{9,13},{10,... | collective-permute-start | bytes 1572872 | tf_op jit(solution)/shard_map/ppermute | solution.py:256
  108.2 0.1 add.68
  108.3 0.1 collective-permute-start.21
  108.4 3.0 %collective-permute-start.20 = (bf16[128,2048]{1,0:T(8,128)(2,1)}, bf16[128,2048]{1,0:T(8,128)(2,1)}, u32[]{:S(2)}, u32[]{:S(2)}) collective-permute-start(bf16[128,2048]{1,0:T(8,128)(2,1)} %get-tuple-element.60), channel_id=1, source_target_pairs={{0,2},{1,3},{2,0},{3,1},{4,6},{5,7},{6,4},{7,5},{8,10},{9,11},{10,... | collective-permute-start | bytes 1572872 | tf_op jit(solution)/shard_map/ppermute | solution.py:256
  111.4 2.6 %reduce-scatter.2.cloned.1.call-done = bf16[896,256]{1,0:T(8,128)(2,1)} async-done(((bf16[7168,256]{1,0:T(8,128)(2,1)}), bf16[896,256]{1,0:T(8,128)(2,1)}) %reduce-scatter.2.cloned.1.call-update) | async-done | bytes 458768 | tf_op jit(solution)/shard_map/reduce_scatter | solution.py:266
  114.1 1.0 dynamic-slice_bitcast_fusion
  115.0 0.1 add_convert_fusion
  115.1 3.2 %collective-permute-start.26 = (bf16[2,128,256]{2,1,0:T(8,128)(2,1)S(1)}, bf16[2,128,256]{2,1,0:T(8,128)(2,1)S(1)}, u32[]{:S(2)}, u32[]{:S(2)}) collective-permute-start(bf16[2,128,256]{2,1,0:T(8,128)(2,1)S(1)} %slice.35), channel_id=1, source_target_pairs={{0,32},{16,48},{32,0},{48,16},{64,96},{80,112},{96,64},{112,80},{1... | collective-permute-start | bytes 393224 | tf_op jit(solution)/shard_map/ppermute | solution.py:323
  118.3 1.8 %collective-permute-start.24 = (bf16[448,256]{1,0:T(8,128)(2,1)S(1)}, bf16[448,256]{1,0:T(8,128)(2,1)S(1)}, u32[]{:S(2)}, u32[]{:S(2)}) collective-permute-start(bf16[448,256]{1,0:T(8,128)(2,1)S(1)} %dynamic-slice_bitcast_fusion), channel_id=1, source_target_pairs={{0,128},{16,144},{32,160},{48,176},{64,192},{80,208},{96,224},{112... | collective-permute-start | bytes 688136 | tf_op jit(solution)/shard_map/ppermute | solution.py:273
  120.1 1.0 collective-permute-done.23.refs_5_
  121.1 10.1 %collective-permute-done.21.refs_4_ = bf16[128,2048]{1,0:T(8,128)(2,1)S(1)} collective-permute-done((bf16[128,2048]{1,0:T(8,128)(2,1)S(1)}, bf16[128,2048]{1,0:T(8,128)(2,1)S(1)}, u32[]{:S(2)}, u32[]{:S(2)}) %collective-permute-start.21) | collective-permute-done | bytes 524320 | tf_op jit(solution)/shard_map/ppermute | solution.py:256
  131.2 7.3 %collective-permute-start.27 = (bf16[1,128,256]{2,1,0:T(8,128)(2,1)S(1)}, bf16[1,128,256]{2,1,0:T(8,128)(2,1)S(1)}, u32[]{:S(2)}, u32[]{:S(2)}) collective-permute-start(bf16[1,128,256]{2,1,0:T(8,128)(2,1)S(1)} %slice.37), channel_id=1, source_target_pairs={{0,64},{16,80},{32,96},{48,112},{64,0},{80,16},{96,32},{112,48},{1... | collective-permute-start | bytes 196616 | tf_op jit(solution)/shard_map/ppermute | solution.py:323
  138.5 4.6 %token_grad.1 = bf16[128,4096]{1,0:T(8,128)(2,1)} custom-call(bf16[128,2048]{1,0:T(8,128)(2,1)} %get-tuple-element.41.low.refs_0_, bf16[128,2048]{1,0:T(8,128)(2,1)} %get-tuple-element.46.high.refs_1_, bf16[128,2048]{1,0:T(8,128)(2,1)} %copy-done.15, bf16[128,2048]{1,0:T(8,128)(2,1)} %collective-permute-done.20.refs_3_, bf16[128,2048]{1,0:T(8,128)(2,1)} %copy-done.16, ...), custom_call_target="tpu_custom_call" | custom-call | flops 2000000000 | bytes 17825792 | tf_op jit(solution)/shard_map/token_grad/pallas_call | solution.py:201
  143.1 0.8 copy.12
  143.9 1.8 %finish.1 = (f32[64,256]{1,0:T(8,128)}, f32[4,64,256]{2,1,0:T(8,128)}, f32[128,256]{1,0:T(8,128)}) custom-call(s32[1]{0:T(128)} %bitcast.side, bf16[2,448,256]{2,1,0:T(8,128)(2,1)} %bitcast.14, bf16[448,256]{1,0:T(8,128)(2,1)} %copy-done.10), custom_call_target="tpu_custom_call" | custom-call | flops 300000 | bytes 4194304 | tf_op jit(solution)/shard_map/finish/pallas_call | solution.py:230
  (59 shorter events, 0.3 us)
Async XLA Ops:
  7.2 14.2 %copy-start = (bf16[128,4096]{1,0:T(8,128)(2,1)S(1)}, bf16[128,4096]{1,0:T(8,128)(2,1)}, u32[]{:S(2)}) copy-start(bf16[128,4096]{1,0:T(8,128)(2,1)} %tok.5) | copy-start | bytes 3145732
  7.2 106.9 %reduce-scatter.2.cloned.1.call-start = ((), (), s32[]{:S(2)}) async-start(), calls=%async_computation.1 | async-start | bytes 4128768 | tf_op jit(solution)/shard_map/reduce_scatter | solution.py:266
  8.4 15.2 %collective-permute-start.2 = (bf16[128,2048]{1,0:T(8,128)(2,1)S(1)}, bf16[128,2048]{1,0:T(8,128)(2,1)S(1)}, u32[]{:S(2)}, u32[]{:S(2)}) collective-permute-start(bf16[128,2048]{1,0:T(8,128)(2,1)S(1)} %slice.24), channel_id=1, source_target_pairs={{0,4},{1,5},{2,6},{3,7},{4,0},{5,1},{6,2},{7,3},{8,12},{9,13},{10,... | collective-permute-start | bytes 1572872 | tf_op jit(solution)/shard_map/ppermute | solution.py:256
  10.7 31.4 %collective-permute-start = (bf16[128,4096]{1,0:T(8,128)(2,1)}, bf16[128,4096]{1,0:T(8,128)(2,1)}, u32[]{:S(2)}, u32[]{:S(2)}) collective-permute-start(bf16[128,4096]{1,0:T(8,128)(2,1)} %tok.5), channel_id=1, source_target_pairs={{0,1},{1,0},{2,3},{3,2},{4,5},{5,4},{6,7},{7,6},{8,9},{9,8},{10,11... | collective-permute-start | bytes 3145736 | tf_op jit(solution)/shard_map/ppermute | solution.py:256
  12.6 4.6 %collective-permute-start.3 = (f32[128,128]{1,0:T(8,128)S(1)}, f32[128,128]{1,0:T(8,128)S(1)}, u32[]{:S(2)}, u32[]{:S(2)}) collective-permute-start(f32[128,128]{1,0:T(8,128)S(1)} %fusion), channel_id=1, source_target_pairs={{0,12},{1,13},{2,14},{3,15},{4,8},{5,9},{6,10},{7,11},{8,4},{9,5},... | collective-permute-start | bytes 196616 | tf_op jit(solution)/shard_map/ppermute | solution.py:256
  17.2 6.3 %collective-permute-start.4 = (f32[128,128]{1,0:T(8,128)S(1)}, f32[128,128]{1,0:T(8,128)S(1)}, u32[]{:S(2)}, u32[]{:S(2)}) collective-permute-start(f32[128,128]{1,0:T(8,128)S(1)} %add.57), channel_id=1, source_target_pairs={{0,4},{1,5},{2,6},{3,7},{4,0},{5,1},{6,2},{7,3},{8,12},{9,13},{10,... | collective-permute-start | bytes 196616 | tf_op jit(solution)/shard_map/ppermute | solution.py:256
  18.6 16.2 %collective-permute-start.1 = (bf16[128,2048]{1,0:T(8,128)(2,1)S(1)}, bf16[128,2048]{1,0:T(8,128)(2,1)S(1)}, u32[]{:S(2)}, u32[]{:S(2)}) collective-permute-start(bf16[128,2048]{1,0:T(8,128)(2,1)S(1)} %slice.24), channel_id=1, source_target_pairs={{0,2},{1,3},{2,0},{3,1},{4,6},{5,7},{6,4},{7,5},{8,10},{9,11},{10,... | collective-permute-start | bytes 1572872 | tf_op jit(solution)/shard_map/ppermute | solution.py:256
  23.6 18.5 %copy-start.6 = (bf16[128,2048]{1,0:T(8,128)(2,1)}, bf16[128,2048]{1,0:T(8,128)(2,1)S(1)}, u32[]{:S(2)}) copy-start(bf16[128,2048]{1,0:T(8,128)(2,1)S(1)} %collective-permute-done.2.m4) | copy-start | bytes 1572868
  23.6 14.1 %collective-permute-start.9 = (bf16[128,2048]{1,0:T(8,128)(2,1)}, bf16[128,2048]{1,0:T(8,128)(2,1)S(1)}, u32[]{:S(2)}, u32[]{:S(2)}) collective-permute-start(bf16[128,2048]{1,0:T(8,128)(2,1)} %slice.25), channel_id=1, source_target_pairs={{0,4},{1,5},{2,6},{3,7},{4,0},{5,1},{6,2},{7,3},{8,12},{9,13},{10,... | collective-permute-start | bytes 1572872 | tf_op jit(solution)/shard_map/ppermute | solution.py:256
  23.9 17.2 %collective-permute-start.5 = (bf16[128,2048]{1,0:T(8,128)(2,1)S(1)}, bf16[128,2048]{1,0:T(8,128)(2,1)S(1)}, u32[]{:S(2)}, u32[]{:S(2)}) collective-permute-start(bf16[128,2048]{1,0:T(8,128)(2,1)S(1)} %collective-permute-done.2.m4), channel_id=1, source_target_pairs={{0,12},{1,13},{2,14},{3,15},{4,8},{5,9},{6,10},{7,11},{8,4},{9,5},... | collective-permute-start | bytes 1572872 | tf_op jit(solution)/shard_map/ppermute | solution.py:256
  26.5 8.3 %collective-permute-start.6 = (f32[128,128]{1,0:T(8,128)S(1)}, f32[128,128]{1,0:T(8,128)S(1)}, u32[]{:S(2)}, u32[]{:S(2)}) collective-permute-start(f32[128,128]{1,0:T(8,128)S(1)} %add.58), channel_id=1, source_target_pairs={{0,2},{1,3},{2,0},{3,1},{4,6},{5,7},{6,4},{7,5},{8,10},{9,11},{10,... | collective-permute-start | bytes 196616 | tf_op jit(solution)/shard_map/ppermute | solution.py:256
  34.8 7.2 %copy-start.7 = (bf16[128,2048]{1,0:T(8,128)(2,1)}, bf16[128,2048]{1,0:T(8,128)(2,1)S(1)}, u32[]{:S(2)}) copy-start(bf16[128,2048]{1,0:T(8,128)(2,1)S(1)} %collective-permute-done.1.m2) | copy-start | bytes 1572868
  34.8 14.9 %collective-permute-start.8 = (bf16[128,2048]{1,0:T(8,128)(2,1)}, bf16[128,2048]{1,0:T(8,128)(2,1)}, u32[]{:S(2)}, u32[]{:S(2)}) collective-permute-start(bf16[128,2048]{1,0:T(8,128)(2,1)} %slice.25), channel_id=1, source_target_pairs={{0,2},{1,3},{2,0},{3,1},{4,6},{5,7},{6,4},{7,5},{8,10},{9,11},{10,... | collective-permute-start | bytes 1572872 | tf_op jit(solution)/shard_map/ppermute | solution.py:256
  37.7 12.0 %copy-start.8 = (bf16[128,2048]{1,0:T(8,128)(2,1)}, bf16[128,2048]{1,0:T(8,128)(2,1)S(1)}, u32[]{:S(2)}) copy-start(bf16[128,2048]{1,0:T(8,128)(2,1)S(1)} %collective-permute-done.9.m4) | copy-start | bytes 1572868
  37.7 12.2 %collective-permute-start.10 = (bf16[128,2048]{1,0:T(8,128)(2,1)S(1)}, bf16[128,2048]{1,0:T(8,128)(2,1)}, u32[]{:S(2)}, u32[]{:S(2)}) collective-permute-start(bf16[128,2048]{1,0:T(8,128)(2,1)S(1)} %collective-permute-done.9.m4), channel_id=1, source_target_pairs={{0,12},{1,13},{2,14},{3,15},{4,8},{5,9},{6,10},{7,11},{8,4},{9,5},... | collective-permute-start | bytes 1572872 | tf_op jit(solution)/shard_map/ppermute | solution.py:256
  39.3 1.3 collective-permute-start.7
  41.2 0.8 copy-start.9
  57.6 1.2 copy-start.1
  57.6 1.9 %copy-start.12 = (f32[128,128]{1,0:T(8,128)S(1)}, f32[128,128]{1,0:T(8,128)}, u32[]{:S(2)}) copy-start(f32[128,128]{1,0:T(8,128)} %get-tuple-element.48) | copy-start | bytes 196612
  57.6 1.9 %copy-start.13 = (f32[128,128]{1,0:T(8,128)S(1)}, f32[128,128]{1,0:T(8,128)}, u32[]{:S(2)}) copy-start(f32[128,128]{1,0:T(8,128)} %get-tuple-element.49) | copy-start | bytes 196612
  58.9 14.0 %collective-permute-start.12 = (bf16[128,2048]{1,0:T(8,128)(2,1)S(1)}, bf16[128,2048]{1,0:T(8,128)(2,1)S(1)}, u32[]{:S(2)}, u32[]{:S(2)}) collective-permute-start(bf16[128,2048]{1,0:T(8,128)(2,1)S(1)} %constant_dynamic-slice_fusion), channel_id=1, source_target_pairs={{0,128},{16,144},{32,160},{48,176},{64,192},{80,208},{96,224},{112... | collective-permute-start | bytes 1572872 | tf_op jit(solution)/shard_map/ppermute | solution.py:273
  59.6 13.3 %collective-permute-start.11 = (f32[128,128]{1,0:T(8,128)S(1)}, f32[128,128]{1,0:T(8,128)S(1)}, u32[]{:S(2)}, u32[]{:S(2)}) collective-permute-start(f32[128,128]{1,0:T(8,128)S(1)} %add.61), channel_id=1, source_target_pairs={{0,12},{1,13},{2,14},{3,15},{4,8},{5,9},{6,10},{7,11},{8,4},{9,5},... | collective-permute-start | bytes 196616 | tf_op jit(solution)/shard_map/ppermute | solution.py:256
  67.9 36.9 %copy-start.5 = (bf16[128,2048]{1,0:T(8,128)(2,1)S(1)}, bf16[128,2048]{1,0:T(8,128)(2,1)}, u32[]{:S(2)}) copy-start(bf16[128,2048]{1,0:T(8,128)(2,1)} %get-tuple-element.63) | copy-start | bytes 1572868
  67.9 40.3 %copy-start.3 = (bf16[128,2048]{1,0:T(8,128)(2,1)S(1)}, bf16[128,2048]{1,0:T(8,128)(2,1)}, u32[]{:S(2)}) copy-start(bf16[128,2048]{1,0:T(8,128)(2,1)} %get-tuple-element.61) | copy-start | bytes 1572868
  72.9 22.6 %copy-start.4 = (bf16[128,2048]{1,0:T(8,128)(2,1)}, bf16[128,2048]{1,0:T(8,128)(2,1)S(1)}, u32[]{:S(2)}) copy-start(bf16[128,2048]{1,0:T(8,128)(2,1)S(1)} %collective-permute-done.12.others) | copy-start | bytes 1572868
  72.9 5.9 %collective-permute-start.13 = (f32[128,128]{1,0:T(8,128)S(1)}, f32[128,128]{1,0:T(8,128)S(1)}, u32[]{:S(2)}, u32[]{:S(2)}) collective-permute-start(f32[128,128]{1,0:T(8,128)S(1)} %add.63), channel_id=1, source_target_pairs={{0,2},{1,3},{2,0},{3,1},{4,6},{5,7},{6,4},{7,5},{8,10},{9,11},{10,... | collective-permute-start | bytes 196616 | tf_op jit(solution)/shard_map/ppermute | solution.py:256
  78.7 9.1 %collective-permute-start.17 = (bf16[128,4096]{1,0:T(8,128)(2,1)}, bf16[128,4096]{1,0:T(8,128)(2,1)}, u32[]{:S(2)}, u32[]{:S(2)}) collective-permute-start(bf16[128,4096]{1,0:T(8,128)(2,1)} %get-tuple-element.55), channel_id=1, source_target_pairs={{0,1},{1,0},{2,3},{3,2},{4,5},{5,4},{6,7},{7,6},{8,9},{9,8},{10,11... | collective-permute-start | bytes 3145736 | tf_op jit(solution)/shard_map/ppermute | solution.py:256
  78.8 15.0 %collective-permute-start.19 = (bf16[128,2048]{1,0:T(8,128)(2,1)}, bf16[128,2048]{1,0:T(8,128)(2,1)S(1)}, u32[]{:S(2)}, u32[]{:S(2)}) collective-permute-start(bf16[128,2048]{1,0:T(8,128)(2,1)} %get-tuple-element.58), channel_id=1, source_target_pairs={{0,12},{1,13},{2,14},{3,15},{4,8},{5,9},{6,10},{7,11},{8,4},{9,5},... | collective-permute-start | bytes 1572872 | tf_op jit(solution)/shard_map/ppermute | solution.py:256
  79.4 16.0 %collective-permute-start.14 = (bf16[128,2048]{1,0:T(8,128)(2,1)}, bf16[128,2048]{1,0:T(8,128)(2,1)S(1)}, u32[]{:S(2)}, u32[]{:S(2)}) collective-permute-start(bf16[128,2048]{1,0:T(8,128)(2,1)} %get-tuple-element.53), channel_id=1, source_target_pairs={{0,2},{1,3},{2,0},{3,1},{4,6},{5,7},{6,4},{7,5},{8,10},{9,11},{10,... | collective-permute-start | bytes 1572872 | tf_op jit(solution)/shard_map/ppermute | solution.py:256
  81.4 4.3 %collective-permute-start.15 = (f32[128,128]{1,0:T(8,128)S(1)}, f32[128,128]{1,0:T(8,128)S(1)}, u32[]{:S(2)}, u32[]{:S(2)}) collective-permute-start(f32[128,128]{1,0:T(8,128)S(1)} %add.64), channel_id=1, source_target_pairs={{0,4},{1,5},{2,6},{3,7},{4,0},{5,1},{6,2},{7,3},{8,12},{9,13},{10,... | collective-permute-start | bytes 196616 | tf_op jit(solution)/shard_map/ppermute | solution.py:256
  85.6 2.2 %collective-permute-start.16 = (f32[128,128]{1,0:T(8,128)S(1)}, f32[128,128]{1,0:T(8,128)S(1)}, u32[]{:S(2)}, u32[]{:S(2)}) collective-permute-start(f32[128,128]{1,0:T(8,128)S(1)} %add.66), channel_id=1, source_target_pairs={{0,1},{1,0},{2,3},{3,2},{4,5},{5,4},{6,7},{7,6},{8,9},{9,8},{10,11... | collective-permute-start | bytes 196616 | tf_op jit(solution)/shard_map/ppermute | solution.py:256
  85.7 19.0 %collective-permute-start.22 = (bf16[128,2048]{1,0:T(8,128)(2,1)}, bf16[128,2048]{1,0:T(8,128)(2,1)}, u32[]{:S(2)}, u32[]{:S(2)}) collective-permute-start(bf16[128,2048]{1,0:T(8,128)(2,1)} %get-tuple-element.65), channel_id=1, source_target_pairs={{0,12},{1,13},{2,14},{3,15},{4,8},{5,9},{6,10},{7,11},{8,4},{9,5},... | collective-permute-start | bytes 1572872 | tf_op jit(solution)/shard_map/ppermute | solution.py:256
  87.9 7.5 %copy-start.11 = (bf16[128,128]{1,0:T(8,128)(2,1)}, bf16[128,128]{1,0:T(8,128)(2,1)S(1)}, u32[]{:S(2)}) copy-start(bf16[128,128]{1,0:T(8,128)(2,1)S(1)} %add_convert_fusion.2.lat.refs_9_) | copy-start | bytes 98308
  87.9 7.5 %collective-permute-start.18 = (bf16[128,128]{1,0:T(8,128)(2,1)S(1)}, bf16[128,128]{1,0:T(8,128)(2,1)S(1)}, u32[]{:S(2)}, u32[]{:S(2)}) collective-permute-start(bf16[128,128]{1,0:T(8,128)(2,1)S(1)} %add_convert_fusion.2.lat.refs_9_), channel_id=1, source_target_pairs={{0,128},{16,144},{32,160},{48,176},{64,192},{80,208},{96,224},{112... | collective-permute-start | bytes 98312 | tf_op jit(solution)/shard_map/ppermute | solution.py:273
  95.4 9.3 %copy-start.15 = (bf16[128,2048]{1,0:T(8,128)(2,1)}, bf16[128,2048]{1,0:T(8,128)(2,1)S(1)}, u32[]{:S(2)}) copy-start(bf16[128,2048]{1,0:T(8,128)(2,1)S(1)} %collective-permute-done.14.refs_2_) | copy-start | bytes 1572868
  95.4 0.7 copy-start.14
  99.2 15.8 %copy-start.2 = (bf16[8,128,256]{2,1,0:T(8,128)(2,1)S(1)}, bf16[8,128,256]{2,1,0:T(8,128)(2,1)}, u32[]{:S(2)}) copy-start(bf16[8,128,256]{2,1,0:T(8,128)(2,1)} %down_part.1) | copy-start | bytes 1572868
  100.9 14.1 %collective-permute-start.25 = (bf16[4,128,256]{2,1,0:T(8,128)(2,1)}, bf16[4,128,256]{2,1,0:T(8,128)(2,1)S(1)}, u32[]{:S(2)}, u32[]{:S(2)}) collective-permute-start(bf16[4,128,256]{2,1,0:T(8,128)(2,1)} %slice.33), channel_id=1, source_target_pairs={{0,16},{16,0},{32,48},{48,32},{64,80},{80,64},{96,112},{112,96},{1... | collective-permute-start | bytes 786440 | tf_op jit(solution)/shard_map/ppermute | solution.py:323
  105.9 15.2 %collective-permute-start.23 = (bf16[128,2048]{1,0:T(8,128)(2,1)S(1)}, bf16[128,2048]{1,0:T(8,128)(2,1)}, u32[]{:S(2)}, u32[]{:S(2)}) collective-permute-start(bf16[128,2048]{1,0:T(8,128)(2,1)S(1)} %add.69), channel_id=1, source_target_pairs={{0,4},{1,5},{2,6},{3,7},{4,0},{5,1},{6,2},{7,3},{8,12},{9,13},{10,... | collective-permute-start | bytes 1572872 | tf_op jit(solution)/shard_map/ppermute | solution.py:256
  108.3 22.8 %collective-permute-start.21 = (bf16[128,2048]{1,0:T(8,128)(2,1)S(1)}, bf16[128,2048]{1,0:T(8,128)(2,1)S(1)}, u32[]{:S(2)}, u32[]{:S(2)}) collective-permute-start(bf16[128,2048]{1,0:T(8,128)(2,1)S(1)} %add.68), channel_id=1, source_target_pairs={{0,4},{1,5},{2,6},{3,7},{4,0},{5,1},{6,2},{7,3},{8,12},{9,13},{10,... | collective-permute-start | bytes 1572872 | tf_op jit(solution)/shard_map/ppermute | solution.py:256
  108.4 30.1 %collective-permute-start.20 = (bf16[128,2048]{1,0:T(8,128)(2,1)}, bf16[128,2048]{1,0:T(8,128)(2,1)}, u32[]{:S(2)}, u32[]{:S(2)}) collective-permute-start(bf16[128,2048]{1,0:T(8,128)(2,1)} %get-tuple-element.60), channel_id=1, source_target_pairs={{0,2},{1,3},{2,0},{3,1},{4,6},{5,7},{6,4},{7,5},{8,10},{9,11},{10,... | collective-permute-start | bytes 1572872 | tf_op jit(solution)/shard_map/ppermute | solution.py:256
  115.1 16.0 %collective-permute-start.26 = (bf16[2,128,256]{2,1,0:T(8,128)(2,1)S(1)}, bf16[2,128,256]{2,1,0:T(8,128)(2,1)S(1)}, u32[]{:S(2)}, u32[]{:S(2)}) collective-permute-start(bf16[2,128,256]{2,1,0:T(8,128)(2,1)S(1)} %slice.35), channel_id=1, source_target_pairs={{0,32},{16,48},{32,0},{48,16},{64,96},{80,112},{96,64},{112,80},{1... | collective-permute-start | bytes 393224 | tf_op jit(solution)/shard_map/ppermute | solution.py:323
  118.3 24.8 %collective-permute-start.24 = (bf16[448,256]{1,0:T(8,128)(2,1)S(1)}, bf16[448,256]{1,0:T(8,128)(2,1)S(1)}, u32[]{:S(2)}, u32[]{:S(2)}) collective-permute-start(bf16[448,256]{1,0:T(8,128)(2,1)S(1)} %dynamic-slice_bitcast_fusion), channel_id=1, source_target_pairs={{0,128},{16,144},{32,160},{48,176},{64,192},{80,208},{96,224},{112... | collective-permute-start | bytes 688136 | tf_op jit(solution)/shard_map/ppermute | solution.py:273
  131.2 7.3 %copy-start.16 = (bf16[128,2048]{1,0:T(8,128)(2,1)}, bf16[128,2048]{1,0:T(8,128)(2,1)S(1)}, u32[]{:S(2)}) copy-start(bf16[128,2048]{1,0:T(8,128)(2,1)S(1)} %collective-permute-done.21.refs_4_) | copy-start | bytes 1572868
  131.2 11.9 %collective-permute-start.27 = (bf16[1,128,256]{2,1,0:T(8,128)(2,1)S(1)}, bf16[1,128,256]{2,1,0:T(8,128)(2,1)S(1)}, u32[]{:S(2)}, u32[]{:S(2)}) collective-permute-start(bf16[1,128,256]{2,1,0:T(8,128)(2,1)S(1)} %slice.37), channel_id=1, source_target_pairs={{0,64},{16,80},{32,96},{48,112},{64,0},{80,16},{96,32},{112,48},{1... | collective-permute-start | bytes 196616 | tf_op jit(solution)/shard_map/ppermute | solution.py:323
  143.1 0.8 copy-start.10
Sparse Core Ops, SparseCore 0:
  57.8 56.2 reduce-scatter.1
